TPU v7x, 512 devices: a whole 4x8x8 slice. The times are simulated.
512 devices in a mesh: row: 64 (over z_lo, y, core), col: 8 (over z_hi, x).
Axes of the slice: x: 4, y: 8, z: 8 (z_hi: 2, z_lo: 4; z = z_hi * 4 + z_lo), core: 2. Of those that a mesh axis runs over, the one named last changes fastest.
Arguments:
- query: bfloat16 [32768, 2560], P(('row', 'col')), may hold values from -6 to 6
- key: bfloat16 [32768, 2560], P(('row', 'col')), may hold values from -6 to 6
- value: bfloat16 [32768, 2560], P(('row', 'col')), may hold values from -6 to 6
- saved_out: bfloat16 [32768, 2560], P(('row', 'col')), may hold values from -6 to 6
- grad_out: bfloat16 [32768, 2560], P(('row', 'col')), may hold values from -6 to 6
- frame_ids: int32 [32768], P(('row', 'col')), may hold values from 0 to 15, never falling along the last dimension, each value on 1 to 4096 neighbouring positions
Outputs:
- grad_query: bfloat16 [32768, 2560], P(('row', 'col'))
- grad_key: bfloat16 [32768, 2560], P(('row', 'col'))
- grad_value: bfloat16 [32768, 2560], P(('row', 'col'))
Inputs may be any that keep to these rules, and one draw needn't show every extreme that they name: `frame_ids`: never falls along the tokens; every frame 0 to 15 is present.
All inputs are finite; a program needn't handle non-finite values.
Results may differ from a plain program's by a relative error of at most 0.015.
Values may be sent and summed in bfloat16 or wider, within the bound.
No kernel may reach another device: no remote copies, remote signals or barrier semaphores. Data moves between devices by JAX's collectives and lax.ppermute only.
A program may use at most 64 MiB of HBM per device.

v0:
```python
import jax
import jax.numpy as jnp
from jax import lax
from jax.sharding import PartitionSpec as P

HEADS = 20
HDIM = 128
WBLK = 4


def passed_along(value, axis, steps):
    count = lax.axis_size(axis)
    first, last = (max(0, -steps), min(count, count - steps))
    return lax.ppermute(value, axis, [(source, source + steps) for source in range(first, last)])


def head_dots(grads, saved):
    count = grads.shape[0]
    product = (grads.astype(jnp.float32) * saved.astype(jnp.float32)).reshape(count, HEADS, HDIM)
    return jnp.sum(product, axis=2).T


def per_device(query, key, value, saved_out, grad_out, frame_ids):
    factor = HDIM ** (-0.5)
    tok_dev = query.shape[0]
    n_col = lax.axis_size("col")
    q_rows = tok_dev * n_col
    k_rows = tok_dev * WBLK
    width = HEADS * HDIM
    row_index = lax.axis_index("row")
    q_block, o_block, g_block, q_frame = (
        lax.all_gather(query, "col", axis=0, tiled=True),
        lax.all_gather(saved_out, "col", axis=0, tiled=True),
        lax.all_gather(grad_out, "col", axis=0, tiled=True),
        lax.all_gather(frame_ids, "col", axis=0, tiled=True),
    )
    dot_block = head_dots(g_block, o_block)
    key_list = [key]
    value_list = [value]
    frame_list = [frame_ids]
    valid_list = []
    for step in range(WBLK):
        if step > 0:
            far_key, far_value, far_frame = passed_along((key, value, frame_ids), "row", step)
            key_list.append(far_key)
            value_list.append(far_value)
            frame_list.append(far_frame)
        valid_list.append(jnp.broadcast_to(row_index - step >= 0, (tok_dev,)))
    k_win = jnp.concatenate(key_list, axis=0)
    v_win = jnp.concatenate(value_list, axis=0)
    k_frame = jnp.concatenate(frame_list, axis=0)
    k_valid = jnp.concatenate(valid_list, axis=0)
    allowed = k_valid[None, :] & (k_frame[None, :] <= q_frame[:, None])

    def head_stats(head):
        q_head = lax.dynamic_slice_in_dim(q_block, head * HDIM, HDIM, 1)
        k_head = lax.dynamic_slice_in_dim(k_win, head * HDIM, HDIM, 1)
        scores = (
            jnp.einsum("qd,kd->qk", q_head, k_head, preferred_element_type=jnp.float32) * factor
        )
        peak = jnp.max(jnp.where(allowed, scores, jnp.float32(-1e30)), axis=1)
        total = jnp.sum(jnp.where(allowed, jnp.exp(scores - peak[:, None]), 0.0), axis=1)
        return (peak, total)

    local_max, local_sum = lax.map(head_stats, jnp.arange(HEADS, dtype=jnp.int32))
    row_max = lax.pmax(local_max.astype(jnp.bfloat16), "col").astype(local_max.dtype)
    row_sum = lax.psum(local_sum * jnp.exp(local_max - row_max), "col")
    log_total = row_max + jnp.log(row_sum)

    def head_grads(head, carry):
        grad_q, grad_k, grad_v = carry
        start = head * HDIM
        q_head = lax.dynamic_slice_in_dim(q_block, start, HDIM, 1)
        g_head = lax.dynamic_slice_in_dim(g_block, start, HDIM, 1)
        k_head = lax.dynamic_slice_in_dim(k_win, start, HDIM, 1)
        v_head = lax.dynamic_slice_in_dim(v_win, start, HDIM, 1)
        scores = (
            jnp.einsum("qd,kd->qk", q_head, k_head, preferred_element_type=jnp.float32) * factor
        )
        head_total = lax.dynamic_index_in_dim(log_total, head, 0, keepdims=False)
        head_dot = lax.dynamic_index_in_dim(dot_block, head, 0, keepdims=False)
        probs = jnp.where(allowed, jnp.exp(scores - head_total[:, None]), 0.0)
        part_v = jnp.einsum(
            "qk,qd->kd", probs.astype(jnp.bfloat16), g_head, preferred_element_type=jnp.float32
        )
        grad_probs = jnp.einsum("qd,kd->qk", g_head, v_head, preferred_element_type=jnp.float32)
        grad_scores = (probs * (grad_probs - head_dot[:, None]) * factor).astype(jnp.bfloat16)
        part_q = jnp.einsum("qk,kd->qd", grad_scores, k_head, preferred_element_type=jnp.float32)
        part_k = jnp.einsum("qk,qd->kd", grad_scores, q_head, preferred_element_type=jnp.float32)
        grad_q = lax.dynamic_update_slice_in_dim(grad_q, part_q, start, 1)
        grad_k = lax.dynamic_update_slice_in_dim(grad_k, part_k, start, 1)
        grad_v = lax.dynamic_update_slice_in_dim(grad_v, part_v, start, 1)
        return (grad_q, grad_k, grad_v)

    empty_grads = (
        jnp.zeros((q_rows, width), jnp.float32),
        jnp.zeros((k_rows, width), jnp.float32),
        jnp.zeros((k_rows, width), jnp.float32),
    )
    grad_q, grad_k, grad_v = lax.fori_loop(0, HEADS, head_grads, empty_grads)
    query_sum = lax.psum_scatter(
        grad_q.astype(jnp.bfloat16), "col", scatter_dimension=0, tiled=True
    )
    key_sum = grad_k[:tok_dev]
    value_sum = grad_v[:tok_dev]
    for step in range(1, WBLK):
        back_key, back_value = (
            passed_along(
                grad_k[step * tok_dev : (step + 1) * tok_dev].astype(jnp.bfloat16), "row", -step
            ).astype(jnp.float32),
            passed_along(
                grad_v[step * tok_dev : (step + 1) * tok_dev].astype(jnp.bfloat16), "row", -step
            ).astype(jnp.float32),
        )
        key_sum = key_sum + back_key
        value_sum = value_sum + back_value
    return (query_sum, key_sum.astype(jnp.bfloat16), value_sum.astype(jnp.bfloat16))


def solution(mesh):
    placed = (
        P(("row", "col"), None),
        P(("row", "col"), None),
        P(("row", "col"), None),
        P(("row", "col"), None),
        P(("row", "col"), None),
        P(("row", "col")),
    )
    return jax.shard_map(
        per_device,
        mesh=mesh,
        in_specs=placed,
        out_specs=(P(("row", "col"), None), P(("row", "col"), None), P(("row", "col"), None)),
        check_vma=False,
    )
```

profile of v0, /device:TPU:16, one launch (start us, length us, event | category | flops | bytes accessed | tf_op | source)
XLA Modules:
  0.0 609.9 jit_solution(17037723539787219402)
XLA Ops:
  8.7 2.9 collective-permute-start.5
  11.6 4.7 collective-permute-start.4
  16.3 2.4 collective-permute-start.3
  18.8 2.6 collective-permute-start.1
  21.4 1.9 collective-permute-start
  27.2 19.6 %all-reduce = s32[512]{0:T(512)S(1)} all-reduce(s32[512]{0:T(512)S(1)} %dynamic-update-slice), channel_id=1, replica_groups=mesh['row'=64,'col'=8] {'col'}, use_global_device_ids=true, to_apply=%add | all-reduce | flops 512 | bytes 4096
  46.9 1.9 collective-permute-start.2
  48.8 4.3 collective-permute-start.7
  53.2 1.9 collective-permute-start.6
  55.8 2.9 collective-permute-start.8
  59.8 8.1 %collective-permute-done.7 = bf16[64,2560]{1,0:T(8,128)(2,1)S(1)} collective-permute-done((bf16[64,2560]{1,0:T(8,128)(2,1)}, bf16[64,2560]{1,0:T(8,128)(2,1)S(1)}, u32[]{:S(2)}, u32[]{:S(2)}) %collective-permute-start.7) | collective-permute-done | bytes 327712 | tf_op jit(solution)/shard_map/ppermute | solution.py:14
  67.9 7.8 %collective-permute-done.6 = bf16[64,2560]{1,0:T(8,128)(2,1)S(1)} collective-permute-done((bf16[64,2560]{1,0:T(8,128)(2,1)}, bf16[64,2560]{1,0:T(8,128)(2,1)S(1)}, u32[]{:S(2)}, u32[]{:S(2)}) %collective-permute-start.6) | collective-permute-done | bytes 327712 | tf_op jit(solution)/shard_map/ppermute | solution.py:14
  75.7 7.1 %collective-permute-done.8 = bf16[64,2560]{1,0:T(8,128)(2,1)S(1)} collective-permute-done((bf16[64,2560]{1,0:T(8,128)(2,1)}, bf16[64,2560]{1,0:T(8,128)(2,1)S(1)}, u32[]{:S(2)}, u32[]{:S(2)}) %collective-permute-start.8) | collective-permute-done | bytes 327712 | tf_op jit(solution)/shard_map/ppermute | solution.py:14
  84.0 23.3 %all-gather.4.cloned.1.call-done = bf16[512,2560]{1,0:T(8,128)(2,1)} async-done(((bf16[64,2560]{1,0:T(8,128)(2,1)}), bf16[512,2560]{1,0:T(8,128)(2,1)}) %all-gather.4.cloned.1.call-update) | async-done | bytes 2621456 | tf_op jit(solution)/shard_map/all_gather | solution.py:32
  107.3 55.7 %while.31 = (s32[]{:T(128)}, f32[20,512]{1,0:T(8,128)S(1)}, f32[20,512]{1,0:T(8,128)S(1)}, s32[20]{0:T(128)S(1)}, bf16[512,2560]{1,0:T(8,128)(2,1)}, /*index=5*/...) while((s32[]{:T(128)}, f32[20,512]{1,0:T(8,128)S(1)}, ...), condition=%wide.region_3.4_spmd.clone, body=%wide.region_0.3_spmd.clone.sunk | while | flops 34864132 | bytes 1267655 | solution.py:65
  164.0 43.3 %all-gather.8.cloned.1.call-done = bf16[512,2560]{1,0:T(8,128)(2,1)} async-done(((bf16[64,2560]{1,0:T(8,128)(2,1)}), bf16[512,2560]{1,0:T(8,128)(2,1)}) %all-gather.8.cloned.1.call-update) | async-done | bytes 2621456 | tf_op jit(solution)/shard_map/all_gather | solution.py:33
  207.3 3.0 copy.13
  210.3 50.1 %pmax.7 = bf16[20,512]{1,0:T(8,128)(2,1)S(1)} all-reduce(bf16[20,512]{1,0:T(8,128)(2,1)S(1)} %convert_element_type.59), channel_id=1, replica_groups=mesh['row'=64,'col'=8] {'col'}, use_global_device_ids=true, to_apply=%region_4.5 | all-reduce | flops 10240 | bytes 40960 | tf_op jit(solution)/shard_map/pmax | solution.py:66
  260.4 53.8 %psum.7 = f32[20,512]{1,0:T(8,128)S(1)} all-reduce(f32[20,512]{1,0:T(8,128)S(1)} %fusion.27), channel_id=1, replica_groups=mesh['row'=64,'col'=8] {'col'}, use_global_device_ids=true, to_apply=%region_5.6 | all-reduce | flops 10240 | bytes 81920 | tf_op jit(solution)/shard_map/psum | solution.py:67
  314.2 4.4 copy.12
  318.7 4.8 convert_multiply_fusion
  323.5 3.2 reduce_sum.18
  326.9 1.8 broadcast.20
  330.4 143.7 %while.32 = (s32[]{:T(128)}, bf16[512,2560]{1,0:T(8,128)(2,1)}, f32[256,2560]{1,0:T(8,128)}, f32[256,2560]{1,0:T(8,128)S(1)}, bf16[512,2560]{1,0:T(8,128)(2,1)},...) while((s32[]{:T(128)}, bf16[512,2560]{1,0:T(8,128)(2,1)}, ...), condition=%wide.region_8.9_spmd.clone, body=%wide.region_7.8_spmd.clone.sunk | while | flops 169082880 | bytes 3625431 | solution.py:100
  334.0 1.9 convolution_dynamic-update-slice_fusion.7
  341.2 1.8 convolution_dynamic-update-slice_fusion.7
  343.1 1.8 convolution_dynamic-update-slice_fusion.6
  348.4 1.9 convolution_dynamic-update-slice_fusion.7
  355.6 1.8 convolution_dynamic-update-slice_fusion.7
  357.5 1.8 convolution_dynamic-update-slice_fusion.6
  362.8 1.8 convolution_dynamic-update-slice_fusion.7
  364.6 1.8 convolution_dynamic-update-slice_fusion.6
  370.0 1.8 convolution_dynamic-update-slice_fusion.7
  371.8 1.8 convolution_dynamic-update-slice_fusion.6
  377.2 1.8 convolution_dynamic-update-slice_fusion.7
  384.4 1.9 convolution_dynamic-update-slice_fusion.7
  391.6 1.8 convolution_dynamic-update-slice_fusion.7
  398.7 1.8 convolution_dynamic-update-slice_fusion.7
  405.9 1.8 convolution_dynamic-update-slice_fusion.7
  413.0 1.9 convolution_dynamic-update-slice_fusion.7
  420.2 1.9 convolution_dynamic-update-slice_fusion.7
  422.1 1.8 convolution_dynamic-update-slice_fusion.6
  427.5 1.8 convolution_dynamic-update-slice_fusion.7
  429.3 1.8 convolution_dynamic-update-slice_fusion.6
  434.6 1.8 convolution_dynamic-update-slice_fusion.7
  441.8 1.9 convolution_dynamic-update-slice_fusion.7
  449.0 1.9 convolution_dynamic-update-slice_fusion.7
  450.8 1.8 convolution_dynamic-update-slice_fusion.6
  456.2 1.9 convolution_dynamic-update-slice_fusion.7
  458.0 1.8 convolution_dynamic-update-slice_fusion.6
  463.4 1.8 convolution_dynamic-update-slice_fusion.7
  470.5 1.9 convolution_dynamic-update-slice_fusion.7
  474.4 2.1 collective-permute-start.12
  476.4 2.5 collective-permute-start.14
  479.0 1.9 collective-permute-start.13
  481.1 2.0 collective-permute-start.9
  483.1 1.9 collective-permute-start.11
  485.0 1.9 collective-permute-start.10
  487.0 5.9 collective-permute-done.14
  492.9 9.3 %collective-permute-done.13 = bf16[64,2560]{1,0:T(8,128)(2,1)S(1)} collective-permute-done((bf16[64,2560]{1,0:T(8,128)(2,1)S(1)}, bf16[64,2560]{1,0:T(8,128)(2,1)S(1)}, u32[]{:S(2)}, u32[]{:S(2)}) %collective-permute-start.13) | collective-permute-done | bytes 327712 | tf_op jit(solution)/shard_map/ppermute | solution.py:14
  503.1 4.0 collective-permute-done.9
  507.2 9.0 %collective-permute-done.11 = bf16[64,2560]{1,0:T(8,128)(2,1)S(1)} collective-permute-done((bf16[64,2560]{1,0:T(8,128)(2,1)S(1)}, bf16[64,2560]{1,0:T(8,128)(2,1)S(1)}, u32[]{:S(2)}, u32[]{:S(2)}) %collective-permute-start.11) | collective-permute-done | bytes 327712 | tf_op jit(solution)/shard_map/ppermute | solution.py:14
  516.1 5.5 collective-permute-done.10
  522.5 80.9 %reduce-scatter.2.cloned.1.call-done = bf16[64,2560]{1,0:T(8,128)(2,1)} async-done(((bf16[512,2560]{1,0:T(8,128)(2,1)}), bf16[64,2560]{1,0:T(8,128)(2,1)}) %reduce-scatter.2.cloned.1.call-update) | async-done | bytes 327696 | tf_op jit(solution)/shard_map/reduce_scatter | solution.py:101
  (242 shorter events, 146.7 us)
Async XLA Ops:
  7.2 75.7 %copy-start.1 = (bf16[64,2560]{1,0:T(8,128)(2,1)S(1)}, bf16[64,2560]{1,0:T(8,128)(2,1)}, u32[]{:S(2)}) copy-start(bf16[64,2560]{1,0:T(8,128)(2,1)} %param.12) | copy-start | bytes 983044
  7.2 100.1 %all-gather.4.cloned.1.call-start = ((), (), s32[]{:S(2)}) async-start(), calls=%async_computation.1 | async-start | bytes 2949120 | tf_op jit(solution)/shard_map/all_gather | solution.py:32
  7.9 199.4 %all-gather.8.cloned.1.call-start = ((), (), s32[]{:S(2)}) async-start(), calls=%async_computation.3 | async-start | bytes 2949120 | tf_op jit(solution)/shard_map/all_gather | solution.py:33
  8.7 305.6 %all-gather.6.cloned.1.call-start = ((), (), s32[]{:S(2)}) async-start(), calls=%async_computation.2 | async-start | bytes 2949120 | tf_op jit(solution)/shard_map/all_gather | solution.py:34
  8.7 38.2 %collective-permute-start.5 = (s32[64]{0:T(128)}, s32[64]{0:T(128)S(1)}, u32[]{:S(2)}, u32[]{:S(2)}) collective-permute-start(s32[64]{0:T(128)} %param.15), channel_id=1, source_target_pairs={{0,24},{8,32},{16,40},{24,48},{32,56},{40,64},{48,72},{56,80},{64,... | collective-permute-start | bytes 776 | tf_op jit(solution)/shard_map/ppermute | solution.py:14
  11.6 37.2 %collective-permute-start.4 = (s32[64]{0:T(128)}, s32[64]{0:T(128)S(1)}, u32[]{:S(2)}, u32[]{:S(2)}) collective-permute-start(s32[64]{0:T(128)} %param.15), channel_id=1, source_target_pairs={{0,16},{8,24},{16,32},{24,40},{32,48},{40,56},{48,64},{56,72},{64,... | collective-permute-start | bytes 776 | tf_op jit(solution)/shard_map/ppermute | solution.py:14
  16.3 36.8 %collective-permute-start.3 = (s32[64]{0:T(128)}, s32[64]{0:T(128)S(1)}, u32[]{:S(2)}, u32[]{:S(2)}) collective-permute-start(s32[64]{0:T(128)} %param.15), channel_id=1, source_target_pairs={{0,8},{8,16},{16,24},{24,32},{32,40},{40,48},{48,56},{56,64},{64,7... | collective-permute-start | bytes 776 | tf_op jit(solution)/shard_map/ppermute | solution.py:14
  18.8 40.0 %collective-permute-start.1 = (bf16[64,2560]{1,0:T(8,128)(2,1)}, bf16[64,2560]{1,0:T(8,128)(2,1)S(1)}, u32[]{:S(2)}, u32[]{:S(2)}) collective-permute-start(bf16[64,2560]{1,0:T(8,128)(2,1)} %param.11), channel_id=1, source_target_pairs={{0,16},{8,24},{16,32},{24,40},{32,48},{40,56},{48,64},{56,72},{64,... | collective-permute-start | bytes 983048 | tf_op jit(solution)/shard_map/ppermute | solution.py:14
  21.4 34.5 %collective-permute-start = (bf16[64,2560]{1,0:T(8,128)(2,1)}, bf16[64,2560]{1,0:T(8,128)(2,1)S(1)}, u32[]{:S(2)}, u32[]{:S(2)}) collective-permute-start(bf16[64,2560]{1,0:T(8,128)(2,1)} %param.11), channel_id=1, source_target_pairs={{0,8},{8,16},{16,24},{24,32},{32,40},{40,48},{48,56},{56,64},{64,7... | collective-permute-start | bytes 983048 | tf_op jit(solution)/shard_map/ppermute | solution.py:14
  23.3 580.1 %reduce-scatter.2.cloned.1.call-start = ((), (), s32[]{:S(2)}) async-start(), calls=%async_computation.4 | async-start | bytes 2949120 | tf_op jit(solution)/shard_map/reduce_scatter | solution.py:101
  46.9 12.9 %collective-permute-start.2 = (bf16[64,2560]{1,0:T(8,128)(2,1)}, bf16[64,2560]{1,0:T(8,128)(2,1)S(1)}, u32[]{:S(2)}, u32[]{:S(2)}) collective-permute-start(bf16[64,2560]{1,0:T(8,128)(2,1)} %param.11), channel_id=1, source_target_pairs={{0,24},{8,32},{16,40},{24,48},{32,56},{40,64},{48,72},{56,80},{64,... | collective-permute-start | bytes 983048 | tf_op jit(solution)/shard_map/ppermute | solution.py:14
  48.8 19.1 %collective-permute-start.7 = (bf16[64,2560]{1,0:T(8,128)(2,1)}, bf16[64,2560]{1,0:T(8,128)(2,1)S(1)}, u32[]{:S(2)}, u32[]{:S(2)}) collective-permute-start(bf16[64,2560]{1,0:T(8,128)(2,1)} %param.12), channel_id=1, source_target_pairs={{0,16},{8,24},{16,32},{24,40},{32,48},{40,56},{48,64},{56,72},{64,... | collective-permute-start | bytes 983048 | tf_op jit(solution)/shard_map/ppermute | solution.py:14
  53.2 22.6 %collective-permute-start.6 = (bf16[64,2560]{1,0:T(8,128)(2,1)}, bf16[64,2560]{1,0:T(8,128)(2,1)S(1)}, u32[]{:S(2)}, u32[]{:S(2)}) collective-permute-start(bf16[64,2560]{1,0:T(8,128)(2,1)} %param.12), channel_id=1, source_target_pairs={{0,8},{8,16},{16,24},{24,32},{32,40},{40,48},{48,56},{56,64},{64,7... | collective-permute-start | bytes 983048 | tf_op jit(solution)/shard_map/ppermute | solution.py:14
  55.8 27.0 %collective-permute-start.8 = (bf16[64,2560]{1,0:T(8,128)(2,1)}, bf16[64,2560]{1,0:T(8,128)(2,1)S(1)}, u32[]{:S(2)}, u32[]{:S(2)}) collective-permute-start(bf16[64,2560]{1,0:T(8,128)(2,1)} %param.12), channel_id=1, source_target_pairs={{0,24},{8,32},{16,40},{24,48},{32,56},{40,64},{48,72},{56,80},{64,... | collective-permute-start | bytes 983048 | tf_op jit(solution)/shard_map/ppermute | solution.py:14
  162.9 1.1 copy-start.2
  474.2 6.7 %copy-start = (f32[256,2560]{1,0:T(8,128)S(1)}, f32[256,2560]{1,0:T(8,128)}, u32[]{:S(2)}) copy-start(f32[256,2560]{1,0:T(8,128)} %get-tuple-element.230) | copy-start | bytes 7864324
  474.4 10.6 %collective-permute-start.12 = (bf16[64,2560]{1,0:T(8,128)(2,1)S(1)}, bf16[64,2560]{1,0:T(8,128)(2,1)S(1)}, u32[]{:S(2)}, u32[]{:S(2)}) collective-permute-start(bf16[64,2560]{1,0:T(8,128)(2,1)S(1)} %get-tuple-element.347), channel_id=1, source_target_pairs={{8,0},{16,8},{24,16},{32,24},{40,32},{48,40},{56,48},{64,56},{72,6... | collective-permute-start | bytes 983048 | tf_op jit(solution)/shard_map/ppermute | solution.py:14
  476.4 16.5 %collective-permute-start.14 = (bf16[64,2560]{1,0:T(8,128)(2,1)S(1)}, bf16[64,2560]{1,0:T(8,128)(2,1)S(1)}, u32[]{:S(2)}, u32[]{:S(2)}) collective-permute-start(bf16[64,2560]{1,0:T(8,128)(2,1)S(1)} %get-tuple-element.348), channel_id=1, source_target_pairs={{24,0},{32,8},{40,16},{48,24},{56,32},{64,40},{72,48},{80,56},{88,... | collective-permute-start | bytes 983048 | tf_op jit(solution)/shard_map/ppermute | solution.py:14
  479.0 23.3 %collective-permute-start.13 = (bf16[64,2560]{1,0:T(8,128)(2,1)S(1)}, bf16[64,2560]{1,0:T(8,128)(2,1)S(1)}, u32[]{:S(2)}, u32[]{:S(2)}) collective-permute-start(bf16[64,2560]{1,0:T(8,128)(2,1)S(1)} %get-tuple-element.349), channel_id=1, source_target_pairs={{16,0},{24,8},{32,16},{40,24},{48,32},{56,40},{64,48},{72,56},{80,... | collective-permute-start | bytes 983048 | tf_op jit(solution)/shard_map/ppermute | solution.py:14
  481.1 26.0 %collective-permute-start.9 = (bf16[64,2560]{1,0:T(8,128)(2,1)S(1)}, bf16[64,2560]{1,0:T(8,128)(2,1)S(1)}, u32[]{:S(2)}, u32[]{:S(2)}) collective-permute-start(bf16[64,2560]{1,0:T(8,128)(2,1)S(1)} %get-tuple-element.350), channel_id=1, source_target_pairs={{8,0},{16,8},{24,16},{32,24},{40,32},{48,40},{56,48},{64,56},{72,6... | collective-permute-start | bytes 983048 | tf_op jit(solution)/shard_map/ppermute | solution.py:14
  483.1 33.0 %collective-permute-start.11 = (bf16[64,2560]{1,0:T(8,128)(2,1)S(1)}, bf16[64,2560]{1,0:T(8,128)(2,1)S(1)}, u32[]{:S(2)}, u32[]{:S(2)}) collective-permute-start(bf16[64,2560]{1,0:T(8,128)(2,1)S(1)} %get-tuple-element.351), channel_id=1, source_target_pairs={{24,0},{32,8},{40,16},{48,24},{56,32},{64,40},{72,48},{80,56},{88,... | collective-permute-start | bytes 983048 | tf_op jit(solution)/shard_map/ppermute | solution.py:14
  485.0 36.6 %collective-permute-start.10 = (bf16[64,2560]{1,0:T(8,128)(2,1)S(1)}, bf16[64,2560]{1,0:T(8,128)(2,1)S(1)}, u32[]{:S(2)}, u32[]{:S(2)}) collective-permute-start(bf16[64,2560]{1,0:T(8,128)(2,1)S(1)} %get-tuple-element.352), channel_id=1, source_target_pairs={{16,0},{24,8},{32,16},{40,24},{48,32},{56,40},{64,48},{72,56},{80,... | collective-permute-start | bytes 983048 | tf_op jit(solution)/shard_map/ppermute | solution.py:14
Sparse Core Ops, SparseCore 0:
  11.2 96.0 all-gather.3
  110.4 96.7 all-gather.7
  210.5 86.8 all-gather.5
  474.3 129.0 reduce-scatter.1
where the time goes:
time: 614 us; the launch traced here: 610 us
  waiting for transfers between devices  207 us (34%)
  matrix products  167 us (27%)
  blocking collectives  123 us (20%)
  starting transfers between devices  38.1 us (6%)
  local copies, waits for them, and re-layouts  30 us (5%)
  other arithmetic  16.2 us (3%)
  between operations  14.8 us (2%)
  loops' own time  14.3 us (2%)
    reduce_scatter x1, waiting for transfers between devices, per_device(): lax.psum_scatter(grad_q.astype(jnp.bfloat16), 'col', scatter_dimension=0,...  80.9 us
    ppermute x15, waiting for transfers between devices, passed_along(): lax.ppermute(value, axis, [(source, source + steps) for source in range(f...  57.8 us
    psum x1, blocking collectives, per_device(): row_sum = lax.psum(local_sum * jnp.exp(local_max - row_max), 'col')  53.8 us
    pmax x1, blocking collectives, per_device(): lax.pmax(local_max.astype(jnp.bfloat16), 'col').astype(local_max.dtype)  50.1 us
    all_gather x1, waiting for transfers between devices, per_device(): lax.all_gather(saved_out, 'col', axis=0, tiled=True)  43.3 us
    ppermute x15, starting transfers between devices, passed_along(): lax.ppermute(value, axis, [(source, source + steps) for source in range(f...  37.9 us
    dot_general x20, matrix products, head_grads(): jnp.einsum('qk,qd->kd', grad_scores, q_head, preferred_element_type=jnp.f...  37.1 us
    dot_general x20, matrix products, head_grads(): jnp.einsum('qk,kd->qd', grad_scores, k_head, preferred_element_type=jnp.f...  35 us
  transfers between devices with their start and end apart: 19, of which 12 were waited for; matrix products, arithmetic and copies ran while one was open for 9% of the time, Pallas kernels for 0%

commit v1 on v0

v1 whole, which is shorter than its diff:
```python
import functools
import math

import jax
import jax.numpy as jnp
from jax import lax
from jax.experimental import pallas as pl
from jax.experimental.pallas import tpu as pltpu
from jax.sharding import PartitionSpec as P

HEADS = 20
HDIM = 128
XN = 4
GROUP = HEADS // XN
NEG = -1e30
FACTOR = HDIM ** (-0.5)
SCALE2 = FACTOR * math.log2(math.e)
FRAME_LANE = 16
BF16 = jnp.bfloat16
F32 = jnp.float32
NT = (((1,), (1,)), ((), ()))
NN = (((1,), (0,)), ((), ()))


def params():
    return pltpu.CompilerParams(vmem_limit_bytes=40 * 1024 * 1024)


def cost(flops, moved, exps=0):
    return pl.CostEstimate(flops=flops, bytes_accessed=moved, transcendentals=exps)


def pack_kernel(x_ref, q_ref, k_ref, v_ref, o_ref, g_ref, f_ref, *outs):
    tok = q_ref.shape[0]
    lane = lax.broadcasted_iota(jnp.int32, (tok, HDIM), 1)
    frame = f_ref[...].astype(F32)
    for step in range(XN):
        qg, kv = outs[step], outs[XN + step]
        group = lax.rem(x_ref[0] + step, XN)
        meta = jnp.where(lane == FRAME_LANE, frame, 0.0)
        for h in range(GROUP):
            cols = pl.ds(pl.multiple_of((group * GROUP + h) * HDIM, HDIM), HDIM)
            grad = g_ref[:, cols]
            dot = jnp.sum(grad.astype(F32) * o_ref[:, cols].astype(F32), axis=1, keepdims=True)
            high = dot.astype(BF16).astype(F32)
            meta = jnp.where(lane == h, high, meta)
            meta = jnp.where(lane == 8 + h, dot - high, meta)
            at = 2 * h * HDIM
            qg[:, at : at + HDIM] = q_ref[:, cols]
            qg[:, at + HDIM : at + 2 * HDIM] = grad
            kv[:, at : at + HDIM] = k_ref[:, cols]
            kv[:, at + HDIM : at + 2 * HDIM] = v_ref[:, cols]
        qg[:, 2 * GROUP * HDIM :] = meta.astype(BF16)


def pack(x, query, key, value, saved_out, grad_out, frames):
    tok, width = query.shape
    wide = 2 * GROUP * HDIM
    vmem = pl.BlockSpec(memory_space=pltpu.VMEM)
    out_shape = [jax.ShapeDtypeStruct((tok, wide + HDIM), BF16)] * XN
    out_shape += [jax.ShapeDtypeStruct((tok, wide), BF16)] * XN
    outs = pl.pallas_call(
        pack_kernel,
        out_shape=out_shape,
        in_specs=[pl.BlockSpec(memory_space=pltpu.SMEM)] + [vmem] * 6,
        out_specs=[vmem] * (2 * XN),
        compiler_params=params(),
        cost_estimate=cost(2 * tok * width, 18 * tok * width),
        name="pack",
    )(x, query, key, value, saved_out, grad_out, frames)
    return outs[:XN], outs[XN:]


def window_scores(queries, keys):
    return lax.dot_general(keys, queries, NT, preferred_element_type=F32) * SCALE2


def meta_rows(own_meta, far_meta):
    return jnp.concatenate([own_meta[...], far_meta[...]], axis=0).astype(F32).T


def stats_kernel(bias_ref, q_own, q_far, m_own, m_far, w0, w1, w2, w3, out_ref):
    head = pl.program_id(0)
    queries = jnp.concatenate([q_own[...], q_far[...]], axis=0)
    rows = meta_rows(m_own, m_far)
    q_frame = rows[FRAME_LANE : FRAME_LANE + 1, :]
    k_frame = m_own[...].astype(F32)[:, FRAME_LANE : FRAME_LANE + 1]

    scores, peaks = [], []
    for at, ref in enumerate((w0, w1, w2, w3)):
        part = window_scores(queries, ref[...])
        if at == 0:
            part = jnp.where(k_frame <= q_frame, part, NEG)
        scores.append(part)
        peaks.append(jnp.max(part, axis=0, keepdims=True) + bias_ref[at])
    peak = functools.reduce(jnp.maximum, peaks)
    total = jnp.zeros_like(peak)
    for at, part in enumerate(scores):
        total += jnp.sum(jnp.exp2(part - (peak - bias_ref[at])), axis=0, keepdims=True)

    @pl.when(head == 0)
    def _():
        out_ref[...] = jnp.zeros_like(out_ref)

    out_ref[pl.ds(head, 1), :] = peak
    out_ref[pl.ds(8 + head, 1), :] = total


def stats(bias, own, far, window):
    half = own.shape[0]
    narrow = pl.BlockSpec((half, HDIM), lambda h: (0, 2 * h))
    meta = pl.BlockSpec((half, HDIM), lambda h: (0, 2 * GROUP))
    pairs = GROUP * 2 * half * 4 * half
    return pl.pallas_call(
        stats_kernel,
        grid=(GROUP,),
        out_shape=jax.ShapeDtypeStruct((16, 2 * half), F32),
        in_specs=[pl.BlockSpec(memory_space=pltpu.SMEM), narrow, narrow, meta, meta] + [narrow] * 4,
        out_specs=pl.BlockSpec((16, 2 * half), lambda h: (0, 0)),
        compiler_params=params(),
        cost_estimate=cost(4 * pairs * HDIM, 6 * half * GROUP * HDIM * 2, pairs),
        name="stats",
    )(bias, own, far, own, far, *window)


def grads_kernel(
    bias_ref, own_stats, far_stats, q_own, q_far, m_own, m_far, w0, w1, w2, w3,
    dq_own, dq_far, d0, d1, d2, d3,
):
    head = pl.program_id(0)
    half = q_own.shape[0]
    queries = jnp.concatenate([q_own[:, :HDIM], q_far[:, :HDIM]], axis=0)
    grads = jnp.concatenate([q_own[:, HDIM:], q_far[:, HDIM:]], axis=0)
    meta = jnp.concatenate([m_own[...], m_far[...]], axis=0).astype(F32)
    lane = lax.broadcasted_iota(jnp.int32, meta.shape, 1)
    dot_col = jnp.sum(
        jnp.where((lane == head) | (lane == head + 8), meta, 0.0), axis=1, keepdims=True
    )
    rows = jnp.where(lane == FRAME_LANE, meta, dot_col).T
    q_frame = rows[FRAME_LANE : FRAME_LANE + 1, :]
    dot = rows[0:1, :]
    k_frame = meta[:half, FRAME_LANE : FRAME_LANE + 1]

    own_peak = own_stats[pl.ds(head, 1), :]
    own_sum = own_stats[pl.ds(8 + head, 1), :]
    far_peak = far_stats[pl.ds(head, 1), :]
    far_sum = far_stats[pl.ds(8 + head, 1), :]
    far_peak = jnp.concatenate([far_peak[:, half:], far_peak[:, :half]], axis=1)
    far_sum = jnp.concatenate([far_sum[:, half:], far_sum[:, :half]], axis=1)
    peak = jnp.maximum(own_peak, far_peak)
    total = peak + jnp.log2(
        own_sum * jnp.exp2(own_peak - peak) + far_sum * jnp.exp2(far_peak - peak)
    )

    dq = jnp.zeros((HDIM, 2 * half), F32)
    for at, (ref, out) in enumerate(((w0, d0), (w1, d1), (w2, d2), (w3, d3))):
        keys, values = ref[:, :HDIM], ref[:, HDIM:]
        part = window_scores(queries, keys)
        if at == 0:
            part = jnp.where(k_frame <= q_frame, part, NEG)
        probs = jnp.exp2(part - (total - bias_ref[at]))
        dv = lax.dot_general(probs.astype(BF16), grads, NN, preferred_element_type=F32)
        dp = lax.dot_general(values, grads, NT, preferred_element_type=F32)
        ds = (probs * (dp - dot)).astype(BF16)
        dk = lax.dot_general(ds, queries, NN, preferred_element_type=F32) * FACTOR
        dq += lax.dot_general(keys.T, ds, NN, preferred_element_type=F32)
        out[:, :HDIM] = dk.astype(out.dtype)
        out[:, HDIM:] = dv.astype(out.dtype)
    dq = (dq * FACTOR).T
    dq_own[...] = dq[:half]
    dq_far[...] = dq[half:].astype(BF16)


def grads(bias, own_stats, far_stats, own, far, window):
    half = own.shape[0]
    pair = pl.BlockSpec((half, 2 * HDIM), lambda h: (0, h))
    narrow = pl.BlockSpec((half, HDIM), lambda h: (0, h))
    meta = pl.BlockSpec((half, HDIM), lambda h: (0, 2 * GROUP))
    vmem = pl.BlockSpec((16, 2 * half), lambda h: (0, 0))
    pairs = GROUP * 2 * half * 4 * half
    wide = GROUP * HDIM
    return pl.pallas_call(
        grads_kernel,
        grid=(GROUP,),
        out_shape=[
            jax.ShapeDtypeStruct((half, wide), F32),
            jax.ShapeDtypeStruct((half, wide), BF16),
            jax.ShapeDtypeStruct((half, 2 * wide), F32),
        ]
        + [jax.ShapeDtypeStruct((half, 2 * wide), BF16)] * 3,
        in_specs=[pl.BlockSpec(memory_space=pltpu.SMEM), vmem, vmem, pair, pair, meta, meta]
        + [pair] * 4,
        out_specs=[narrow, narrow] + [pair] * 4,
        compiler_params=params(),
        cost_estimate=cost(20 * pairs * HDIM, 18 * half * wide * 2, pairs),
        name="grads",
    )(bias, own_stats, far_stats, own, far, own, far, *window)


def close_kernel(even_ref, dq_own, dq_far, d0, back, side, *outs):
    even = even_ref[0].astype(F32)
    tok = outs[0].shape[0]
    for step in range(XN):
        rows = pl.ds(step * tok, tok)
        kv = d0[rows, :] + back[rows, :].astype(F32) + side[rows, :].astype(F32) * even
        wide = kv.shape[1]
        outs[step][:, :wide] = kv.astype(BF16)
        outs[step][:, wide:] = (dq_own[rows, :] + dq_far[rows, :].astype(F32)).astype(BF16)


def close(even, dq_own, dq_far, d0, back, side):
    half, wide = dq_own.shape
    tok = half // XN
    vmem = pl.BlockSpec(memory_space=pltpu.VMEM)
    return pl.pallas_call(
        close_kernel,
        out_shape=[jax.ShapeDtypeStruct((tok, 3 * wide), BF16)] * XN,
        in_specs=[pl.BlockSpec(memory_space=pltpu.SMEM)] + [vmem] * 5,
        out_specs=[vmem] * XN,
        compiler_params=params(),
        cost_estimate=cost(5 * half * wide, 28 * half * wide),
        name="close",
    )(even, dq_own, dq_far, d0, back, side)


def unpack_kernel(x_ref, *refs):
    parts, (dq, dk, dv) = refs[:XN], refs[XN:]
    base = 2 * GROUP * HDIM
    for step in range(XN):
        group = lax.rem(x_ref[0] + step, XN)
        for h in range(GROUP):
            cols = pl.ds(pl.multiple_of((group * GROUP + h) * HDIM, HDIM), HDIM)
            at = 2 * h * HDIM
            dk[:, cols] = parts[step][:, at : at + HDIM]
            dv[:, cols] = parts[step][:, at + HDIM : at + 2 * HDIM]
            dq[:, cols] = parts[step][:, base + h * HDIM : base + (h + 1) * HDIM]


def unpack(x, parts):
    tok = parts[0].shape[0]
    vmem = pl.BlockSpec(memory_space=pltpu.VMEM)
    return pl.pallas_call(
        unpack_kernel,
        out_shape=[jax.ShapeDtypeStruct((tok, HEADS * HDIM), BF16)] * 3,
        in_specs=[pl.BlockSpec(memory_space=pltpu.SMEM)] + [vmem] * XN,
        out_specs=[vmem] * 3,
        compiler_params=params(),
        cost_estimate=cost(0, 12 * tok * HEADS * HDIM),
        name="unpack",
    )(x, *parts)


def along_x(value, steps):
    count = lax.axis_size("col")
    moves = [(c, c // XN * XN + (c + steps) % XN) for c in range(count)]
    return lax.ppermute(value, "col", moves)


def across_z(value):
    count = lax.axis_size("col")
    return lax.ppermute(value, "col", [(c, (c + XN) % count) for c in range(count)])


def along_row(value, steps):
    count = lax.axis_size("row")
    first, last = max(0, -steps), min(count, count - steps)
    return lax.ppermute(value, "row", [(r, r + steps) for r in range(first, last)])


def in_chip(value):
    count = lax.axis_size("row")
    return lax.ppermute(value, "row", [(r, r ^ 1) for r in range(count)])


def per_device(query, key, value, saved_out, grad_out, frame_ids):
    row = lax.axis_index("row")
    x = (lax.axis_index("col") % XN).astype(jnp.int32).reshape(1)
    is_even = row % 2 == 0
    even = is_even.astype(jnp.int32).reshape(1)

    qg, kv = pack(x, query, key, value, saved_out, grad_out, frame_ids[:, None])
    own = jnp.concatenate([qg[0]] + [along_x(qg[s], s) for s in range(1, XN)], axis=0)
    far = across_z(own)
    w0 = jnp.concatenate([kv[0]] + [along_x(kv[s], s) for s in range(1, XN)], axis=0)
    w1 = along_row(w0, 2)
    w2 = in_chip(w1)
    w3 = along_row(jnp.where(is_even, w0, w1), 1)
    held = jnp.stack(
        [
            row >= 0,
            row >= 2,
            jnp.where(is_even, row >= 1, row >= 3),
            jnp.where(is_even, row >= 3, row >= 1),
        ]
    )
    bias = jnp.where(held, 0.0, NEG).astype(F32)
    window = (w0, w1, w2, w3)

    own_stats = stats(bias, own, far, window)
    far_stats = across_z(own_stats)
    dq_own, dq_far, d0, d1, d2, d3 = grads(bias, own_stats, far_stats, own, far, window)

    dq_back = across_z(dq_far)
    side = along_row(d3, -1)
    swapped = in_chip(d2)
    turned = jnp.where(is_even, jnp.zeros_like(side), side)
    d1 = (d1.astype(F32) + swapped.astype(F32) + turned.astype(F32)).astype(BF16)
    back = along_row(d1, -2)

    parts = close(even, dq_own, dq_back, d0, back, side)
    parts = [parts[0]] + [along_x(parts[s], -s) for s in range(1, XN)]
    return tuple(unpack(x, parts))


def solution(mesh):
    placed = P(("row", "col"), None)
    return jax.shard_map(
        per_device,
        mesh=mesh,
        in_specs=(placed,) * 5 + (P(("row", "col")),),
        out_specs=(placed,) * 3,
        check_vma=False,
    )
```

time: 614 us -> 188 us (0.31)
  the two profiles are of different devices: /device:TPU:16 before, /device:TPU:121 now
where the time goes in v1:
time: 188 us; the launch traced here: 187 us
  waiting for transfers between devices  83.7 us (45%)
  starting transfers between devices  71.6 us (38%)
  Pallas kernels  21.1 us (11%)
  local copies, waits for them, and re-layouts  8.15 us (4%)
    ppermute x3, waiting for transfers between devices, across_z(): lax.ppermute(value, 'col', [(c, (c + XN) % count) for c in range(count)])  39.4 us
    ppermute x4, waiting for transfers between devices, along_row(): lax.ppermute(value, 'row', [(r, r + steps) for r in range(first, last)])  33 us
    ppermute x9, starting transfers between devices, along_x(): return lax.ppermute(value, 'col', moves)  27.9 us
    ppermute x3, starting transfers between devices, across_z(): lax.ppermute(value, 'col', [(c, (c + XN) % count) for c in range(count)])  19.9 us
    ppermute x4, starting transfers between devices, along_row(): lax.ppermute(value, 'row', [(r, r + steps) for r in range(first, last)])  16.3 us
    pallas_call x1, Pallas kernels, grads(): pl.pallas_call(grads_kernel, grid=(GROUP,), out_shape=[jax.ShapeDtypeStru...  13.9 us
    ppermute x9, waiting for transfers between devices, along_x(): return lax.ppermute(value, 'col', moves)  11.3 us
    ppermute x2, starting transfers between devices, in_chip(): return lax.ppermute(value, 'row', [(r, r ^ 1) for r in range(count)])  7.53 us
  transfers between devices with their start and end apart: 18, of which 10 were waited for; matrix products, arithmetic and copies ran while one was open for 1% of the time, Pallas kernels for 0%

profile of v1, /device:TPU:121, one launch (start us, length us, event | category | flops | bytes accessed | tf_op | source)
XLA Modules:
  0.0 186.9 jit_solution(7868856910179797925)
XLA Ops:
  0.6 0.7 copy.9.f_ref
  1.4 0.0 copy-start.4
  1.4 1.0 copy-done.4
  2.4 0.0 copy-start.5
  2.4 1.0 copy-done.5
  3.3 0.0 copy-start.6
  3.3 1.0 copy-done.6
  4.3 0.0 copy-start.7
  4.3 1.0 copy-done.7
  5.3 0.0 copy-start.8
  5.3 1.0 copy-done.8
  6.3 0.4 pack.1
  6.6 3.1 %collective-permute-start.4 = (bf16[64,1280]{1,0:T(8,128)(2,1)S(1)}, bf16[64,1280]{1,0:T(8,128)(2,1)S(1)}, u32[]{:S(2)}, u32[]{:S(2)}) collective-permute-start(bf16[64,1280]{1,0:T(8,128)(2,1)S(1)} %get-tuple-element.26), channel_id=1, source_target_pairs={{0,1},{1,2},{2,3},{3,0},{4,5},{5,6},{6,7},{7,4},{8,9},{9,10},{10,1... | collective-permute-start | bytes 491528 | tf_op jit(solution)/shard_map/ppermute | solution.py:256
  9.8 4.4 %collective-permute-start.5 = (bf16[64,1280]{1,0:T(8,128)(2,1)S(1)}, bf16[64,1280]{1,0:T(8,128)(2,1)S(1)}, u32[]{:S(2)}, u32[]{:S(2)}) collective-permute-start(bf16[64,1280]{1,0:T(8,128)(2,1)S(1)} %get-tuple-element.27), channel_id=1, source_target_pairs={{0,2},{1,3},{2,0},{3,1},{4,6},{5,7},{6,4},{7,5},{8,10},{9,11},{10,... | collective-permute-start | bytes 491528 | tf_op jit(solution)/shard_map/ppermute | solution.py:256
  14.1 3.1 %collective-permute-start.6 = (bf16[64,1280]{1,0:T(8,128)(2,1)S(1)}, bf16[64,1280]{1,0:T(8,128)(2,1)S(1)}, u32[]{:S(2)}, u32[]{:S(2)}) collective-permute-start(bf16[64,1280]{1,0:T(8,128)(2,1)S(1)} %get-tuple-element.28), channel_id=1, source_target_pairs={{0,3},{1,0},{2,1},{3,2},{4,7},{5,4},{6,5},{7,6},{8,11},{9,8},{10,9... | collective-permute-start | bytes 491528 | tf_op jit(solution)/shard_map/ppermute | solution.py:256
  17.2 2.2 %collective-permute-start = (bf16[64,1408]{1,0:T(8,128)(2,1)S(1)}, bf16[64,1408]{1,0:T(8,128)(2,1)S(1)}, u32[]{:S(2)}, u32[]{:S(2)}) collective-permute-start(bf16[64,1408]{1,0:T(8,128)(2,1)S(1)} %get-tuple-element.22), channel_id=1, source_target_pairs={{0,1},{1,2},{2,3},{3,0},{4,5},{5,6},{6,7},{7,4},{8,9},{9,10},{10,1... | collective-permute-start | bytes 540680 | tf_op jit(solution)/shard_map/ppermute | solution.py:256
  19.4 2.8 %collective-permute-start.1 = (bf16[64,1408]{1,0:T(8,128)(2,1)S(1)}, bf16[64,1408]{1,0:T(8,128)(2,1)S(1)}, u32[]{:S(2)}, u32[]{:S(2)}) collective-permute-start(bf16[64,1408]{1,0:T(8,128)(2,1)S(1)} %get-tuple-element.23), channel_id=1, source_target_pairs={{0,2},{1,3},{2,0},{3,1},{4,6},{5,7},{6,4},{7,5},{8,10},{9,11},{10,... | collective-permute-start | bytes 540680 | tf_op jit(solution)/shard_map/ppermute | solution.py:256
  22.3 0.0 collective-permute-done.4
  22.3 3.4 %collective-permute-start.2 = (bf16[64,1408]{1,0:T(8,128)(2,1)S(1)}, bf16[64,1408]{1,0:T(8,128)(2,1)S(1)}, u32[]{:S(2)}, u32[]{:S(2)}) collective-permute-start(bf16[64,1408]{1,0:T(8,128)(2,1)S(1)} %get-tuple-element.24), channel_id=1, source_target_pairs={{0,3},{1,0},{2,1},{3,2},{4,7},{5,4},{6,5},{7,6},{8,11},{9,8},{10,9... | collective-permute-start | bytes 540680 | tf_op jit(solution)/shard_map/ppermute | solution.py:256
  25.8 0.0 collective-permute-done.5
  25.8 0.0 collective-permute-done.6
  25.8 3.2 %collective-permute-start.7 = (bf16[256,1280]{1,0:T(8,128)(2,1)S(1)}, bf16[256,1280]{1,0:T(8,128)(2,1)S(1)}, u32[]{:S(2)}, u32[]{:S(2)}) collective-permute-start(bf16[256,1280]{1,0:T(8,128)(2,1)S(1)} %constant_dynamic-update-slice_fusion.4.w0), channel_id=1, source_target_pairs={{0,16},{8,24},{16,32},{24,40},{32,48},{40,56},{48,64},{56,72},{64,... | collective-permute-start | bytes 1966088 | tf_op jit(solution)/shard_map/ppermute | solution.py:267
  29.0 0.0 collective-permute-done
  29.1 0.0 collective-permute-done.1
  29.1 1.7 collective-permute-done.2
  30.8 9.7 %collective-permute-start.3 = (bf16[256,1408]{1,0:T(8,128)(2,1)S(1)}, bf16[256,1408]{1,0:T(8,128)(2,1)S(1)}, u32[]{:S(2)}, u32[]{:S(2)}) collective-permute-start(bf16[256,1408]{1,0:T(8,128)(2,1)S(1)} %constant_dynamic-update-slice_fusion.q_own.m_own), channel_id=1, source_target_pairs={{0,4},{1,5},{2,6},{3,7},{4,0},{5,1},{6,2},{7,3},{8,12},{9,13},{10,... | collective-permute-start | bytes 2162696 | tf_op jit(solution)/shard_map/ppermute | solution.py:261
  40.6 1.3 collective-permute-done.7.w1
  41.9 0.9 broadcast_select_fusion
  42.8 9.2 %collective-permute-start.9 = (bf16[256,1280]{1,0:T(8,128)(2,1)}, bf16[256,1280]{1,0:T(8,128)(2,1)S(1)}, u32[]{:S(2)}, u32[]{:S(2)}) collective-permute-start(bf16[256,1280]{1,0:T(8,128)(2,1)} %broadcast_select_fusion), channel_id=1, source_target_pairs={{0,8},{8,16},{16,24},{24,32},{32,40},{40,48},{48,56},{56,64},{64,7... | collective-permute-start | bytes 1966088 | tf_op jit(solution)/shard_map/ppermute | solution.py:267
  52.0 1.9 %collective-permute-start.8 = (bf16[256,1280]{1,0:T(8,128)(2,1)S(1)}, bf16[256,1280]{1,0:T(8,128)(2,1)}, u32[]{:S(2)}, u32[]{:S(2)}) collective-permute-start(bf16[256,1280]{1,0:T(8,128)(2,1)S(1)} %collective-permute-done.7.w1), channel_id=1, source_target_pairs={{0,8},{8,0},{16,24},{24,16},{32,40},{40,32},{48,56},{56,48},{64,72... | collective-permute-start | bytes 1966088 | tf_op jit(solution)/shard_map/ppermute | solution.py:272
  54.0 0.1 add_select_fusion.bias_ref
  54.1 16.7 %collective-permute-done.3.q_far.m_far = bf16[256,1408]{1,0:T(8,128)(2,1)S(1)} collective-permute-done((bf16[256,1408]{1,0:T(8,128)(2,1)S(1)}, bf16[256,1408]{1,0:T(8,128)(2,1)S(1)}, u32[]{:S(2)}, u32[]{:S(2)}) %collective-permute-start.3) | collective-permute-done | bytes 720928 | tf_op jit(solution)/shard_map/ppermute | solution.py:261
  70.7 0.0 collective-permute-done.9.w3
  70.7 0.0 copy-start.2
  70.7 0.0 collective-permute-done.8.w2
  70.8 5.4 %stats.1.own_stats = f32[16,512]{1,0:T(8,128)S(1)} custom-call(f32[4]{0:T(128)S(1)} %add_select_fusion.bias_ref, bf16[256,1408]{1,0:T(8,128)(2,1)S(1)} %constant_dynamic-update-slice_fusion.q_own.m_own, bf16[256,1408]{1,0:T(8,128)(2,1)S(1)} %collective-permute-done.3.q_far.m_far, bf16[256,1408]{1,0:T(8,128)(2,1)S(1)} %constant_dynamic-update-slice_fusion.q_own.m_own, ...), custom_call_target="tpu_custom_call" | custom-call | flops 1342177280 | bytes 1966080 | tf_op jit(solution)/shard_map/stats/pallas_call | solution.py:114
  76.2 0.0 copy-done.2
  76.2 7.0 %collective-permute-start.10 = (f32[16,512]{1,0:T(8,128)S(1)}, f32[16,512]{1,0:T(8,128)S(1)}, u32[]{:S(2)}, u32[]{:S(2)}) collective-permute-start(f32[16,512]{1,0:T(8,128)S(1)} %stats.1.own_stats), channel_id=1, source_target_pairs={{0,4},{1,5},{2,6},{3,7},{4,0},{5,1},{6,2},{7,3},{8,12},{9,13},{10,... | collective-permute-start | bytes 98312 | tf_op jit(solution)/shard_map/ppermute | solution.py:261
  83.2 1.5 collective-permute-done.10.far_stats
  84.7 0.0 copy-start.3
  84.7 1.1 copy-done.3
  85.8 13.9 %grads.1 = (f32[256,640]{1,0:T(8,128)S(1)}, bf16[256,640]{1,0:T(8,128)(2,1)}, f32[256,1280]{1,0:T(8,128)S(1)}, bf16[256,1280]{1,0:T(8,128)(2,1)S(1)}, bf16[256,1...) custom-call(f32[4]{0:T(128)S(1)} %add_select_fusion.bias_ref, f32[16,512]{1,0:T(8,128)S(1)} %stats.1.own_stats, ...), custom_call_target="tpu_custom_call" | custom-call | flops 6710886400 | bytes 5898240 | tf_op jit(solution)/shard_map/grads/pallas_call | solution.py:182
  99.7 0.0 copy-start
  99.7 5.6 %collective-permute-start.12 = (bf16[256,1280]{1,0:T(8,128)(2,1)S(1)}, bf16[256,1280]{1,0:T(8,128)(2,1)S(1)}, u32[]{:S(2)}, u32[]{:S(2)}) collective-permute-start(bf16[256,1280]{1,0:T(8,128)(2,1)S(1)} %get-tuple-element.33), channel_id=1, source_target_pairs={{0,8},{8,0},{16,24},{24,16},{32,40},{40,32},{48,56},{56,48},{64,72... | collective-permute-start | bytes 1966088 | tf_op jit(solution)/shard_map/ppermute | solution.py:272
  105.3 1.9 %collective-permute-start.13 = (bf16[256,1280]{1,0:T(8,128)(2,1)S(1)}, bf16[256,1280]{1,0:T(8,128)(2,1)S(1)}, u32[]{:S(2)}, u32[]{:S(2)}) collective-permute-start(bf16[256,1280]{1,0:T(8,128)(2,1)S(1)} %get-tuple-element.34), channel_id=1, source_target_pairs={{8,0},{16,8},{24,16},{32,24},{40,32},{48,40},{56,48},{64,56},{72,6... | collective-permute-start | bytes 1966088 | tf_op jit(solution)/shard_map/ppermute | solution.py:267
  107.2 0.0 collective-permute-done.12
  107.2 27.5 %collective-permute-done.13.side = bf16[256,1280]{1,0:T(8,128)(2,1)S(1)} collective-permute-done((bf16[256,1280]{1,0:T(8,128)(2,1)S(1)}, bf16[256,1280]{1,0:T(8,128)(2,1)S(1)}, u32[]{:S(2)}, u32[]{:S(2)}) %collective-permute-start.13) | collective-permute-done | bytes 655392 | tf_op jit(solution)/shard_map/ppermute | solution.py:267
  134.8 0.3 add_convert_fusion
  135.1 0.0 copy-done
  135.1 1.9 %collective-permute-start.14 = (bf16[256,1280]{1,0:T(8,128)(2,1)S(1)}, bf16[256,1280]{1,0:T(8,128)(2,1)S(1)}, u32[]{:S(2)}, u32[]{:S(2)}) collective-permute-start(bf16[256,1280]{1,0:T(8,128)(2,1)S(1)} %add_convert_fusion), channel_id=1, source_target_pairs={{16,0},{24,8},{32,16},{40,24},{48,32},{56,40},{64,48},{72,56},{80,... | collective-permute-start | bytes 1966088 | tf_op jit(solution)/shard_map/ppermute | solution.py:267
  137.0 3.1 %collective-permute-start.11 = (bf16[256,640]{1,0:T(8,128)(2,1)}, bf16[256,640]{1,0:T(8,128)(2,1)S(1)}, u32[]{:S(2)}, u32[]{:S(2)}) collective-permute-start(bf16[256,640]{1,0:T(8,128)(2,1)} %get-tuple-element.30), channel_id=1, source_target_pairs={{0,4},{1,5},{2,6},{3,7},{4,0},{5,1},{6,2},{7,3},{8,12},{9,13},{10,... | collective-permute-start | bytes 983048 | tf_op jit(solution)/shard_map/ppermute | solution.py:261
  140.2 21.3 %collective-permute-done.11.dq_far = bf16[256,640]{1,0:T(8,128)(2,1)S(1)} collective-permute-done((bf16[256,640]{1,0:T(8,128)(2,1)}, bf16[256,640]{1,0:T(8,128)(2,1)S(1)}, u32[]{:S(2)}, u32[]{:S(2)}) %collective-permute-start.11) | collective-permute-done | bytes 327712 | tf_op jit(solution)/shard_map/ppermute | solution.py:261
  161.4 4.2 %collective-permute-done.14.back = bf16[256,1280]{1,0:T(8,128)(2,1)S(1)} collective-permute-done((bf16[256,1280]{1,0:T(8,128)(2,1)S(1)}, bf16[256,1280]{1,0:T(8,128)(2,1)S(1)}, u32[]{:S(2)}, u32[]{:S(2)}) %collective-permute-start.14) | collective-permute-done | bytes 655392 | tf_op jit(solution)/shard_map/ppermute | solution.py:267
  165.7 0.0 copy-start.1
  165.7 1.3 copy-done.1
  167.0 0.3 close.1
  167.3 1.9 %collective-permute-start.15 = (bf16[64,1920]{1,0:T(8,128)(2,1)S(1)}, bf16[64,1920]{1,0:T(8,128)(2,1)S(1)}, u32[]{:S(2)}, u32[]{:S(2)}) collective-permute-start(bf16[64,1920]{1,0:T(8,128)(2,1)S(1)} %get-tuple-element.36), channel_id=1, source_target_pairs={{0,3},{1,0},{2,1},{3,2},{4,7},{5,4},{6,5},{7,6},{8,11},{9,8},{10,9... | collective-permute-start | bytes 737288 | tf_op jit(solution)/shard_map/ppermute | solution.py:256
  169.2 4.2 %collective-permute-start.16 = (bf16[64,1920]{1,0:T(8,128)(2,1)S(1)}, bf16[64,1920]{1,0:T(8,128)(2,1)S(1)}, u32[]{:S(2)}, u32[]{:S(2)}) collective-permute-start(bf16[64,1920]{1,0:T(8,128)(2,1)S(1)} %get-tuple-element.37), channel_id=1, source_target_pairs={{0,2},{1,3},{2,0},{3,1},{4,6},{5,7},{6,4},{7,5},{8,10},{9,11},{10,... | collective-permute-start | bytes 737288 | tf_op jit(solution)/shard_map/ppermute | solution.py:256
  173.4 2.8 %collective-permute-start.17 = (bf16[64,1920]{1,0:T(8,128)(2,1)S(1)}, bf16[64,1920]{1,0:T(8,128)(2,1)S(1)}, u32[]{:S(2)}, u32[]{:S(2)}) collective-permute-start(bf16[64,1920]{1,0:T(8,128)(2,1)S(1)} %get-tuple-element.38), channel_id=1, source_target_pairs={{0,1},{1,2},{2,3},{3,0},{4,5},{5,6},{6,7},{7,4},{8,9},{9,10},{10,1... | collective-permute-start | bytes 737288 | tf_op jit(solution)/shard_map/ppermute | solution.py:256
  176.2 3.7 %collective-permute-done.15.refs_1_ = bf16[64,1920]{1,0:T(8,128)(2,1)S(1)} collective-permute-done((bf16[64,1920]{1,0:T(8,128)(2,1)S(1)}, bf16[64,1920]{1,0:T(8,128)(2,1)S(1)}, u32[]{:S(2)}, u32[]{:S(2)}) %collective-permute-start.15) | collective-permute-done | bytes 245792 | tf_op jit(solution)/shard_map/ppermute | solution.py:256
  179.9 0.3 collective-permute-done.16.refs_2_
  180.2 5.5 %collective-permute-done.17.refs_3_ = bf16[64,1920]{1,0:T(8,128)(2,1)S(1)} collective-permute-done((bf16[64,1920]{1,0:T(8,128)(2,1)S(1)}, bf16[64,1920]{1,0:T(8,128)(2,1)S(1)}, u32[]{:S(2)}, u32[]{:S(2)}) %collective-permute-start.17) | collective-permute-done | bytes 245792 | tf_op jit(solution)/shard_map/ppermute | solution.py:256
  185.7 1.1 unpack.1
  (8 shorter events, 0.1 us)
Async XLA Ops:
  1.4 1.0 copy-start.4
  2.4 1.0 copy-start.5
  3.3 1.0 copy-start.6
  4.3 1.0 copy-start.7
  5.3 1.0 copy-start.8
  6.6 15.7 %collective-permute-start.4 = (bf16[64,1280]{1,0:T(8,128)(2,1)S(1)}, bf16[64,1280]{1,0:T(8,128)(2,1)S(1)}, u32[]{:S(2)}, u32[]{:S(2)}) collective-permute-start(bf16[64,1280]{1,0:T(8,128)(2,1)S(1)} %get-tuple-element.26), channel_id=1, source_target_pairs={{0,1},{1,2},{2,3},{3,0},{4,5},{5,6},{6,7},{7,4},{8,9},{9,10},{10,1... | collective-permute-start | bytes 491528 | tf_op jit(solution)/shard_map/ppermute | solution.py:256
  9.8 16.0 %collective-permute-start.5 = (bf16[64,1280]{1,0:T(8,128)(2,1)S(1)}, bf16[64,1280]{1,0:T(8,128)(2,1)S(1)}, u32[]{:S(2)}, u32[]{:S(2)}) collective-permute-start(bf16[64,1280]{1,0:T(8,128)(2,1)S(1)} %get-tuple-element.27), channel_id=1, source_target_pairs={{0,2},{1,3},{2,0},{3,1},{4,6},{5,7},{6,4},{7,5},{8,10},{9,11},{10,... | collective-permute-start | bytes 491528 | tf_op jit(solution)/shard_map/ppermute | solution.py:256
  14.1 11.7 %collective-permute-start.6 = (bf16[64,1280]{1,0:T(8,128)(2,1)S(1)}, bf16[64,1280]{1,0:T(8,128)(2,1)S(1)}, u32[]{:S(2)}, u32[]{:S(2)}) collective-permute-start(bf16[64,1280]{1,0:T(8,128)(2,1)S(1)} %get-tuple-element.28), channel_id=1, source_target_pairs={{0,3},{1,0},{2,1},{3,2},{4,7},{5,4},{6,5},{7,6},{8,11},{9,8},{10,9... | collective-permute-start | bytes 491528 | tf_op jit(solution)/shard_map/ppermute | solution.py:256
  17.2 11.8 %collective-permute-start = (bf16[64,1408]{1,0:T(8,128)(2,1)S(1)}, bf16[64,1408]{1,0:T(8,128)(2,1)S(1)}, u32[]{:S(2)}, u32[]{:S(2)}) collective-permute-start(bf16[64,1408]{1,0:T(8,128)(2,1)S(1)} %get-tuple-element.22), channel_id=1, source_target_pairs={{0,1},{1,2},{2,3},{3,0},{4,5},{5,6},{6,7},{7,4},{8,9},{9,10},{10,1... | collective-permute-start | bytes 540680 | tf_op jit(solution)/shard_map/ppermute | solution.py:256
  19.4 9.7 %collective-permute-start.1 = (bf16[64,1408]{1,0:T(8,128)(2,1)S(1)}, bf16[64,1408]{1,0:T(8,128)(2,1)S(1)}, u32[]{:S(2)}, u32[]{:S(2)}) collective-permute-start(bf16[64,1408]{1,0:T(8,128)(2,1)S(1)} %get-tuple-element.23), channel_id=1, source_target_pairs={{0,2},{1,3},{2,0},{3,1},{4,6},{5,7},{6,4},{7,5},{8,10},{9,11},{10,... | collective-permute-start | bytes 540680 | tf_op jit(solution)/shard_map/ppermute | solution.py:256
  22.3 8.5 %collective-permute-start.2 = (bf16[64,1408]{1,0:T(8,128)(2,1)S(1)}, bf16[64,1408]{1,0:T(8,128)(2,1)S(1)}, u32[]{:S(2)}, u32[]{:S(2)}) collective-permute-start(bf16[64,1408]{1,0:T(8,128)(2,1)S(1)} %get-tuple-element.24), channel_id=1, source_target_pairs={{0,3},{1,0},{2,1},{3,2},{4,7},{5,4},{6,5},{7,6},{8,11},{9,8},{10,9... | collective-permute-start | bytes 540680 | tf_op jit(solution)/shard_map/ppermute | solution.py:256
  25.8 16.0 %collective-permute-start.7 = (bf16[256,1280]{1,0:T(8,128)(2,1)S(1)}, bf16[256,1280]{1,0:T(8,128)(2,1)S(1)}, u32[]{:S(2)}, u32[]{:S(2)}) collective-permute-start(bf16[256,1280]{1,0:T(8,128)(2,1)S(1)} %constant_dynamic-update-slice_fusion.4.w0), channel_id=1, source_target_pairs={{0,16},{8,24},{16,32},{24,40},{32,48},{40,56},{48,64},{56,72},{64,... | collective-permute-start | bytes 1966088 | tf_op jit(solution)/shard_map/ppermute | solution.py:267
  30.8 39.9 %collective-permute-start.3 = (bf16[256,1408]{1,0:T(8,128)(2,1)S(1)}, bf16[256,1408]{1,0:T(8,128)(2,1)S(1)}, u32[]{:S(2)}, u32[]{:S(2)}) collective-permute-start(bf16[256,1408]{1,0:T(8,128)(2,1)S(1)} %constant_dynamic-update-slice_fusion.q_own.m_own), channel_id=1, source_target_pairs={{0,4},{1,5},{2,6},{3,7},{4,0},{5,1},{6,2},{7,3},{8,12},{9,13},{10,... | collective-permute-start | bytes 2162696 | tf_op jit(solution)/shard_map/ppermute | solution.py:261
  42.8 27.9 %collective-permute-start.9 = (bf16[256,1280]{1,0:T(8,128)(2,1)}, bf16[256,1280]{1,0:T(8,128)(2,1)S(1)}, u32[]{:S(2)}, u32[]{:S(2)}) collective-permute-start(bf16[256,1280]{1,0:T(8,128)(2,1)} %broadcast_select_fusion), channel_id=1, source_target_pairs={{0,8},{8,16},{16,24},{24,32},{32,40},{40,48},{48,56},{56,64},{64,7... | collective-permute-start | bytes 1966088 | tf_op jit(solution)/shard_map/ppermute | solution.py:267
  52.0 18.7 %collective-permute-start.8 = (bf16[256,1280]{1,0:T(8,128)(2,1)S(1)}, bf16[256,1280]{1,0:T(8,128)(2,1)}, u32[]{:S(2)}, u32[]{:S(2)}) collective-permute-start(bf16[256,1280]{1,0:T(8,128)(2,1)S(1)} %collective-permute-done.7.w1), channel_id=1, source_target_pairs={{0,8},{8,0},{16,24},{24,16},{32,40},{40,32},{48,56},{56,48},{64,72... | collective-permute-start | bytes 1966088 | tf_op jit(solution)/shard_map/ppermute | solution.py:272
  70.7 5.4 %copy-start.2 = (bf16[256,1280]{1,0:T(8,128)(2,1)}, bf16[256,1280]{1,0:T(8,128)(2,1)S(1)}, u32[]{:S(2)}) copy-start(bf16[256,1280]{1,0:T(8,128)(2,1)S(1)} %collective-permute-done.9.w3) | copy-start | bytes 1966084
  76.2 8.6 %collective-permute-start.10 = (f32[16,512]{1,0:T(8,128)S(1)}, f32[16,512]{1,0:T(8,128)S(1)}, u32[]{:S(2)}, u32[]{:S(2)}) collective-permute-start(f32[16,512]{1,0:T(8,128)S(1)} %stats.1.own_stats), channel_id=1, source_target_pairs={{0,4},{1,5},{2,6},{3,7},{4,0},{5,1},{6,2},{7,3},{8,12},{9,13},{10,... | collective-permute-start | bytes 98312 | tf_op jit(solution)/shard_map/ppermute | solution.py:261
  84.7 1.1 copy-start.3
  99.7 35.4 %copy-start = (f32[256,1280]{1,0:T(8,128)}, f32[256,1280]{1,0:T(8,128)S(1)}, u32[]{:S(2)}) copy-start(f32[256,1280]{1,0:T(8,128)S(1)} %get-tuple-element.31.d0) | copy-start | bytes 3932164
  99.7 7.5 %collective-permute-start.12 = (bf16[256,1280]{1,0:T(8,128)(2,1)S(1)}, bf16[256,1280]{1,0:T(8,128)(2,1)S(1)}, u32[]{:S(2)}, u32[]{:S(2)}) collective-permute-start(bf16[256,1280]{1,0:T(8,128)(2,1)S(1)} %get-tuple-element.33), channel_id=1, source_target_pairs={{0,8},{8,0},{16,24},{24,16},{32,40},{40,32},{48,56},{56,48},{64,72... | collective-permute-start | bytes 1966088 | tf_op jit(solution)/shard_map/ppermute | solution.py:272
  105.3 29.5 %collective-permute-start.13 = (bf16[256,1280]{1,0:T(8,128)(2,1)S(1)}, bf16[256,1280]{1,0:T(8,128)(2,1)S(1)}, u32[]{:S(2)}, u32[]{:S(2)}) collective-permute-start(bf16[256,1280]{1,0:T(8,128)(2,1)S(1)} %get-tuple-element.34), channel_id=1, source_target_pairs={{8,0},{16,8},{24,16},{32,24},{40,32},{48,40},{56,48},{64,56},{72,6... | collective-permute-start | bytes 1966088 | tf_op jit(solution)/shard_map/ppermute | solution.py:267
  135.1 30.6 %collective-permute-start.14 = (bf16[256,1280]{1,0:T(8,128)(2,1)S(1)}, bf16[256,1280]{1,0:T(8,128)(2,1)S(1)}, u32[]{:S(2)}, u32[]{:S(2)}) collective-permute-start(bf16[256,1280]{1,0:T(8,128)(2,1)S(1)} %add_convert_fusion), channel_id=1, source_target_pairs={{16,0},{24,8},{32,16},{40,24},{48,32},{56,40},{64,48},{72,56},{80,... | collective-permute-start | bytes 1966088 | tf_op jit(solution)/shard_map/ppermute | solution.py:267
  137.0 24.4 %collective-permute-start.11 = (bf16[256,640]{1,0:T(8,128)(2,1)}, bf16[256,640]{1,0:T(8,128)(2,1)S(1)}, u32[]{:S(2)}, u32[]{:S(2)}) collective-permute-start(bf16[256,640]{1,0:T(8,128)(2,1)} %get-tuple-element.30), channel_id=1, source_target_pairs={{0,4},{1,5},{2,6},{3,7},{4,0},{5,1},{6,2},{7,3},{8,12},{9,13},{10,... | collective-permute-start | bytes 983048 | tf_op jit(solution)/shard_map/ppermute | solution.py:261
  165.7 1.3 copy-start.1
  167.3 12.6 %collective-permute-start.15 = (bf16[64,1920]{1,0:T(8,128)(2,1)S(1)}, bf16[64,1920]{1,0:T(8,128)(2,1)S(1)}, u32[]{:S(2)}, u32[]{:S(2)}) collective-permute-start(bf16[64,1920]{1,0:T(8,128)(2,1)S(1)} %get-tuple-element.36), channel_id=1, source_target_pairs={{0,3},{1,0},{2,1},{3,2},{4,7},{5,4},{6,5},{7,6},{8,11},{9,8},{10,9... | collective-permute-start | bytes 737288 | tf_op jit(solution)/shard_map/ppermute | solution.py:256
  169.2 11.0 %collective-permute-start.16 = (bf16[64,1920]{1,0:T(8,128)(2,1)S(1)}, bf16[64,1920]{1,0:T(8,128)(2,1)S(1)}, u32[]{:S(2)}, u32[]{:S(2)}) collective-permute-start(bf16[64,1920]{1,0:T(8,128)(2,1)S(1)} %get-tuple-element.37), channel_id=1, source_target_pairs={{0,2},{1,3},{2,0},{3,1},{4,6},{5,7},{6,4},{7,5},{8,10},{9,11},{10,... | collective-permute-start | bytes 737288 | tf_op jit(solution)/shard_map/ppermute | solution.py:256
  173.4 12.3 %collective-permute-start.17 = (bf16[64,1920]{1,0:T(8,128)(2,1)S(1)}, bf16[64,1920]{1,0:T(8,128)(2,1)S(1)}, u32[]{:S(2)}, u32[]{:S(2)}) collective-permute-start(bf16[64,1920]{1,0:T(8,128)(2,1)S(1)} %get-tuple-element.38), channel_id=1, source_target_pairs={{0,1},{1,2},{2,3},{3,0},{4,5},{5,6},{6,7},{7,4},{8,9},{9,10},{10,1... | collective-permute-start | bytes 737288 | tf_op jit(solution)/shard_map/ppermute | solution.py:256

commit v2 on v1

v2 whole, which is shorter than its diff:
```python
import functools
import math

import jax
import jax.numpy as jnp
from jax import lax
from jax.experimental import pallas as pl
from jax.experimental.pallas import tpu as pltpu
from jax.sharding import PartitionSpec as P

HEADS = 20
HDIM = 128
XN = 4
GROUP = HEADS // XN
NEG = -1e30
FACTOR = HDIM ** (-0.5)
SCALE2 = FACTOR * math.log2(math.e)
FRAME_LANE = 16
BF16 = jnp.bfloat16
F32 = jnp.float32
NT = (((1,), (1,)), ((), ()))
NN = (((1,), (0,)), ((), ()))


def params(room=40):
    return pltpu.CompilerParams(vmem_limit_bytes=room * 1024 * 1024)


def cost(flops, moved, exps=0):
    return pl.CostEstimate(flops=flops, bytes_accessed=moved, transcendentals=exps)


def pack_kernel(q_any, k_any, v_any, o_any, g_any, f_ref, qk, gv, held, sems):
    copies = []
    for at, src in enumerate((q_any, k_any, g_any, o_any, v_any)):
        copies.append(pltpu.make_async_copy(src, held.at[at], sems.at[at]))
    for copy in copies:
        copy.start()
    for copy in copies:
        copy.wait()
    tok = held.shape[1]
    wide = GROUP * HDIM
    lane = lax.broadcasted_iota(jnp.int32, (tok, HDIM), 1)
    frame = f_ref[...].astype(F32)
    for group in range(XN):
        here = slice(group * wide, (group + 1) * wide)
        meta = jnp.where(lane == FRAME_LANE, frame, 0.0)
        for h in range(GROUP):
            cols = slice((group * GROUP + h) * HDIM, (group * GROUP + h + 1) * HDIM)
            product = held[2, :, cols].astype(F32) * held[3, :, cols].astype(F32)
            dot = jnp.sum(product, axis=1, keepdims=True)
            high = dot.astype(BF16).astype(F32)
            meta = jnp.where(lane == h, high, meta)
            meta = jnp.where(lane == 8 + h, dot - high, meta)
        qk[group, :, :wide] = held[0, :, here]
        qk[group, :, wide : wide + HDIM] = meta.astype(BF16)
        qk[group, :, wide + HDIM :] = held[1, :, here]
        gv[group, :, :wide] = held[2, :, here]
        gv[group, :, wide:] = held[4, :, here]


def pack(query, key, value, saved_out, grad_out, frames):
    tok, width = query.shape
    wide = GROUP * HDIM
    vmem = pl.BlockSpec(memory_space=pltpu.VMEM)
    return pl.pallas_call(
        pack_kernel,
        out_shape=[
            jax.ShapeDtypeStruct((XN, tok, 2 * wide + HDIM), BF16),
            jax.ShapeDtypeStruct((XN, tok, 2 * wide), BF16),
        ],
        in_specs=[pl.BlockSpec(memory_space=pl.ANY)] * 5 + [vmem],
        out_specs=[vmem] * 2,
        scratch_shapes=[pltpu.VMEM((5, tok, width), BF16), pltpu.SemaphoreType.DMA((5,))],
        compiler_params=params(60),
        cost_estimate=cost(2 * tok * width, 18 * tok * width),
        name="pack",
    )(query, key, value, saved_out, grad_out, frames)


def window_scores(queries, keys):
    return lax.dot_general(keys, queries, NT, preferred_element_type=F32) * SCALE2


def both(own, far):
    return jnp.concatenate([own[...], far[...]], axis=0)


def stats_kernel(bias_ref, q_own, q_far, m_own, m_far, w0, w1, w2, w3, out_ref):
    head = pl.program_id(0)
    queries = both(q_own, q_far)
    rows = both(m_own, m_far).astype(F32).T
    q_frame = rows[FRAME_LANE : FRAME_LANE + 1, :]
    k_frame = m_own[...].astype(F32)[:, FRAME_LANE : FRAME_LANE + 1]

    scores, peaks = [], []
    for at, ref in enumerate((w0, w1, w2, w3)):
        part = window_scores(queries, ref[...])
        if at == 0:
            part = jnp.where(k_frame <= q_frame, part, NEG)
        scores.append(part)
        peaks.append(jnp.max(part, axis=0, keepdims=True) + bias_ref[at])
    peak = functools.reduce(jnp.maximum, peaks)
    total = jnp.zeros_like(peak)
    for at, part in enumerate(scores):
        total += jnp.sum(jnp.exp2(part - (peak - bias_ref[at])), axis=0, keepdims=True)

    @pl.when(head == 0)
    def _():
        out_ref[...] = jnp.zeros_like(out_ref)

    out_ref[pl.ds(head, 1), :] = peak
    out_ref[pl.ds(8 + head, 1), :] = total


def head_block(half):
    return pl.BlockSpec((half, HDIM), lambda h: (0, h))


def meta_block(half):
    return pl.BlockSpec((half, HDIM), lambda h: (0, GROUP))


def whole(shape):
    return pl.BlockSpec(shape, lambda h: (0, 0))


def smem():
    return pl.BlockSpec(memory_space=pltpu.SMEM)


def stats(bias, q_own, q_far, keys):
    half = q_own.shape[0]
    narrow, meta = head_block(half), meta_block(half)
    pairs = GROUP * 2 * half * 4 * half
    return pl.pallas_call(
        stats_kernel,
        grid=(GROUP,),
        out_shape=jax.ShapeDtypeStruct((16, 2 * half), F32),
        in_specs=[smem(), narrow, narrow, meta, meta] + [narrow] * 4,
        out_specs=whole((16, 2 * half)),
        compiler_params=params(),
        cost_estimate=cost(4 * pairs * HDIM, 6 * half * GROUP * HDIM * 2, pairs),
        name="stats",
    )(bias, q_own, q_far, q_own, q_far, *keys)


def log_total(head, half, own_stats, far_stats):
    own_peak = own_stats[pl.ds(head, 1), :]
    own_sum = own_stats[pl.ds(8 + head, 1), :]
    far_peak = far_stats[pl.ds(head, 1), :]
    far_sum = far_stats[pl.ds(8 + head, 1), :]
    far_peak = jnp.concatenate([far_peak[:, half:], far_peak[:, :half]], axis=1)
    far_sum = jnp.concatenate([far_sum[:, half:], far_sum[:, :half]], axis=1)
    peak = jnp.maximum(own_peak, far_peak)
    own_part = own_sum * jnp.exp2(own_peak - peak)
    return peak + jnp.log2(own_part + far_sum * jnp.exp2(far_peak - peak))


def dot_and_frame(head, m_own, m_far):
    meta = both(m_own, m_far).astype(F32)
    lane = lax.broadcasted_iota(jnp.int32, meta.shape, 1)
    picked = (lane == head) | (lane == head + 8)
    dot_col = jnp.sum(jnp.where(picked, meta, 0.0), axis=1, keepdims=True)
    rows = jnp.where(lane == FRAME_LANE, meta, dot_col).T
    return rows[0:1, :], rows[FRAME_LANE : FRAME_LANE + 1, :]


def block_grads(scores, total, dot, queries, grads, keys, values):
    probs = jnp.exp2(scores - total)
    dv = lax.dot_general(probs.astype(BF16), grads, NN, preferred_element_type=F32)
    dp = lax.dot_general(values, grads, NT, preferred_element_type=F32)
    ds = (probs * (dp - dot)).astype(BF16)
    dk = lax.dot_general(ds, queries, NN, preferred_element_type=F32) * FACTOR
    dq = lax.dot_general(keys.T, ds, NN, preferred_element_type=F32)
    return dq, dk, dv


def earlier_kernel(
    bias_ref, own_stats, far_stats, q_own, q_far, g_own, g_far, m_own, m_far,
    k1, k2, k3, v1, v2, v3, dq_ref, dk1, dk2, dk3, dv1, dv2, dv3,
):
    head = pl.program_id(0)
    queries, grads = both(q_own, q_far), both(g_own, g_far)
    dot, _ = dot_and_frame(head, m_own, m_far)
    total = log_total(head, q_own.shape[0], own_stats, far_stats)
    dq_sum = jnp.zeros(dq_ref.shape, F32)
    blocks = ((k1, v1, dk1, dv1), (k2, v2, dk2, dv2), (k3, v3, dk3, dv3))
    for at, (k_ref, v_ref, dk_ref, dv_ref) in enumerate(blocks):
        keys = k_ref[...]
        scores = window_scores(queries, keys)
        bound = total - bias_ref[at + 1]
        dq, dk, dv = block_grads(scores, bound, dot, queries, grads, keys, v_ref[...])
        dq_sum += dq
        dk_ref[...] = dk.astype(BF16)
        dv_ref[...] = dv.astype(BF16)
    dq_ref[...] = dq_sum


def earlier(bias, own_stats, far_stats, q_own, q_far, g_own, g_far, keys, values):
    half = q_own.shape[0]
    wide = GROUP * HDIM
    narrow, meta = head_block(half), meta_block(half)
    stat = whole((16, 2 * half))
    pairs = GROUP * 2 * half * 3 * half
    outs = pl.pallas_call(
        earlier_kernel,
        grid=(GROUP,),
        out_shape=[jax.ShapeDtypeStruct((wide, 2 * half), F32)]
        + [jax.ShapeDtypeStruct((half, wide), BF16)] * 6,
        in_specs=[smem(), stat, stat] + [narrow] * 4 + [meta] * 2 + [narrow] * 6,
        out_specs=[pl.BlockSpec((HDIM, 2 * half), lambda h: (h, 0))] + [narrow] * 6,
        compiler_params=params(),
        cost_estimate=cost(10 * pairs * HDIM, 20 * half * wide * 2, pairs),
        name="earlier",
    )(bias, own_stats, far_stats, q_own, q_far, g_own, g_far, q_own, q_far, *keys, *values)
    return outs[0], outs[1:4], outs[4:7]


def same_kernel(
    own_stats, far_stats, q_own, q_far, g_own, g_far, m_own, m_far,
    k_ref, v_ref, dq_ref, dq_own, dq_far, dk_ref, dv_ref,
):
    head = pl.program_id(0)
    half = q_own.shape[0]
    queries, grads = both(q_own, q_far), both(g_own, g_far)
    dot, q_frame = dot_and_frame(head, m_own, m_far)
    k_frame = m_own[...].astype(F32)[:, FRAME_LANE : FRAME_LANE + 1]
    total = log_total(head, half, own_stats, far_stats)
    keys = k_ref[...]
    scores = jnp.where(k_frame <= q_frame, window_scores(queries, keys), NEG)
    dq, dk, dv = block_grads(scores, total, dot, queries, grads, keys, v_ref[...])
    dq = ((dq + dq_ref[...]) * FACTOR).T
    dq_own[...] = dq[:half]
    dq_far[...] = dq[half:].astype(BF16)
    dk_ref[...] = dk
    dv_ref[...] = dv


def same(own_stats, far_stats, q_own, q_far, g_own, g_far, keys, values, dq):
    half = q_own.shape[0]
    wide = GROUP * HDIM
    narrow, meta = head_block(half), meta_block(half)
    stat = whole((16, 2 * half))
    pairs = GROUP * 2 * half * half
    turned = pl.BlockSpec((HDIM, 2 * half), lambda h: (h, 0))
    return pl.pallas_call(
        same_kernel,
        grid=(GROUP,),
        out_shape=[
            jax.ShapeDtypeStruct((half, wide), F32),
            jax.ShapeDtypeStruct((half, wide), BF16),
            jax.ShapeDtypeStruct((half, wide), F32),
            jax.ShapeDtypeStruct((half, wide), F32),
        ],
        in_specs=[stat, stat] + [narrow] * 4 + [meta] * 2 + [narrow] * 2 + [turned],
        out_specs=[narrow] * 4,
        compiler_params=params(),
        cost_estimate=cost(10 * pairs * HDIM, 16 * half * wide * 2, pairs),
        name="same",
    )(own_stats, far_stats, q_own, q_far, g_own, g_far, q_own, q_far, keys, values, dq)


def close_kernel(even_ref, dq_own, dq_far, dk, dv, k_back, v_back, k_side, v_side, out):
    even = even_ref[0].astype(F32)
    tok = out.shape[1]
    wide = dq_own.shape[1]
    for step in range(XN):
        rows = slice(step * tok, (step + 1) * tok)
        grad_q = dq_own[rows, :] + dq_far[rows, :].astype(F32)
        grad_k = dk[rows, :] + k_back[rows, :].astype(F32) + k_side[rows, :].astype(F32) * even
        grad_v = dv[rows, :] + v_back[rows, :].astype(F32) + v_side[rows, :].astype(F32) * even
        out[step, :, :wide] = grad_q.astype(BF16)
        out[step, :, wide : 2 * wide] = grad_k.astype(BF16)
        out[step, :, 2 * wide :] = grad_v.astype(BF16)


def close(even, dq_own, dq_far, dk, dv, k_back, v_back, k_side, v_side):
    half, wide = dq_own.shape
    tok = half // XN
    vmem = pl.BlockSpec(memory_space=pltpu.VMEM)
    return pl.pallas_call(
        close_kernel,
        out_shape=jax.ShapeDtypeStruct((XN, tok, 3 * wide), BF16),
        in_specs=[smem()] + [vmem] * 8,
        out_specs=vmem,
        compiler_params=params(),
        cost_estimate=cost(5 * half * wide, 28 * half * wide),
        name="close",
    )(even, dq_own, dq_far, dk, dv, k_back, v_back, k_side, v_side)


def unpack_kernel(parts, dq, dk, dv):
    wide = GROUP * HDIM
    for group in range(XN):
        here = slice(group * wide, (group + 1) * wide)
        dq[:, here] = parts[group, :, :wide]
        dk[:, here] = parts[group, :, wide : 2 * wide]
        dv[:, here] = parts[group, :, 2 * wide :]


def unpack(parts):
    tok = parts.shape[1]
    vmem = pl.BlockSpec(memory_space=pltpu.VMEM)
    return pl.pallas_call(
        unpack_kernel,
        out_shape=[jax.ShapeDtypeStruct((tok, HEADS * HDIM), BF16)] * 3,
        in_specs=[vmem],
        out_specs=[vmem] * 3,
        compiler_params=params(),
        cost_estimate=cost(0, 12 * tok * HEADS * HDIM),
        name="unpack",
    )(parts)


def over_x(value):
    groups = [[z * XN + x for x in range(XN)] for z in range(lax.axis_size("col") // XN)]
    return lax.all_to_all(value, "col", 0, 0, axis_index_groups=groups)


def across_z(value):
    count = lax.axis_size("col")
    return lax.ppermute(value, "col", [(c, (c + XN) % count) for c in range(count)])


def along_row(value, steps):
    count = lax.axis_size("row")
    first, last = max(0, -steps), min(count, count - steps)
    return lax.ppermute(value, "row", [(r, r + steps) for r in range(first, last)])


def in_chip(value):
    count = lax.axis_size("row")
    return lax.ppermute(value, "row", [(r, r ^ 1) for r in range(count)])


def halo(own, is_even):
    second = along_row(own, 2)
    swapped = in_chip(second)
    third = along_row(jnp.where(is_even, own, second), 1)
    return own, second, swapped, third


def halo_back(second, swapped, third, is_even):
    side = along_row(third, -1)
    turned = jnp.where(is_even, jnp.zeros_like(side), side)
    held = second.astype(F32) + in_chip(swapped).astype(F32) + turned.astype(F32)
    return along_row(held.astype(BF16), -2), side


def per_device(query, key, value, saved_out, grad_out, frame_ids):
    row = lax.axis_index("row")
    is_even = row % 2 == 0
    even = is_even.astype(jnp.int32).reshape(1)
    wide = GROUP * HDIM
    half = query.shape[0] * XN

    qk, gv = pack(query, key, value, saved_out, grad_out, frame_ids[:, None])
    qk = over_x(qk)
    gv = over_x(gv)
    q_own = qk[:, :, : wide + HDIM].reshape(half, wide + HDIM)
    g_own = gv[:, :, :wide].reshape(half, wide)
    q_far = across_z(q_own)
    g_far = across_z(g_own)
    keys = halo(qk[:, :, wide + HDIM :].reshape(half, wide), is_even)
    values = halo(gv[:, :, wide:].reshape(half, wide), is_even)
    held = jnp.stack(
        [
            row >= 0,
            row >= 2,
            jnp.where(is_even, row >= 1, row >= 3),
            jnp.where(is_even, row >= 3, row >= 1),
        ]
    )
    bias = jnp.where(held, 0.0, NEG).astype(F32)

    own_stats = stats(bias, q_own, q_far, keys)
    far_stats = across_z(own_stats)
    tokens = (own_stats, far_stats, q_own, q_far, g_own, g_far)
    dq_part, dk_parts, dv_parts = earlier(bias, *tokens, keys[1:], values[1:])
    dq_own, dq_far, dk, dv = same(*tokens, keys[0], values[0], dq_part)

    k_back, k_side = halo_back(*dk_parts, is_even)
    v_back, v_side = halo_back(*dv_parts, is_even)
    dq_far = across_z(dq_far)
    parts = close(even, dq_own, dq_far, dk, dv, k_back, v_back, k_side, v_side)
    return tuple(unpack(over_x(parts)))


def solution(mesh):
    placed = P(("row", "col"), None)
    return jax.shard_map(
        per_device,
        mesh=mesh,
        in_specs=(placed,) * 5 + (P(("row", "col")),),
        out_specs=(placed,) * 3,
        check_vma=False,
    )
```

time: 188 us -> 180 us (0.957)
  the two profiles are of different devices: /device:TPU:121 before, /device:TPU:248 now
where the time goes in v2:
time: 180 us; the launch traced here: 179 us
  starting transfers between devices  59.2 us (33%)
  waiting for transfers between devices  56.8 us (32%)
  blocking collectives  31.3 us (17%)
  Pallas kernels  25.5 us (14%)
  local copies, waits for them, and re-layouts  3.66 us (2%)
  other arithmetic  1.95 us (1%)
    ppermute x4, waiting for transfers between devices, across_z(): lax.ppermute(value, 'col', [(c, (c + XN) % count) for c in range(count)])  48.5 us
    all_to_all x2, blocking collectives, over_x(): return lax.all_to_all(value, 'col', 0, 0, axis_index_groups=groups)  31.3 us
    ppermute x4, starting transfers between devices, across_z(): lax.ppermute(value, 'col', [(c, (c + XN) % count) for c in range(count)])  26.7 us
    ppermute x8, starting transfers between devices, along_row(): lax.ppermute(value, 'row', [(r, r + steps) for r in range(first, last)])  21.4 us
    pallas_call x1, Pallas kernels, earlier(): pl.pallas_call(earlier_kernel, grid=(GROUP,), out_shape=[jax.ShapeDtypeSt...  9.83 us
    all_to_all x1, waiting for transfers between devices, over_x(): return lax.all_to_all(value, 'col', 0, 0, axis_index_groups=groups)  8.31 us
    ppermute x4, starting transfers between devices, in_chip(): return lax.ppermute(value, 'row', [(r, r ^ 1) for r in range(count)])  7.67 us
    pallas_call x1, Pallas kernels, same(): pl.pallas_call(same_kernel, grid=(GROUP,), out_shape=[jax.ShapeDtypeStruc...  5.79 us
  transfers between devices with their start and end apart: 17, of which 4 were waited for; matrix products, arithmetic and copies ran while one was open for 1% of the time, Pallas kernels for 6%

profile of v2, /device:TPU:248, one launch (start us, length us, event | category | flops | bytes accessed | tf_op | source)
XLA Modules:
  0.0 179.4 jit_solution(14801228777059503451)
XLA Ops:
  0.6 1.4 copy.9.f_ref
  2.0 3.6 %pack.1 = (bf16[4,64,1408]{2,1,0:T(8,128)(2,1)}, bf16[4,64,1280]{2,1,0:T(8,128)(2,1)}) custom-call(bf16[64,2560]{1,0:T(8,128)(2,1)} %q_any.1, bf16[64,2560]{1,0:T(8,128)(2,1)} %k_any.1, bf16[64,2560]{1,0:T(8,128)(2,1)} %v_any.1, bf16[64,2560]{1,0:T(8,128)(2,1)} %o_any.1, bf16[64,2560]{1,0:T(8,128)(2,1)} %g_any.1, s32[64,1]{1,0:T(8,128)} %copy.9.f_ref), custom_call_target="tpu_custom_call" | custom-call | flops 327680 | bytes 2949120 | tf_op jit(solution)/shard_map/pack/pallas_call | solution.py:66
  5.6 15.9 %all_to_all.15 = bf16[4,64,1408]{2,1,0:T(8,128)(2,1)S(1)} all-to-all(bf16[4,64,1408]{2,1,0:T(8,128)(2,1)} %get-tuple-element.16), channel_id=1, replica_groups={{0,1,2,3},{4,5,6,7},{8,9,10,11},{12,13,14,15},{16,17,18,19},{20,21,22,2..., dimensions={0} | all-to-all | bytes 1441792 | tf_op jit(solution)/shard_map/all_to_all | solution.py:318
  21.4 3.5 %all-to-all-start.1 = ((bf16[4,64,1280]{2,1,0:T(8,128)(2,1)}), bf16[4,64,1280]{2,1,0:T(8,128)(2,1)S(1)}, u32[]{:S(2)}, u32[]{:S(2)}) async-start(bf16[4,64,1280]{2,1,0:T(8,128)(2,1)} %get-tuple-element.17), calls=%async_computation.1 | async-start | bytes 1310720 | tf_op jit(solution)/shard_map/all_to_all | solution.py:318
  25.0 1.3 collective-permute-start.1
  26.3 8.3 %all-to-all-done.1 = bf16[4,64,1280]{2,1,0:T(8,128)(2,1)S(1)} async-done(((bf16[4,64,1280]{2,1,0:T(8,128)(2,1)}), bf16[4,64,1280]{2,1,0:T(8,128)(2,1)S(1)}, u32[]{:S(2)}, u32[]{:S(2)}) %all-to-all-start.1) | async-done | bytes 655392 | tf_op jit(solution)/shard_map/all_to_all | solution.py:318
  34.6 0.1 fusion
  34.6 1.3 collective-permute-start.6
  36.0 8.2 %collective-permute-start.5 = (bf16[256,640]{1,0:T(8,128)(2,1)S(1)}, bf16[256,640]{1,0:T(8,128)(2,1)S(1)}, u32[]{:S(2)}, u32[]{:S(2)}) collective-permute-start(bf16[256,640]{1,0:T(8,128)(2,1)S(1)} %bitcast.24), channel_id=1, source_target_pairs={{0,4},{1,5},{2,6},{3,7},{4,0},{5,1},{6,2},{7,3},{8,12},{9,13},{10,... | collective-permute-start | bytes 983048 | tf_op jit(solution)/shard_map/ppermute | solution.py:323
  44.2 1.9 %collective-permute-start = (bf16[256,768]{1,0:T(8,128)(2,1)S(1)}, bf16[256,768]{1,0:T(8,128)(2,1)S(1)}, u32[]{:S(2)}, u32[]{:S(2)}) collective-permute-start(bf16[256,768]{1,0:T(8,128)(2,1)S(1)} %bitcast.12), channel_id=1, source_target_pairs={{0,4},{1,5},{2,6},{3,7},{4,0},{5,1},{6,2},{7,3},{8,12},{9,13},{10,... | collective-permute-start | bytes 1179656 | tf_op jit(solution)/shard_map/ppermute | solution.py:323
  46.2 0.0 collective-permute-done.1.w1.k1
  46.2 0.8 broadcast_select_fusion.1
  47.0 1.9 %collective-permute-start.3 = (bf16[256,640]{1,0:T(8,128)(2,1)}, bf16[256,640]{1,0:T(8,128)(2,1)S(1)}, u32[]{:S(2)}, u32[]{:S(2)}) collective-permute-start(bf16[256,640]{1,0:T(8,128)(2,1)} %broadcast_select_fusion.1), channel_id=1, source_target_pairs={{0,8},{8,16},{16,24},{24,32},{32,40},{40,48},{48,56},{56,64},{64,7... | collective-permute-start | bytes 983048 | tf_op jit(solution)/shard_map/ppermute | solution.py:329
  48.9 1.9 %collective-permute-start.2 = (bf16[256,640]{1,0:T(8,128)(2,1)S(1)}, bf16[256,640]{1,0:T(8,128)(2,1)S(1)}, u32[]{:S(2)}, u32[]{:S(2)}) collective-permute-start(bf16[256,640]{1,0:T(8,128)(2,1)S(1)} %collective-permute-done.1.w1.k1), channel_id=1, source_target_pairs={{0,8},{8,0},{16,24},{24,16},{32,40},{40,32},{48,56},{56,48},{64,72... | collective-permute-start | bytes 983048 | tf_op jit(solution)/shard_map/ppermute | solution.py:334
  50.8 0.0 collective-permute-done.6.v1
  50.8 0.8 broadcast_select_fusion
  51.6 2.4 %collective-permute-start.8 = (bf16[256,640]{1,0:T(8,128)(2,1)}, bf16[256,640]{1,0:T(8,128)(2,1)}, u32[]{:S(2)}, u32[]{:S(2)}) collective-permute-start(bf16[256,640]{1,0:T(8,128)(2,1)} %broadcast_select_fusion), channel_id=1, source_target_pairs={{0,8},{8,16},{16,24},{24,32},{32,40},{40,48},{48,56},{56,64},{64,7... | collective-permute-start | bytes 983048 | tf_op jit(solution)/shard_map/ppermute | solution.py:329
  54.0 17.6 %collective-permute-done.q_far.m_far = bf16[256,768]{1,0:T(8,128)(2,1)S(1)} collective-permute-done((bf16[256,768]{1,0:T(8,128)(2,1)S(1)}, bf16[256,768]{1,0:T(8,128)(2,1)S(1)}, u32[]{:S(2)}, u32[]{:S(2)}) %collective-permute-start) | collective-permute-done | bytes 393248 | tf_op jit(solution)/shard_map/ppermute | solution.py:323
  71.6 1.9 %collective-permute-start.7 = (bf16[256,640]{1,0:T(8,128)(2,1)S(1)}, bf16[256,640]{1,0:T(8,128)(2,1)}, u32[]{:S(2)}, u32[]{:S(2)}) collective-permute-start(bf16[256,640]{1,0:T(8,128)(2,1)S(1)} %collective-permute-done.6.v1), channel_id=1, source_target_pairs={{0,8},{8,0},{16,24},{24,16},{32,40},{40,32},{48,56},{56,48},{64,72... | collective-permute-start | bytes 983048 | tf_op jit(solution)/shard_map/ppermute | solution.py:334
  73.5 0.1 add_select_fusion.bias_ref
  73.6 0.0 collective-permute-done.3.w3.k3
  73.6 0.0 collective-permute-done.2.w2.k2
  73.6 5.0 %stats.1.own_stats = f32[16,512]{1,0:T(8,128)S(1)} custom-call(f32[4]{0:T(128)S(1)} %add_select_fusion.bias_ref, bf16[256,768]{1,0:T(8,128)(2,1)S(1)} %bitcast.13, bf16[256,768]{1,0:T(8,128)(2,1)S(1)} %collective-permute-done.q_far.m_far, bf16[256,768]{1,0:T(8,128)(2,1)S(1)} %bitcast.14, bf16[256,768]{1,0:T(8,128)(2,1)S(1)} %collective-permute-done.q_far.m_far, ...), custom_call_target="tpu_custom_call" | custom-call | flops 1342177280 | bytes 1966080 | tf_op jit(solution)/shard_map/stats/pallas_call | solution.py:136
  78.6 8.3 %collective-permute-start.4 = (f32[16,512]{1,0:T(8,128)S(1)}, f32[16,512]{1,0:T(8,128)S(1)}, u32[]{:S(2)}, u32[]{:S(2)}) collective-permute-start(f32[16,512]{1,0:T(8,128)S(1)} %stats.1.own_stats), channel_id=1, source_target_pairs={{0,4},{1,5},{2,6},{3,7},{4,0},{5,1},{6,2},{7,3},{8,12},{9,13},{10,... | collective-permute-start | bytes 98312 | tf_op jit(solution)/shard_map/ppermute | solution.py:323
  86.9 0.0 collective-permute-done.5.g_far
  87.0 0.0 collective-permute-done.8.v3
  87.0 0.0 collective-permute-done.7.v2
  87.0 2.1 %collective-permute-done.4.far_stats = f32[16,512]{1,0:T(8,128)S(1)} collective-permute-done((f32[16,512]{1,0:T(8,128)S(1)}, f32[16,512]{1,0:T(8,128)S(1)}, u32[]{:S(2)}, u32[]{:S(2)}) %collective-permute-start.4) | collective-permute-done | bytes 32800 | tf_op jit(solution)/shard_map/ppermute | solution.py:323
  89.1 9.8 %earlier.1 = (f32[640,512]{1,0:T(8,128)S(1)}, bf16[256,640]{1,0:T(8,128)(2,1)S(1)}, bf16[256,640]{1,0:T(8,128)(2,1)S(1)}, bf16[256,640]{1,0:T(8,128)(2,1)S(1)}, ...) custom-call(f32[4]{0:T(128)S(1)} %add_select_fusion.bias_ref, ...), custom_call_target="tpu_custom_call" | custom-call | flops 2516582400 | bytes 6553600 | tf_op jit(solution)/shard_map/earlier/pallas_call | solution.py:206
  98.9 1.9 %collective-permute-start.13 = (bf16[256,640]{1,0:T(8,128)(2,1)S(1)}, bf16[256,640]{1,0:T(8,128)(2,1)S(1)}, u32[]{:S(2)}, u32[]{:S(2)}) collective-permute-start(bf16[256,640]{1,0:T(8,128)(2,1)S(1)} %get-tuple-element.27), channel_id=1, source_target_pairs={{0,8},{8,0},{16,24},{24,16},{32,40},{40,32},{48,56},{56,48},{64,72... | collective-permute-start | bytes 983048 | tf_op jit(solution)/shard_map/ppermute | solution.py:334
  100.8 3.4 %collective-permute-start.14 = (bf16[256,640]{1,0:T(8,128)(2,1)S(1)}, bf16[256,640]{1,0:T(8,128)(2,1)S(1)}, u32[]{:S(2)}, u32[]{:S(2)}) collective-permute-start(bf16[256,640]{1,0:T(8,128)(2,1)S(1)} %get-tuple-element.28), channel_id=1, source_target_pairs={{8,0},{16,8},{24,16},{32,24},{40,32},{48,40},{56,48},{64,56},{72,6... | collective-permute-start | bytes 983048 | tf_op jit(solution)/shard_map/ppermute | solution.py:329
  104.2 1.9 %collective-permute-start.10 = (bf16[256,640]{1,0:T(8,128)(2,1)S(1)}, bf16[256,640]{1,0:T(8,128)(2,1)S(1)}, u32[]{:S(2)}, u32[]{:S(2)}) collective-permute-start(bf16[256,640]{1,0:T(8,128)(2,1)S(1)} %get-tuple-element.24), channel_id=1, source_target_pairs={{0,8},{8,0},{16,24},{24,16},{32,40},{40,32},{48,56},{56,48},{64,72... | collective-permute-start | bytes 983048 | tf_op jit(solution)/shard_map/ppermute | solution.py:334
  106.2 3.4 %collective-permute-start.11 = (bf16[256,640]{1,0:T(8,128)(2,1)S(1)}, bf16[256,640]{1,0:T(8,128)(2,1)S(1)}, u32[]{:S(2)}, u32[]{:S(2)}) collective-permute-start(bf16[256,640]{1,0:T(8,128)(2,1)S(1)} %get-tuple-element.25), channel_id=1, source_target_pairs={{8,0},{16,8},{24,16},{32,24},{40,32},{48,40},{56,48},{64,56},{72,6... | collective-permute-start | bytes 983048 | tf_op jit(solution)/shard_map/ppermute | solution.py:329
  109.5 5.8 %same.1 = (f32[256,640]{1,0:T(8,128)S(1)}, bf16[256,640]{1,0:T(8,128)(2,1)}, f32[256,640]{1,0:T(8,128)S(1)}, f32[256,640]{1,0:T(8,128)S(1)}) custom-call(f32[16,512]{1,0:T(8,128)S(1)} %stats.1.own_stats, f32[16,512]{1,0:T(8,128)S(1)} %collective-permute-done.4.far_stats, bf16[256,768]{1,0:T(8,128)(2,1)S(1)} %bitcast.17, ...), custom_call_target="tpu_custom_call" | custom-call | flops 838860800 | bytes 5242880 | tf_op jit(solution)/shard_map/same/pallas_call | solution.py:247
  115.3 0.0 copy-start
  115.3 0.0 copy-start.2
  115.3 8.2 %collective-permute-start.9 = (bf16[256,640]{1,0:T(8,128)(2,1)}, bf16[256,640]{1,0:T(8,128)(2,1)S(1)}, u32[]{:S(2)}, u32[]{:S(2)}) collective-permute-start(bf16[256,640]{1,0:T(8,128)(2,1)} %get-tuple-element.20), channel_id=1, source_target_pairs={{0,4},{1,5},{2,6},{3,7},{4,0},{5,1},{6,2},{7,3},{8,12},{9,13},{10,... | collective-permute-start | bytes 983048 | tf_op jit(solution)/shard_map/ppermute | solution.py:323
  123.5 0.0 collective-permute-done.13
  123.6 0.0 collective-permute-done.14.v_side
  123.6 0.1 add_convert_fusion
  123.7 3.3 %collective-permute-start.15 = (bf16[256,640]{1,0:T(8,128)(2,1)S(1)}, bf16[256,640]{1,0:T(8,128)(2,1)S(1)}, u32[]{:S(2)}, u32[]{:S(2)}) collective-permute-start(bf16[256,640]{1,0:T(8,128)(2,1)S(1)} %add_convert_fusion), channel_id=1, source_target_pairs={{16,0},{24,8},{32,16},{40,24},{48,32},{56,40},{64,48},{72,56},{80,... | collective-permute-start | bytes 983048 | tf_op jit(solution)/shard_map/ppermute | solution.py:329
  127.0 0.0 collective-permute-done.10
  127.0 0.0 collective-permute-done.11.k_side
  127.0 0.1 add_convert_fusion.1
  127.2 0.0 copy-done
  127.2 0.0 copy-done.2
  127.2 4.5 %collective-permute-start.12 = (bf16[256,640]{1,0:T(8,128)(2,1)S(1)}, bf16[256,640]{1,0:T(8,128)(2,1)S(1)}, u32[]{:S(2)}, u32[]{:S(2)}) collective-permute-start(bf16[256,640]{1,0:T(8,128)(2,1)S(1)} %add_convert_fusion.1), channel_id=1, source_target_pairs={{16,0},{24,8},{32,16},{40,24},{48,32},{56,40},{64,48},{72,56},{80,... | collective-permute-start | bytes 983048 | tf_op jit(solution)/shard_map/ppermute | solution.py:329
  131.7 28.9 %collective-permute-done.9.dq_far = bf16[256,640]{1,0:T(8,128)(2,1)S(1)} collective-permute-done((bf16[256,640]{1,0:T(8,128)(2,1)}, bf16[256,640]{1,0:T(8,128)(2,1)S(1)}, u32[]{:S(2)}, u32[]{:S(2)}) %collective-permute-start.9) | collective-permute-done | bytes 327712 | tf_op jit(solution)/shard_map/ppermute | solution.py:323
  160.5 0.0 collective-permute-done.15.v_back
  160.5 0.0 collective-permute-done.12.k_back
  160.5 0.0 copy-start.1
  160.5 1.1 copy-done.1
  161.6 0.0 copy-start.3
  161.6 1.1 copy-done.3
  162.7 0.3 close.1
  163.0 15.4 %all_to_all.16.parts = bf16[4,64,1920]{2,1,0:T(8,128)(2,1)S(1)} all-to-all(bf16[4,64,1920]{2,1,0:T(8,128)(2,1)S(1)} %close.1), channel_id=1, replica_groups={{0,1,2,3},{4,5,6,7},{8,9,10,11},{12,13,14,15},{16,17,18,19},{20,21,22,2..., dimensions={0} | all-to-all | bytes 1966080 | tf_op jit(solution)/shard_map/all_to_all | solution.py:318
  178.4 1.0 unpack.1
  (2 shorter events, 0.1 us)
Async XLA Ops:
  21.4 13.1 %all-to-all-start.1 = ((bf16[4,64,1280]{2,1,0:T(8,128)(2,1)}), bf16[4,64,1280]{2,1,0:T(8,128)(2,1)S(1)}, u32[]{:S(2)}, u32[]{:S(2)}) async-start(bf16[4,64,1280]{2,1,0:T(8,128)(2,1)} %get-tuple-element.17), calls=%async_computation.1 | async-start | bytes 1310720 | tf_op jit(solution)/shard_map/all_to_all | solution.py:318
  25.0 21.2 %collective-permute-start.1 = (bf16[256,640]{1,0:T(8,128)(2,1)S(1)}, bf16[256,640]{1,0:T(8,128)(2,1)S(1)}, u32[]{:S(2)}, u32[]{:S(2)}) collective-permute-start(bf16[256,640]{1,0:T(8,128)(2,1)S(1)} %bitcast.21), channel_id=1, source_target_pairs={{0,16},{8,24},{16,32},{24,40},{32,48},{40,56},{48,64},{56,72},{64,... | collective-permute-start | bytes 983048 | tf_op jit(solution)/shard_map/ppermute | solution.py:329
  34.6 16.2 %collective-permute-start.6 = (bf16[256,640]{1,0:T(8,128)(2,1)S(1)}, bf16[256,640]{1,0:T(8,128)(2,1)S(1)}, u32[]{:S(2)}, u32[]{:S(2)}) collective-permute-start(bf16[256,640]{1,0:T(8,128)(2,1)S(1)} %bitcast.19), channel_id=1, source_target_pairs={{0,16},{8,24},{16,32},{24,40},{32,48},{40,56},{48,64},{56,72},{64,... | collective-permute-start | bytes 983048 | tf_op jit(solution)/shard_map/ppermute | solution.py:329
  36.0 51.0 %collective-permute-start.5 = (bf16[256,640]{1,0:T(8,128)(2,1)S(1)}, bf16[256,640]{1,0:T(8,128)(2,1)S(1)}, u32[]{:S(2)}, u32[]{:S(2)}) collective-permute-start(bf16[256,640]{1,0:T(8,128)(2,1)S(1)} %bitcast.24), channel_id=1, source_target_pairs={{0,4},{1,5},{2,6},{3,7},{4,0},{5,1},{6,2},{7,3},{8,12},{9,13},{10,... | collective-permute-start | bytes 983048 | tf_op jit(solution)/shard_map/ppermute | solution.py:323
  44.2 27.3 %collective-permute-start = (bf16[256,768]{1,0:T(8,128)(2,1)S(1)}, bf16[256,768]{1,0:T(8,128)(2,1)S(1)}, u32[]{:S(2)}, u32[]{:S(2)}) collective-permute-start(bf16[256,768]{1,0:T(8,128)(2,1)S(1)} %bitcast.12), channel_id=1, source_target_pairs={{0,4},{1,5},{2,6},{3,7},{4,0},{5,1},{6,2},{7,3},{8,12},{9,13},{10,... | collective-permute-start | bytes 1179656 | tf_op jit(solution)/shard_map/ppermute | solution.py:323
  47.0 26.6 %collective-permute-start.3 = (bf16[256,640]{1,0:T(8,128)(2,1)}, bf16[256,640]{1,0:T(8,128)(2,1)S(1)}, u32[]{:S(2)}, u32[]{:S(2)}) collective-permute-start(bf16[256,640]{1,0:T(8,128)(2,1)} %broadcast_select_fusion.1), channel_id=1, source_target_pairs={{0,8},{8,16},{16,24},{24,32},{32,40},{40,48},{48,56},{56,64},{64,7... | collective-permute-start | bytes 983048 | tf_op jit(solution)/shard_map/ppermute | solution.py:329
  48.9 24.7 %collective-permute-start.2 = (bf16[256,640]{1,0:T(8,128)(2,1)S(1)}, bf16[256,640]{1,0:T(8,128)(2,1)S(1)}, u32[]{:S(2)}, u32[]{:S(2)}) collective-permute-start(bf16[256,640]{1,0:T(8,128)(2,1)S(1)} %collective-permute-done.1.w1.k1), channel_id=1, source_target_pairs={{0,8},{8,0},{16,24},{24,16},{32,40},{40,32},{48,56},{56,48},{64,72... | collective-permute-start | bytes 983048 | tf_op jit(solution)/shard_map/ppermute | solution.py:334
  51.6 35.4 %collective-permute-start.8 = (bf16[256,640]{1,0:T(8,128)(2,1)}, bf16[256,640]{1,0:T(8,128)(2,1)}, u32[]{:S(2)}, u32[]{:S(2)}) collective-permute-start(bf16[256,640]{1,0:T(8,128)(2,1)} %broadcast_select_fusion), channel_id=1, source_target_pairs={{0,8},{8,16},{16,24},{24,32},{32,40},{40,48},{48,56},{56,64},{64,7... | collective-permute-start | bytes 983048 | tf_op jit(solution)/shard_map/ppermute | solution.py:329
  71.6 15.4 %collective-permute-start.7 = (bf16[256,640]{1,0:T(8,128)(2,1)S(1)}, bf16[256,640]{1,0:T(8,128)(2,1)}, u32[]{:S(2)}, u32[]{:S(2)}) collective-permute-start(bf16[256,640]{1,0:T(8,128)(2,1)S(1)} %collective-permute-done.6.v1), channel_id=1, source_target_pairs={{0,8},{8,0},{16,24},{24,16},{32,40},{40,32},{48,56},{56,48},{64,72... | collective-permute-start | bytes 983048 | tf_op jit(solution)/shard_map/ppermute | solution.py:334
  78.6 10.4 %collective-permute-start.4 = (f32[16,512]{1,0:T(8,128)S(1)}, f32[16,512]{1,0:T(8,128)S(1)}, u32[]{:S(2)}, u32[]{:S(2)}) collective-permute-start(f32[16,512]{1,0:T(8,128)S(1)} %stats.1.own_stats), channel_id=1, source_target_pairs={{0,4},{1,5},{2,6},{3,7},{4,0},{5,1},{6,2},{7,3},{8,12},{9,13},{10,... | collective-permute-start | bytes 98312 | tf_op jit(solution)/shard_map/ppermute | solution.py:323
  98.9 24.7 %collective-permute-start.13 = (bf16[256,640]{1,0:T(8,128)(2,1)S(1)}, bf16[256,640]{1,0:T(8,128)(2,1)S(1)}, u32[]{:S(2)}, u32[]{:S(2)}) collective-permute-start(bf16[256,640]{1,0:T(8,128)(2,1)S(1)} %get-tuple-element.27), channel_id=1, source_target_pairs={{0,8},{8,0},{16,24},{24,16},{32,40},{40,32},{48,56},{56,48},{64,72... | collective-permute-start | bytes 983048 | tf_op jit(solution)/shard_map/ppermute | solution.py:334
  100.8 22.7 %collective-permute-start.14 = (bf16[256,640]{1,0:T(8,128)(2,1)S(1)}, bf16[256,640]{1,0:T(8,128)(2,1)S(1)}, u32[]{:S(2)}, u32[]{:S(2)}) collective-permute-start(bf16[256,640]{1,0:T(8,128)(2,1)S(1)} %get-tuple-element.28), channel_id=1, source_target_pairs={{8,0},{16,8},{24,16},{32,24},{40,32},{48,40},{56,48},{64,56},{72,6... | collective-permute-start | bytes 983048 | tf_op jit(solution)/shard_map/ppermute | solution.py:329
  104.2 22.8 %collective-permute-start.10 = (bf16[256,640]{1,0:T(8,128)(2,1)S(1)}, bf16[256,640]{1,0:T(8,128)(2,1)S(1)}, u32[]{:S(2)}, u32[]{:S(2)}) collective-permute-start(bf16[256,640]{1,0:T(8,128)(2,1)S(1)} %get-tuple-element.24), channel_id=1, source_target_pairs={{0,8},{8,0},{16,24},{24,16},{32,40},{40,32},{48,56},{56,48},{64,72... | collective-permute-start | bytes 983048 | tf_op jit(solution)/shard_map/ppermute | solution.py:334
  106.2 20.9 %collective-permute-start.11 = (bf16[256,640]{1,0:T(8,128)(2,1)S(1)}, bf16[256,640]{1,0:T(8,128)(2,1)S(1)}, u32[]{:S(2)}, u32[]{:S(2)}) collective-permute-start(bf16[256,640]{1,0:T(8,128)(2,1)S(1)} %get-tuple-element.25), channel_id=1, source_target_pairs={{8,0},{16,8},{24,16},{32,24},{40,32},{48,40},{56,48},{64,56},{72,6... | collective-permute-start | bytes 983048 | tf_op jit(solution)/shard_map/ppermute | solution.py:329
  115.3 11.9 %copy-start = (f32[256,640]{1,0:T(8,128)}, f32[256,640]{1,0:T(8,128)S(1)}, u32[]{:S(2)}) copy-start(f32[256,640]{1,0:T(8,128)S(1)} %get-tuple-element.21.dk) | copy-start | bytes 1966084
  115.3 11.9 %copy-start.2 = (f32[256,640]{1,0:T(8,128)}, f32[256,640]{1,0:T(8,128)S(1)}, u32[]{:S(2)}) copy-start(f32[256,640]{1,0:T(8,128)S(1)} %get-tuple-element.22.dv) | copy-start | bytes 1966084
  115.3 45.2 %collective-permute-start.9 = (bf16[256,640]{1,0:T(8,128)(2,1)}, bf16[256,640]{1,0:T(8,128)(2,1)S(1)}, u32[]{:S(2)}, u32[]{:S(2)}) collective-permute-start(bf16[256,640]{1,0:T(8,128)(2,1)} %get-tuple-element.20), channel_id=1, source_target_pairs={{0,4},{1,5},{2,6},{3,7},{4,0},{5,1},{6,2},{7,3},{8,12},{9,13},{10,... | collective-permute-start | bytes 983048 | tf_op jit(solution)/shard_map/ppermute | solution.py:323
  123.7 36.8 %collective-permute-start.15 = (bf16[256,640]{1,0:T(8,128)(2,1)S(1)}, bf16[256,640]{1,0:T(8,128)(2,1)S(1)}, u32[]{:S(2)}, u32[]{:S(2)}) collective-permute-start(bf16[256,640]{1,0:T(8,128)(2,1)S(1)} %add_convert_fusion), channel_id=1, source_target_pairs={{16,0},{24,8},{32,16},{40,24},{48,32},{56,40},{64,48},{72,56},{80,... | collective-permute-start | bytes 983048 | tf_op jit(solution)/shard_map/ppermute | solution.py:329
  127.2 33.3 %collective-permute-start.12 = (bf16[256,640]{1,0:T(8,128)(2,1)S(1)}, bf16[256,640]{1,0:T(8,128)(2,1)S(1)}, u32[]{:S(2)}, u32[]{:S(2)}) collective-permute-start(bf16[256,640]{1,0:T(8,128)(2,1)S(1)} %add_convert_fusion.1), channel_id=1, source_target_pairs={{16,0},{24,8},{32,16},{40,24},{48,32},{56,40},{64,48},{72,56},{80,... | collective-permute-start | bytes 983048 | tf_op jit(solution)/shard_map/ppermute | solution.py:329
  160.5 1.1 copy-start.1
  161.6 1.1 copy-start.3

commit v3 on v2

v3 whole, which is shorter than its diff:
```python
import functools
import math

import jax
import jax.numpy as jnp
from jax import lax
from jax.experimental import pallas as pl
from jax.experimental.pallas import tpu as pltpu
from jax.sharding import PartitionSpec as P

HEADS = 20
HDIM = 128
XN = 4
GROUP = HEADS // XN
NEG = -1e30
FACTOR = HDIM ** (-0.5)
SCALE2 = FACTOR * math.log2(math.e)
LOW_LANE = 32
FRAME_LANE = 64
BF16 = jnp.bfloat16
F32 = jnp.float32
NT = (((1,), (1,)), ((), ()))
NN = (((1,), (0,)), ((), ()))


def params(room=40):
    return pltpu.CompilerParams(vmem_limit_bytes=room * 1024 * 1024)


def cost(flops, moved, exps=0):
    return pl.CostEstimate(flops=flops, bytes_accessed=moved, transcendentals=exps)


def pack_kernel(q_any, k_any, v_any, o_any, g_any, f_ref, kv, qg, held, sems):
    copies = []
    for at, src in enumerate((k_any, v_any, g_any, o_any, q_any)):
        copies.append(pltpu.make_async_copy(src, held.at[at], sems.at[at]))
    for copy in copies:
        copy.start()
    for copy in copies:
        copy.wait()
    tok = held.shape[1]
    wide = GROUP * HDIM
    lane = lax.broadcasted_iota(jnp.int32, (tok, HDIM), 1)
    meta = jnp.where(lane == FRAME_LANE, f_ref[...].astype(F32), 0.0)
    for head in range(HEADS):
        group, h = divmod(head, GROUP)
        cols = slice(head * HDIM, (head + 1) * HDIM)
        product = held[2, :, cols].astype(F32) * held[3, :, cols].astype(F32)
        dot = jnp.sum(product, axis=1, keepdims=True)
        high = dot.astype(BF16).astype(F32)
        meta = jnp.where(lane == head, high, meta)
        meta = jnp.where(lane == LOW_LANE + head, dot - high, meta)
        kv[group, :, 2 * h * HDIM : (2 * h + 1) * HDIM] = held[0, :, cols]
        kv[group, :, (2 * h + 1) * HDIM : (2 * h + 2) * HDIM] = held[1, :, cols]
    meta = meta.astype(BF16)
    for target in range(qg.shape[0]):
        group = target % XN
        here = slice(group * wide, (group + 1) * wide)
        qg[target, :, :wide] = held[4, :, here]
        qg[target, :, wide : 2 * wide] = held[2, :, here]
        qg[target, :, 2 * wide :] = meta


def pack(query, key, value, saved_out, grad_out, frames):
    tok, width = query.shape
    wide = GROUP * HDIM
    vmem = pl.BlockSpec(memory_space=pltpu.VMEM)
    return pl.pallas_call(
        pack_kernel,
        out_shape=[
            jax.ShapeDtypeStruct((XN, tok, 2 * wide), BF16),
            jax.ShapeDtypeStruct((lax.axis_size("col"), tok, 2 * wide + HDIM), BF16),
        ],
        in_specs=[pl.BlockSpec(memory_space=pl.ANY)] * 5 + [vmem],
        out_specs=[vmem] * 2,
        scratch_shapes=[pltpu.VMEM((5, tok, width), BF16), pltpu.SemaphoreType.DMA((5,))],
        compiler_params=params(60),
        cost_estimate=cost(2 * tok * width, 18 * tok * width),
        name="pack",
    )(query, key, value, saved_out, grad_out, frames)


def window_scores(queries, keys):
    return lax.dot_general(keys, queries, NT, preferred_element_type=F32) * SCALE2


def key_frames(place, meta):
    half = meta.shape[0] // 2
    frames = meta[:, FRAME_LANE : FRAME_LANE + 1]
    return jnp.where(place[1] == 0, frames[:half], frames[half:])


def stats_kernel(bias_ref, place, q_ref, m_ref, w0, w1, w2, w3, out_ref):
    head = pl.program_id(0)
    queries = q_ref[...]
    meta = m_ref[...].astype(F32)
    q_frame = meta.T[FRAME_LANE : FRAME_LANE + 1, :]

    scores, peaks = [], []
    for at, ref in enumerate((w0, w1, w2, w3)):
        part = window_scores(queries, ref[...])
        if at == 0:
            part = jnp.where(key_frames(place, meta) <= q_frame, part, NEG)
        scores.append(part)
        peaks.append(jnp.max(part, axis=0, keepdims=True) + bias_ref[at])
    peak = functools.reduce(jnp.maximum, peaks)
    total = jnp.zeros_like(peak)
    for at, part in enumerate(scores):
        total += jnp.sum(jnp.exp2(part - (peak - bias_ref[at])), axis=0, keepdims=True)

    @pl.when(head == 0)
    def _():
        out_ref[...] = jnp.zeros_like(out_ref)

    out_ref[pl.ds(head, 1), :] = peak
    out_ref[pl.ds(8 + head, 1), :] = total


def part_block(half, first):
    return pl.BlockSpec((half, HDIM), lambda h: (0, first + h))


def meta_block(half):
    return pl.BlockSpec((half, HDIM), lambda h: (0, 2 * GROUP))


def key_block(half):
    return pl.BlockSpec((half, HDIM), lambda h: (0, 2 * h))


def pair_block(half):
    return pl.BlockSpec((half, 2 * HDIM), lambda h: (0, h))


def whole(shape):
    return pl.BlockSpec(shape, lambda h: (0, 0))


def smem():
    return pl.BlockSpec(memory_space=pltpu.SMEM)


def stats(bias, place, qg, window):
    count, half = qg.shape[0], window[0].shape[0]
    pairs = GROUP * count * 4 * half
    return pl.pallas_call(
        stats_kernel,
        grid=(GROUP,),
        out_shape=jax.ShapeDtypeStruct((16, count), F32),
        in_specs=[smem(), smem(), part_block(count, 0), meta_block(count)] + [key_block(half)] * 4,
        out_specs=whole((16, count)),
        compiler_params=params(),
        cost_estimate=cost(4 * pairs * HDIM, 6 * half * GROUP * HDIM * 2, pairs),
        name="stats",
    )(bias, place, qg, qg, *window)


def log_total(head, own_stats, far_stats):
    own_peak = own_stats[pl.ds(head, 1), :]
    own_sum = own_stats[pl.ds(8 + head, 1), :]
    far_peak = far_stats[pl.ds(head, 1), :]
    far_sum = far_stats[pl.ds(8 + head, 1), :]
    peak = jnp.maximum(own_peak, far_peak)
    own_part = own_sum * jnp.exp2(own_peak - peak)
    return peak + jnp.log2(own_part + far_sum * jnp.exp2(far_peak - peak))


def dot_and_frame(head, meta):
    lane = lax.broadcasted_iota(jnp.int32, meta.shape, 1)
    picked = (lane == head) | (lane == head + LOW_LANE)
    dot_col = jnp.sum(jnp.where(picked, meta, 0.0), axis=1, keepdims=True)
    rows = jnp.where(lane == FRAME_LANE, meta, dot_col).T
    return rows[0:1, :], rows[FRAME_LANE : FRAME_LANE + 1, :]


def block_grads(scores, total, dot, queries, grads, keys, values):
    probs = jnp.exp2(scores - total)
    dv = lax.dot_general(probs.astype(BF16), grads, NN, preferred_element_type=F32)
    dp = lax.dot_general(values, grads, NT, preferred_element_type=F32)
    ds = (probs * (dp - dot)).astype(BF16)
    dk = lax.dot_general(ds, queries, NN, preferred_element_type=F32) * FACTOR
    dq = lax.dot_general(keys.T, ds, NN, preferred_element_type=F32)
    return dq, dk, dv


def earlier_kernel(
    bias_ref, place, own_stats, far_stats, q_ref, g_ref, m_ref, w1, w2, w3, dq_ref, d1, d2, d3
):
    head = pl.program_id(0)
    queries, grads = q_ref[...], g_ref[...]
    dot, _ = dot_and_frame(place[0] * GROUP + head, m_ref[...].astype(F32))
    total = log_total(head, own_stats, far_stats)
    dq_sum = jnp.zeros(dq_ref.shape, F32)
    for at, (ref, out) in enumerate(((w1, d1), (w2, d2), (w3, d3))):
        keys, values = ref[:, :HDIM], ref[:, HDIM:]
        scores = window_scores(queries, keys)
        bound = total - bias_ref[at + 1]
        dq, dk, dv = block_grads(scores, bound, dot, queries, grads, keys, values)
        dq_sum += dq
        out[:, :HDIM] = dk.astype(BF16)
        out[:, HDIM:] = dv.astype(BF16)
    dq_ref[...] = dq_sum


def query_specs(count):
    stat = whole((16, count))
    parts = [part_block(count, 0), part_block(count, GROUP), meta_block(count)]
    return [smem(), stat, stat] + parts


def turned_block(count):
    return pl.BlockSpec((HDIM, count), lambda h: (h, 0))


def earlier(bias, place, own_stats, far_stats, qg, window):
    count, half = qg.shape[0], window[0].shape[0]
    wide = GROUP * HDIM
    pairs = GROUP * count * 3 * half
    return pl.pallas_call(
        earlier_kernel,
        grid=(GROUP,),
        out_shape=[jax.ShapeDtypeStruct((wide, count), F32)]
        + [jax.ShapeDtypeStruct((half, 2 * wide), BF16)] * 3,
        in_specs=[smem()] + query_specs(count) + [pair_block(half)] * 3,
        out_specs=[turned_block(count)] + [pair_block(half)] * 3,
        compiler_params=params(),
        cost_estimate=cost(10 * pairs * HDIM, 20 * half * wide * 2, pairs),
        name="earlier",
    )(bias, place, own_stats, far_stats, qg, qg, qg, *window)


def same_kernel(
    place, own_stats, far_stats, q_ref, g_ref, m_ref, w0, dq_ref, dq_out, d0
):
    head = pl.program_id(0)
    queries, grads = q_ref[...], g_ref[...]
    meta = m_ref[...].astype(F32)
    dot, q_frame = dot_and_frame(place[0] * GROUP + head, meta)
    total = log_total(head, own_stats, far_stats)
    keys, values = w0[:, :HDIM], w0[:, HDIM:]
    scores = window_scores(queries, keys)
    scores = jnp.where(key_frames(place, meta) <= q_frame, scores, NEG)
    dq, dk, dv = block_grads(scores, total, dot, queries, grads, keys, values)
    dq_out[...] = ((dq + dq_ref[...]) * FACTOR).T.astype(BF16)
    d0[:, :HDIM] = dk
    d0[:, HDIM:] = dv


def same(place, own_stats, far_stats, qg, w0, dq):
    count, half = qg.shape[0], w0.shape[0]
    wide = GROUP * HDIM
    pairs = GROUP * count * half
    return pl.pallas_call(
        same_kernel,
        grid=(GROUP,),
        out_shape=[
            jax.ShapeDtypeStruct((count, wide), BF16),
            jax.ShapeDtypeStruct((half, 2 * wide), F32),
        ],
        in_specs=query_specs(count) + [pair_block(half), turned_block(count)],
        out_specs=[part_block(count, 0), pair_block(half)],
        compiler_params=params(),
        cost_estimate=cost(10 * pairs * HDIM, 16 * half * wide * 2, pairs),
        name="same",
    )(place, own_stats, far_stats, qg, qg, qg, w0, dq)


def close_kernel(even_ref, d0, back, side, out):
    even = even_ref[0].astype(F32)
    tok = out.shape[1]
    for step in range(XN):
        rows = slice(step * tok, (step + 1) * tok)
        pair = d0[rows, :] + back[rows, :].astype(F32) + side[rows, :].astype(F32) * even
        out[step] = pair.astype(BF16)


def close(even, d0, back, side):
    half, wide = d0.shape
    tok = half // XN
    vmem = pl.BlockSpec(memory_space=pltpu.VMEM)
    return pl.pallas_call(
        close_kernel,
        out_shape=jax.ShapeDtypeStruct((XN, tok, wide), BF16),
        in_specs=[smem()] + [vmem] * 3,
        out_specs=vmem,
        compiler_params=params(),
        cost_estimate=cost(3 * half * wide, 10 * half * wide),
        name="close",
    )(even, d0, back, side)


def unpack_kernel(parts, halves, dq, dk, dv):
    wide = GROUP * HDIM
    for group in range(XN):
        total = halves[group].astype(F32) + halves[XN + group].astype(F32)
        dq[:, group * wide : (group + 1) * wide] = total.astype(BF16)
        for h in range(GROUP):
            at = 2 * h * HDIM
            cols = slice((group * GROUP + h) * HDIM, (group * GROUP + h + 1) * HDIM)
            dk[:, cols] = parts[group, :, at : at + HDIM]
            dv[:, cols] = parts[group, :, at + HDIM : at + 2 * HDIM]


def unpack(parts, halves):
    tok = parts.shape[1]
    vmem = pl.BlockSpec(memory_space=pltpu.VMEM)
    return pl.pallas_call(
        unpack_kernel,
        out_shape=[jax.ShapeDtypeStruct((tok, HEADS * HDIM), BF16)] * 3,
        in_specs=[vmem] * 2,
        out_specs=[vmem] * 3,
        compiler_params=params(),
        cost_estimate=cost(0, 14 * tok * HEADS * HDIM),
        name="unpack",
    )(parts, halves)


def over_x(value):
    groups = [[z * XN + x for x in range(XN)] for z in range(lax.axis_size("col") // XN)]
    return lax.all_to_all(value, "col", 0, 0, axis_index_groups=groups)


def across_z(value):
    count = lax.axis_size("col")
    return lax.ppermute(value, "col", [(c, (c + XN) % count) for c in range(count)])


def along_row(value, steps):
    count = lax.axis_size("row")
    first, last = max(0, -steps), min(count, count - steps)
    return lax.ppermute(value, "row", [(r, r + steps) for r in range(first, last)])


def in_chip(value):
    count = lax.axis_size("row")
    return lax.ppermute(value, "row", [(r, r ^ 1) for r in range(count)])


def halo(own, is_even):
    second = along_row(own, 2)
    swapped = in_chip(second)
    third = along_row(jnp.where(is_even, own, second), 1)
    return own, second, swapped, third


def halo_back(second, swapped, third, is_even):
    side = along_row(third, -1)
    turned = jnp.where(is_even, jnp.zeros_like(side), side)
    held = second.astype(F32) + in_chip(swapped).astype(F32) + turned.astype(F32)
    return along_row(held.astype(BF16), -2), side


def per_device(query, key, value, saved_out, grad_out, frame_ids):
    row, col = lax.axis_index("row"), lax.axis_index("col")
    place = jnp.stack([col % XN, col // XN]).astype(jnp.int32)
    is_even = row % 2 == 0
    even = is_even.astype(jnp.int32).reshape(1)
    tok = query.shape[0]
    count = lax.axis_size("col") * tok

    kv, qg = pack(query, key, value, saved_out, grad_out, frame_ids[:, None])
    qg = lax.all_to_all(qg, "col", 0, 0).reshape(count, -1)
    window = halo(over_x(kv).reshape(XN * tok, -1), is_even)
    held = jnp.stack(
        [
            row >= 0,
            row >= 2,
            jnp.where(is_even, row >= 1, row >= 3),
            jnp.where(is_even, row >= 3, row >= 1),
        ]
    )
    bias = jnp.where(held, 0.0, NEG).astype(F32)

    own_stats = stats(bias, place, qg, window)
    far_stats = across_z(own_stats)
    dq_part, *earlier_grads = earlier(bias, place, own_stats, far_stats, qg, window[1:])
    dq, d0 = same(place, own_stats, far_stats, qg, window[0], dq_part)

    back, side = halo_back(*earlier_grads, is_even)
    halves = lax.all_to_all(dq.reshape(-1, tok, GROUP * HDIM), "col", 0, 0)
    return tuple(unpack(over_x(close(even, d0, back, side)), halves))


def solution(mesh):
    placed = P(("row", "col"), None)
    return jax.shard_map(
        per_device,
        mesh=mesh,
        in_specs=(placed,) * 5 + (P(("row", "col")),),
        out_specs=(placed,) * 3,
        check_vma=False,
    )
```

time: 180 us -> 173 us (0.961)
  the two profiles are of different devices: /device:TPU:248 before, /device:TPU:120 now
where the time goes in v3:
time: 173 us; the launch traced here: 172 us
  waiting for transfers between devices  73.4 us (42%)
  starting transfers between devices  35 us (20%)
  blocking collectives  30.3 us (18%)
  Pallas kernels  26.5 us (15%)
  local copies, waits for them, and re-layouts  4.59 us (3%)
    ppermute x4, waiting for transfers between devices, along_row(): lax.ppermute(value, 'row', [(r, r + steps) for r in range(first, last)])  59.9 us
    all_to_all x2, blocking collectives, over_x(): return lax.all_to_all(value, 'col', 0, 0, axis_index_groups=groups)  30.3 us
    ppermute x4, starting transfers between devices, along_row(): lax.ppermute(value, 'row', [(r, r + steps) for r in range(first, last)])  11.1 us
    pallas_call x1, Pallas kernels, earlier(): pl.pallas_call(earlier_kernel, grid=(GROUP,), out_shape=[jax.ShapeDtypeSt...  10.1 us
    all_to_all x1, starting transfers between devices, per_device(): qg = lax.all_to_all(qg, 'col', 0, 0).reshape(count, -1)  9.99 us
    ppermute x1, waiting for transfers between devices, across_z(): lax.ppermute(value, 'col', [(c, (c + XN) % count) for c in range(count)])  7.33 us
    ppermute x2, starting transfers between devices, in_chip(): return lax.ppermute(value, 'row', [(r, r ^ 1) for r in range(count)])  6.95 us
    all_to_all x1, waiting for transfers between devices, per_device(): qg = lax.all_to_all(qg, 'col', 0, 0).reshape(count, -1)  6.13 us
  transfers between devices with their start and end apart: 9, of which 5 were waited for; matrix products, arithmetic and copies ran while one was open for 1% of the time, Pallas kernels for 4%

profile of v3, /device:TPU:120, one launch (start us, length us, event | category | flops | bytes accessed | tf_op | source)
XLA Modules:
  0.0 171.8 jit_solution(4081746124806613093)
XLA Ops:
  0.6 1.4 copy.9.f_ref
  2.0 3.8 %pack.1 = (bf16[4,64,1280]{2,1,0:T(8,128)(2,1)}, bf16[8,64,1408]{2,1,0:T(8,128)(2,1)}) custom-call(bf16[64,2560]{1,0:T(8,128)(2,1)} %q_any.1, bf16[64,2560]{1,0:T(8,128)(2,1)} %k_any.1, bf16[64,2560]{1,0:T(8,128)(2,1)} %v_any.1, bf16[64,2560]{1,0:T(8,128)(2,1)} %o_any.1, bf16[64,2560]{1,0:T(8,128)(2,1)} %g_any.1, s32[64,1]{1,0:T(8,128)} %copy.9.f_ref), custom_call_target="tpu_custom_call" | custom-call | flops 327680 | bytes 2949120 | tf_op jit(solution)/shard_map/pack/pallas_call | solution.py:69
  5.8 15.2 %all_to_all.20 = bf16[4,64,1280]{2,1,0:T(8,128)(2,1)S(1)} all-to-all(bf16[4,64,1280]{2,1,0:T(8,128)(2,1)} %get-tuple-element.12), channel_id=1, replica_groups={{0,1,2,3},{4,5,6,7},{8,9,10,11},{12,13,14,15},{16,17,18,19},{20,21,22,2..., dimensions={0} | all-to-all | bytes 1310720 | tf_op jit(solution)/shard_map/all_to_all | solution.py:321
  21.0 10.0 %all-to-all-start = ((bf16[8,64,1408]{2,1,0:T(8,128)(2,1)}), bf16[8,64,1408]{2,1,0:T(8,128)(2,1)S(1)}, u32[]{:S(2)}, u32[]{:S(2)}) async-start(bf16[8,64,1408]{2,1,0:T(8,128)(2,1)} %get-tuple-element.11), calls=%async_computation | async-start | bytes 2883584 | tf_op jit(solution)/shard_map/all_to_all | solution.py:363
  31.0 2.6 %collective-permute-start = (bf16[256,1280]{1,0:T(8,128)(2,1)S(1)}, bf16[256,1280]{1,0:T(8,128)(2,1)S(1)}, u32[]{:S(2)}, u32[]{:S(2)}) collective-permute-start(bf16[256,1280]{1,0:T(8,128)(2,1)S(1)} %bitcast.20), channel_id=1, source_target_pairs={{0,16},{8,24},{16,32},{24,40},{32,48},{40,56},{48,64},{56,72},{64,... | collective-permute-start | bytes 1966088 | tf_op jit(solution)/shard_map/ppermute | solution.py:332
  33.5 14.3 %collective-permute-done.w1 = bf16[256,1280]{1,0:T(8,128)(2,1)S(1)} collective-permute-done((bf16[256,1280]{1,0:T(8,128)(2,1)S(1)}, bf16[256,1280]{1,0:T(8,128)(2,1)S(1)}, u32[]{:S(2)}, u32[]{:S(2)}) %collective-permute-start) | collective-permute-done | bytes 655392 | tf_op jit(solution)/shard_map/ppermute | solution.py:332
  47.8 0.9 broadcast_select_fusion
  48.8 1.9 %collective-permute-start.2 = (bf16[256,1280]{1,0:T(8,128)(2,1)}, bf16[256,1280]{1,0:T(8,128)(2,1)S(1)}, u32[]{:S(2)}, u32[]{:S(2)}) collective-permute-start(bf16[256,1280]{1,0:T(8,128)(2,1)} %broadcast_select_fusion), channel_id=1, source_target_pairs={{0,8},{8,16},{16,24},{24,32},{32,40},{40,48},{48,56},{56,64},{64,7... | collective-permute-start | bytes 1966088 | tf_op jit(solution)/shard_map/ppermute | solution.py:332
  50.7 5.0 %collective-permute-start.1 = (bf16[256,1280]{1,0:T(8,128)(2,1)S(1)}, bf16[256,1280]{1,0:T(8,128)(2,1)}, u32[]{:S(2)}, u32[]{:S(2)}) collective-permute-start(bf16[256,1280]{1,0:T(8,128)(2,1)S(1)} %collective-permute-done.w1), channel_id=1, source_target_pairs={{0,8},{8,0},{16,24},{24,16},{32,40},{40,32},{48,56},{56,48},{64,72... | collective-permute-start | bytes 1966088 | tf_op jit(solution)/shard_map/ppermute | solution.py:337
  55.8 0.1 pad_add_fusion.place
  55.9 0.1 add_select_fusion.bias_ref
  55.9 4.9 %collective-permute-done.2.w3 = bf16[256,1280]{1,0:T(8,128)(2,1)S(1)} collective-permute-done((bf16[256,1280]{1,0:T(8,128)(2,1)}, bf16[256,1280]{1,0:T(8,128)(2,1)S(1)}, u32[]{:S(2)}, u32[]{:S(2)}) %collective-permute-start.2) | collective-permute-done | bytes 655392 | tf_op jit(solution)/shard_map/ppermute | solution.py:332
  60.9 0.0 collective-permute-done.1.w2
  60.9 6.1 %all-to-all-done = bf16[8,64,1408]{2,1,0:T(8,128)(2,1)S(1)} async-done(((bf16[8,64,1408]{2,1,0:T(8,128)(2,1)}), bf16[8,64,1408]{2,1,0:T(8,128)(2,1)S(1)}, u32[]{:S(2)}, u32[]{:S(2)}) %all-to-all-start) | async-done | bytes 1441824 | tf_op jit(solution)/shard_map/all_to_all | solution.py:363
  67.0 5.2 %stats.1.own_stats = f32[16,512]{1,0:T(8,128)S(1)} custom-call(f32[4]{0:T(128)S(1)} %add_select_fusion.bias_ref, s32[2]{0:T(128)S(1)} %pad_add_fusion.place, bf16[512,1408]{1,0:T(8,128)(2,1)S(1)} %bitcast.12, bf16[512,1408]{1,0:T(8,128)(2,1)S(1)} %bitcast.13, bf16[256,1280]{1,0:T(8,128)(2,1)S(1)} %bitcast.21, bf16[256,1280]{1,0:T(8,128)(2,1)S(1)} %collective-permute-done.w1, ...), custom_call_target="tpu_custom_call" | custom-call | flops 1342177280 | bytes 1966080 | tf_op jit(solution)/shard_map/stats/pallas_call | solution.py:147
  72.2 2.6 %collective-permute-start.3 = (f32[16,512]{1,0:T(8,128)S(1)}, f32[16,512]{1,0:T(8,128)S(1)}, u32[]{:S(2)}, u32[]{:S(2)}) collective-permute-start(f32[16,512]{1,0:T(8,128)S(1)} %stats.1.own_stats), channel_id=1, source_target_pairs={{0,4},{1,5},{2,6},{3,7},{4,0},{5,1},{6,2},{7,3},{8,12},{9,13},{10,... | collective-permute-start | bytes 98312 | tf_op jit(solution)/shard_map/ppermute | solution.py:326
  74.9 7.3 %collective-permute-done.3.far_stats = f32[16,512]{1,0:T(8,128)S(1)} collective-permute-done((f32[16,512]{1,0:T(8,128)S(1)}, f32[16,512]{1,0:T(8,128)S(1)}, u32[]{:S(2)}, u32[]{:S(2)}) %collective-permute-start.3) | collective-permute-done | bytes 32800 | tf_op jit(solution)/shard_map/ppermute | solution.py:326
  82.2 10.1 %earlier.1 = (f32[640,512]{1,0:T(8,128)S(1)}, bf16[256,1280]{1,0:T(8,128)(2,1)S(1)}, bf16[256,1280]{1,0:T(8,128)(2,1)}, bf16[256,1280]{1,0:T(8,128)(2,1)}) custom-call(f32[4]{0:T(128)S(1)} %add_select_fusion.bias_ref, s32[2]{0:T(128)S(1)} %pad_add_fusion.place, f32[16,512]{1,0:T(8,128)S(1)} %stats.1.own_stats, ...), custom_call_target="tpu_custom_call" | custom-call | flops 2516582400 | bytes 6553600 | tf_op jit(solution)/shard_map/earlier/pallas_call | solution.py:220
  92.3 0.0 copy-start.2
  92.3 0.9 copy-done.2
  93.2 1.9 %collective-permute-start.4 = (bf16[256,1280]{1,0:T(8,128)(2,1)}, bf16[256,1280]{1,0:T(8,128)(2,1)S(1)}, u32[]{:S(2)}, u32[]{:S(2)}) collective-permute-start(bf16[256,1280]{1,0:T(8,128)(2,1)} %get-tuple-element.16), channel_id=1, source_target_pairs={{0,8},{8,0},{16,24},{24,16},{32,40},{40,32},{48,56},{56,48},{64,72... | collective-permute-start | bytes 1966088 | tf_op jit(solution)/shard_map/ppermute | solution.py:337
  95.1 3.4 %collective-permute-start.5 = (bf16[256,1280]{1,0:T(8,128)(2,1)}, bf16[256,1280]{1,0:T(8,128)(2,1)S(1)}, u32[]{:S(2)}, u32[]{:S(2)}) collective-permute-start(bf16[256,1280]{1,0:T(8,128)(2,1)} %get-tuple-element.17), channel_id=1, source_target_pairs={{8,0},{16,8},{24,16},{32,24},{40,32},{48,40},{56,48},{64,56},{72,6... | collective-permute-start | bytes 1966088 | tf_op jit(solution)/shard_map/ppermute | solution.py:332
  98.5 6.0 %same.1 = (bf16[512,640]{1,0:T(8,128)(2,1)}, f32[256,1280]{1,0:T(8,128)S(1)}) custom-call(s32[2]{0:T(128)S(1)} %pad_add_fusion.place, f32[16,512]{1,0:T(8,128)S(1)} %stats.1.own_stats, f32[16,512]{1,0:T(8,128)S(1)} %collective-permute-done.3.far_stats, bf16[512,1408]{1,0:T(8,128)(2,1)S(1)} %bitcast.17, bf16[512,1408]{1,0:T(8,128)(2,1)S(1)} %bitcast.18, ...), custom_call_target="tpu_custom_call" | custom-call | flops 838860800 | bytes 5242880 | tf_op jit(solution)/shard_map/same/pallas_call | solution.py:254
  104.5 0.0 copy-start
  104.5 1.1 copy-done
  105.6 0.0 copy-start.3
  105.6 4.3 %all-to-all-start.3 = ((bf16[8,64,640]{2,1,0:T(8,128)(2,1)}), bf16[8,64,640]{2,1,0:T(8,128)(2,1)S(1)}, u32[]{:S(2)}, u32[]{:S(2)}) async-start(bf16[8,64,640]{2,1,0:T(8,128)(2,1)} %bitcast.10), calls=%async_computation.3 | async-start | bytes 1310720 | tf_op jit(solution)/shard_map/all_to_all | solution.py:381
  109.9 0.0 collective-permute-done.4
  109.9 0.0 collective-permute-done.5.side
  109.9 0.0 copy-done.3
  109.9 0.3 add_convert_fusion
  110.2 3.3 %collective-permute-start.6 = (bf16[256,1280]{1,0:T(8,128)(2,1)S(1)}, bf16[256,1280]{1,0:T(8,128)(2,1)S(1)}, u32[]{:S(2)}, u32[]{:S(2)}) collective-permute-start(bf16[256,1280]{1,0:T(8,128)(2,1)S(1)} %add_convert_fusion), channel_id=1, source_target_pairs={{16,0},{24,8},{32,16},{40,24},{48,32},{56,40},{64,48},{72,56},{80,... | collective-permute-start | bytes 1966088 | tf_op jit(solution)/shard_map/ppermute | solution.py:332
  113.5 40.6 %collective-permute-done.6.back = bf16[256,1280]{1,0:T(8,128)(2,1)S(1)} collective-permute-done((bf16[256,1280]{1,0:T(8,128)(2,1)S(1)}, bf16[256,1280]{1,0:T(8,128)(2,1)S(1)}, u32[]{:S(2)}, u32[]{:S(2)}) %collective-permute-start.6) | collective-permute-done | bytes 655392 | tf_op jit(solution)/shard_map/ppermute | solution.py:332
  154.1 0.0 copy-start.1
  154.1 1.3 copy-done.1
  155.4 0.2 close.1
  155.7 0.0 all-to-all-done.3.halves
  155.7 15.1 %all_to_all.21.parts = bf16[4,64,1280]{2,1,0:T(8,128)(2,1)S(1)} all-to-all(bf16[4,64,1280]{2,1,0:T(8,128)(2,1)S(1)} %close.1), channel_id=1, replica_groups={{0,1,2,3},{4,5,6,7},{8,9,10,11},{12,13,14,15},{16,17,18,19},{20,21,22,2..., dimensions={0} | all-to-all | bytes 1310720 | tf_op jit(solution)/shard_map/all_to_all | solution.py:321
  170.8 1.1 unpack.1
Async XLA Ops:
  21.0 46.1 %all-to-all-start = ((bf16[8,64,1408]{2,1,0:T(8,128)(2,1)}), bf16[8,64,1408]{2,1,0:T(8,128)(2,1)S(1)}, u32[]{:S(2)}, u32[]{:S(2)}) async-start(bf16[8,64,1408]{2,1,0:T(8,128)(2,1)} %get-tuple-element.11), calls=%async_computation | async-start | bytes 2883584 | tf_op jit(solution)/shard_map/all_to_all | solution.py:363
  31.0 16.9 %collective-permute-start = (bf16[256,1280]{1,0:T(8,128)(2,1)S(1)}, bf16[256,1280]{1,0:T(8,128)(2,1)S(1)}, u32[]{:S(2)}, u32[]{:S(2)}) collective-permute-start(bf16[256,1280]{1,0:T(8,128)(2,1)S(1)} %bitcast.20), channel_id=1, source_target_pairs={{0,16},{8,24},{16,32},{24,40},{32,48},{40,56},{48,64},{56,72},{64,... | collective-permute-start | bytes 1966088 | tf_op jit(solution)/shard_map/ppermute | solution.py:332
  48.8 12.1 %collective-permute-start.2 = (bf16[256,1280]{1,0:T(8,128)(2,1)}, bf16[256,1280]{1,0:T(8,128)(2,1)S(1)}, u32[]{:S(2)}, u32[]{:S(2)}) collective-permute-start(bf16[256,1280]{1,0:T(8,128)(2,1)} %broadcast_select_fusion), channel_id=1, source_target_pairs={{0,8},{8,16},{16,24},{24,32},{32,40},{40,48},{48,56},{56,64},{64,7... | collective-permute-start | bytes 1966088 | tf_op jit(solution)/shard_map/ppermute | solution.py:332
  50.7 10.2 %collective-permute-start.1 = (bf16[256,1280]{1,0:T(8,128)(2,1)S(1)}, bf16[256,1280]{1,0:T(8,128)(2,1)}, u32[]{:S(2)}, u32[]{:S(2)}) collective-permute-start(bf16[256,1280]{1,0:T(8,128)(2,1)S(1)} %collective-permute-done.w1), channel_id=1, source_target_pairs={{0,8},{8,0},{16,24},{24,16},{32,40},{40,32},{48,56},{56,48},{64,72... | collective-permute-start | bytes 1966088 | tf_op jit(solution)/shard_map/ppermute | solution.py:337
  72.2 10.0 %collective-permute-start.3 = (f32[16,512]{1,0:T(8,128)S(1)}, f32[16,512]{1,0:T(8,128)S(1)}, u32[]{:S(2)}, u32[]{:S(2)}) collective-permute-start(f32[16,512]{1,0:T(8,128)S(1)} %stats.1.own_stats), channel_id=1, source_target_pairs={{0,4},{1,5},{2,6},{3,7},{4,0},{5,1},{6,2},{7,3},{8,12},{9,13},{10,... | collective-permute-start | bytes 98312 | tf_op jit(solution)/shard_map/ppermute | solution.py:326
  92.3 0.9 copy-start.2
  93.2 16.7 %collective-permute-start.4 = (bf16[256,1280]{1,0:T(8,128)(2,1)}, bf16[256,1280]{1,0:T(8,128)(2,1)S(1)}, u32[]{:S(2)}, u32[]{:S(2)}) collective-permute-start(bf16[256,1280]{1,0:T(8,128)(2,1)} %get-tuple-element.16), channel_id=1, source_target_pairs={{0,8},{8,0},{16,24},{24,16},{32,40},{40,32},{48,56},{56,48},{64,72... | collective-permute-start | bytes 1966088 | tf_op jit(solution)/shard_map/ppermute | solution.py:337
  95.1 14.8 %collective-permute-start.5 = (bf16[256,1280]{1,0:T(8,128)(2,1)}, bf16[256,1280]{1,0:T(8,128)(2,1)S(1)}, u32[]{:S(2)}, u32[]{:S(2)}) collective-permute-start(bf16[256,1280]{1,0:T(8,128)(2,1)} %get-tuple-element.17), channel_id=1, source_target_pairs={{8,0},{16,8},{24,16},{32,24},{40,32},{48,40},{56,48},{64,56},{72,6... | collective-permute-start | bytes 1966088 | tf_op jit(solution)/shard_map/ppermute | solution.py:332
  104.5 1.1 copy-start
  105.6 4.3 %copy-start.3 = (bf16[256,1280]{1,0:T(8,128)(2,1)S(1)}, bf16[256,1280]{1,0:T(8,128)(2,1)}, u32[]{:S(2)}) copy-start(bf16[256,1280]{1,0:T(8,128)(2,1)} %copy-done.2) | copy-start | bytes 1966084
  105.6 50.1 %all-to-all-start.3 = ((bf16[8,64,640]{2,1,0:T(8,128)(2,1)}), bf16[8,64,640]{2,1,0:T(8,128)(2,1)S(1)}, u32[]{:S(2)}, u32[]{:S(2)}) async-start(bf16[8,64,640]{2,1,0:T(8,128)(2,1)} %bitcast.10), calls=%async_computation.3 | async-start | bytes 1310720 | tf_op jit(solution)/shard_map/all_to_all | solution.py:381
  110.2 43.9 %collective-permute-start.6 = (bf16[256,1280]{1,0:T(8,128)(2,1)S(1)}, bf16[256,1280]{1,0:T(8,128)(2,1)S(1)}, u32[]{:S(2)}, u32[]{:S(2)}) collective-permute-start(bf16[256,1280]{1,0:T(8,128)(2,1)S(1)} %add_convert_fusion), channel_id=1, source_target_pairs={{16,0},{24,8},{32,16},{40,24},{48,32},{56,40},{64,48},{72,56},{80,... | collective-permute-start | bytes 1966088 | tf_op jit(solution)/shard_map/ppermute | solution.py:332
  154.1 1.3 copy-start.1

commit v4 on v3

--- a/solution.py
+++ b/solution.py
@@ -31,64 +31,93 @@
     return pl.CostEstimate(flops=flops, bytes_accessed=moved, transcendentals=exps)
 
 
-def pack_kernel(q_any, k_any, v_any, o_any, g_any, f_ref, kv, qg, held, sems):
-    copies = []
-    for at, src in enumerate((k_any, v_any, g_any, o_any, q_any)):
-        copies.append(pltpu.make_async_copy(src, held.at[at], sems.at[at]))
+def load_all(sources, held, sems):
+    copies = [
+        pltpu.make_async_copy(src, held.at[at], sems.at[at]) for at, src in enumerate(sources)
+    ]
     for copy in copies:
         copy.start()
     for copy in copies:
         copy.wait()
+
+
+def pack_queries_kernel(q_any, o_any, g_any, f_ref, out, held, sems):
+    load_all((q_any, o_any, g_any), held, sems)
     tok = held.shape[1]
     wide = GROUP * HDIM
     lane = lax.broadcasted_iota(jnp.int32, (tok, HDIM), 1)
     meta = jnp.where(lane == FRAME_LANE, f_ref[...].astype(F32), 0.0)
     for head in range(HEADS):
-        group, h = divmod(head, GROUP)
         cols = slice(head * HDIM, (head + 1) * HDIM)
-        product = held[2, :, cols].astype(F32) * held[3, :, cols].astype(F32)
+        product = held[2, :, cols].astype(F32) * held[1, :, cols].astype(F32)
         dot = jnp.sum(product, axis=1, keepdims=True)
         high = dot.astype(BF16).astype(F32)
         meta = jnp.where(lane == head, high, meta)
         meta = jnp.where(lane == LOW_LANE + head, dot - high, meta)
-        kv[group, :, 2 * h * HDIM : (2 * h + 1) * HDIM] = held[0, :, cols]
-        kv[group, :, (2 * h + 1) * HDIM : (2 * h + 2) * HDIM] = held[1, :, cols]
     meta = meta.astype(BF16)
-    for target in range(qg.shape[0]):
+    for target in range(out.shape[0]):
         group = target % XN
         here = slice(group * wide, (group + 1) * wide)
-        qg[target, :, :wide] = held[4, :, here]
-        qg[target, :, wide : 2 * wide] = held[2, :, here]
-        qg[target, :, 2 * wide :] = meta
-
-
-def pack(query, key, value, saved_out, grad_out, frames):
+        out[target, :, :wide] = held[0, :, here]
+        out[target, :, wide : 2 * wide] = held[2, :, here]
+        out[target, :, 2 * wide :] = meta
+
+
+def pack_queries(query, saved_out, grad_out, frames):
     tok, width = query.shape
-    wide = GROUP * HDIM
     vmem = pl.BlockSpec(memory_space=pltpu.VMEM)
-    return pl.pallas_call(
-        pack_kernel,
-        out_shape=[
-            jax.ShapeDtypeStruct((XN, tok, 2 * wide), BF16),
-            jax.ShapeDtypeStruct((lax.axis_size("col"), tok, 2 * wide + HDIM), BF16),
-        ],
-        in_specs=[pl.BlockSpec(memory_space=pl.ANY)] * 5 + [vmem],
-        out_specs=[vmem] * 2,
-        scratch_shapes=[pltpu.VMEM((5, tok, width), BF16), pltpu.SemaphoreType.DMA((5,))],
+    shape = (lax.axis_size("col"), tok, 2 * GROUP * HDIM + HDIM)
+    return pl.pallas_call(
+        pack_queries_kernel,
+        out_shape=jax.ShapeDtypeStruct(shape, BF16),
+        in_specs=[pl.BlockSpec(memory_space=pl.ANY)] * 3 + [vmem],
+        out_specs=vmem,
+        scratch_shapes=[pltpu.VMEM((3, tok, width), BF16), pltpu.SemaphoreType.DMA((3,))],
         compiler_params=params(60),
-        cost_estimate=cost(2 * tok * width, 18 * tok * width),
-        name="pack",
-    )(query, key, value, saved_out, grad_out, frames)
+        cost_estimate=cost(2 * tok * width, 14 * tok * width),
+        name="pack_queries",
+    )(query, saved_out, grad_out, frames)
+
+
+def head_columns(place, step, h):
+    group = lax.rem(place[0] + step, XN)
+    return pl.ds(pl.multiple_of((group * GROUP + h) * HDIM, HDIM), HDIM)
+
+
+def pack_keys_kernel(place, k_ref, v_ref, k2_ref, v2_ref, *outs):
+    for step in range(XN):
+        for h in range(GROUP):
+            cols = head_columns(place, step, h)
+            for at, ref in enumerate((k_ref, v_ref, k2_ref, v2_ref)):
+                first = (2 * (at // 2 * GROUP + h) + at % 2) * HDIM
+                outs[step][:, first : first + HDIM] = ref[:, cols]
+
+
+def pack_keys(place, key, value, far_key, far_value):
+    tok, width = key.shape
+    return pl.pallas_call(
+        pack_keys_kernel,
+        out_shape=[jax.ShapeDtypeStruct((tok, 4 * GROUP * HDIM), BF16)] * XN,
+        in_specs=[smem()] + [pl.BlockSpec(memory_space=pltpu.VMEM)] * 4,
+        out_specs=[pl.BlockSpec(memory_space=pltpu.VMEM)] * XN,
+        compiler_params=params(),
+        cost_estimate=cost(0, 16 * tok * width),
+        name="pack_keys",
+    )(place, key, value, far_key, far_value)
 
 
 def window_scores(queries, keys):
     return lax.dot_general(keys, queries, NT, preferred_element_type=F32) * SCALE2
 
 
-def key_frames(place, meta):
-    half = meta.shape[0] // 2
-    frames = meta[:, FRAME_LANE : FRAME_LANE + 1]
-    return jnp.where(place[1] == 0, frames[:half], frames[half:])
+def key_frames(place, m_ref):
+    tok = m_ref.shape[0] // (2 * XN)
+    pieces = []
+    for step in range(XN):
+        piece = place[1] * XN + lax.rem(place[0] + XN - step, XN)
+        rows = pl.ds(pl.multiple_of(piece * tok, tok), tok)
+        pieces.append(m_ref[rows, :].astype(F32)[:, FRAME_LANE : FRAME_LANE + 1])
+    return jnp.concatenate(pieces, axis=0)
 
 
 def stats_kernel(bias_ref, place, q_ref, m_ref, w0, w1, w2, w3, out_ref):
@@ -101,7 +130,7 @@
     for at, ref in enumerate((w0, w1, w2, w3)):
         part = window_scores(queries, ref[...])
         if at == 0:
-            part = jnp.where(key_frames(place, meta) <= q_frame, part, NEG)
+            part = jnp.where(key_frames(place, m_ref) <= q_frame, part, NEG)
         scores.append(part)
         peaks.append(jnp.max(part, axis=0, keepdims=True) + bias_ref[at])
     peak = functools.reduce(jnp.maximum, peaks)
@@ -125,12 +154,12 @@
     return pl.BlockSpec((half, HDIM), lambda h: (0, 2 * GROUP))
 
 
-def key_block(half):
-    return pl.BlockSpec((half, HDIM), lambda h: (0, 2 * h))
-
-
-def pair_block(half):
-    return pl.BlockSpec((half, 2 * HDIM), lambda h: (0, h))
+def key_block(half, first=0):
+    return pl.BlockSpec((half, HDIM), lambda h: (0, 2 * (first + h)))
+
+
+def pair_block(half, first=0):
+    return pl.BlockSpec((half, 2 * HDIM), lambda h: (0, first + h))
 
 
 def whole(shape):
@@ -148,7 +177,8 @@
         stats_kernel,
         grid=(GROUP,),
         out_shape=jax.ShapeDtypeStruct((16, count), F32),
-        in_specs=[smem(), smem(), part_block(count, 0), meta_block(count)] + [key_block(half)] * 4,
+        in_specs=[smem(), smem(), part_block(count, 0), meta_block(count)]
+        + [key_block(half), key_block(half, GROUP), key_block(half), key_block(half)],
         out_specs=whole((16, count)),
         compiler_params=params(),
         cost_estimate=cost(4 * pairs * HDIM, 6 * half * GROUP * HDIM * 2, pairs),
@@ -222,7 +252,9 @@
         grid=(GROUP,),
         out_shape=[jax.ShapeDtypeStruct((wide, count), F32)]
         + [jax.ShapeDtypeStruct((half, 2 * wide), BF16)] * 3,
-        in_specs=[smem()] + query_specs(count) + [pair_block(half)] * 3,
+        in_specs=[smem()]
+        + query_specs(count)
+        + [pair_block(half, GROUP), pair_block(half), pair_block(half)],
         out_specs=[turned_block(count)] + [pair_block(half)] * 3,
         compiler_params=params(),
         cost_estimate=cost(10 * pairs * HDIM, 20 * half * wide * 2, pairs),
@@ -240,7 +272,7 @@
     total = log_total(head, own_stats, far_stats)
     keys, values = w0[:, :HDIM], w0[:, HDIM:]
     scores = window_scores(queries, keys)
-    scores = jnp.where(key_frames(place, meta) <= q_frame, scores, NEG)
+    scores = jnp.where(key_frames(place, m_ref) <= q_frame, scores, NEG)
     dq, dk, dv = block_grads(scores, total, dot, queries, grads, keys, values)
     dq_out[...] = ((dq + dq_ref[...]) * FACTOR).T.astype(BF16)
     d0[:, :HDIM] = dk
@@ -266,59 +298,93 @@
     )(place, own_stats, far_stats, qg, qg, qg, w0, dq)
 
 
-def close_kernel(even_ref, d0, back, side, out):
+def close_kernel(even_ref, d0, d1, swapped, side, *outs):
     even = even_ref[0].astype(F32)
-    tok = out.shape[1]
-    for step in range(XN):
+    tok, wide = outs[0].shape[0], d0.shape[1]
+    for step, out in enumerate(outs):
         rows = slice(step * tok, (step + 1) * tok)
-        pair = d0[rows, :] + back[rows, :].astype(F32) + side[rows, :].astype(F32) * even
-        out[step] = pair.astype(BF16)
-
-
-def close(even, d0, back, side):
+        turned = side[rows, :].astype(F32)
+        out[:, :wide] = (d0[rows, :] + turned * even).astype(BF16)
+        held = d1[rows, :].astype(F32) + swapped[rows, :].astype(F32) + turned * (1.0 - even)
+        out[:, wide:] = held.astype(BF16)
+
+
+def close(even, d0, d1, swapped, side):
     half, wide = d0.shape
     tok = half // XN
     vmem = pl.BlockSpec(memory_space=pltpu.VMEM)
     return pl.pallas_call(
         close_kernel,
-        out_shape=jax.ShapeDtypeStruct((XN, tok, wide), BF16),
-        in_specs=[smem()] + [vmem] * 3,
+        out_shape=[jax.ShapeDtypeStruct((tok, 2 * wide), BF16)] * XN,
+        in_specs=[smem()] + [vmem] * 4,
+        out_specs=[vmem] * XN,
+        compiler_params=params(),
+        cost_estimate=cost(6 * half * wide, 14 * half * wide),
+        name="close",
+    )(even, d0, d1, swapped, side)
+
+
+def turn_kernel(place, *refs):
+    parts, out = refs[:XN], refs[XN]
+    for step, part in enumerate(parts):
+        for h in range(GROUP):
+            cols = head_columns(place, step, h)
+            at = 2 * (GROUP + h) * HDIM
+            out[0, :, cols] = part[:, at : at + HDIM]
+            out[1, :, cols] = part[:, at + HDIM : at + 2 * HDIM]
+
+
+def turn(place, parts):
+    tok = parts[0].shape[0]
+    vmem = pl.BlockSpec(memory_space=pltpu.VMEM)
+    return pl.pallas_call(
+        turn_kernel,
+        out_shape=jax.ShapeDtypeStruct((2, tok, HEADS * HDIM), BF16),
+        in_specs=[smem()] + [vmem] * XN,
         out_specs=vmem,
         compiler_params=params(),
-        cost_estimate=cost(3 * half * wide, 10 * half * wide),
-        name="close",
-    )(even, d0, back, side)
-
-
-def unpack_kernel(parts, halves, dq, dk, dv):
+        cost_estimate=cost(0, 8 * tok * HEADS * HDIM),
+        name="turn",
+    )(place, *parts)
+
+
+def unpack_kernel(place, *refs):
+    parts, (back, halves, dq, dk, dv) = refs[:XN], refs[XN:]
     wide = GROUP * HDIM
     for group in range(XN):
         total = halves[group].astype(F32) + halves[XN + group].astype(F32)
         dq[:, group * wide : (group + 1) * wide] = total.astype(BF16)
+    for step, part in enumerate(parts):
         for h in range(GROUP):
+            cols = head_columns(place, step, h)
             at = 2 * h * HDIM
-            cols = slice((group * GROUP + h) * HDIM, (group * GROUP + h + 1) * HDIM)
-            dk[:, cols] = parts[group, :, at : at + HDIM]
-            dv[:, cols] = parts[group, :, at + HDIM : at + 2 * HDIM]
-
-
-def unpack(parts, halves):
-    tok = parts.shape[1]
+            dk_sum = part[:, at : at + HDIM].astype(F32) + back[0, :, cols].astype(F32)
+            dk[:, cols] = dk_sum.astype(BF16)
+            dv_sum = part[:, at + HDIM : at + 2 * HDIM].astype(F32) + back[1, :, cols].astype(F32)
+            dv[:, cols] = dv_sum.astype(BF16)
+
+
+def unpack(place, parts, back, halves):
+    tok = parts[0].shape[0]
     vmem = pl.BlockSpec(memory_space=pltpu.VMEM)
     return pl.pallas_call(
         unpack_kernel,
         out_shape=[jax.ShapeDtypeStruct((tok, HEADS * HDIM), BF16)] * 3,
-        in_specs=[vmem] * 2,
+        in_specs=[smem()] + [vmem] * (XN + 2),
         out_specs=[vmem] * 3,
         compiler_params=params(),
-        cost_estimate=cost(0, 14 * tok * HEADS * HDIM),
+        cost_estimate=cost(0, 22 * tok * HEADS * HDIM),
         name="unpack",
-    )(parts, halves)
-
-
-def over_x(value):
-    groups = [[z * XN + x for x in range(XN)] for z in range(lax.axis_size("col") // XN)]
-    return lax.all_to_all(value, "col", 0, 0, axis_index_groups=groups)
+    )(place, *parts, back, halves)
+
+
+def over_x(chunks, sign):
+    moved = [chunks[0]]
+    for step in range(1, XN):
+        count = lax.axis_size("col")
+        pairs = [(c, c // XN * XN + (c + sign * step) % XN) for c in range(count)]
+        moved.append(lax.ppermute(chunks[step], "col", pairs))
+    return moved
 
 
 def across_z(value):
@@ -335,20 +401,6 @@
 def in_chip(value):
     count = lax.axis_size("row")
     return lax.ppermute(value, "row", [(r, r ^ 1) for r in range(count)])
-
-
-def halo(own, is_even):
-    second = along_row(own, 2)
-    swapped = in_chip(second)
-    third = along_row(jnp.where(is_even, own, second), 1)
-    return own, second, swapped, third
-
-
-def halo_back(second, swapped, third, is_even):
-    side = along_row(third, -1)
-    turned = jnp.where(is_even, jnp.zeros_like(side), side)
-    held = second.astype(F32) + in_chip(swapped).astype(F32) + turned.astype(F32)
-    return along_row(held.astype(BF16), -2), side
 
 
 def per_device(query, key, value, saved_out, grad_out, frame_ids):
@@ -358,10 +410,15 @@
     even = is_even.astype(jnp.int32).reshape(1)
     tok = query.shape[0]
     count = lax.axis_size("col") * tok
-
-    kv, qg = pack(query, key, value, saved_out, grad_out, frame_ids[:, None])
+    wide = 2 * GROUP * HDIM
+
+    far_key, far_value = along_row(key, 2), along_row(value, 2)
+    qg = pack_queries(query, saved_out, grad_out, frame_ids[:, None])
     qg = lax.all_to_all(qg, "col", 0, 0).reshape(count, -1)
-    window = halo(over_x(kv).reshape(XN * tok, -1), is_even)
+    near = jnp.concatenate(over_x(pack_keys(place, key, value, far_key, far_value), 1), axis=0)
+    w0, w1 = near[:, :wide], near[:, wide:]
+    w3 = along_row(jnp.where(is_even, w0, w1), 1)
+    w2 = in_chip(w1)
     held = jnp.stack(
         [
             row >= 0,
@@ -372,14 +429,16 @@
     )
     bias = jnp.where(held, 0.0, NEG).astype(F32)
 
-    own_stats = stats(bias, place, qg, window)
+    own_stats = stats(bias, place, qg, (near, near, w2, w3))
     far_stats = across_z(own_stats)
-    dq_part, *earlier_grads = earlier(bias, place, own_stats, far_stats, qg, window[1:])
-    dq, d0 = same(place, own_stats, far_stats, qg, window[0], dq_part)
-
-    back, side = halo_back(*earlier_grads, is_even)
+    dq_part, d1, d2, d3 = earlier(bias, place, own_stats, far_stats, qg, (near, w2, w3))
+    dq, d0 = same(place, own_stats, far_stats, qg, near, dq_part)
+
+    side = along_row(d3, -1)
     halves = lax.all_to_all(dq.reshape(-1, tok, GROUP * HDIM), "col", 0, 0)
-    return tuple(unpack(over_x(close(even, d0, back, side)), halves))
+    parts = over_x(close(even, d0, d1, in_chip(d2), side), -1)
+    back = along_row(turn(place, parts), -2)
+    return tuple(unpack(place, parts, back, halves))
 
 
 def solution(mesh):

time: 173 us -> 169 us (0.977)
  starting transfers between devices: 35 us -> 69.2 us
  blocking collectives: 30.3 us -> 0 us
  waiting for transfers between devices: 73.4 us -> 62.7 us
  Pallas kernels: 26.5 us -> 30.4 us
    ppermute x0 -> x6, waiting for transfers between devices: none -> 35.5 us  [over_x(): moved.append(lax.ppermute(chunks[step], 'col', pairs))]
    ppermute x4 -> x5, waiting for transfers between devices: 59.9 us -> 25.3 us  [along_row(): lax.ppermute(value, 'row', [(r, r + steps) for r in range(first, last)])]
    all_to_all x2 -> x0, blocking collectives: 30.3 us -> none  [over_x(): return lax.all_to_all(value, 'col', 0, 0, axis_index_groups=groups)]
    ppermute x0 -> x6, starting transfers between devices: none -> 22.5 us  [over_x(): moved.append(lax.ppermute(chunks[step], 'col', pairs))]
    ppermute x1, starting transfers between devices: 2.64 us -> 8.87 us  [across_z(): lax.ppermute(value, 'col', [(c, (c + XN) % count) for c in range(count)])]
    all_to_all x1, waiting for transfers between devices: 6.13 us -> 0.01 us  [per_device(): qg = lax.all_to_all(qg, 'col', 0, 0).reshape(count, -1)]
    ppermute x1, waiting for transfers between devices: 7.33 us -> 1.88 us  [across_z(): lax.ppermute(value, 'col', [(c, (c + XN) % count) for c in range(count)])]
    all_to_all x1, starting transfers between devices: 4.31 us -> 7.61 us  [per_device(): halves = lax.all_to_all(dq.reshape(-1, tok, GROUP * HDIM), 'col', 0, 0)]
  transfers between devices with their start and end apart: 9 -> 16, of which waited for: 5 -> 9; matrix products, arithmetic and copies ran while one was open for 1% -> 2% of each run, Pallas kernels for 4% -> 8%
where the time goes in v4:
time: 169 us; the launch traced here: 168 us
  starting transfers between devices  69.2 us (41%)
  waiting for transfers between devices  62.7 us (37%)
  Pallas kernels  30.4 us (18%)
  local copies, waits for them, and re-layouts  3.62 us (2%)
    ppermute x6, waiting for transfers between devices, over_x(): moved.append(lax.ppermute(chunks[step], 'col', pairs))  35.5 us
    ppermute x5, waiting for transfers between devices, along_row(): lax.ppermute(value, 'row', [(r, r + steps) for r in range(first, last)])  25.3 us
    ppermute x6, starting transfers between devices, over_x(): moved.append(lax.ppermute(chunks[step], 'col', pairs))  22.5 us
    ppermute x5, starting transfers between devices, along_row(): lax.ppermute(value, 'row', [(r, r + steps) for r in range(first, last)])  13.6 us
    all_to_all x1, starting transfers between devices, per_device(): qg = lax.all_to_all(qg, 'col', 0, 0).reshape(count, -1)  11.1 us
    pallas_call x1, Pallas kernels, earlier(): pl.pallas_call(earlier_kernel, grid=(GROUP,), out_shape=[jax.ShapeDtypeSt...  10.1 us
    ppermute x1, starting transfers between devices, across_z(): lax.ppermute(value, 'col', [(c, (c + XN) % count) for c in range(count)])  8.87 us
    all_to_all x1, starting transfers between devices, per_device(): halves = lax.all_to_all(dq.reshape(-1, tok, GROUP * HDIM), 'col', 0, 0)  7.61 us
  transfers between devices with their start and end apart: 16, of which 9 were waited for; matrix products, arithmetic and copies ran while one was open for 2% of the time, Pallas kernels for 8%

profile of v4, /device:TPU:120, one launch (start us, length us, event | category | flops | bytes accessed | tf_op | source)
XLA Modules:
  0.0 168.1 jit_solution(14524918197018391515)
XLA Ops:
  0.6 3.5 %collective-permute-start = (bf16[64,2560]{1,0:T(8,128)(2,1)}, bf16[64,2560]{1,0:T(8,128)(2,1)S(1)}, u32[]{:S(2)}, u32[]{:S(2)}) collective-permute-start(bf16[64,2560]{1,0:T(8,128)(2,1)} %k_ref.1), channel_id=1, source_target_pairs={{0,16},{8,24},{16,32},{24,40},{32,48},{40,56},{48,64},{56,72},{64,... | collective-permute-start | bytes 983048 | tf_op jit(solution)/shard_map/ppermute | solution.py:398
  4.1 3.5 %collective-permute-start.1 = (bf16[64,2560]{1,0:T(8,128)(2,1)}, bf16[64,2560]{1,0:T(8,128)(2,1)S(1)}, u32[]{:S(2)}, u32[]{:S(2)}) collective-permute-start(bf16[64,2560]{1,0:T(8,128)(2,1)} %v_ref.1), channel_id=1, source_target_pairs={{0,16},{8,24},{16,32},{24,40},{32,48},{40,56},{48,64},{56,72},{64,... | collective-permute-start | bytes 983048 | tf_op jit(solution)/shard_map/ppermute | solution.py:398
  7.6 1.4 copy.9.f_ref
  9.0 3.4 %pack_queries.1 = bf16[8,64,1408]{2,1,0:T(8,128)(2,1)} custom-call(bf16[64,2560]{1,0:T(8,128)(2,1)} %q_any.1, bf16[64,2560]{1,0:T(8,128)(2,1)} %o_any.1, bf16[64,2560]{1,0:T(8,128)(2,1)} %g_any.1, s32[64,1]{1,0:T(8,128)} %copy.9.f_ref), custom_call_target="tpu_custom_call" | custom-call | flops 327680 | bytes 2293760 | tf_op jit(solution)/shard_map/pack_queries/pallas_call | solution.py:70
  12.4 0.0 copy-start.4
  12.4 0.0 copy-start.5
  12.4 11.1 %all-to-all-start = ((bf16[8,64,1408]{2,1,0:T(8,128)(2,1)}), bf16[8,64,1408]{2,1,0:T(8,128)(2,1)S(1)}, u32[]{:S(2)}, u32[]{:S(2)}) async-start(bf16[8,64,1408]{2,1,0:T(8,128)(2,1)} %pack_queries.1), calls=%async_computation | async-start | bytes 2883584 | tf_op jit(solution)/shard_map/all_to_all | solution.py:417
  23.5 0.1 pad_add_fusion.place
  23.6 0.0 collective-permute-done.k2_ref
  23.6 0.0 collective-permute-done.1.v2_ref
  23.6 0.0 copy-done.4
  23.6 0.0 copy-done.5
  23.6 0.8 pack_keys.1
  24.4 3.9 %collective-permute-start.2 = (bf16[64,2560]{1,0:T(8,128)(2,1)S(1)}, bf16[64,2560]{1,0:T(8,128)(2,1)S(1)}, u32[]{:S(2)}, u32[]{:S(2)}) collective-permute-start(bf16[64,2560]{1,0:T(8,128)(2,1)S(1)} %get-tuple-element.18), channel_id=1, source_target_pairs={{0,1},{1,2},{2,3},{3,0},{4,5},{5,6},{6,7},{7,4},{8,9},{9,10},{10,1... | collective-permute-start | bytes 983048 | tf_op jit(solution)/shard_map/ppermute | solution.py:386
  28.4 4.6 %collective-permute-start.3 = (bf16[64,2560]{1,0:T(8,128)(2,1)S(1)}, bf16[64,2560]{1,0:T(8,128)(2,1)S(1)}, u32[]{:S(2)}, u32[]{:S(2)}) collective-permute-start(bf16[64,2560]{1,0:T(8,128)(2,1)S(1)} %get-tuple-element.19), channel_id=1, source_target_pairs={{0,2},{1,3},{2,0},{3,1},{4,6},{5,7},{6,4},{7,5},{8,10},{9,11},{10,... | collective-permute-start | bytes 983048 | tf_op jit(solution)/shard_map/ppermute | solution.py:386
  32.9 3.4 %collective-permute-start.4 = (bf16[64,2560]{1,0:T(8,128)(2,1)S(1)}, bf16[64,2560]{1,0:T(8,128)(2,1)S(1)}, u32[]{:S(2)}, u32[]{:S(2)}) collective-permute-start(bf16[64,2560]{1,0:T(8,128)(2,1)S(1)} %get-tuple-element.20), channel_id=1, source_target_pairs={{0,3},{1,0},{2,1},{3,2},{4,7},{5,4},{6,5},{7,6},{8,11},{9,8},{10,9... | collective-permute-start | bytes 983048 | tf_op jit(solution)/shard_map/ppermute | solution.py:386
  36.4 6.6 %collective-permute-done.2 = bf16[64,2560]{1,0:T(8,128)(2,1)S(1)} collective-permute-done((bf16[64,2560]{1,0:T(8,128)(2,1)S(1)}, bf16[64,2560]{1,0:T(8,128)(2,1)S(1)}, u32[]{:S(2)}, u32[]{:S(2)}) %collective-permute-start.2) | collective-permute-done | bytes 327712 | tf_op jit(solution)/shard_map/ppermute | solution.py:386
  42.9 5.7 %collective-permute-done.3 = bf16[64,2560]{1,0:T(8,128)(2,1)S(1)} collective-permute-done((bf16[64,2560]{1,0:T(8,128)(2,1)S(1)}, bf16[64,2560]{1,0:T(8,128)(2,1)S(1)}, u32[]{:S(2)}, u32[]{:S(2)}) %collective-permute-start.3) | collective-permute-done | bytes 327712 | tf_op jit(solution)/shard_map/ppermute | solution.py:386
  48.7 6.1 %collective-permute-done.4 = bf16[64,2560]{1,0:T(8,128)(2,1)S(1)} collective-permute-done((bf16[64,2560]{1,0:T(8,128)(2,1)S(1)}, bf16[64,2560]{1,0:T(8,128)(2,1)S(1)}, u32[]{:S(2)}, u32[]{:S(2)}) %collective-permute-start.4) | collective-permute-done | bytes 327712 | tf_op jit(solution)/shard_map/ppermute | solution.py:386
  54.8 1.2 slice_select_fusion
  56.0 1.9 %collective-permute-start.6 = (bf16[256,1280]{1,0:T(8,128)(2,1)}, bf16[256,1280]{1,0:T(8,128)(2,1)S(1)}, u32[]{:S(2)}, u32[]{:S(2)}) collective-permute-start(bf16[256,1280]{1,0:T(8,128)(2,1)} %get-tuple-element.31), channel_id=1, source_target_pairs={{0,8},{8,16},{16,24},{24,32},{32,40},{40,48},{48,56},{56,64},{64,7... | collective-permute-start | bytes 1966088 | tf_op jit(solution)/shard_map/ppermute | solution.py:398
  57.9 3.6 %collective-permute-start.5 = (bf16[256,1280]{1,0:T(8,128)(2,1)}, bf16[256,1280]{1,0:T(8,128)(2,1)}, u32[]{:S(2)}, u32[]{:S(2)}) collective-permute-start(bf16[256,1280]{1,0:T(8,128)(2,1)} %get-tuple-element.32), channel_id=1, source_target_pairs={{0,8},{8,0},{16,24},{24,16},{32,40},{40,32},{48,56},{56,48},{64,72... | collective-permute-start | bytes 1966088 | tf_op jit(solution)/shard_map/ppermute | solution.py:403
  61.5 0.1 add_select_fusion.bias_ref
  61.6 6.5 %collective-permute-done.6.w3 = bf16[256,1280]{1,0:T(8,128)(2,1)S(1)} collective-permute-done((bf16[256,1280]{1,0:T(8,128)(2,1)}, bf16[256,1280]{1,0:T(8,128)(2,1)S(1)}, u32[]{:S(2)}, u32[]{:S(2)}) %collective-permute-start.6) | collective-permute-done | bytes 655392 | tf_op jit(solution)/shard_map/ppermute | solution.py:398
  68.1 0.0 copy-start.2
  68.1 0.0 collective-permute-done.5.w2
  68.1 0.0 all-to-all-done
  68.1 5.4 %stats.1.own_stats = f32[16,512]{1,0:T(8,128)S(1)} custom-call(f32[4]{0:T(128)S(1)} %add_select_fusion.bias_ref, s32[2]{0:T(128)S(1)} %pad_add_fusion.place, bf16[512,1408]{1,0:T(8,128)(2,1)S(1)} %bitcast.10, bf16[512,1408]{1,0:T(8,128)(2,1)S(1)} %bitcast.11, bf16[256,2560]{1,0:T(8,128)(2,1)S(1)} %constant_dynamic-update-slice_fusion.w0.w1, ...), custom_call_target="tpu_custom_call" | custom-call | flops 1342177280 | bytes 1966080 | tf_op jit(solution)/shard_map/stats/pallas_call | solution.py:176
  73.5 0.0 copy-done.2
  73.5 8.9 %collective-permute-start.7 = (f32[16,512]{1,0:T(8,128)S(1)}, f32[16,512]{1,0:T(8,128)S(1)}, u32[]{:S(2)}, u32[]{:S(2)}) collective-permute-start(f32[16,512]{1,0:T(8,128)S(1)} %stats.1.own_stats), channel_id=1, source_target_pairs={{0,4},{1,5},{2,6},{3,7},{4,0},{5,1},{6,2},{7,3},{8,12},{9,13},{10,... | collective-permute-start | bytes 98312 | tf_op jit(solution)/shard_map/ppermute | solution.py:392
  82.4 1.9 %collective-permute-done.7.far_stats = f32[16,512]{1,0:T(8,128)S(1)} collective-permute-done((f32[16,512]{1,0:T(8,128)S(1)}, f32[16,512]{1,0:T(8,128)S(1)}, u32[]{:S(2)}, u32[]{:S(2)}) %collective-permute-start.7) | collective-permute-done | bytes 32800 | tf_op jit(solution)/shard_map/ppermute | solution.py:392
  84.2 0.0 copy-start.3
  84.2 1.1 copy-done.3
  85.3 10.1 %earlier.1 = (f32[640,512]{1,0:T(8,128)S(1)}, bf16[256,1280]{1,0:T(8,128)(2,1)S(1)}, bf16[256,1280]{1,0:T(8,128)(2,1)}, bf16[256,1280]{1,0:T(8,128)(2,1)}) custom-call(f32[4]{0:T(128)S(1)} %add_select_fusion.bias_ref, s32[2]{0:T(128)S(1)} %pad_add_fusion.place, f32[16,512]{1,0:T(8,128)S(1)} %stats.1.own_stats, ...), custom_call_target="tpu_custom_call" | custom-call | flops 2516582400 | bytes 6553600 | tf_op jit(solution)/shard_map/earlier/pallas_call | solution.py:250
  95.4 1.9 %collective-permute-start.8 = (bf16[256,1280]{1,0:T(8,128)(2,1)}, bf16[256,1280]{1,0:T(8,128)(2,1)}, u32[]{:S(2)}, u32[]{:S(2)}) collective-permute-start(bf16[256,1280]{1,0:T(8,128)(2,1)} %get-tuple-element.24), channel_id=1, source_target_pairs={{0,8},{8,0},{16,24},{24,16},{32,40},{40,32},{48,56},{56,48},{64,72... | collective-permute-start | bytes 1966088 | tf_op jit(solution)/shard_map/ppermute | solution.py:403
  97.3 2.8 %collective-permute-start.9 = (bf16[256,1280]{1,0:T(8,128)(2,1)}, bf16[256,1280]{1,0:T(8,128)(2,1)}, u32[]{:S(2)}, u32[]{:S(2)}) collective-permute-start(bf16[256,1280]{1,0:T(8,128)(2,1)} %get-tuple-element.25), channel_id=1, source_target_pairs={{8,0},{16,8},{24,16},{32,24},{40,32},{48,40},{56,48},{64,56},{72,6... | collective-permute-start | bytes 1966088 | tf_op jit(solution)/shard_map/ppermute | solution.py:398
  100.1 6.1 %same.1 = (bf16[512,640]{1,0:T(8,128)(2,1)}, f32[256,1280]{1,0:T(8,128)S(1)}) custom-call(s32[2]{0:T(128)S(1)} %pad_add_fusion.place, f32[16,512]{1,0:T(8,128)S(1)} %stats.1.own_stats, f32[16,512]{1,0:T(8,128)S(1)} %collective-permute-done.7.far_stats, bf16[512,1408]{1,0:T(8,128)(2,1)S(1)} %bitcast.15, bf16[512,1408]{1,0:T(8,128)(2,1)S(1)} %bitcast.16, ...), custom_call_target="tpu_custom_call" | custom-call | flops 838860800 | bytes 5242880 | tf_op jit(solution)/shard_map/same/pallas_call | solution.py:286
  106.2 0.0 copy-start
  106.2 1.1 copy-done
  107.2 0.0 copy-start.1
  107.2 7.6 %all-to-all-start.1 = ((bf16[8,64,640]{2,1,0:T(8,128)(2,1)}), bf16[8,64,640]{2,1,0:T(8,128)(2,1)S(1)}, u32[]{:S(2)}, u32[]{:S(2)}) async-start(bf16[8,64,640]{2,1,0:T(8,128)(2,1)} %bitcast.9), calls=%async_computation.1 | async-start | bytes 1310720 | tf_op jit(solution)/shard_map/all_to_all | solution.py:438
  114.8 0.0 collective-permute-done.8.swapped
  114.8 0.0 collective-permute-done.9.side
  114.9 0.0 copy-done.1
  114.9 1.7 %close.1 = (bf16[64,2560]{1,0:T(8,128)(2,1)S(1)}, bf16[64,2560]{1,0:T(8,128)(2,1)S(1)}, bf16[64,2560]{1,0:T(8,128)(2,1)S(1)}, bf16[64,2560]{1,0:T(8,128)(2,1)S(1)}) custom-call(s32[1]{0:T(128)} %bitcast.2.even_ref, f32[256,1280]{1,0:T(8,128)S(1)} %copy-done.1, bf16[256,1280]{1,0:T(8,128)(2,1)S(1)} %get-tuple-element.23.d1, ...), custom_call_target="tpu_custom_call" | custom-call | flops 1966080 | bytes 4587520 | tf_op jit(solution)/shard_map/close/pallas_call | solution.py:316
  116.6 5.1 %collective-permute-start.10 = (bf16[64,2560]{1,0:T(8,128)(2,1)S(1)}, bf16[64,2560]{1,0:T(8,128)(2,1)S(1)}, u32[]{:S(2)}, u32[]{:S(2)}) collective-permute-start(bf16[64,2560]{1,0:T(8,128)(2,1)S(1)} %get-tuple-element.27), channel_id=1, source_target_pairs={{0,3},{1,0},{2,1},{3,2},{4,7},{5,4},{6,5},{7,6},{8,11},{9,8},{10,9... | collective-permute-start | bytes 983048 | tf_op jit(solution)/shard_map/ppermute | solution.py:386
  121.7 2.8 %collective-permute-start.11 = (bf16[64,2560]{1,0:T(8,128)(2,1)S(1)}, bf16[64,2560]{1,0:T(8,128)(2,1)S(1)}, u32[]{:S(2)}, u32[]{:S(2)}) collective-permute-start(bf16[64,2560]{1,0:T(8,128)(2,1)S(1)} %get-tuple-element.28), channel_id=1, source_target_pairs={{0,2},{1,3},{2,0},{3,1},{4,6},{5,7},{6,4},{7,5},{8,10},{9,11},{10,... | collective-permute-start | bytes 983048 | tf_op jit(solution)/shard_map/ppermute | solution.py:386
  124.5 2.8 %collective-permute-start.12 = (bf16[64,2560]{1,0:T(8,128)(2,1)S(1)}, bf16[64,2560]{1,0:T(8,128)(2,1)S(1)}, u32[]{:S(2)}, u32[]{:S(2)}) collective-permute-start(bf16[64,2560]{1,0:T(8,128)(2,1)S(1)} %get-tuple-element.29), channel_id=1, source_target_pairs={{0,1},{1,2},{2,3},{3,0},{4,5},{5,6},{6,7},{7,4},{8,9},{9,10},{10,1... | collective-permute-start | bytes 983048 | tf_op jit(solution)/shard_map/ppermute | solution.py:386
  127.3 10.9 %collective-permute-done.10.refs_1_ = bf16[64,2560]{1,0:T(8,128)(2,1)S(1)} collective-permute-done((bf16[64,2560]{1,0:T(8,128)(2,1)S(1)}, bf16[64,2560]{1,0:T(8,128)(2,1)S(1)}, u32[]{:S(2)}, u32[]{:S(2)}) %collective-permute-start.10) | collective-permute-done | bytes 327712 | tf_op jit(solution)/shard_map/ppermute | solution.py:386
  138.2 1.2 collective-permute-done.11.refs_2_
  139.3 5.1 %collective-permute-done.12.refs_3_ = bf16[64,2560]{1,0:T(8,128)(2,1)S(1)} collective-permute-done((bf16[64,2560]{1,0:T(8,128)(2,1)S(1)}, bf16[64,2560]{1,0:T(8,128)(2,1)S(1)}, u32[]{:S(2)}, u32[]{:S(2)}) %collective-permute-start.12) | collective-permute-done | bytes 327712 | tf_op jit(solution)/shard_map/ppermute | solution.py:386
  144.4 0.7 turn.1
  145.1 1.9 %collective-permute-start.13 = (bf16[2,64,2560]{2,1,0:T(8,128)(2,1)S(1)}, bf16[2,64,2560]{2,1,0:T(8,128)(2,1)}, u32[]{:S(2)}, u32[]{:S(2)}) collective-permute-start(bf16[2,64,2560]{2,1,0:T(8,128)(2,1)S(1)} %turn.1), channel_id=1, source_target_pairs={{16,0},{24,8},{32,16},{40,24},{48,32},{56,40},{64,48},{72,56},{80,... | collective-permute-start | bytes 1966088 | tf_op jit(solution)/shard_map/ppermute | solution.py:398
  147.1 0.0 all-to-all-done.1.refs_5_
  147.1 18.8 %collective-permute-done.13.refs_4_ = bf16[2,64,2560]{2,1,0:T(8,128)(2,1)} collective-permute-done((bf16[2,64,2560]{2,1,0:T(8,128)(2,1)S(1)}, bf16[2,64,2560]{2,1,0:T(8,128)(2,1)}, u32[]{:S(2)}, u32[]{:S(2)}) %collective-permute-start.13) | collective-permute-done | bytes 655392 | tf_op jit(solution)/shard_map/ppermute | solution.py:398
  165.9 2.2 %unpack.1 = (bf16[64,2560]{1,0:T(8,128)(2,1)}, bf16[64,2560]{1,0:T(8,128)(2,1)}, bf16[64,2560]{1,0:T(8,128)(2,1)}) custom-call(s32[2]{0:T(128)S(1)} %pad_add_fusion.place, bf16[64,2560]{1,0:T(8,128)(2,1)S(1)} %get-tuple-element.26.refs_0_, bf16[64,2560]{1,0:T(8,128)(2,1)S(1)} %collective-permute-done.10.refs_1_, ...), custom_call_target="tpu_custom_call" | custom-call | bytes 3604480 | tf_op jit(solution)/shard_map/unpack/pallas_call | solution.py:370
  (4 shorter events, 0.1 us)
Async XLA Ops:
  0.6 23.0 %collective-permute-start = (bf16[64,2560]{1,0:T(8,128)(2,1)}, bf16[64,2560]{1,0:T(8,128)(2,1)S(1)}, u32[]{:S(2)}, u32[]{:S(2)}) collective-permute-start(bf16[64,2560]{1,0:T(8,128)(2,1)} %k_ref.1), channel_id=1, source_target_pairs={{0,16},{8,24},{16,32},{24,40},{32,48},{40,56},{48,64},{56,72},{64,... | collective-permute-start | bytes 983048 | tf_op jit(solution)/shard_map/ppermute | solution.py:398
  4.1 19.5 %collective-permute-start.1 = (bf16[64,2560]{1,0:T(8,128)(2,1)}, bf16[64,2560]{1,0:T(8,128)(2,1)S(1)}, u32[]{:S(2)}, u32[]{:S(2)}) collective-permute-start(bf16[64,2560]{1,0:T(8,128)(2,1)} %v_ref.1), channel_id=1, source_target_pairs={{0,16},{8,24},{16,32},{24,40},{32,48},{40,56},{48,64},{56,72},{64,... | collective-permute-start | bytes 983048 | tf_op jit(solution)/shard_map/ppermute | solution.py:398
  12.4 11.2 %copy-start.4 = (bf16[64,2560]{1,0:T(8,128)(2,1)S(1)}, bf16[64,2560]{1,0:T(8,128)(2,1)}, u32[]{:S(2)}) copy-start(bf16[64,2560]{1,0:T(8,128)(2,1)} %k_ref.1) | copy-start | bytes 983044
  12.4 11.2 %copy-start.5 = (bf16[64,2560]{1,0:T(8,128)(2,1)S(1)}, bf16[64,2560]{1,0:T(8,128)(2,1)}, u32[]{:S(2)}) copy-start(bf16[64,2560]{1,0:T(8,128)(2,1)} %v_ref.1) | copy-start | bytes 983044
  12.4 55.7 %all-to-all-start = ((bf16[8,64,1408]{2,1,0:T(8,128)(2,1)}), bf16[8,64,1408]{2,1,0:T(8,128)(2,1)S(1)}, u32[]{:S(2)}, u32[]{:S(2)}) async-start(bf16[8,64,1408]{2,1,0:T(8,128)(2,1)} %pack_queries.1), calls=%async_computation | async-start | bytes 2883584 | tf_op jit(solution)/shard_map/all_to_all | solution.py:417
  24.4 18.5 %collective-permute-start.2 = (bf16[64,2560]{1,0:T(8,128)(2,1)S(1)}, bf16[64,2560]{1,0:T(8,128)(2,1)S(1)}, u32[]{:S(2)}, u32[]{:S(2)}) collective-permute-start(bf16[64,2560]{1,0:T(8,128)(2,1)S(1)} %get-tuple-element.18), channel_id=1, source_target_pairs={{0,1},{1,2},{2,3},{3,0},{4,5},{5,6},{6,7},{7,4},{8,9},{9,10},{10,1... | collective-permute-start | bytes 983048 | tf_op jit(solution)/shard_map/ppermute | solution.py:386
  28.4 20.3 %collective-permute-start.3 = (bf16[64,2560]{1,0:T(8,128)(2,1)S(1)}, bf16[64,2560]{1,0:T(8,128)(2,1)S(1)}, u32[]{:S(2)}, u32[]{:S(2)}) collective-permute-start(bf16[64,2560]{1,0:T(8,128)(2,1)S(1)} %get-tuple-element.19), channel_id=1, source_target_pairs={{0,2},{1,3},{2,0},{3,1},{4,6},{5,7},{6,4},{7,5},{8,10},{9,11},{10,... | collective-permute-start | bytes 983048 | tf_op jit(solution)/shard_map/ppermute | solution.py:386
  32.9 21.9 %collective-permute-start.4 = (bf16[64,2560]{1,0:T(8,128)(2,1)S(1)}, bf16[64,2560]{1,0:T(8,128)(2,1)S(1)}, u32[]{:S(2)}, u32[]{:S(2)}) collective-permute-start(bf16[64,2560]{1,0:T(8,128)(2,1)S(1)} %get-tuple-element.20), channel_id=1, source_target_pairs={{0,3},{1,0},{2,1},{3,2},{4,7},{5,4},{6,5},{7,6},{8,11},{9,8},{10,9... | collective-permute-start | bytes 983048 | tf_op jit(solution)/shard_map/ppermute | solution.py:386
  56.0 12.1 %collective-permute-start.6 = (bf16[256,1280]{1,0:T(8,128)(2,1)}, bf16[256,1280]{1,0:T(8,128)(2,1)S(1)}, u32[]{:S(2)}, u32[]{:S(2)}) collective-permute-start(bf16[256,1280]{1,0:T(8,128)(2,1)} %get-tuple-element.31), channel_id=1, source_target_pairs={{0,8},{8,16},{16,24},{24,32},{32,40},{40,48},{48,56},{56,64},{64,7... | collective-permute-start | bytes 1966088 | tf_op jit(solution)/shard_map/ppermute | solution.py:398
  57.9 10.2 %collective-permute-start.5 = (bf16[256,1280]{1,0:T(8,128)(2,1)}, bf16[256,1280]{1,0:T(8,128)(2,1)}, u32[]{:S(2)}, u32[]{:S(2)}) collective-permute-start(bf16[256,1280]{1,0:T(8,128)(2,1)} %get-tuple-element.32), channel_id=1, source_target_pairs={{0,8},{8,0},{16,24},{24,16},{32,40},{40,32},{48,56},{56,48},{64,72... | collective-permute-start | bytes 1966088 | tf_op jit(solution)/shard_map/ppermute | solution.py:403
  68.1 5.4 %copy-start.2 = (bf16[256,1280]{1,0:T(8,128)(2,1)}, bf16[256,1280]{1,0:T(8,128)(2,1)S(1)}, u32[]{:S(2)}) copy-start(bf16[256,1280]{1,0:T(8,128)(2,1)S(1)} %collective-permute-done.6.w3) | copy-start | bytes 1966084
  73.5 10.8 %collective-permute-start.7 = (f32[16,512]{1,0:T(8,128)S(1)}, f32[16,512]{1,0:T(8,128)S(1)}, u32[]{:S(2)}, u32[]{:S(2)}) collective-permute-start(f32[16,512]{1,0:T(8,128)S(1)} %stats.1.own_stats), channel_id=1, source_target_pairs={{0,4},{1,5},{2,6},{3,7},{4,0},{5,1},{6,2},{7,3},{8,12},{9,13},{10,... | collective-permute-start | bytes 98312 | tf_op jit(solution)/shard_map/ppermute | solution.py:392
  84.2 1.1 copy-start.3
  95.4 19.4 %collective-permute-start.8 = (bf16[256,1280]{1,0:T(8,128)(2,1)}, bf16[256,1280]{1,0:T(8,128)(2,1)}, u32[]{:S(2)}, u32[]{:S(2)}) collective-permute-start(bf16[256,1280]{1,0:T(8,128)(2,1)} %get-tuple-element.24), channel_id=1, source_target_pairs={{0,8},{8,0},{16,24},{24,16},{32,40},{40,32},{48,56},{56,48},{64,72... | collective-permute-start | bytes 1966088 | tf_op jit(solution)/shard_map/ppermute | solution.py:403
  97.3 17.5 %collective-permute-start.9 = (bf16[256,1280]{1,0:T(8,128)(2,1)}, bf16[256,1280]{1,0:T(8,128)(2,1)}, u32[]{:S(2)}, u32[]{:S(2)}) collective-permute-start(bf16[256,1280]{1,0:T(8,128)(2,1)} %get-tuple-element.25), channel_id=1, source_target_pairs={{8,0},{16,8},{24,16},{32,24},{40,32},{48,40},{56,48},{64,56},{72,6... | collective-permute-start | bytes 1966088 | tf_op jit(solution)/shard_map/ppermute | solution.py:398
  106.2 1.1 copy-start
  107.2 7.6 %copy-start.1 = (f32[256,1280]{1,0:T(8,128)S(1)}, f32[256,1280]{1,0:T(8,128)}, u32[]{:S(2)}) copy-start(f32[256,1280]{1,0:T(8,128)} %copy-done) | copy-start | bytes 3932164
  107.2 39.9 %all-to-all-start.1 = ((bf16[8,64,640]{2,1,0:T(8,128)(2,1)}), bf16[8,64,640]{2,1,0:T(8,128)(2,1)S(1)}, u32[]{:S(2)}, u32[]{:S(2)}) async-start(bf16[8,64,640]{2,1,0:T(8,128)(2,1)} %bitcast.9), calls=%async_computation.1 | async-start | bytes 1310720 | tf_op jit(solution)/shard_map/all_to_all | solution.py:438
  116.6 21.6 %collective-permute-start.10 = (bf16[64,2560]{1,0:T(8,128)(2,1)S(1)}, bf16[64,2560]{1,0:T(8,128)(2,1)S(1)}, u32[]{:S(2)}, u32[]{:S(2)}) collective-permute-start(bf16[64,2560]{1,0:T(8,128)(2,1)S(1)} %get-tuple-element.27), channel_id=1, source_target_pairs={{0,3},{1,0},{2,1},{3,2},{4,7},{5,4},{6,5},{7,6},{8,11},{9,8},{10,9... | collective-permute-start | bytes 983048 | tf_op jit(solution)/shard_map/ppermute | solution.py:386
  121.7 17.6 %collective-permute-start.11 = (bf16[64,2560]{1,0:T(8,128)(2,1)S(1)}, bf16[64,2560]{1,0:T(8,128)(2,1)S(1)}, u32[]{:S(2)}, u32[]{:S(2)}) collective-permute-start(bf16[64,2560]{1,0:T(8,128)(2,1)S(1)} %get-tuple-element.28), channel_id=1, source_target_pairs={{0,2},{1,3},{2,0},{3,1},{4,6},{5,7},{6,4},{7,5},{8,10},{9,11},{10,... | collective-permute-start | bytes 983048 | tf_op jit(solution)/shard_map/ppermute | solution.py:386
  124.5 19.9 %collective-permute-start.12 = (bf16[64,2560]{1,0:T(8,128)(2,1)S(1)}, bf16[64,2560]{1,0:T(8,128)(2,1)S(1)}, u32[]{:S(2)}, u32[]{:S(2)}) collective-permute-start(bf16[64,2560]{1,0:T(8,128)(2,1)S(1)} %get-tuple-element.29), channel_id=1, source_target_pairs={{0,1},{1,2},{2,3},{3,0},{4,5},{5,6},{6,7},{7,4},{8,9},{9,10},{10,1... | collective-permute-start | bytes 983048 | tf_op jit(solution)/shard_map/ppermute | solution.py:386
  145.1 20.8 %collective-permute-start.13 = (bf16[2,64,2560]{2,1,0:T(8,128)(2,1)S(1)}, bf16[2,64,2560]{2,1,0:T(8,128)(2,1)}, u32[]{:S(2)}, u32[]{:S(2)}) collective-permute-start(bf16[2,64,2560]{2,1,0:T(8,128)(2,1)S(1)} %turn.1), channel_id=1, source_target_pairs={{16,0},{24,8},{32,16},{40,24},{48,32},{56,40},{64,48},{72,56},{80,... | collective-permute-start | bytes 1966088 | tf_op jit(solution)/shard_map/ppermute | solution.py:398

commit v5 on v2

v5 whole, which is shorter than its diff:
```python
import functools
import math

import jax
import jax.numpy as jnp
from jax import lax
from jax.experimental import pallas as pl
from jax.experimental.pallas import tpu as pltpu
from jax.sharding import PartitionSpec as P

HEADS = 20
HDIM = 128
XN = 4
GROUP = HEADS // XN
NEG = -1e30
FACTOR = HDIM ** (-0.5)
SCALE2 = FACTOR * math.log2(math.e)
LOW_LANE = 32
FRAME_LANE = 64
BF16 = jnp.bfloat16
F32 = jnp.float32
NT = (((1,), (1,)), ((), ()))
NN = (((1,), (0,)), ((), ()))


def params(room=20):
    return pltpu.CompilerParams(vmem_limit_bytes=room * 1024 * 1024)


def cost(flops, moved, exps=0):
    return pl.CostEstimate(flops=flops, bytes_accessed=moved, transcendentals=exps)


def load_all(sources, held, sems):
    copies = [
        pltpu.make_async_copy(src, held.at[at], sems.at[at]) for at, src in enumerate(sources)
    ]
    for copy in copies:
        copy.start()
    for copy in copies:
        copy.wait()


def pack_queries_kernel(q_any, o_any, g_any, f_ref, out, held, sems):
    load_all((q_any, o_any, g_any), held, sems)
    tok = held.shape[1]
    wide = GROUP * HDIM
    lane = lax.broadcasted_iota(jnp.int32, (tok, HDIM), 1)
    meta = jnp.where(lane == FRAME_LANE, f_ref[...].astype(F32), 0.0)
    for head in range(HEADS):
        cols = slice(head * HDIM, (head + 1) * HDIM)
        product = held[2, :, cols].astype(F32) * held[1, :, cols].astype(F32)
        dot = jnp.sum(product, axis=1, keepdims=True)
        high = dot.astype(BF16).astype(F32)
        meta = jnp.where(lane == head, high, meta)
        meta = jnp.where(lane == LOW_LANE + head, dot - high, meta)
    meta = meta.astype(BF16)
    for group in range(XN):
        here = slice(group * wide, (group + 1) * wide)
        out[group, :, :wide] = held[0, :, here]
        out[group, :, wide : wide + HDIM] = meta
        out[group, :, wide + HDIM :] = held[2, :, here]


def pack_queries(query, saved_out, grad_out, frames):
    tok, width = query.shape
    vmem = pl.BlockSpec(memory_space=pltpu.VMEM)
    shape = (XN, tok, 2 * GROUP * HDIM + HDIM)
    return pl.pallas_call(
        pack_queries_kernel,
        out_shape=jax.ShapeDtypeStruct(shape, BF16),
        in_specs=[pl.BlockSpec(memory_space=pl.ANY)] * 3 + [vmem],
        out_specs=vmem,
        scratch_shapes=[pltpu.VMEM((3, tok, width), BF16), pltpu.SemaphoreType.DMA((3,))],
        compiler_params=params(60),
        cost_estimate=cost(2 * tok * width, 14 * tok * width),
        name="pack_queries",
    )(query, saved_out, grad_out, frames)


def pack_keys_kernel(k_ref, v_ref, k2_ref, v2_ref, out):
    for head in range(HEADS):
        group, h = divmod(head, GROUP)
        cols = slice(head * HDIM, (head + 1) * HDIM)
        for at, ref in enumerate((k_ref, v_ref, k2_ref, v2_ref)):
            first = (2 * (at // 2 * GROUP + h) + at % 2) * HDIM
            out[group, :, first : first + HDIM] = ref[:, cols]


def pack_keys(key, value, far_key, far_value):
    tok, width = key.shape
    vmem = pl.BlockSpec(memory_space=pltpu.VMEM)
    return pl.pallas_call(
        pack_keys_kernel,
        out_shape=jax.ShapeDtypeStruct((XN, tok, 4 * GROUP * HDIM), BF16),
        in_specs=[vmem] * 4,
        out_specs=vmem,
        compiler_params=params(),
        cost_estimate=cost(0, 16 * tok * width),
        name="pack_keys",
    )(key, value, far_key, far_value)


def window_scores(queries, keys):
    return lax.dot_general(keys, queries, NT, preferred_element_type=F32) * SCALE2


def both(own, far):
    return jnp.concatenate([own[...], far[...]], axis=0)


def turn_meta(rows, m_own, m_far):
    @pl.when(pl.program_id(0) == 0)
    def _():
        rows[...] = both(m_own, m_far).astype(F32).T


def seen(rows, m_own):
    k_frame = m_own[...].astype(F32)[:, FRAME_LANE : FRAME_LANE + 1]
    return k_frame <= rows[FRAME_LANE : FRAME_LANE + 1, :]


def stats_kernel(bias_ref, q_own, q_far, m_own, m_far, w0, w1, w2, w3, out_ref, rows):
    head = pl.program_id(0)
    turn_meta(rows, m_own, m_far)
    queries = both(q_own, q_far)

    scores, peaks = [], []
    for at, ref in enumerate((w0, w1, w2, w3)):
        part = window_scores(queries, ref[...])
        if at == 0:
            part = jnp.where(seen(rows, m_own), part, NEG)
        scores.append(part)
        peaks.append(jnp.max(part, axis=0, keepdims=True) + bias_ref[at])
    peak = functools.reduce(jnp.maximum, peaks)
    total = jnp.zeros_like(peak)
    for at, part in enumerate(scores):
        total += jnp.sum(jnp.exp2(part - (peak - bias_ref[at])), axis=0, keepdims=True)

    @pl.when(head == 0)
    def _():
        out_ref[...] = jnp.zeros_like(out_ref)

    out_ref[pl.ds(head, 1), :] = peak
    out_ref[pl.ds(8 + head, 1), :] = total


def head_block(half):
    return pl.BlockSpec((half, HDIM), lambda h: (0, h))


def meta_block(half):
    return pl.BlockSpec((half, HDIM), lambda h: (0, GROUP))


def key_block(half, first=0):
    return pl.BlockSpec((half, HDIM), lambda h: (0, 2 * (first + h)))


def pair_block(half, first=0):
    return pl.BlockSpec((half, 2 * HDIM), lambda h: (0, first + h))


def turned_block(half):
    return pl.BlockSpec((HDIM, 2 * half), lambda h: (h, 0))


def whole(shape):
    return pl.BlockSpec(shape, lambda h: (0, 0))


def smem():
    return pl.BlockSpec(memory_space=pltpu.SMEM)


def meta_rows(half):
    return [pltpu.VMEM((HDIM, 2 * half), F32)]


def stats(bias, q_own, q_far, near, w2, w3):
    half = q_own.shape[0]
    pairs = GROUP * 2 * half * 4 * half
    return pl.pallas_call(
        stats_kernel,
        grid=(GROUP,),
        out_shape=jax.ShapeDtypeStruct((16, 2 * half), F32),
        in_specs=[smem(), head_block(half), head_block(half), meta_block(half), meta_block(half)]
        + [key_block(half), key_block(half, GROUP), key_block(half), key_block(half)],
        out_specs=whole((16, 2 * half)),
        scratch_shapes=meta_rows(half),
        compiler_params=params(),
        cost_estimate=cost(4 * pairs * HDIM, 6 * half * GROUP * HDIM * 2, pairs),
        name="stats",
    )(bias, q_own, q_far, q_own, q_far, near, near, w2, w3)


def log_total(head, half, own_stats, far_stats):
    own_peak = own_stats[pl.ds(head, 1), :]
    own_sum = own_stats[pl.ds(8 + head, 1), :]
    far_peak = far_stats[pl.ds(head, 1), :]
    far_sum = far_stats[pl.ds(8 + head, 1), :]
    far_peak = jnp.concatenate([far_peak[:, half:], far_peak[:, :half]], axis=1)
    far_sum = jnp.concatenate([far_sum[:, half:], far_sum[:, :half]], axis=1)
    peak = jnp.maximum(own_peak, far_peak)
    own_part = own_sum * jnp.exp2(own_peak - peak)
    return peak + jnp.log2(own_part + far_sum * jnp.exp2(far_peak - peak))


def block_grads(scores, total, dot, queries, grads, keys, values):
    probs = jnp.exp2(scores - total)
    dv = lax.dot_general(probs.astype(BF16), grads, NN, preferred_element_type=F32)
    dp = lax.dot_general(values, grads, NT, preferred_element_type=F32)
    ds = (probs * (dp - dot)).astype(BF16)
    dk = lax.dot_general(ds, queries, NN, preferred_element_type=F32) * FACTOR
    dq = lax.dot_general(keys.T, ds, NN, preferred_element_type=F32)
    return dq, dk, dv


def grads_kernel(
    roles, bias_ref, place, own_stats, far_stats, q_own, q_far, g_own, g_far, m_own, m_far, *rest
):
    *rest, rows = rest
    blocks, rest = rest[: len(roles)], rest[len(roles) :]
    head = pl.program_id(0)
    half = q_own.shape[0]
    turn_meta(rows, m_own, m_far)
    queries, grads = both(q_own, q_far), both(g_own, g_far)
    first = place[0] * GROUP + head
    dot = rows[pl.ds(first, 1), :] + rows[pl.ds(LOW_LANE + first, 1), :]
    total = log_total(head, half, own_stats, far_stats)
    if 0 in roles:
        dq_part, dq_own, dq_far, *outs = rest
        dq_sum = dq_part[...]
    else:
        dq_part, *outs = rest
        dq_sum = jnp.zeros(dq_part.shape, F32)
    for role, ref, out in zip(roles, blocks, outs):
        keys, values = ref[:, :HDIM], ref[:, HDIM:]
        scores = window_scores(queries, keys)
        if role == 0:
            scores = jnp.where(seen(rows, m_own), scores, NEG)
        bound = total - bias_ref[role]
        dq, dk, dv = block_grads(scores, bound, dot, queries, grads, keys, values)
        dq_sum += dq
        out[:, :HDIM] = dk.astype(out.dtype)
        out[:, HDIM:] = dv.astype(out.dtype)
    if 0 in roles:
        turned = (dq_sum * FACTOR).T
        dq_own[...] = turned[:half]
        dq_far[...] = turned[half:].astype(BF16)
    else:
        dq_part[...] = dq_sum


def grads(bias, place, own_stats, far_stats, q, g, roles, blocks, dq_part=None):
    half = q[0].shape[0]
    wide = GROUP * HDIM
    head, meta = head_block(half), meta_block(half)
    stat = whole((16, 2 * half))
    pairs = GROUP * 2 * half * len(roles) * half
    specs = [pair_block(half, GROUP if role == 1 else 0) for role in roles]
    turned = jax.ShapeDtypeStruct((wide, 2 * half), F32)
    outs = [
        jax.ShapeDtypeStruct((half, 2 * wide), F32 if role == 0 else BF16) for role in roles
    ]
    if 0 in roles:
        extra, extra_specs = [dq_part], [turned_block(half)]
        dq_outs = [
            jax.ShapeDtypeStruct((half, wide), F32),
            jax.ShapeDtypeStruct((half, wide), BF16),
        ]
        dq_specs = [head, head]
    else:
        extra, extra_specs = [], []
        dq_outs, dq_specs = [turned], [turned_block(half)]
    return pl.pallas_call(
        functools.partial(grads_kernel, roles),
        grid=(GROUP,),
        out_shape=dq_outs + outs,
        in_specs=[smem(), smem(), stat, stat, head, head, head, head, meta, meta]
        + specs
        + extra_specs,
        out_specs=dq_specs + [pair_block(half)] * len(roles),
        scratch_shapes=meta_rows(half),
        compiler_params=params(),
        cost_estimate=cost(10 * pairs * HDIM, 18 * half * wide * 2, pairs),
        name="grads" + "".join(str(role) for role in roles),
    )(bias, place, own_stats, far_stats, *q, *g, *q, *blocks, *extra)


def fold_kernel(even_ref, d1, swapped, side, out):
    odd = 1.0 - even_ref[0].astype(F32)
    total = d1[...].astype(F32) + swapped[...].astype(F32) + side[...].astype(F32) * odd
    out[...] = total.astype(BF16)


def fold(even, d1, swapped, side):
    vmem = pl.BlockSpec(memory_space=pltpu.VMEM)
    return pl.pallas_call(
        fold_kernel,
        out_shape=jax.ShapeDtypeStruct(d1.shape, BF16),
        in_specs=[smem()] + [vmem] * 3,
        out_specs=vmem,
        compiler_params=params(),
        cost_estimate=cost(3 * d1.size, 8 * d1.size),
        name="fold",
    )(even, d1, swapped, side)


def close_kernel(even_ref, dq_own, dq_far, d0, back, side, out):
    even = even_ref[0].astype(F32)
    tok = out.shape[1]
    wide = dq_own.shape[1]
    for step in range(XN):
        rows = slice(step * tok, (step + 1) * tok)
        grad_q = dq_own[rows, :] + dq_far[rows, :].astype(F32)
        pair = d0[rows, :] + back[rows, :].astype(F32) + side[rows, :].astype(F32) * even
        out[step, :, :wide] = grad_q.astype(BF16)
        out[step, :, wide:] = pair.astype(BF16)


def close(even, dq_own, dq_far, d0, back, side):
    half, wide = dq_own.shape
    tok = half // XN
    vmem = pl.BlockSpec(memory_space=pltpu.VMEM)
    return pl.pallas_call(
        close_kernel,
        out_shape=jax.ShapeDtypeStruct((XN, tok, 3 * wide), BF16),
        in_specs=[smem()] + [vmem] * 5,
        out_specs=vmem,
        compiler_params=params(),
        cost_estimate=cost(5 * half * wide, 28 * half * wide),
        name="close",
    )(even, dq_own, dq_far, d0, back, side)


def unpack_kernel(parts, dq, dk, dv):
    wide = GROUP * HDIM
    for group in range(XN):
        dq[:, group * wide : (group + 1) * wide] = parts[group, :, :wide]
        for h in range(GROUP):
            at = wide + 2 * h * HDIM
            cols = slice((group * GROUP + h) * HDIM, (group * GROUP + h + 1) * HDIM)
            dk[:, cols] = parts[group, :, at : at + HDIM]
            dv[:, cols] = parts[group, :, at + HDIM : at + 2 * HDIM]


def unpack(parts):
    tok = parts.shape[1]
    vmem = pl.BlockSpec(memory_space=pltpu.VMEM)
    return pl.pallas_call(
        unpack_kernel,
        out_shape=[jax.ShapeDtypeStruct((tok, HEADS * HDIM), BF16)] * 3,
        in_specs=[vmem],
        out_specs=[vmem] * 3,
        compiler_params=params(),
        cost_estimate=cost(0, 12 * tok * HEADS * HDIM),
        name="unpack",
    )(parts)


def over_x(value):
    groups = [[z * XN + x for x in range(XN)] for z in range(lax.axis_size("col") // XN)]
    return lax.all_to_all(value, "col", 0, 0, axis_index_groups=groups)


def across_z(value):
    count = lax.axis_size("col")
    return lax.ppermute(value, "col", [(c, (c + XN) % count) for c in range(count)])


def along_row(value, steps):
    count = lax.axis_size("row")
    first, last = max(0, -steps), min(count, count - steps)
    return lax.ppermute(value, "row", [(r, r + steps) for r in range(first, last)])


def in_chip(value):
    count = lax.axis_size("row")
    return lax.ppermute(value, "row", [(r, r ^ 1) for r in range(count)])


def per_device(query, key, value, saved_out, grad_out, frame_ids):
    row, col = lax.axis_index("row"), lax.axis_index("col")
    place = (col % XN).astype(jnp.int32).reshape(1)
    is_even = row % 2 == 0
    even = is_even.astype(jnp.int32).reshape(1)
    half = query.shape[0] * XN
    wide = GROUP * HDIM

    far_key, far_value = along_row(key, 2), along_row(value, 2)
    qg = over_x(pack_queries(query, saved_out, grad_out, frame_ids[:, None]))
    q_own = qg[:, :, : wide + HDIM].reshape(half, wide + HDIM)
    g_own = qg[:, :, wide + HDIM :].reshape(half, wide)
    q_far = across_z(q_own)
    near = over_x(pack_keys(key, value, far_key, far_value)).reshape(half, -1)
    near, q_far, g_own = lax.optimization_barrier((near, q_far, g_own))
    w0, w1 = near[:, : 2 * wide], near[:, 2 * wide :]
    w3 = along_row(jnp.where(is_even, w0, w1), 1)
    w2 = in_chip(w1)
    g_far = across_z(g_own)
    held = jnp.stack(
        [
            row >= 0,
            row >= 2,
            jnp.where(is_even, row >= 1, row >= 3),
            jnp.where(is_even, row >= 3, row >= 1),
        ]
    )
    bias = jnp.where(held, 0.0, NEG).astype(F32)

    own_stats = stats(bias, q_own, q_far, near, w2, w3)
    far_stats = across_z(own_stats)
    common = (bias, place, own_stats, far_stats, (q_own, q_far), (g_own, g_far))
    dq_part, d2, d3 = grads(*common, (2, 3), (w2, w3))
    dq_own, dq_far, d0, d1 = grads(*common, (0, 1), (near, near), dq_part)

    side = along_row(d3, -1)
    back = along_row(fold(even, d1, in_chip(d2), side), -2)
    dq_far = across_z(dq_far)
    return tuple(unpack(over_x(close(even, dq_own, dq_far, d0, back, side))))


def solution(mesh):
    placed = P(("row", "col"), None)
    return jax.shard_map(
        per_device,
        mesh=mesh,
        in_specs=(placed,) * 5 + (P(("row", "col")),),
        out_specs=(placed,) * 3,
        check_vma=False,
    )
```

time: 180 us -> 174 us (0.967)
  the two profiles are of different devices: /device:TPU:248 before, /device:TPU:120 now
where the time goes in v5:
time: 174 us; the launch traced here: 173 us
  waiting for transfers between devices  60.5 us (35%)
  starting transfers between devices  60.2 us (35%)
  Pallas kernels  27.9 us (16%)
  blocking collectives  18.8 us (11%)
  local copies, waits for them, and re-layouts  3.81 us (2%)
    ppermute x4, waiting for transfers between devices, across_z(): lax.ppermute(value, 'col', [(c, (c + XN) % count) for c in range(count)])  48.5 us
    ppermute x4, starting transfers between devices, across_z(): lax.ppermute(value, 'col', [(c, (c + XN) % count) for c in range(count)])  31.8 us
    all_to_all x1, blocking collectives, over_x(): return lax.all_to_all(value, 'col', 0, 0, axis_index_groups=groups)  18.8 us
    ppermute x5, starting transfers between devices, along_row(): lax.ppermute(value, 'row', [(r, r + steps) for r in range(first, last)])  15.8 us
    pallas_call x2, Pallas kernels, grads(): pl.pallas_call(functools.partial(grads_kernel, roles), grid=(GROUP,), out...  15.1 us
    ppermute x5, waiting for transfers between devices, along_row(): lax.ppermute(value, 'row', [(r, r + steps) for r in range(first, last)])  12 us
    all_to_all x2, starting transfers between devices, over_x(): return lax.all_to_all(value, 'col', 0, 0, axis_index_groups=groups)  8.82 us
    pallas_call x1, Pallas kernels, stats(): pl.pallas_call(stats_kernel, grid=(GROUP,), out_shape=jax.ShapeDtypeStruc...  5.52 us
  transfers between devices with their start and end apart: 13, of which 7 were waited for; matrix products, arithmetic and copies ran while one was open for 0% of the time, Pallas kernels for 8%

profile of v5, /device:TPU:120, one launch (start us, length us, event | category | flops | bytes accessed | tf_op | source)
XLA Modules:
  0.0 173.3 jit_solution(7573991106512597622)
XLA Ops:
  0.6 1.4 copy.9.f_ref
  2.0 0.0 copy-start.2
  2.0 0.0 copy-start.3
  2.0 3.2 %pack_queries.1 = bf16[4,64,1408]{2,1,0:T(8,128)(2,1)} custom-call(bf16[64,2560]{1,0:T(8,128)(2,1)} %q_any.1, bf16[64,2560]{1,0:T(8,128)(2,1)} %o_any.1, bf16[64,2560]{1,0:T(8,128)(2,1)} %g_any.1, s32[64,1]{1,0:T(8,128)} %copy.9.f_ref), custom_call_target="tpu_custom_call" | custom-call | flops 327680 | bytes 2293760 | tf_op jit(solution)/shard_map/pack_queries/pallas_call | solution.py:69
  5.2 4.3 %all-to-all-start = ((bf16[4,64,1408]{2,1,0:T(8,128)(2,1)}), bf16[4,64,1408]{2,1,0:T(8,128)(2,1)S(1)}, u32[]{:S(2)}, u32[]{:S(2)}) async-start(bf16[4,64,1408]{2,1,0:T(8,128)(2,1)} %pack_queries.1), calls=%async_computation | async-start | bytes 1441792 | tf_op jit(solution)/shard_map/all_to_all | solution.py:364
  9.5 0.0 copy-done.2
  9.5 3.5 %collective-permute-start = (bf16[64,2560]{1,0:T(8,128)(2,1)S(1)}, bf16[64,2560]{1,0:T(8,128)(2,1)S(1)}, u32[]{:S(2)}, u32[]{:S(2)}) collective-permute-start(bf16[64,2560]{1,0:T(8,128)(2,1)S(1)} %copy-done.2), channel_id=1, source_target_pairs={{0,16},{8,24},{16,32},{24,40},{32,48},{40,56},{48,64},{56,72},{64,... | collective-permute-start | bytes 983048 | tf_op jit(solution)/shard_map/ppermute | solution.py:375
  13.0 0.0 copy-done.3
  13.0 3.5 %collective-permute-start.1 = (bf16[64,2560]{1,0:T(8,128)(2,1)S(1)}, bf16[64,2560]{1,0:T(8,128)(2,1)S(1)}, u32[]{:S(2)}, u32[]{:S(2)}) collective-permute-start(bf16[64,2560]{1,0:T(8,128)(2,1)S(1)} %copy-done.3), channel_id=1, source_target_pairs={{0,16},{8,24},{16,32},{24,40},{32,48},{40,56},{48,64},{56,72},{64,... | collective-permute-start | bytes 983048 | tf_op jit(solution)/shard_map/ppermute | solution.py:375
  16.5 5.5 %collective-permute-done.k2_ref = bf16[64,2560]{1,0:T(8,128)(2,1)S(1)} collective-permute-done((bf16[64,2560]{1,0:T(8,128)(2,1)S(1)}, bf16[64,2560]{1,0:T(8,128)(2,1)S(1)}, u32[]{:S(2)}, u32[]{:S(2)}) %collective-permute-start) | collective-permute-done | bytes 327712 | tf_op jit(solution)/shard_map/ppermute | solution.py:375
  22.0 5.6 %collective-permute-done.1.v2_ref = bf16[64,2560]{1,0:T(8,128)(2,1)S(1)} collective-permute-done((bf16[64,2560]{1,0:T(8,128)(2,1)S(1)}, bf16[64,2560]{1,0:T(8,128)(2,1)S(1)}, u32[]{:S(2)}, u32[]{:S(2)}) %collective-permute-start.1) | collective-permute-done | bytes 327712 | tf_op jit(solution)/shard_map/ppermute | solution.py:375
  27.6 1.3 pack_keys.1
  28.9 0.0 all-to-all-done
  28.9 4.5 %all-to-all-start.1 = ((bf16[4,64,2560]{2,1,0:T(8,128)(2,1)}), bf16[4,64,2560]{2,1,0:T(8,128)(2,1)S(1)}, u32[]{:S(2)}, u32[]{:S(2)}) async-start(bf16[4,64,2560]{2,1,0:T(8,128)(2,1)} %pack_keys.1), calls=%async_computation.1 | async-start | bytes 2621440 | tf_op jit(solution)/shard_map/all_to_all | solution.py:364
  33.4 10.0 %collective-permute-start.2 = (bf16[256,768]{1,0:T(8,128)(2,1)S(1)}, bf16[256,768]{1,0:T(8,128)(2,1)S(1)}, u32[]{:S(2)}, u32[]{:S(2)}) collective-permute-start(bf16[256,768]{1,0:T(8,128)(2,1)S(1)} %bitcast.15), channel_id=1, source_target_pairs={{0,4},{1,5},{2,6},{3,7},{4,0},{5,1},{6,2},{7,3},{8,12},{9,13},{10,... | collective-permute-start | bytes 1179656 | tf_op jit(solution)/shard_map/ppermute | solution.py:369
  43.5 16.0 %collective-permute-done.2.q_far.m_far = bf16[256,768]{1,0:T(8,128)(2,1)S(1)} collective-permute-done((bf16[256,768]{1,0:T(8,128)(2,1)S(1)}, bf16[256,768]{1,0:T(8,128)(2,1)S(1)}, u32[]{:S(2)}, u32[]{:S(2)}) %collective-permute-start.2) | collective-permute-done | bytes 393248 | tf_op jit(solution)/shard_map/ppermute | solution.py:369
  59.5 0.0 all-to-all-done.1
  59.5 1.2 slice_select_fusion
  60.6 1.9 %collective-permute-start.4 = (bf16[256,1280]{1,0:T(8,128)(2,1)}, bf16[256,1280]{1,0:T(8,128)(2,1)S(1)}, u32[]{:S(2)}, u32[]{:S(2)}) collective-permute-start(bf16[256,1280]{1,0:T(8,128)(2,1)} %get-tuple-element.23), channel_id=1, source_target_pairs={{0,8},{8,16},{16,24},{24,32},{32,40},{40,48},{48,56},{56,64},{64,7... | collective-permute-start | bytes 1966088 | tf_op jit(solution)/shard_map/ppermute | solution.py:375
  62.6 1.9 %collective-permute-start.3 = (bf16[256,1280]{1,0:T(8,128)(2,1)}, bf16[256,1280]{1,0:T(8,128)(2,1)}, u32[]{:S(2)}, u32[]{:S(2)}) collective-permute-start(bf16[256,1280]{1,0:T(8,128)(2,1)} %get-tuple-element.24), channel_id=1, source_target_pairs={{0,8},{8,0},{16,24},{24,16},{32,40},{40,32},{48,56},{56,48},{64,72... | collective-permute-start | bytes 1966088 | tf_op jit(solution)/shard_map/ppermute | solution.py:380
  64.5 7.2 %collective-permute-start.6 = (bf16[256,640]{1,0:T(8,128)(2,1)S(1)}, bf16[256,640]{1,0:T(8,128)(2,1)S(1)}, u32[]{:S(2)}, u32[]{:S(2)}) collective-permute-start(bf16[256,640]{1,0:T(8,128)(2,1)S(1)} %bitcast.22), channel_id=1, source_target_pairs={{0,4},{1,5},{2,6},{3,7},{4,0},{5,1},{6,2},{7,3},{8,12},{9,13},{10,... | collective-permute-start | bytes 983048 | tf_op jit(solution)/shard_map/ppermute | solution.py:369
  71.8 0.1 add_select_fusion.bias_ref
  71.8 0.9 collective-permute-done.4.w3.rest_1_
  72.7 0.0 collective-permute-done.3.w2.rest_0_
  72.8 5.5 %stats.1.own_stats = f32[16,512]{1,0:T(8,128)S(1)} custom-call(f32[4]{0:T(128)S(1)} %add_select_fusion.bias_ref, bf16[256,768]{1,0:T(8,128)(2,1)S(1)} %bitcast.16, bf16[256,768]{1,0:T(8,128)(2,1)S(1)} %collective-permute-done.2.q_far.m_far, bf16[256,768]{1,0:T(8,128)(2,1)S(1)} %bitcast.17, bf16[256,768]{1,0:T(8,128)(2,1)S(1)} %collective-permute-done.2.q_far.m_far, ...), custom_call_target="tpu_custom_call" | custom-call | flops 1342177280 | bytes 1966080 | tf_op jit(solution)/shard_map/stats/pallas_call | solution.py:183
  78.3 7.2 %collective-permute-start.5 = (f32[16,512]{1,0:T(8,128)S(1)}, f32[16,512]{1,0:T(8,128)S(1)}, u32[]{:S(2)}, u32[]{:S(2)}) collective-permute-start(f32[16,512]{1,0:T(8,128)S(1)} %stats.1.own_stats), channel_id=1, source_target_pairs={{0,4},{1,5},{2,6},{3,7},{4,0},{5,1},{6,2},{7,3},{8,12},{9,13},{10,... | collective-permute-start | bytes 98312 | tf_op jit(solution)/shard_map/ppermute | solution.py:369
  85.5 1.8 %collective-permute-done.6.g_far = bf16[256,640]{1,0:T(8,128)(2,1)S(1)} collective-permute-done((bf16[256,640]{1,0:T(8,128)(2,1)S(1)}, bf16[256,640]{1,0:T(8,128)(2,1)S(1)}, u32[]{:S(2)}, u32[]{:S(2)}) %collective-permute-start.6) | collective-permute-done | bytes 327712 | tf_op jit(solution)/shard_map/ppermute | solution.py:369
  87.4 0.7 collective-permute-done.5.far_stats
  88.0 7.6 %grads23.1 = (f32[640,512]{1,0:T(8,128)S(1)}, bf16[256,1280]{1,0:T(8,128)(2,1)}, bf16[256,1280]{1,0:T(8,128)(2,1)}) custom-call(f32[4]{0:T(128)S(1)} %add_select_fusion.bias_ref, s32[1]{0:T(128)} %bitcast.5.place, f32[16,512]{1,0:T(8,128)S(1)} %stats.1.own_stats, f32[16,512]{1,0:T(8,128)S(1)} %collective-permute-done.5.far_stats, ...), custom_call_target="tpu_custom_call" | custom-call | flops 1677721600 | bytes 5898240 | tf_op jit(solution)/shard_map/grads23/pallas_call | solution.py:276
  95.6 0.0 copy-start
  95.6 1.1 copy-done
  96.7 1.9 %collective-permute-start.8 = (bf16[256,1280]{1,0:T(8,128)(2,1)}, bf16[256,1280]{1,0:T(8,128)(2,1)}, u32[]{:S(2)}, u32[]{:S(2)}) collective-permute-start(bf16[256,1280]{1,0:T(8,128)(2,1)} %get-tuple-element.21), channel_id=1, source_target_pairs={{0,8},{8,0},{16,24},{24,16},{32,40},{40,32},{48,56},{56,48},{64,72... | collective-permute-start | bytes 1966088 | tf_op jit(solution)/shard_map/ppermute | solution.py:380
  98.6 3.6 %collective-permute-start.9 = (bf16[256,1280]{1,0:T(8,128)(2,1)}, bf16[256,1280]{1,0:T(8,128)(2,1)S(1)}, u32[]{:S(2)}, u32[]{:S(2)}) collective-permute-start(bf16[256,1280]{1,0:T(8,128)(2,1)} %get-tuple-element.22), channel_id=1, source_target_pairs={{8,0},{16,8},{24,16},{32,24},{40,32},{48,40},{56,48},{64,56},{72,6... | collective-permute-start | bytes 1966088 | tf_op jit(solution)/shard_map/ppermute | solution.py:375
  102.2 0.0 copy-start.1
  102.2 1.3 copy-done.1
  103.6 7.6 %grads01.1 = (f32[256,640]{1,0:T(8,128)S(1)}, bf16[256,640]{1,0:T(8,128)(2,1)S(1)}, f32[256,1280]{1,0:T(8,128)S(1)}, bf16[256,1280]{1,0:T(8,128)(2,1)S(1)}) custom-call(f32[4]{0:T(128)S(1)} %add_select_fusion.bias_ref, s32[1]{0:T(128)} %bitcast.5.place, f32[16,512]{1,0:T(8,128)S(1)} %stats.1.own_stats, f32[16,512]{1,0:T(8,128)S(1)} %collective-permute-done.5.far_stats, ...), custom_call_target="tpu_custom_call" | custom-call | flops 1677721600 | bytes 5898240 | tf_op jit(solution)/shard_map/grads01/pallas_call | solution.py:276
  111.1 0.0 collective-permute-done.8.swapped
  111.1 0.0 collective-permute-done.9.side
  111.1 1.4 fold.1
  112.5 3.3 %collective-permute-start.10 = (bf16[256,1280]{1,0:T(8,128)(2,1)S(1)}, bf16[256,1280]{1,0:T(8,128)(2,1)S(1)}, u32[]{:S(2)}, u32[]{:S(2)}) collective-permute-start(bf16[256,1280]{1,0:T(8,128)(2,1)S(1)} %fold.1), channel_id=1, source_target_pairs={{16,0},{24,8},{32,16},{40,24},{48,32},{56,40},{64,48},{72,56},{80,... | collective-permute-start | bytes 1966088 | tf_op jit(solution)/shard_map/ppermute | solution.py:375
  115.8 7.3 %collective-permute-start.7 = (bf16[256,640]{1,0:T(8,128)(2,1)S(1)}, bf16[256,640]{1,0:T(8,128)(2,1)S(1)}, u32[]{:S(2)}, u32[]{:S(2)}) collective-permute-start(bf16[256,640]{1,0:T(8,128)(2,1)S(1)} %get-tuple-element.18), channel_id=1, source_target_pairs={{0,4},{1,5},{2,6},{3,7},{4,0},{5,1},{6,2},{7,3},{8,12},{9,13},{10,... | collective-permute-start | bytes 983048 | tf_op jit(solution)/shard_map/ppermute | solution.py:369
  123.1 30.0 %collective-permute-done.7.dq_far = bf16[256,640]{1,0:T(8,128)(2,1)S(1)} collective-permute-done((bf16[256,640]{1,0:T(8,128)(2,1)S(1)}, bf16[256,640]{1,0:T(8,128)(2,1)S(1)}, u32[]{:S(2)}, u32[]{:S(2)}) %collective-permute-start.7) | collective-permute-done | bytes 327712 | tf_op jit(solution)/shard_map/ppermute | solution.py:369
  153.1 0.0 collective-permute-done.10.back
  153.1 0.3 close.1
  153.4 18.8 %all_to_all.15.parts = bf16[4,64,1920]{2,1,0:T(8,128)(2,1)S(1)} all-to-all(bf16[4,64,1920]{2,1,0:T(8,128)(2,1)S(1)} %close.1), channel_id=1, replica_groups={{0,1,2,3},{4,5,6,7},{8,9,10,11},{12,13,14,15},{16,17,18,19},{20,21,22,2..., dimensions={0} | all-to-all | bytes 1966080 | tf_op jit(solution)/shard_map/all_to_all | solution.py:364
  172.2 1.1 unpack.1
  (2 shorter events, 0.1 us)
Async XLA Ops:
  2.0 7.5 %copy-start.2 = (bf16[64,2560]{1,0:T(8,128)(2,1)S(1)}, bf16[64,2560]{1,0:T(8,128)(2,1)}, u32[]{:S(2)}) copy-start(bf16[64,2560]{1,0:T(8,128)(2,1)} %k_ref.1) | copy-start | bytes 983044
  2.0 11.0 %copy-start.3 = (bf16[64,2560]{1,0:T(8,128)(2,1)S(1)}, bf16[64,2560]{1,0:T(8,128)(2,1)}, u32[]{:S(2)}) copy-start(bf16[64,2560]{1,0:T(8,128)(2,1)} %v_ref.1) | copy-start | bytes 983044
  5.2 23.7 %all-to-all-start = ((bf16[4,64,1408]{2,1,0:T(8,128)(2,1)}), bf16[4,64,1408]{2,1,0:T(8,128)(2,1)S(1)}, u32[]{:S(2)}, u32[]{:S(2)}) async-start(bf16[4,64,1408]{2,1,0:T(8,128)(2,1)} %pack_queries.1), calls=%async_computation | async-start | bytes 1441792 | tf_op jit(solution)/shard_map/all_to_all | solution.py:364
  9.5 12.5 %collective-permute-start = (bf16[64,2560]{1,0:T(8,128)(2,1)S(1)}, bf16[64,2560]{1,0:T(8,128)(2,1)S(1)}, u32[]{:S(2)}, u32[]{:S(2)}) collective-permute-start(bf16[64,2560]{1,0:T(8,128)(2,1)S(1)} %copy-done.2), channel_id=1, source_target_pairs={{0,16},{8,24},{16,32},{24,40},{32,48},{40,56},{48,64},{56,72},{64,... | collective-permute-start | bytes 983048 | tf_op jit(solution)/shard_map/ppermute | solution.py:375
  13.0 14.6 %collective-permute-start.1 = (bf16[64,2560]{1,0:T(8,128)(2,1)S(1)}, bf16[64,2560]{1,0:T(8,128)(2,1)S(1)}, u32[]{:S(2)}, u32[]{:S(2)}) collective-permute-start(bf16[64,2560]{1,0:T(8,128)(2,1)S(1)} %copy-done.3), channel_id=1, source_target_pairs={{0,16},{8,24},{16,32},{24,40},{32,48},{40,56},{48,64},{56,72},{64,... | collective-permute-start | bytes 983048 | tf_op jit(solution)/shard_map/ppermute | solution.py:375
  28.9 30.6 %all-to-all-start.1 = ((bf16[4,64,2560]{2,1,0:T(8,128)(2,1)}), bf16[4,64,2560]{2,1,0:T(8,128)(2,1)S(1)}, u32[]{:S(2)}, u32[]{:S(2)}) async-start(bf16[4,64,2560]{2,1,0:T(8,128)(2,1)} %pack_keys.1), calls=%async_computation.1 | async-start | bytes 2621440 | tf_op jit(solution)/shard_map/all_to_all | solution.py:364
  33.4 26.1 %collective-permute-start.2 = (bf16[256,768]{1,0:T(8,128)(2,1)S(1)}, bf16[256,768]{1,0:T(8,128)(2,1)S(1)}, u32[]{:S(2)}, u32[]{:S(2)}) collective-permute-start(bf16[256,768]{1,0:T(8,128)(2,1)S(1)} %bitcast.15), channel_id=1, source_target_pairs={{0,4},{1,5},{2,6},{3,7},{4,0},{5,1},{6,2},{7,3},{8,12},{9,13},{10,... | collective-permute-start | bytes 1179656 | tf_op jit(solution)/shard_map/ppermute | solution.py:369
  60.6 12.1 %collective-permute-start.4 = (bf16[256,1280]{1,0:T(8,128)(2,1)}, bf16[256,1280]{1,0:T(8,128)(2,1)S(1)}, u32[]{:S(2)}, u32[]{:S(2)}) collective-permute-start(bf16[256,1280]{1,0:T(8,128)(2,1)} %get-tuple-element.23), channel_id=1, source_target_pairs={{0,8},{8,16},{16,24},{24,32},{32,40},{40,48},{48,56},{56,64},{64,7... | collective-permute-start | bytes 1966088 | tf_op jit(solution)/shard_map/ppermute | solution.py:375
  62.6 10.2 %collective-permute-start.3 = (bf16[256,1280]{1,0:T(8,128)(2,1)}, bf16[256,1280]{1,0:T(8,128)(2,1)}, u32[]{:S(2)}, u32[]{:S(2)}) collective-permute-start(bf16[256,1280]{1,0:T(8,128)(2,1)} %get-tuple-element.24), channel_id=1, source_target_pairs={{0,8},{8,0},{16,24},{24,16},{32,40},{40,32},{48,56},{56,48},{64,72... | collective-permute-start | bytes 1966088 | tf_op jit(solution)/shard_map/ppermute | solution.py:380
  64.5 22.9 %collective-permute-start.6 = (bf16[256,640]{1,0:T(8,128)(2,1)S(1)}, bf16[256,640]{1,0:T(8,128)(2,1)S(1)}, u32[]{:S(2)}, u32[]{:S(2)}) collective-permute-start(bf16[256,640]{1,0:T(8,128)(2,1)S(1)} %bitcast.22), channel_id=1, source_target_pairs={{0,4},{1,5},{2,6},{3,7},{4,0},{5,1},{6,2},{7,3},{8,12},{9,13},{10,... | collective-permute-start | bytes 983048 | tf_op jit(solution)/shard_map/ppermute | solution.py:369
  78.3 9.7 %collective-permute-start.5 = (f32[16,512]{1,0:T(8,128)S(1)}, f32[16,512]{1,0:T(8,128)S(1)}, u32[]{:S(2)}, u32[]{:S(2)}) collective-permute-start(f32[16,512]{1,0:T(8,128)S(1)} %stats.1.own_stats), channel_id=1, source_target_pairs={{0,4},{1,5},{2,6},{3,7},{4,0},{5,1},{6,2},{7,3},{8,12},{9,13},{10,... | collective-permute-start | bytes 98312 | tf_op jit(solution)/shard_map/ppermute | solution.py:369
  95.6 1.1 copy-start
  96.7 14.4 %collective-permute-start.8 = (bf16[256,1280]{1,0:T(8,128)(2,1)}, bf16[256,1280]{1,0:T(8,128)(2,1)}, u32[]{:S(2)}, u32[]{:S(2)}) collective-permute-start(bf16[256,1280]{1,0:T(8,128)(2,1)} %get-tuple-element.21), channel_id=1, source_target_pairs={{0,8},{8,0},{16,24},{24,16},{32,40},{40,32},{48,56},{56,48},{64,72... | collective-permute-start | bytes 1966088 | tf_op jit(solution)/shard_map/ppermute | solution.py:380
  98.6 12.5 %collective-permute-start.9 = (bf16[256,1280]{1,0:T(8,128)(2,1)}, bf16[256,1280]{1,0:T(8,128)(2,1)S(1)}, u32[]{:S(2)}, u32[]{:S(2)}) collective-permute-start(bf16[256,1280]{1,0:T(8,128)(2,1)} %get-tuple-element.22), channel_id=1, source_target_pairs={{8,0},{16,8},{24,16},{32,24},{40,32},{48,40},{56,48},{64,56},{72,6... | collective-permute-start | bytes 1966088 | tf_op jit(solution)/shard_map/ppermute | solution.py:375
  102.2 1.3 copy-start.1
  112.5 40.6 %collective-permute-start.10 = (bf16[256,1280]{1,0:T(8,128)(2,1)S(1)}, bf16[256,1280]{1,0:T(8,128)(2,1)S(1)}, u32[]{:S(2)}, u32[]{:S(2)}) collective-permute-start(bf16[256,1280]{1,0:T(8,128)(2,1)S(1)} %fold.1), channel_id=1, source_target_pairs={{16,0},{24,8},{32,16},{40,24},{48,32},{56,40},{64,48},{72,56},{80,... | collective-permute-start | bytes 1966088 | tf_op jit(solution)/shard_map/ppermute | solution.py:375
  115.8 37.3 %collective-permute-start.7 = (bf16[256,640]{1,0:T(8,128)(2,1)S(1)}, bf16[256,640]{1,0:T(8,128)(2,1)S(1)}, u32[]{:S(2)}, u32[]{:S(2)}) collective-permute-start(bf16[256,640]{1,0:T(8,128)(2,1)S(1)} %get-tuple-element.18), channel_id=1, source_target_pairs={{0,4},{1,5},{2,6},{3,7},{4,0},{5,1},{6,2},{7,3},{8,12},{9,13},{10,... | collective-permute-start | bytes 983048 | tf_op jit(solution)/shard_map/ppermute | solution.py:369

commit v6 on v5

--- a/solution.py
+++ b/solution.py
@@ -58,8 +58,8 @@
     for group in range(XN):
         here = slice(group * wide, (group + 1) * wide)
         out[group, :, :wide] = held[0, :, here]
-        out[group, :, wide : wide + HDIM] = meta
-        out[group, :, wide + HDIM :] = held[2, :, here]
+        out[group, :, wide : 2 * wide] = held[2, :, here]
+        out[group, :, 2 * wide :] = meta
 
 
 def pack_queries(query, saved_out, grad_out, frames):
@@ -78,27 +78,28 @@
     )(query, saved_out, grad_out, frames)
 
 
-def pack_keys_kernel(k_ref, v_ref, k2_ref, v2_ref, out):
+def pack_keys_kernel(near, far, out):
     for head in range(HEADS):
         group, h = divmod(head, GROUP)
         cols = slice(head * HDIM, (head + 1) * HDIM)
-        for at, ref in enumerate((k_ref, v_ref, k2_ref, v2_ref)):
-            first = (2 * (at // 2 * GROUP + h) + at % 2) * HDIM
-            out[group, :, first : first + HDIM] = ref[:, cols]
-
-
-def pack_keys(key, value, far_key, far_value):
-    tok, width = key.shape
+        for block, ref in enumerate((near, far)):
+            for at in range(2):
+                first = (2 * (block * GROUP + h) + at) * HDIM
+                out[group, :, first : first + HDIM] = ref[at, :, cols]
+
+
+def pack_keys(near, far):
+    _, tok, width = near.shape
     vmem = pl.BlockSpec(memory_space=pltpu.VMEM)
     return pl.pallas_call(
         pack_keys_kernel,
         out_shape=jax.ShapeDtypeStruct((XN, tok, 4 * GROUP * HDIM), BF16),
-        in_specs=[vmem] * 4,
+        in_specs=[vmem] * 2,
         out_specs=vmem,
         compiler_params=params(),
         cost_estimate=cost(0, 16 * tok * width),
         name="pack_keys",
-    )(key, value, far_key, far_value)
+    )(near, far)
 
 
 def window_scores(queries, keys):
@@ -145,12 +146,12 @@
     out_ref[pl.ds(8 + head, 1), :] = total
 
 
-def head_block(half):
-    return pl.BlockSpec((half, HDIM), lambda h: (0, h))
+def head_block(half, first=0):
+    return pl.BlockSpec((half, HDIM), lambda h: (0, first + h))
 
 
 def meta_block(half):
-    return pl.BlockSpec((half, HDIM), lambda h: (0, GROUP))
+    return pl.BlockSpec((half, HDIM), lambda h: (0, 2 * GROUP))
 
 
 def key_block(half, first=0):
@@ -177,8 +178,8 @@
     return [pltpu.VMEM((HDIM, 2 * half), F32)]
 
 
-def stats(bias, q_own, q_far, near, w2, w3):
-    half = q_own.shape[0]
+def stats(bias, own, far, near, w2, w3):
+    half = own.shape[0]
     pairs = GROUP * 2 * half * 4 * half
     return pl.pallas_call(
         stats_kernel,
@@ -191,7 +192,7 @@
         compiler_params=params(),
         cost_estimate=cost(4 * pairs * HDIM, 6 * half * GROUP * HDIM * 2, pairs),
         name="stats",
-    )(bias, q_own, q_far, q_own, q_far, near, near, w2, w3)
+    )(bias, own, far, own, far, near, near, w2, w3)
 
 
 def log_total(head, half, own_stats, far_stats):
@@ -228,12 +229,12 @@
     first = place[0] * GROUP + head
     dot = rows[pl.ds(first, 1), :] + rows[pl.ds(LOW_LANE + first, 1), :]
     total = log_total(head, half, own_stats, far_stats)
-    if 0 in roles:
-        dq_part, dq_own, dq_far, *outs = rest
+    if 3 in roles:
+        dq_out, *outs = rest
+        dq_sum = jnp.zeros(dq_out.shape, F32)
+    else:
+        dq_part, dq_out, *outs = rest
         dq_sum = dq_part[...]
-    else:
-        dq_part, *outs = rest
-        dq_sum = jnp.zeros(dq_part.shape, F32)
     for role, ref, out in zip(roles, blocks, outs):
         keys, values = ref[:, :HDIM], ref[:, HDIM:]
         scores = window_scores(queries, keys)
@@ -245,47 +246,44 @@
         out[:, :HDIM] = dk.astype(out.dtype)
         out[:, HDIM:] = dv.astype(out.dtype)
     if 0 in roles:
-        turned = (dq_sum * FACTOR).T
-        dq_own[...] = turned[:half]
-        dq_far[...] = turned[half:].astype(BF16)
+        turned = (dq_sum * FACTOR).T.astype(BF16)
+        near_rows = pl.multiple_of(place[1] * half, half)
+        far_rows = pl.multiple_of((1 - place[1]) * half, half)
+        dq_out[pl.ds(near_rows, half), :] = turned[:half]
+        dq_out[pl.ds(far_rows, half), :] = turned[half:]
     else:
-        dq_part[...] = dq_sum
-
-
-def grads(bias, place, own_stats, far_stats, q, g, roles, blocks, dq_part=None):
-    half = q[0].shape[0]
+        dq_out[...] = dq_sum
+
+
+def grads(bias, place, own_stats, far_stats, own, far, roles, blocks, dq_part=None):
+    half = own.shape[0]
     wide = GROUP * HDIM
-    head, meta = head_block(half), meta_block(half)
+    query, cotangent, meta = head_block(half), head_block(half, GROUP), meta_block(half)
     stat = whole((16, 2 * half))
     pairs = GROUP * 2 * half * len(roles) * half
     specs = [pair_block(half, GROUP if role == 1 else 0) for role in roles]
-    turned = jax.ShapeDtypeStruct((wide, 2 * half), F32)
     outs = [
         jax.ShapeDtypeStruct((half, 2 * wide), F32 if role == 0 else BF16) for role in roles
     ]
+    extra = [] if dq_part is None else [dq_part]
     if 0 in roles:
-        extra, extra_specs = [dq_part], [turned_block(half)]
-        dq_outs = [
-            jax.ShapeDtypeStruct((half, wide), F32),
-            jax.ShapeDtypeStruct((half, wide), BF16),
-        ]
-        dq_specs = [head, head]
+        dq_out = jax.ShapeDtypeStruct((2 * half, wide), BF16)
+        dq_spec = head_block(2 * half)
     else:
-        extra, extra_specs = [], []
-        dq_outs, dq_specs = [turned], [turned_block(half)]
+        dq_out, dq_spec = jax.ShapeDtypeStruct((wide, 2 * half), F32), turned_block(half)
     return pl.pallas_call(
         functools.partial(grads_kernel, roles),
         grid=(GROUP,),
-        out_shape=dq_outs + outs,
-        in_specs=[smem(), smem(), stat, stat, head, head, head, head, meta, meta]
+        out_shape=[dq_out] + outs,
+        in_specs=[smem(), smem(), stat, stat, query, query, cotangent, cotangent, meta, meta]
         + specs
-        + extra_specs,
-        out_specs=dq_specs + [pair_block(half)] * len(roles),
+        + [turned_block(half)] * len(extra),
+        out_specs=[dq_spec] + [pair_block(half)] * len(roles),
         scratch_shapes=meta_rows(half),
         compiler_params=params(),
         cost_estimate=cost(10 * pairs * HDIM, 18 * half * wide * 2, pairs),
         name="grads" + "".join(str(role) for role in roles),
-    )(bias, place, own_stats, far_stats, *q, *g, *q, *blocks, *extra)
+    )(bias, place, own_stats, far_stats, own, far, own, far, own, far, *blocks, *extra)
 
 
 def fold_kernel(even_ref, d1, swapped, side, out):
@@ -307,56 +305,54 @@
     )(even, d1, swapped, side)
 
 
-def close_kernel(even_ref, dq_own, dq_far, d0, back, side, out):
+def close_kernel(even_ref, d0, back, side, out):
     even = even_ref[0].astype(F32)
     tok = out.shape[1]
-    wide = dq_own.shape[1]
     for step in range(XN):
         rows = slice(step * tok, (step + 1) * tok)
-        grad_q = dq_own[rows, :] + dq_far[rows, :].astype(F32)
         pair = d0[rows, :] + back[rows, :].astype(F32) + side[rows, :].astype(F32) * even
-        out[step, :, :wide] = grad_q.astype(BF16)
-        out[step, :, wide:] = pair.astype(BF16)
-
-
-def close(even, dq_own, dq_far, d0, back, side):
-    half, wide = dq_own.shape
+        out[step] = pair.astype(BF16)
+
+
+def close(even, d0, back, side):
+    half, wide = d0.shape
     tok = half // XN
     vmem = pl.BlockSpec(memory_space=pltpu.VMEM)
     return pl.pallas_call(
         close_kernel,
-        out_shape=jax.ShapeDtypeStruct((XN, tok, 3 * wide), BF16),
-        in_specs=[smem()] + [vmem] * 5,
+        out_shape=jax.ShapeDtypeStruct((XN, tok, wide), BF16),
+        in_specs=[smem()] + [vmem] * 3,
         out_specs=vmem,
         compiler_params=params(),
-        cost_estimate=cost(5 * half * wide, 28 * half * wide),
+        cost_estimate=cost(3 * half * wide, 10 * half * wide),
         name="close",
-    )(even, dq_own, dq_far, d0, back, side)
-
-
-def unpack_kernel(parts, dq, dk, dv):
+    )(even, d0, back, side)
+
+
+def unpack_kernel(parts, halves, dq, dk, dv):
     wide = GROUP * HDIM
     for group in range(XN):
-        dq[:, group * wide : (group + 1) * wide] = parts[group, :, :wide]
+        total = halves[group].astype(F32) + halves[XN + group].astype(F32)
+        dq[:, group * wide : (group + 1) * wide] = total.astype(BF16)
         for h in range(GROUP):
-            at = wide + 2 * h * HDIM
+            at = 2 * h * HDIM
             cols = slice((group * GROUP + h) * HDIM, (group * GROUP + h + 1) * HDIM)
             dk[:, cols] = parts[group, :, at : at + HDIM]
             dv[:, cols] = parts[group, :, at + HDIM : at + 2 * HDIM]
 
 
-def unpack(parts):
+def unpack(parts, halves):
     tok = parts.shape[1]
     vmem = pl.BlockSpec(memory_space=pltpu.VMEM)
     return pl.pallas_call(
         unpack_kernel,
         out_shape=[jax.ShapeDtypeStruct((tok, HEADS * HDIM), BF16)] * 3,
-        in_specs=[vmem],
+        in_specs=[vmem] * 2,
         out_specs=[vmem] * 3,
         compiler_params=params(),
-        cost_estimate=cost(0, 12 * tok * HEADS * HDIM),
+        cost_estimate=cost(0, 14 * tok * HEADS * HDIM),
         name="unpack",
-    )(parts)
+    )(parts, halves)
 
 
 def over_x(value):
@@ -382,23 +378,21 @@
 
 def per_device(query, key, value, saved_out, grad_out, frame_ids):
     row, col = lax.axis_index("row"), lax.axis_index("col")
-    place = (col % XN).astype(jnp.int32).reshape(1)
+    place = jnp.stack([col % XN, col // XN]).astype(jnp.int32)
     is_even = row % 2 == 0
     even = is_even.astype(jnp.int32).reshape(1)
-    half = query.shape[0] * XN
-    wide = GROUP * HDIM
-
-    far_key, far_value = along_row(key, 2), along_row(value, 2)
-    qg = over_x(pack_queries(query, saved_out, grad_out, frame_ids[:, None]))
-    q_own = qg[:, :, : wide + HDIM].reshape(half, wide + HDIM)
-    g_own = qg[:, :, wide + HDIM :].reshape(half, wide)
-    q_far = across_z(q_own)
-    near = over_x(pack_keys(key, value, far_key, far_value)).reshape(half, -1)
-    near, q_far, g_own = lax.optimization_barrier((near, q_far, g_own))
-    w0, w1 = near[:, : 2 * wide], near[:, 2 * wide :]
+    tok = query.shape[0]
+    half = XN * tok
+    wide = 2 * GROUP * HDIM
+
+    kv = jnp.stack([key, value])
+    kv_far = along_row(kv, 2)
+    own = over_x(pack_queries(query, saved_out, grad_out, frame_ids[:, None])).reshape(half, -1)
+    far = across_z(own)
+    near = over_x(pack_keys(kv, kv_far)).reshape(half, -1)
+    w0, w1 = near[:, :wide], near[:, wide:]
     w3 = along_row(jnp.where(is_even, w0, w1), 1)
     w2 = in_chip(w1)
-    g_far = across_z(g_own)
     held = jnp.stack(
         [
             row >= 0,
@@ -409,16 +403,17 @@
     )
     bias = jnp.where(held, 0.0, NEG).astype(F32)
 
-    own_stats = stats(bias, q_own, q_far, near, w2, w3)
-    far_stats = across_z(own_stats)
-    common = (bias, place, own_stats, far_stats, (q_own, q_far), (g_own, g_far))
+    own_stats = stats(bias, own, far, near, w2, w3)
+    common = (bias, place, own_stats, across_z(own_stats), own, far)
     dq_part, d2, d3 = grads(*common, (2, 3), (w2, w3))
-    dq_own, dq_far, d0, d1 = grads(*common, (0, 1), (near, near), dq_part)
-
-    side = along_row(d3, -1)
-    back = along_row(fold(even, d1, in_chip(d2), side), -2)
-    dq_far = across_z(dq_far)
-    return tuple(unpack(over_x(close(even, dq_own, dq_far, d0, back, side))))
+    side, swapped = along_row(d3, -1), in_chip(d2)
+    dq_part, d1 = grads(*common, (1,), (near,), dq_part)
+    held = fold(even, d1, swapped, side)
+    back = along_row(held, -2)
+    dq_part, held = lax.optimization_barrier((dq_part, held))
+    dq, d0 = grads(*common, (0,), (near,), dq_part)
+    halves = lax.all_to_all(dq.reshape(-1, tok, GROUP * HDIM), "col", 0, 0)
+    return tuple(unpack(over_x(close(even, d0, back, side)), halves))
 
 
 def solution(mesh):

time: 174 us -> 179 us (1.029)
  the two profiles are of different devices: /device:TPU:120 before, /device:TPU:129 now
where the time goes in v6:
time: 179 us; the launch traced here: 177 us
  waiting for transfers between devices  56.7 us (32%)
  starting transfers between devices  42.7 us (24%)
  blocking collectives  41.8 us (23%)
  Pallas kernels  29.6 us (17%)
  local copies, waits for them, and re-layouts  3.12 us (2%)
  other arithmetic  2.46 us (1%)
    ppermute x2, waiting for transfers between devices, across_z(): lax.ppermute(value, 'col', [(c, (c + XN) % count) for c in range(count)])  27.7 us
    all_to_all x1, blocking collectives, per_device(): halves = lax.all_to_all(dq.reshape(-1, tok, GROUP * HDIM), 'col', 0, 0)  27.2 us
    ppermute x4, waiting for transfers between devices, along_row(): lax.ppermute(value, 'row', [(r, r + steps) for r in range(first, last)])  21.6 us
    pallas_call x3, Pallas kernels, grads(): pl.pallas_call(functools.partial(grads_kernel, roles), grid=(GROUP,), out...  17 us
    ppermute x4, starting transfers between devices, along_row(): lax.ppermute(value, 'row', [(r, r + steps) for r in range(first, last)])  14.9 us
    ppermute x2, starting transfers between devices, across_z(): lax.ppermute(value, 'col', [(c, (c + XN) % count) for c in range(count)])  14.7 us
    all_to_all x1, blocking collectives, over_x(): return lax.all_to_all(value, 'col', 0, 0, axis_index_groups=groups)  14.6 us
    all_to_all x2, starting transfers between devices, over_x(): return lax.all_to_all(value, 'col', 0, 0, axis_index_groups=groups)  7.56 us
  transfers between devices with their start and end apart: 10, of which 7 were waited for; matrix products, arithmetic and copies ran while one was open for 1% of the time, Pallas kernels for 8%

profile of v6, /device:TPU:129, one launch (start us, length us, event | category | flops | bytes accessed | tf_op | source)
XLA Modules:
  0.0 177.2 jit_solution(17404827472918117400)
XLA Ops:
  0.6 0.0 copy-start.2
  0.6 1.1 pad_maximum_fusion.near
  1.8 3.2 %collective-permute-start.1 = (bf16[2,64,2560]{2,1,0:T(8,128)(2,1)S(1)}, bf16[2,64,2560]{2,1,0:T(8,128)(2,1)S(1)}, u32[]{:S(2)}, u32[]{:S(2)}) collective-permute-start(bf16[2,64,2560]{2,1,0:T(8,128)(2,1)S(1)} %pad_maximum_fusion.near), channel_id=1, source_target_pairs={{0,16},{8,24},{16,32},{24,40},{32,48},{40,56},{48,64},{56,72},{64,... | collective-permute-start | bytes 1966088 | tf_op jit(solution)/shard_map/ppermute | solution.py:371
  5.0 0.0 copy-done.2
  5.0 0.7 copy.9.f_ref
  5.7 3.1 %pack_queries.1 = bf16[4,64,1408]{2,1,0:T(8,128)(2,1)} custom-call(bf16[64,2560]{1,0:T(8,128)(2,1)} %q_any.1, bf16[64,2560]{1,0:T(8,128)(2,1)} %o_any.1, bf16[64,2560]{1,0:T(8,128)(2,1)} %g_any.1, s32[64,1]{1,0:T(8,128)} %copy.9.f_ref), custom_call_target="tpu_custom_call" | custom-call | flops 327680 | bytes 2293760 | tf_op jit(solution)/shard_map/pack_queries/pallas_call | solution.py:69
  8.8 4.0 %all-to-all-start = ((bf16[4,64,1408]{2,1,0:T(8,128)(2,1)}), bf16[4,64,1408]{2,1,0:T(8,128)(2,1)S(1)}, u32[]{:S(2)}, u32[]{:S(2)}) async-start(bf16[4,64,1408]{2,1,0:T(8,128)(2,1)} %pack_queries.1), calls=%async_computation | async-start | bytes 1441792 | tf_op jit(solution)/shard_map/all_to_all | solution.py:360
  12.8 8.6 %collective-permute-done.1.far = bf16[2,64,2560]{2,1,0:T(8,128)(2,1)S(1)} collective-permute-done((bf16[2,64,2560]{2,1,0:T(8,128)(2,1)S(1)}, bf16[2,64,2560]{2,1,0:T(8,128)(2,1)S(1)}, u32[]{:S(2)}, u32[]{:S(2)}) %collective-permute-start.1) | collective-permute-done | bytes 655392 | tf_op jit(solution)/shard_map/ppermute | solution.py:371
  21.4 1.3 pack_keys.1
  22.7 0.5 all-to-all-done
  23.2 3.5 %all-to-all-start.1 = ((bf16[4,64,2560]{2,1,0:T(8,128)(2,1)}), bf16[4,64,2560]{2,1,0:T(8,128)(2,1)S(1)}, u32[]{:S(2)}, u32[]{:S(2)}) async-start(bf16[4,64,2560]{2,1,0:T(8,128)(2,1)} %pack_keys.1), calls=%async_computation.1 | async-start | bytes 2621440 | tf_op jit(solution)/shard_map/all_to_all | solution.py:360
  26.8 8.8 %collective-permute-start = (bf16[256,1408]{1,0:T(8,128)(2,1)S(1)}, bf16[256,1408]{1,0:T(8,128)(2,1)S(1)}, u32[]{:S(2)}, u32[]{:S(2)}) collective-permute-start(bf16[256,1408]{1,0:T(8,128)(2,1)S(1)} %bitcast.13), channel_id=1, source_target_pairs={{0,4},{1,5},{2,6},{3,7},{4,0},{5,1},{6,2},{7,3},{8,12},{9,13},{10,... | collective-permute-start | bytes 2162696 | tf_op jit(solution)/shard_map/ppermute | solution.py:365
  35.6 6.9 %all-to-all-done.1 = bf16[4,64,2560]{2,1,0:T(8,128)(2,1)S(1)} async-done(((bf16[4,64,2560]{2,1,0:T(8,128)(2,1)}), bf16[4,64,2560]{2,1,0:T(8,128)(2,1)S(1)}, u32[]{:S(2)}, u32[]{:S(2)}) %all-to-all-start.1) | async-done | bytes 1310752 | tf_op jit(solution)/shard_map/all_to_all | solution.py:360
  42.5 1.2 slice_select_fusion
  43.7 6.2 %collective-permute-start.3 = (bf16[256,1280]{1,0:T(8,128)(2,1)}, bf16[256,1280]{1,0:T(8,128)(2,1)S(1)}, u32[]{:S(2)}, u32[]{:S(2)}) collective-permute-start(bf16[256,1280]{1,0:T(8,128)(2,1)} %get-tuple-element.19), channel_id=1, source_target_pairs={{0,8},{8,16},{16,24},{24,32},{32,40},{40,48},{48,56},{56,64},{64,7... | collective-permute-start | bytes 1966088 | tf_op jit(solution)/shard_map/ppermute | solution.py:371
  49.8 1.9 %collective-permute-start.2 = (bf16[256,1280]{1,0:T(8,128)(2,1)}, bf16[256,1280]{1,0:T(8,128)(2,1)}, u32[]{:S(2)}, u32[]{:S(2)}) collective-permute-start(bf16[256,1280]{1,0:T(8,128)(2,1)} %get-tuple-element.20), channel_id=1, source_target_pairs={{0,8},{8,0},{16,24},{24,16},{32,40},{40,32},{48,56},{56,48},{64,72... | collective-permute-start | bytes 1966088 | tf_op jit(solution)/shard_map/ppermute | solution.py:376
  51.8 0.1 add_select_fusion.bias_ref
  51.9 25.1 %collective-permute-done.q_far.m_far.g_far = bf16[256,1408]{1,0:T(8,128)(2,1)S(1)} collective-permute-done((bf16[256,1408]{1,0:T(8,128)(2,1)S(1)}, bf16[256,1408]{1,0:T(8,128)(2,1)S(1)}, u32[]{:S(2)}, u32[]{:S(2)}) %collective-permute-start) | collective-permute-done | bytes 720928 | tf_op jit(solution)/shard_map/ppermute | solution.py:365
  77.0 0.0 collective-permute-done.3.w3.rest_1_
  77.0 0.0 collective-permute-done.2.w2.rest_0_
  77.0 5.5 %stats.1.own_stats = f32[16,512]{1,0:T(8,128)S(1)} custom-call(f32[4]{0:T(128)S(1)} %add_select_fusion.bias_ref, bf16[256,1408]{1,0:T(8,128)(2,1)S(1)} %bitcast.14, bf16[256,1408]{1,0:T(8,128)(2,1)S(1)} %collective-permute-done.q_far.m_far.g_far, bf16[256,1408]{1,0:T(8,128)(2,1)S(1)} %bitcast.15, ...), custom_call_target="tpu_custom_call" | custom-call | flops 1342177280 | bytes 1966080 | tf_op jit(solution)/shard_map/stats/pallas_call | solution.py:184
  82.5 5.8 %collective-permute-start.4 = (f32[16,512]{1,0:T(8,128)S(1)}, f32[16,512]{1,0:T(8,128)S(1)}, u32[]{:S(2)}, u32[]{:S(2)}) collective-permute-start(f32[16,512]{1,0:T(8,128)S(1)} %stats.1.own_stats), channel_id=1, source_target_pairs={{0,4},{1,5},{2,6},{3,7},{4,0},{5,1},{6,2},{7,3},{8,12},{9,13},{10,... | collective-permute-start | bytes 98312 | tf_op jit(solution)/shard_map/ppermute | solution.py:365
  88.3 0.1 pad_add_fusion.place
  88.4 2.7 %collective-permute-done.4.far_stats = f32[16,512]{1,0:T(8,128)S(1)} collective-permute-done((f32[16,512]{1,0:T(8,128)S(1)}, f32[16,512]{1,0:T(8,128)S(1)}, u32[]{:S(2)}, u32[]{:S(2)}) %collective-permute-start.4) | collective-permute-done | bytes 32800 | tf_op jit(solution)/shard_map/ppermute | solution.py:365
  91.1 7.6 %grads23.1 = (f32[640,512]{1,0:T(8,128)S(1)}, bf16[256,1280]{1,0:T(8,128)(2,1)}, bf16[256,1280]{1,0:T(8,128)(2,1)}) custom-call(f32[4]{0:T(128)S(1)} %add_select_fusion.bias_ref, s32[2]{0:T(128)S(1)} %pad_add_fusion.place, f32[16,512]{1,0:T(8,128)S(1)} %stats.1.own_stats, f32[16,512]{1,0:T(8,128)S(1)} %collective-permute-done.4.far_stats, ...), custom_call_target="tpu_custom_call" | custom-call | flops 1677721600 | bytes 5898240 | tf_op jit(solution)/shard_map/grads23/pallas_call | solution.py:274
  98.7 0.0 copy-start
  98.7 1.1 copy-done
  99.8 3.6 %collective-permute-start.5 = (bf16[256,1280]{1,0:T(8,128)(2,1)}, bf16[256,1280]{1,0:T(8,128)(2,1)}, u32[]{:S(2)}, u32[]{:S(2)}) collective-permute-start(bf16[256,1280]{1,0:T(8,128)(2,1)} %get-tuple-element.14), channel_id=1, source_target_pairs={{0,8},{8,0},{16,24},{24,16},{32,40},{40,32},{48,56},{56,48},{64,72... | collective-permute-start | bytes 1966088 | tf_op jit(solution)/shard_map/ppermute | solution.py:376
  103.4 1.9 %collective-permute-start.6 = (bf16[256,1280]{1,0:T(8,128)(2,1)}, bf16[256,1280]{1,0:T(8,128)(2,1)S(1)}, u32[]{:S(2)}, u32[]{:S(2)}) collective-permute-start(bf16[256,1280]{1,0:T(8,128)(2,1)} %get-tuple-element.15), channel_id=1, source_target_pairs={{8,0},{16,8},{24,16},{32,24},{40,32},{48,40},{56,48},{64,56},{72,6... | collective-permute-start | bytes 1966088 | tf_op jit(solution)/shard_map/ppermute | solution.py:371
  105.3 0.0 copy-start.1
  105.3 1.3 copy-done.1
  106.6 4.3 %grads1.1 = (f32[640,512]{1,0:T(8,128)S(1)}, bf16[256,1280]{1,0:T(8,128)(2,1)S(1)}) custom-call(f32[4]{0:T(128)S(1)} %add_select_fusion.bias_ref, s32[2]{0:T(128)S(1)} %pad_add_fusion.place, f32[16,512]{1,0:T(8,128)S(1)} %stats.1.own_stats, f32[16,512]{1,0:T(8,128)S(1)} %collective-permute-done.4.far_stats, bf16[256,1408]{1,0:T(8,128)(2,1)S(1)} %bitcast.19, ...), custom_call_target="tpu_custom_call" | custom-call | flops 838860800 | bytes 5898240 | tf_op jit(solution)/shard_map/grads1/pallas_call | solution.py:274
  111.0 0.0 collective-permute-done.5.swapped
  111.0 4.5 %collective-permute-done.6.side = bf16[256,1280]{1,0:T(8,128)(2,1)S(1)} collective-permute-done((bf16[256,1280]{1,0:T(8,128)(2,1)}, bf16[256,1280]{1,0:T(8,128)(2,1)S(1)}, u32[]{:S(2)}, u32[]{:S(2)}) %collective-permute-start.6) | collective-permute-done | bytes 655392 | tf_op jit(solution)/shard_map/ppermute | solution.py:371
  115.5 1.4 fold.1
  116.9 3.6 %collective-permute-start.7 = (bf16[256,1280]{1,0:T(8,128)(2,1)S(1)}, bf16[256,1280]{1,0:T(8,128)(2,1)S(1)}, u32[]{:S(2)}, u32[]{:S(2)}) collective-permute-start(bf16[256,1280]{1,0:T(8,128)(2,1)S(1)} %fold.1), channel_id=1, source_target_pairs={{16,0},{24,8},{32,16},{40,24},{48,32},{56,40},{64,48},{72,56},{80,... | collective-permute-start | bytes 1966088 | tf_op jit(solution)/shard_map/ppermute | solution.py:371
  120.5 5.0 %grads0.1 = (bf16[512,640]{1,0:T(8,128)(2,1)S(1)}, f32[256,1280]{1,0:T(8,128)S(1)}) custom-call(f32[4]{0:T(128)S(1)} %add_select_fusion.bias_ref, s32[2]{0:T(128)S(1)} %pad_add_fusion.place, f32[16,512]{1,0:T(8,128)S(1)} %stats.1.own_stats, f32[16,512]{1,0:T(8,128)S(1)} %collective-permute-done.4.far_stats, bf16[256,1408]{1,0:T(8,128)(2,1)S(1)} %bitcast.22, ...), custom_call_target="tpu_custom_call" | custom-call | flops 838860800 | bytes 5898240 | tf_op jit(solution)/shard_map/grads0/pallas_call | solution.py:274
  125.5 8.5 %collective-permute-done.7.back = bf16[256,1280]{1,0:T(8,128)(2,1)S(1)} collective-permute-done((bf16[256,1280]{1,0:T(8,128)(2,1)S(1)}, bf16[256,1280]{1,0:T(8,128)(2,1)S(1)}, u32[]{:S(2)}, u32[]{:S(2)}) %collective-permute-start.7) | collective-permute-done | bytes 655392 | tf_op jit(solution)/shard_map/ppermute | solution.py:371
  134.0 0.2 close.1
  134.2 14.6 %all_to_all.20.parts = bf16[4,64,1280]{2,1,0:T(8,128)(2,1)S(1)} all-to-all(bf16[4,64,1280]{2,1,0:T(8,128)(2,1)S(1)} %close.1), channel_id=1, replica_groups={{0,1,2,3},{4,5,6,7},{8,9,10,11},{12,13,14,15},{16,17,18,19},{20,21,22,2..., dimensions={0} | all-to-all | bytes 1310720 | tf_op jit(solution)/shard_map/all_to_all | solution.py:360
  148.9 27.2 %all_to_all.21.halves = bf16[8,64,640]{2,1,0:T(8,128)(2,1)S(1)} all-to-all(bf16[8,64,640]{2,1,0:T(8,128)(2,1)S(1)} %bitcast.30), channel_id=1, replica_groups=mesh['row'=64,'col'=8] {'col'}, dimensions={0} | all-to-all | bytes 1310720 | tf_op jit(solution)/shard_map/all_to_all | solution.py:415
  176.1 1.1 unpack.1
Async XLA Ops:
  0.6 4.4 %copy-start.2 = (s32[64]{0:T(128)S(1)}, s32[64]{0:T(128)}, u32[]{:S(2)}) copy-start(s32[64]{0:T(128)} %param.11) | copy-start | bytes 772
  1.8 19.6 %collective-permute-start.1 = (bf16[2,64,2560]{2,1,0:T(8,128)(2,1)S(1)}, bf16[2,64,2560]{2,1,0:T(8,128)(2,1)S(1)}, u32[]{:S(2)}, u32[]{:S(2)}) collective-permute-start(bf16[2,64,2560]{2,1,0:T(8,128)(2,1)S(1)} %pad_maximum_fusion.near), channel_id=1, source_target_pairs={{0,16},{8,24},{16,32},{24,40},{32,48},{40,56},{48,64},{56,72},{64,... | collective-permute-start | bytes 1966088 | tf_op jit(solution)/shard_map/ppermute | solution.py:371
  8.8 14.4 %all-to-all-start = ((bf16[4,64,1408]{2,1,0:T(8,128)(2,1)}), bf16[4,64,1408]{2,1,0:T(8,128)(2,1)S(1)}, u32[]{:S(2)}, u32[]{:S(2)}) async-start(bf16[4,64,1408]{2,1,0:T(8,128)(2,1)} %pack_queries.1), calls=%async_computation | async-start | bytes 1441792 | tf_op jit(solution)/shard_map/all_to_all | solution.py:360
  23.2 19.3 %all-to-all-start.1 = ((bf16[4,64,2560]{2,1,0:T(8,128)(2,1)}), bf16[4,64,2560]{2,1,0:T(8,128)(2,1)S(1)}, u32[]{:S(2)}, u32[]{:S(2)}) async-start(bf16[4,64,2560]{2,1,0:T(8,128)(2,1)} %pack_keys.1), calls=%async_computation.1 | async-start | bytes 2621440 | tf_op jit(solution)/shard_map/all_to_all | solution.py:360
  26.8 50.2 %collective-permute-start = (bf16[256,1408]{1,0:T(8,128)(2,1)S(1)}, bf16[256,1408]{1,0:T(8,128)(2,1)S(1)}, u32[]{:S(2)}, u32[]{:S(2)}) collective-permute-start(bf16[256,1408]{1,0:T(8,128)(2,1)S(1)} %bitcast.13), channel_id=1, source_target_pairs={{0,4},{1,5},{2,6},{3,7},{4,0},{5,1},{6,2},{7,3},{8,12},{9,13},{10,... | collective-permute-start | bytes 2162696 | tf_op jit(solution)/shard_map/ppermute | solution.py:365
  43.7 33.3 %collective-permute-start.3 = (bf16[256,1280]{1,0:T(8,128)(2,1)}, bf16[256,1280]{1,0:T(8,128)(2,1)S(1)}, u32[]{:S(2)}, u32[]{:S(2)}) collective-permute-start(bf16[256,1280]{1,0:T(8,128)(2,1)} %get-tuple-element.19), channel_id=1, source_target_pairs={{0,8},{8,16},{16,24},{24,32},{32,40},{40,48},{48,56},{56,64},{64,7... | collective-permute-start | bytes 1966088 | tf_op jit(solution)/shard_map/ppermute | solution.py:371
  49.8 27.1 %collective-permute-start.2 = (bf16[256,1280]{1,0:T(8,128)(2,1)}, bf16[256,1280]{1,0:T(8,128)(2,1)}, u32[]{:S(2)}, u32[]{:S(2)}) collective-permute-start(bf16[256,1280]{1,0:T(8,128)(2,1)} %get-tuple-element.20), channel_id=1, source_target_pairs={{0,8},{8,0},{16,24},{24,16},{32,40},{40,32},{48,56},{56,48},{64,72... | collective-permute-start | bytes 1966088 | tf_op jit(solution)/shard_map/ppermute | solution.py:376
  82.5 8.6 %collective-permute-start.4 = (f32[16,512]{1,0:T(8,128)S(1)}, f32[16,512]{1,0:T(8,128)S(1)}, u32[]{:S(2)}, u32[]{:S(2)}) collective-permute-start(f32[16,512]{1,0:T(8,128)S(1)} %stats.1.own_stats), channel_id=1, source_target_pairs={{0,4},{1,5},{2,6},{3,7},{4,0},{5,1},{6,2},{7,3},{8,12},{9,13},{10,... | collective-permute-start | bytes 98312 | tf_op jit(solution)/shard_map/ppermute | solution.py:365
  98.7 1.1 copy-start
  99.8 11.2 %collective-permute-start.5 = (bf16[256,1280]{1,0:T(8,128)(2,1)}, bf16[256,1280]{1,0:T(8,128)(2,1)}, u32[]{:S(2)}, u32[]{:S(2)}) collective-permute-start(bf16[256,1280]{1,0:T(8,128)(2,1)} %get-tuple-element.14), channel_id=1, source_target_pairs={{0,8},{8,0},{16,24},{24,16},{32,40},{40,32},{48,56},{56,48},{64,72... | collective-permute-start | bytes 1966088 | tf_op jit(solution)/shard_map/ppermute | solution.py:376
  103.4 12.1 %collective-permute-start.6 = (bf16[256,1280]{1,0:T(8,128)(2,1)}, bf16[256,1280]{1,0:T(8,128)(2,1)S(1)}, u32[]{:S(2)}, u32[]{:S(2)}) collective-permute-start(bf16[256,1280]{1,0:T(8,128)(2,1)} %get-tuple-element.15), channel_id=1, source_target_pairs={{8,0},{16,8},{24,16},{32,24},{40,32},{48,40},{56,48},{64,56},{72,6... | collective-permute-start | bytes 1966088 | tf_op jit(solution)/shard_map/ppermute | solution.py:371
  105.3 1.3 copy-start.1
  116.9 17.1 %collective-permute-start.7 = (bf16[256,1280]{1,0:T(8,128)(2,1)S(1)}, bf16[256,1280]{1,0:T(8,128)(2,1)S(1)}, u32[]{:S(2)}, u32[]{:S(2)}) collective-permute-start(bf16[256,1280]{1,0:T(8,128)(2,1)S(1)} %fold.1), channel_id=1, source_target_pairs={{16,0},{24,8},{32,16},{40,24},{48,32},{56,40},{64,48},{72,56},{80,... | collective-permute-start | bytes 1966088 | tf_op jit(solution)/shard_map/ppermute | solution.py:371

commit v7 on v6

v7 whole, which is shorter than its diff:
```python
import functools
import math

import jax
import jax.numpy as jnp
from jax import lax
from jax.experimental import pallas as pl
from jax.experimental.pallas import tpu as pltpu
from jax.sharding import PartitionSpec as P

HEADS = 20
HDIM = 128
XN = 4
GROUP = HEADS // XN
NEG = -1e30
FACTOR = HDIM ** (-0.5)
SCALE2 = FACTOR * math.log2(math.e)
LOW_LANE = 32
FRAME_LANE = 64
BF16 = jnp.bfloat16
F32 = jnp.float32


def params(room=20):
    return pltpu.CompilerParams(vmem_limit_bytes=room * 1024 * 1024)


def cost(flops, moved, exps=0):
    return pl.CostEstimate(flops=flops, bytes_accessed=moved, transcendentals=exps)


def load_all(sources, held, sems):
    copies = [
        pltpu.make_async_copy(src, held.at[at], sems.at[at]) for at, src in enumerate(sources)
    ]
    for copy in copies:
        copy.start()
    for copy in copies:
        copy.wait()


def pack_queries_kernel(q_any, o_any, g_any, f_ref, out, held, sems):
    load_all((q_any, o_any, g_any), held, sems)
    tok = held.shape[1]
    wide = GROUP * HDIM
    lane = lax.broadcasted_iota(jnp.int32, (tok, HDIM), 1)
    meta = jnp.where(lane == FRAME_LANE, f_ref[...].astype(F32), 0.0)
    for head in range(HEADS):
        cols = slice(head * HDIM, (head + 1) * HDIM)
        product = held[2, :, cols].astype(F32) * held[1, :, cols].astype(F32)
        dot = jnp.sum(product, axis=1, keepdims=True)
        high = dot.astype(BF16).astype(F32)
        meta = jnp.where(lane == head, high, meta)
        meta = jnp.where(lane == LOW_LANE + head, dot - high, meta)
    meta = meta.astype(BF16)
    for group in range(XN):
        here = slice(group * wide, (group + 1) * wide)
        out[group, :, :wide] = held[0, :, here]
        out[group, :, wide : 2 * wide] = held[2, :, here]
        out[group, :, 2 * wide :] = meta


def pack_queries(query, saved_out, grad_out, frames):
    tok, width = query.shape
    shape = (XN, tok, 2 * GROUP * HDIM + HDIM)
    return pl.pallas_call(
        pack_queries_kernel,
        out_shape=jax.ShapeDtypeStruct(shape, BF16),
        in_specs=[pl.BlockSpec(memory_space=pl.ANY)] * 3 + [vmem()],
        out_specs=vmem(),
        scratch_shapes=[pltpu.VMEM((3, tok, width), BF16), pltpu.SemaphoreType.DMA((3,))],
        compiler_params=params(60),
        cost_estimate=cost(2 * tok * width, 14 * tok * width),
        name="pack_queries",
    )(query, saved_out, grad_out, frames)


def pack_keys_kernel(near, far, out):
    for head in range(HEADS):
        group, h = divmod(head, GROUP)
        cols = slice(head * HDIM, (head + 1) * HDIM)
        for block, ref in enumerate((near, far)):
            for at in range(2):
                first = (2 * (block * GROUP + h) + at) * HDIM
                out[group, :, first : first + HDIM] = ref[at, :, cols]


def pack_keys(near, far):
    _, tok, width = near.shape
    return pl.pallas_call(
        pack_keys_kernel,
        out_shape=jax.ShapeDtypeStruct((XN, tok, 4 * GROUP * HDIM), BF16),
        in_specs=[vmem()] * 2,
        out_specs=vmem(),
        compiler_params=params(),
        cost_estimate=cost(0, 16 * tok * width),
        name="pack_keys",
    )(near, far)


def both(own, far, cols):
    return jnp.concatenate([own[:, cols], far[:, cols]], axis=0)


META = slice(2 * GROUP * HDIM, (2 * GROUP + 1) * HDIM)


def head_slice(at):
    return slice(at * HDIM, (at + 1) * HDIM)


def seen(rows, own):
    k_frame = own[:, META].astype(F32)[:, FRAME_LANE : FRAME_LANE + 1]
    return k_frame <= rows[FRAME_LANE : FRAME_LANE + 1, :]


def stats_kernel(bias_ref, own, far, near, w2, w3, out_ref):
    half = own.shape[0]
    rows = both(own, far, META).astype(F32).T
    mask = seen(rows, own)
    out_ref[...] = jnp.zeros_like(out_ref)
    for head in range(GROUP):
        queries = both(own, far, head_slice(head)).T
        at = head_slice(2 * head)
        keys = [near[:, at], near[:, head_slice(2 * (GROUP + head))], w2[:, at], w3[:, at]]
        scores = jnp.dot(
            jnp.concatenate(keys, axis=0), queries, preferred_element_type=F32
        ) * SCALE2
        parts = [scores[role * half : (role + 1) * half] for role in range(4)]
        parts[0] = jnp.where(mask, parts[0], NEG)
        peaks = [
            jnp.max(part, axis=0, keepdims=True) + bias_ref[role]
            for role, part in enumerate(parts)
        ]
        peak = functools.reduce(jnp.maximum, peaks)
        total = jnp.zeros_like(peak)
        for role, part in enumerate(parts):
            total += jnp.sum(jnp.exp2(part - (peak - bias_ref[role])), axis=0, keepdims=True)
        out_ref[head : head + 1, :] = peak
        out_ref[8 + head : 9 + head, :] = total


def smem():
    return pl.BlockSpec(memory_space=pltpu.SMEM)


def vmem():
    return pl.BlockSpec(memory_space=pltpu.VMEM)


def stats(bias, own, far, near, w2, w3):
    half = own.shape[0]
    pairs = GROUP * 2 * half * 4 * half
    return pl.pallas_call(
        stats_kernel,
        out_shape=jax.ShapeDtypeStruct((16, 2 * half), F32),
        in_specs=[smem()] + [vmem()] * 5,
        out_specs=vmem(),
        compiler_params=params(),
        cost_estimate=cost(4 * pairs * HDIM, 6 * half * GROUP * HDIM * 2, pairs),
        name="stats",
    )(bias, own, far, near, w2, w3)


def log_total(own_stats, far_stats):
    half = own_stats.shape[1] // 2
    turned = jnp.concatenate([far_stats[:, half:], far_stats[:, :half]], axis=1)
    own_peak, own_sum = own_stats[:8, :], own_stats[8:, :]
    far_peak, far_sum = turned[:8], turned[8:]
    peak = jnp.maximum(own_peak, far_peak)
    own_part = own_sum * jnp.exp2(own_peak - peak)
    return peak + jnp.log2(own_part + far_sum * jnp.exp2(far_peak - peak))


def grads_kernel(roles, bias_ref, place, own_stats, far_stats, own, far, *rest):
    *rest, rows = rest
    blocks, rest = rest[: len(roles)], rest[len(roles) :]
    if 3 in roles:
        dq_out, *outs = rest
    else:
        dq_part, dq_out, *outs = rest
    half = own.shape[0]
    rows[...] = both(own, far, META).astype(F32).T
    totals = log_total(own_stats, far_stats)
    for head in range(GROUP):
        q_cols, g_cols = head_slice(head), head_slice(GROUP + head)
        queries, grads = both(own, far, q_cols), both(own, far, g_cols)
        first = place[0] * GROUP + head
        dot = rows[pl.ds(first, 1), :] + rows[pl.ds(LOW_LANE + first, 1), :]
        total = totals[head : head + 1]
        at = [2 * (GROUP + head) if role == 1 else 2 * head for role in roles]
        keys = jnp.concatenate([ref[:, head_slice(a)] for ref, a in zip(blocks, at)], axis=0)
        values = jnp.concatenate([ref[:, head_slice(a + 1)] for ref, a in zip(blocks, at)], axis=0)
        scores = jnp.dot(keys, queries.T, preferred_element_type=F32) * SCALE2
        if 0 in roles:
            scores = jnp.where(seen(rows, own), scores, NEG)
        bounds = [total - bias_ref[role] for role in roles]
        parts = [
            jnp.exp2(scores[i * half : (i + 1) * half] - bound) for i, bound in enumerate(bounds)
        ]
        probs = jnp.concatenate(parts, axis=0)
        dv = jnp.dot(probs.astype(BF16), grads, preferred_element_type=F32)
        dp = jnp.dot(values, grads.T, preferred_element_type=F32)
        ds = (probs * (dp - dot)).astype(BF16)
        dk = jnp.dot(ds, queries, preferred_element_type=F32) * FACTOR
        dq = jnp.dot(keys.T, ds, preferred_element_type=F32)
        for i, out in enumerate(outs):
            out[:, head_slice(2 * head)] = dk[i * half : (i + 1) * half].astype(out.dtype)
            out[:, head_slice(2 * head + 1)] = dv[i * half : (i + 1) * half].astype(out.dtype)
        if 3 not in roles:
            dq += dq_part[q_cols, :]
        if 0 in roles:
            turned = (dq * FACTOR).T.astype(BF16)
            near_rows = pl.multiple_of(place[1] * half, half)
            far_rows = pl.multiple_of((1 - place[1]) * half, half)
            dq_out[pl.ds(near_rows, half), q_cols] = turned[:half]
            dq_out[pl.ds(far_rows, half), q_cols] = turned[half:]
        else:
            dq_out[q_cols, :] = dq


def grads(bias, place, own_stats, far_stats, own, far, roles, blocks, dq_part=None):
    half = own.shape[0]
    wide = GROUP * HDIM
    pairs = GROUP * 2 * half * len(roles) * half
    outs = [
        jax.ShapeDtypeStruct((half, 2 * wide), F32 if role == 0 else BF16) for role in roles
    ]
    extra = [] if dq_part is None else [dq_part]
    if 0 in roles:
        dq_out = jax.ShapeDtypeStruct((2 * half, wide), BF16)
    else:
        dq_out = jax.ShapeDtypeStruct((wide, 2 * half), F32)
    return pl.pallas_call(
        functools.partial(grads_kernel, roles),
        out_shape=[dq_out] + outs,
        in_specs=[smem(), smem()] + [vmem()] * (4 + len(blocks) + len(extra)),
        out_specs=[vmem()] * (1 + len(outs)),
        scratch_shapes=[pltpu.VMEM((HDIM, 2 * half), F32)],
        compiler_params=params(),
        cost_estimate=cost(10 * pairs * HDIM, 18 * half * wide * 2, pairs),
        name="grads" + "".join(str(role) for role in roles),
    )(bias, place, own_stats, far_stats, own, far, *blocks, *extra)


def fold_kernel(even_ref, d1, swapped, side, out):
    odd = 1.0 - even_ref[0].astype(F32)
    total = d1[...].astype(F32) + swapped[...].astype(F32) + side[...].astype(F32) * odd
    out[...] = total.astype(BF16)


def fold(even, d1, swapped, side):
    return pl.pallas_call(
        fold_kernel,
        out_shape=jax.ShapeDtypeStruct(d1.shape, BF16),
        in_specs=[smem()] + [vmem()] * 3,
        out_specs=vmem(),
        compiler_params=params(),
        cost_estimate=cost(3 * d1.size, 8 * d1.size),
        name="fold",
    )(even, d1, swapped, side)


def close_kernel(even_ref, d0, back, side, out):
    even = even_ref[0].astype(F32)
    tok = out.shape[1]
    for step in range(XN):
        rows = slice(step * tok, (step + 1) * tok)
        pair = d0[rows, :] + back[rows, :].astype(F32) + side[rows, :].astype(F32) * even
        out[step] = pair.astype(BF16)


def close(even, d0, back, side):
    half, wide = d0.shape
    tok = half // XN
    return pl.pallas_call(
        close_kernel,
        out_shape=jax.ShapeDtypeStruct((XN, tok, wide), BF16),
        in_specs=[smem()] + [vmem()] * 3,
        out_specs=vmem(),
        compiler_params=params(),
        cost_estimate=cost(3 * half * wide, 10 * half * wide),
        name="close",
    )(even, d0, back, side)


def unpack_kernel(parts, halves, dq, dk, dv):
    wide = GROUP * HDIM
    for group in range(XN):
        total = halves[group].astype(F32) + halves[XN + group].astype(F32)
        dq[:, group * wide : (group + 1) * wide] = total.astype(BF16)
        for h in range(GROUP):
            at = 2 * h * HDIM
            cols = slice((group * GROUP + h) * HDIM, (group * GROUP + h + 1) * HDIM)
            dk[:, cols] = parts[group, :, at : at + HDIM]
            dv[:, cols] = parts[group, :, at + HDIM : at + 2 * HDIM]


def unpack(parts, halves):
    tok = parts.shape[1]
    return pl.pallas_call(
        unpack_kernel,
        out_shape=[jax.ShapeDtypeStruct((tok, HEADS * HDIM), BF16)] * 3,
        in_specs=[vmem()] * 2,
        out_specs=[vmem()] * 3,
        compiler_params=params(),
        cost_estimate=cost(0, 14 * tok * HEADS * HDIM),
        name="unpack",
    )(parts, halves)


def over_x(value):
    groups = [[z * XN + x for x in range(XN)] for z in range(lax.axis_size("col") // XN)]
    return lax.all_to_all(value, "col", 0, 0, axis_index_groups=groups)


def across_z(value):
    count = lax.axis_size("col")
    return lax.ppermute(value, "col", [(c, (c + XN) % count) for c in range(count)])


def along_row(value, steps):
    count = lax.axis_size("row")
    first, last = max(0, -steps), min(count, count - steps)
    return lax.ppermute(value, "row", [(r, r + steps) for r in range(first, last)])


def in_chip(value):
    count = lax.axis_size("row")
    return lax.ppermute(value, "row", [(r, r ^ 1) for r in range(count)])


def per_device(query, key, value, saved_out, grad_out, frame_ids):
    row, col = lax.axis_index("row"), lax.axis_index("col")
    place = jnp.stack([col % XN, col // XN]).astype(jnp.int32)
    is_even = row % 2 == 0
    even = is_even.astype(jnp.int32).reshape(1)
    tok = query.shape[0]
    half = XN * tok
    wide = 2 * GROUP * HDIM

    kv = jnp.stack([key, value])
    kv_far = along_row(kv, 2)
    own = over_x(pack_queries(query, saved_out, grad_out, frame_ids[:, None])).reshape(half, -1)
    far = across_z(own)
    near = over_x(pack_keys(kv, kv_far)).reshape(half, -1)
    w0, w1 = near[:, :wide], near[:, wide:]
    w3 = along_row(jnp.where(is_even, w0, w1), 1)
    w2 = in_chip(w1)
    held = jnp.stack(
        [
            row >= 0,
            row >= 2,
            jnp.where(is_even, row >= 1, row >= 3),
            jnp.where(is_even, row >= 3, row >= 1),
        ]
    )
    bias = jnp.where(held, 0.0, NEG).astype(F32)

    own_stats = stats(bias, own, far, near, w2, w3)
    common = (bias, place, own_stats, across_z(own_stats), own, far)
    dq_part, d2, d3 = grads(*common, (2, 3), (w2, w3))
    side, swapped = along_row(d3, -1), in_chip(d2)
    dq_part, d1 = grads(*common, (1,), (near,), dq_part)
    held = fold(even, d1, swapped, side)
    back = along_row(held, -2)
    dq_part, held = lax.optimization_barrier((dq_part, held))
    dq, d0 = grads(*common, (0,), (near,), dq_part)
    halves = lax.all_to_all(dq.reshape(-1, tok, GROUP * HDIM), "col", 0, 0)
    back, halves = lax.optimization_barrier((back, halves))
    return tuple(unpack(over_x(close(even, d0, back, side)), halves))


def solution(mesh):
    placed = P(("row", "col"), None)
    return jax.shard_map(
        per_device,
        mesh=mesh,
        in_specs=(placed,) * 5 + (P(("row", "col")),),
        out_specs=(placed,) * 3,
        check_vma=False,
    )
```

time: 179 us -> 168 us (0.939)
  the two profiles are of different devices: /device:TPU:129 before, /device:TPU:121 now
where the time goes in v7:
time: 168 us
  waiting for transfers between devices  70 us (42%)
  starting transfers between devices  51.5 us (31%)
  Pallas kernels  23.1 us (14%)
  blocking collectives  13.8 us (8%)
  local copies, waits for them, and re-layouts  5.84 us (3%)
  other arithmetic  2.46 us (1%)
    ppermute x4, waiting for transfers between devices, along_row(): lax.ppermute(value, 'row', [(r, r + steps) for r in range(first, last)])  37.4 us
    ppermute x2, waiting for transfers between devices, across_z(): lax.ppermute(value, 'col', [(c, (c + XN) % count) for c in range(count)])  16 us
    ppermute x2, starting transfers between devices, across_z(): lax.ppermute(value, 'col', [(c, (c + XN) % count) for c in range(count)])  15.9 us
    all_to_all x1, blocking collectives, over_x(): return lax.all_to_all(value, 'col', 0, 0, axis_index_groups=groups)  13.8 us
    ppermute x4, starting transfers between devices, along_row(): lax.ppermute(value, 'row', [(r, r + steps) for r in range(first, last)])  13.4 us
    pallas_call x3, Pallas kernels, grads(): pl.pallas_call(functools.partial(grads_kernel, roles), out_shape=[dq_out]...  11.7 us
    all_to_all x2, waiting for transfers between devices, over_x(): return lax.all_to_all(value, 'col', 0, 0, axis_index_groups=groups)  9.54 us
    all_to_all x1, starting transfers between devices, per_device(): halves = lax.all_to_all(dq.reshape(-1, tok, GROUP * HDIM), 'col', 0, 0)  7.85 us
  transfers between devices with their start and end apart: 11, of which 8 were waited for; matrix products, arithmetic and copies ran while one was open for 1% of the time, Pallas kernels for 4%

profile of v7, /device:TPU:121, one launch (start us, length us, event | category | flops | bytes accessed | tf_op | source)
XLA Modules:
  0.0 167.6 jit_solution(10977936420514288920)
XLA Ops:
  0.6 0.0 copy-start.6
  0.6 1.1 pad_maximum_fusion.near
  1.8 3.2 %collective-permute-start.1 = (bf16[2,64,2560]{2,1,0:T(8,128)(2,1)S(1)}, bf16[2,64,2560]{2,1,0:T(8,128)(2,1)S(1)}, u32[]{:S(2)}, u32[]{:S(2)}) collective-permute-start(bf16[2,64,2560]{2,1,0:T(8,128)(2,1)S(1)} %pad_maximum_fusion.near), channel_id=1, source_target_pairs={{0,16},{8,24},{16,32},{24,40},{32,48},{40,56},{48,64},{56,72},{64,... | collective-permute-start | bytes 1966088 | tf_op jit(solution)/shard_map/ppermute | solution.py:325
  5.0 0.0 copy-done.6
  5.0 0.7 copy.9.f_ref
  5.7 3.1 %pack_queries.1 = bf16[4,64,1408]{2,1,0:T(8,128)(2,1)} custom-call(bf16[64,2560]{1,0:T(8,128)(2,1)} %q_any.1, bf16[64,2560]{1,0:T(8,128)(2,1)} %o_any.1, bf16[64,2560]{1,0:T(8,128)(2,1)} %g_any.1, s32[64,1]{1,0:T(8,128)} %copy.9.f_ref), custom_call_target="tpu_custom_call" | custom-call | flops 327680 | bytes 2293760 | tf_op jit(solution)/shard_map/pack_queries/pallas_call | solution.py:66
  8.8 4.0 %all-to-all-start = ((bf16[4,64,1408]{2,1,0:T(8,128)(2,1)}), bf16[4,64,1408]{2,1,0:T(8,128)(2,1)S(1)}, u32[]{:S(2)}, u32[]{:S(2)}) async-start(bf16[4,64,1408]{2,1,0:T(8,128)(2,1)} %pack_queries.1), calls=%async_computation | async-start | bytes 1441792 | tf_op jit(solution)/shard_map/all_to_all | solution.py:314
  12.9 6.4 %collective-permute-done.1.far = bf16[2,64,2560]{2,1,0:T(8,128)(2,1)S(1)} collective-permute-done((bf16[2,64,2560]{2,1,0:T(8,128)(2,1)S(1)}, bf16[2,64,2560]{2,1,0:T(8,128)(2,1)S(1)}, u32[]{:S(2)}, u32[]{:S(2)}) %collective-permute-start.1) | collective-permute-done | bytes 655392 | tf_op jit(solution)/shard_map/ppermute | solution.py:325
  19.3 1.3 pack_keys.1
  20.6 2.7 %all-to-all-done = bf16[4,64,1408]{2,1,0:T(8,128)(2,1)S(1)} async-done(((bf16[4,64,1408]{2,1,0:T(8,128)(2,1)}), bf16[4,64,1408]{2,1,0:T(8,128)(2,1)S(1)}, u32[]{:S(2)}, u32[]{:S(2)}) %all-to-all-start) | async-done | bytes 720928 | tf_op jit(solution)/shard_map/all_to_all | solution.py:314
  23.2 3.5 %all-to-all-start.1 = ((bf16[4,64,2560]{2,1,0:T(8,128)(2,1)}), bf16[4,64,2560]{2,1,0:T(8,128)(2,1)S(1)}, u32[]{:S(2)}, u32[]{:S(2)}) async-start(bf16[4,64,2560]{2,1,0:T(8,128)(2,1)} %pack_keys.1), calls=%async_computation.1 | async-start | bytes 2621440 | tf_op jit(solution)/shard_map/all_to_all | solution.py:314
  26.8 8.8 %collective-permute-start = (bf16[256,1408]{1,0:T(8,128)(2,1)S(1)}, bf16[256,1408]{1,0:T(8,128)(2,1)S(1)}, u32[]{:S(2)}, u32[]{:S(2)}) collective-permute-start(bf16[256,1408]{1,0:T(8,128)(2,1)S(1)} %bitcast.17), channel_id=1, source_target_pairs={{0,4},{1,5},{2,6},{3,7},{4,0},{5,1},{6,2},{7,3},{8,12},{9,13},{10,... | collective-permute-start | bytes 2162696 | tf_op jit(solution)/shard_map/ppermute | solution.py:319
  35.6 6.9 %all-to-all-done.1 = bf16[4,64,2560]{2,1,0:T(8,128)(2,1)S(1)} async-done(((bf16[4,64,2560]{2,1,0:T(8,128)(2,1)}), bf16[4,64,2560]{2,1,0:T(8,128)(2,1)S(1)}, u32[]{:S(2)}, u32[]{:S(2)}) %all-to-all-start.1) | async-done | bytes 1310752 | tf_op jit(solution)/shard_map/all_to_all | solution.py:314
  42.5 1.2 slice_select_fusion
  43.7 6.2 %collective-permute-start.3 = (bf16[256,1280]{1,0:T(8,128)(2,1)}, bf16[256,1280]{1,0:T(8,128)(2,1)S(1)}, u32[]{:S(2)}, u32[]{:S(2)}) collective-permute-start(bf16[256,1280]{1,0:T(8,128)(2,1)} %get-tuple-element.23), channel_id=1, source_target_pairs={{0,8},{8,16},{16,24},{24,32},{32,40},{40,48},{48,56},{56,64},{64,7... | collective-permute-start | bytes 1966088 | tf_op jit(solution)/shard_map/ppermute | solution.py:325
  49.9 1.9 %collective-permute-start.2 = (bf16[256,1280]{1,0:T(8,128)(2,1)}, bf16[256,1280]{1,0:T(8,128)(2,1)}, u32[]{:S(2)}, u32[]{:S(2)}) collective-permute-start(bf16[256,1280]{1,0:T(8,128)(2,1)} %get-tuple-element.24), channel_id=1, source_target_pairs={{0,8},{8,0},{16,24},{24,16},{32,40},{40,32},{48,56},{56,48},{64,72... | collective-permute-start | bytes 1966088 | tf_op jit(solution)/shard_map/ppermute | solution.py:330
  51.8 0.1 add_select_fusion.bias_ref
  51.9 14.6 %collective-permute-done.far = bf16[256,1408]{1,0:T(8,128)(2,1)S(1)} collective-permute-done((bf16[256,1408]{1,0:T(8,128)(2,1)S(1)}, bf16[256,1408]{1,0:T(8,128)(2,1)S(1)}, u32[]{:S(2)}, u32[]{:S(2)}) %collective-permute-start) | collective-permute-done | bytes 720928 | tf_op jit(solution)/shard_map/ppermute | solution.py:319
  66.5 0.0 collective-permute-done.3.w3.rest_1_
  66.5 0.0 collective-permute-done.2.w2.rest_0_
  66.5 4.3 %stats.1.own_stats = f32[16,512]{1,0:T(8,128)S(1)} custom-call(f32[4]{0:T(128)S(1)} %add_select_fusion.bias_ref, bf16[256,1408]{1,0:T(8,128)(2,1)S(1)} %bitcast.18, bf16[256,1408]{1,0:T(8,128)(2,1)S(1)} %collective-permute-done.far, bf16[256,2560]{1,0:T(8,128)(2,1)S(1)} %bitcast.14, bf16[256,1280]{1,0:T(8,128)(2,1)} %collective-permute-done.2.w2.rest_0_, ...), custom_call_target="tpu_custom_call" | custom-call | flops 1342177280 | bytes 1966080 | tf_op jit(solution)/shard_map/stats/pallas_call | solution.py:154
  70.8 7.1 %collective-permute-start.4 = (f32[16,512]{1,0:T(8,128)S(1)}, f32[16,512]{1,0:T(8,128)S(1)}, u32[]{:S(2)}, u32[]{:S(2)}) collective-permute-start(f32[16,512]{1,0:T(8,128)S(1)} %stats.1.own_stats), channel_id=1, source_target_pairs={{0,4},{1,5},{2,6},{3,7},{4,0},{5,1},{6,2},{7,3},{8,12},{9,13},{10,... | collective-permute-start | bytes 98312 | tf_op jit(solution)/shard_map/ppermute | solution.py:319
  77.9 0.1 pad_add_fusion.place
  78.0 1.4 collective-permute-done.4.far_stats
  79.4 5.4 %grads23.1 = (f32[640,512]{1,0:T(8,128)S(1)}, bf16[256,1280]{1,0:T(8,128)(2,1)}, bf16[256,1280]{1,0:T(8,128)(2,1)}) custom-call(f32[4]{0:T(128)S(1)} %add_select_fusion.bias_ref, s32[2]{0:T(128)S(1)} %pad_add_fusion.place, f32[16,512]{1,0:T(8,128)S(1)} %stats.1.own_stats, f32[16,512]{1,0:T(8,128)S(1)} %collective-permute-done.4.far_stats, ...), custom_call_target="tpu_custom_call" | custom-call | flops 1677721600 | bytes 5898240 | tf_op jit(solution)/shard_map/grads23/pallas_call | solution.py:234
  84.8 0.0 copy-start.2
  84.9 1.1 copy-done.2
  85.9 4.9 %collective-permute-start.5 = (bf16[256,1280]{1,0:T(8,128)(2,1)}, bf16[256,1280]{1,0:T(8,128)(2,1)}, u32[]{:S(2)}, u32[]{:S(2)}) collective-permute-start(bf16[256,1280]{1,0:T(8,128)(2,1)} %get-tuple-element.16), channel_id=1, source_target_pairs={{0,8},{8,0},{16,24},{24,16},{32,40},{40,32},{48,56},{56,48},{64,72... | collective-permute-start | bytes 1966088 | tf_op jit(solution)/shard_map/ppermute | solution.py:330
  90.8 2.1 %collective-permute-start.6 = (bf16[256,1280]{1,0:T(8,128)(2,1)}, bf16[256,1280]{1,0:T(8,128)(2,1)S(1)}, u32[]{:S(2)}, u32[]{:S(2)}) collective-permute-start(bf16[256,1280]{1,0:T(8,128)(2,1)} %get-tuple-element.17), channel_id=1, source_target_pairs={{8,0},{16,8},{24,16},{32,24},{40,32},{48,40},{56,48},{64,56},{72,6... | collective-permute-start | bytes 1966088 | tf_op jit(solution)/shard_map/ppermute | solution.py:325
  92.9 0.0 copy-start.3
  92.9 1.3 copy-done.3
  94.2 3.1 %grads1.1 = (f32[640,512]{1,0:T(8,128)S(1)}, bf16[256,1280]{1,0:T(8,128)(2,1)S(1)}) custom-call(f32[4]{0:T(128)S(1)} %add_select_fusion.bias_ref, s32[2]{0:T(128)S(1)} %pad_add_fusion.place, f32[16,512]{1,0:T(8,128)S(1)} %stats.1.own_stats, f32[16,512]{1,0:T(8,128)S(1)} %collective-permute-done.4.far_stats, bf16[256,1408]{1,0:T(8,128)(2,1)S(1)} %bitcast.20, ...), custom_call_target="tpu_custom_call" | custom-call | flops 838860800 | bytes 5898240 | tf_op jit(solution)/shard_map/grads1/pallas_call | solution.py:234
  97.3 0.0 collective-permute-done.5.swapped
  97.3 14.3 %collective-permute-done.6.side = bf16[256,1280]{1,0:T(8,128)(2,1)S(1)} collective-permute-done((bf16[256,1280]{1,0:T(8,128)(2,1)}, bf16[256,1280]{1,0:T(8,128)(2,1)S(1)}, u32[]{:S(2)}, u32[]{:S(2)}) %collective-permute-start.6) | collective-permute-done | bytes 655392 | tf_op jit(solution)/shard_map/ppermute | solution.py:325
  111.6 1.4 fold.1
  112.9 0.0 copy-start.5
  112.9 0.9 copy-done.5
  113.8 3.2 %grads0.1 = (bf16[512,640]{1,0:T(8,128)(2,1)S(1)}, f32[256,1280]{1,0:T(8,128)S(1)}) custom-call(f32[4]{0:T(128)S(1)} %add_select_fusion.bias_ref, s32[2]{0:T(128)S(1)} %pad_add_fusion.place, f32[16,512]{1,0:T(8,128)S(1)} %stats.1.own_stats, f32[16,512]{1,0:T(8,128)S(1)} %collective-permute-done.4.far_stats, bf16[256,1408]{1,0:T(8,128)(2,1)S(1)} %bitcast.21, ...), custom_call_target="tpu_custom_call" | custom-call | flops 838860800 | bytes 5898240 | tf_op jit(solution)/shard_map/grads0/pallas_call | solution.py:234
  117.0 0.0 copy-start
  117.0 1.1 copy-done
  118.1 0.0 copy-start.4
  118.1 0.8 copy-done.4
  118.9 0.0 copy-start.1
  118.9 7.8 %all-to-all-start.2 = ((bf16[8,64,640]{2,1,0:T(8,128)(2,1)}), bf16[8,64,640]{2,1,0:T(8,128)(2,1)S(1)}, u32[]{:S(2)}, u32[]{:S(2)}) async-start(bf16[8,64,640]{2,1,0:T(8,128)(2,1)} %bitcast.22), calls=%async_computation.2 | async-start | bytes 1310720 | tf_op jit(solution)/shard_map/all_to_all | solution.py:369
  126.8 1.9 %collective-permute-start.7 = (bf16[256,1280]{1,0:T(8,128)(2,1)}, bf16[256,1280]{1,0:T(8,128)(2,1)S(1)}, u32[]{:S(2)}, u32[]{:S(2)}) collective-permute-start(bf16[256,1280]{1,0:T(8,128)(2,1)} %copy-done.5), channel_id=1, source_target_pairs={{16,0},{24,8},{32,16},{40,24},{48,32},{56,40},{64,48},{72,56},{80,... | collective-permute-start | bytes 1966088 | tf_op jit(solution)/shard_map/ppermute | solution.py:325
  128.7 16.8 %collective-permute-done.7.back = bf16[256,1280]{1,0:T(8,128)(2,1)S(1)} collective-permute-done((bf16[256,1280]{1,0:T(8,128)(2,1)}, bf16[256,1280]{1,0:T(8,128)(2,1)S(1)}, u32[]{:S(2)}, u32[]{:S(2)}) %collective-permute-start.7) | collective-permute-done | bytes 655392 | tf_op jit(solution)/shard_map/ppermute | solution.py:325
  145.5 7.0 %all-to-all-done.2.halves = bf16[8,64,640]{2,1,0:T(8,128)(2,1)S(1)} async-done(((bf16[8,64,640]{2,1,0:T(8,128)(2,1)}), bf16[8,64,640]{2,1,0:T(8,128)(2,1)S(1)}, u32[]{:S(2)}, u32[]{:S(2)}) %all-to-all-start.2) | async-done | bytes 655392 | tf_op jit(solution)/shard_map/all_to_all | solution.py:369
  152.4 0.0 copy-done.1
  152.5 0.2 close.1
  152.7 13.8 %all_to_all.20.parts = bf16[4,64,1280]{2,1,0:T(8,128)(2,1)S(1)} all-to-all(bf16[4,64,1280]{2,1,0:T(8,128)(2,1)S(1)} %close.1), channel_id=1, replica_groups={{0,1,2,3},{4,5,6,7},{8,9,10,11},{12,13,14,15},{16,17,18,19},{20,21,22,2..., dimensions={0} | all-to-all | bytes 1310720 | tf_op jit(solution)/shard_map/all_to_all | solution.py:314
  166.5 1.1 unpack.1
Async XLA Ops:
  0.6 4.4 %copy-start.6 = (s32[64]{0:T(128)S(1)}, s32[64]{0:T(128)}, u32[]{:S(2)}) copy-start(s32[64]{0:T(128)} %param.11) | copy-start | bytes 772
  1.8 17.5 %collective-permute-start.1 = (bf16[2,64,2560]{2,1,0:T(8,128)(2,1)S(1)}, bf16[2,64,2560]{2,1,0:T(8,128)(2,1)S(1)}, u32[]{:S(2)}, u32[]{:S(2)}) collective-permute-start(bf16[2,64,2560]{2,1,0:T(8,128)(2,1)S(1)} %pad_maximum_fusion.near), channel_id=1, source_target_pairs={{0,16},{8,24},{16,32},{24,40},{32,48},{40,56},{48,64},{56,72},{64,... | collective-permute-start | bytes 1966088 | tf_op jit(solution)/shard_map/ppermute | solution.py:325
  8.8 14.4 %all-to-all-start = ((bf16[4,64,1408]{2,1,0:T(8,128)(2,1)}), bf16[4,64,1408]{2,1,0:T(8,128)(2,1)S(1)}, u32[]{:S(2)}, u32[]{:S(2)}) async-start(bf16[4,64,1408]{2,1,0:T(8,128)(2,1)} %pack_queries.1), calls=%async_computation | async-start | bytes 1441792 | tf_op jit(solution)/shard_map/all_to_all | solution.py:314
  23.2 19.3 %all-to-all-start.1 = ((bf16[4,64,2560]{2,1,0:T(8,128)(2,1)}), bf16[4,64,2560]{2,1,0:T(8,128)(2,1)S(1)}, u32[]{:S(2)}, u32[]{:S(2)}) async-start(bf16[4,64,2560]{2,1,0:T(8,128)(2,1)} %pack_keys.1), calls=%async_computation.1 | async-start | bytes 2621440 | tf_op jit(solution)/shard_map/all_to_all | solution.py:314
  26.8 39.7 %collective-permute-start = (bf16[256,1408]{1,0:T(8,128)(2,1)S(1)}, bf16[256,1408]{1,0:T(8,128)(2,1)S(1)}, u32[]{:S(2)}, u32[]{:S(2)}) collective-permute-start(bf16[256,1408]{1,0:T(8,128)(2,1)S(1)} %bitcast.17), channel_id=1, source_target_pairs={{0,4},{1,5},{2,6},{3,7},{4,0},{5,1},{6,2},{7,3},{8,12},{9,13},{10,... | collective-permute-start | bytes 2162696 | tf_op jit(solution)/shard_map/ppermute | solution.py:319
  43.7 22.8 %collective-permute-start.3 = (bf16[256,1280]{1,0:T(8,128)(2,1)}, bf16[256,1280]{1,0:T(8,128)(2,1)S(1)}, u32[]{:S(2)}, u32[]{:S(2)}) collective-permute-start(bf16[256,1280]{1,0:T(8,128)(2,1)} %get-tuple-element.23), channel_id=1, source_target_pairs={{0,8},{8,16},{16,24},{24,32},{32,40},{40,48},{48,56},{56,64},{64,7... | collective-permute-start | bytes 1966088 | tf_op jit(solution)/shard_map/ppermute | solution.py:325
  49.9 16.7 %collective-permute-start.2 = (bf16[256,1280]{1,0:T(8,128)(2,1)}, bf16[256,1280]{1,0:T(8,128)(2,1)}, u32[]{:S(2)}, u32[]{:S(2)}) collective-permute-start(bf16[256,1280]{1,0:T(8,128)(2,1)} %get-tuple-element.24), channel_id=1, source_target_pairs={{0,8},{8,0},{16,24},{24,16},{32,40},{40,32},{48,56},{56,48},{64,72... | collective-permute-start | bytes 1966088 | tf_op jit(solution)/shard_map/ppermute | solution.py:330
  70.8 8.6 %collective-permute-start.4 = (f32[16,512]{1,0:T(8,128)S(1)}, f32[16,512]{1,0:T(8,128)S(1)}, u32[]{:S(2)}, u32[]{:S(2)}) collective-permute-start(f32[16,512]{1,0:T(8,128)S(1)} %stats.1.own_stats), channel_id=1, source_target_pairs={{0,4},{1,5},{2,6},{3,7},{4,0},{5,1},{6,2},{7,3},{8,12},{9,13},{10,... | collective-permute-start | bytes 98312 | tf_op jit(solution)/shard_map/ppermute | solution.py:319
  84.8 1.1 copy-start.2
  85.9 11.4 %collective-permute-start.5 = (bf16[256,1280]{1,0:T(8,128)(2,1)}, bf16[256,1280]{1,0:T(8,128)(2,1)}, u32[]{:S(2)}, u32[]{:S(2)}) collective-permute-start(bf16[256,1280]{1,0:T(8,128)(2,1)} %get-tuple-element.16), channel_id=1, source_target_pairs={{0,8},{8,0},{16,24},{24,16},{32,40},{40,32},{48,56},{56,48},{64,72... | collective-permute-start | bytes 1966088 | tf_op jit(solution)/shard_map/ppermute | solution.py:330
  90.8 20.8 %collective-permute-start.6 = (bf16[256,1280]{1,0:T(8,128)(2,1)}, bf16[256,1280]{1,0:T(8,128)(2,1)S(1)}, u32[]{:S(2)}, u32[]{:S(2)}) collective-permute-start(bf16[256,1280]{1,0:T(8,128)(2,1)} %get-tuple-element.17), channel_id=1, source_target_pairs={{8,0},{16,8},{24,16},{32,24},{40,32},{48,40},{56,48},{64,56},{72,6... | collective-permute-start | bytes 1966088 | tf_op jit(solution)/shard_map/ppermute | solution.py:325
  92.9 1.3 copy-start.3
  112.9 0.9 copy-start.5
  117.0 1.1 copy-start
  118.1 0.8 copy-start.4
  118.9 33.5 %copy-start.1 = (f32[256,1280]{1,0:T(8,128)S(1)}, f32[256,1280]{1,0:T(8,128)}, u32[]{:S(2)}) copy-start(f32[256,1280]{1,0:T(8,128)} %copy-done) | copy-start | bytes 3932164
  118.9 33.5 %all-to-all-start.2 = ((bf16[8,64,640]{2,1,0:T(8,128)(2,1)}), bf16[8,64,640]{2,1,0:T(8,128)(2,1)S(1)}, u32[]{:S(2)}, u32[]{:S(2)}) async-start(bf16[8,64,640]{2,1,0:T(8,128)(2,1)} %bitcast.22), calls=%async_computation.2 | async-start | bytes 1310720 | tf_op jit(solution)/shard_map/all_to_all | solution.py:369
  126.8 18.7 %collective-permute-start.7 = (bf16[256,1280]{1,0:T(8,128)(2,1)}, bf16[256,1280]{1,0:T(8,128)(2,1)S(1)}, u32[]{:S(2)}, u32[]{:S(2)}) collective-permute-start(bf16[256,1280]{1,0:T(8,128)(2,1)} %copy-done.5), channel_id=1, source_target_pairs={{16,0},{24,8},{32,16},{40,24},{48,32},{56,40},{64,48},{72,56},{80,... | collective-permute-start | bytes 1966088 | tf_op jit(solution)/shard_map/ppermute | solution.py:325

commit v8 on v7

--- a/solution.py
+++ b/solution.py
@@ -98,10 +98,6 @@
     )(near, far)
 
 
-def both(own, far, cols):
-    return jnp.concatenate([own[:, cols], far[:, cols]], axis=0)
-
-
 META = slice(2 * GROUP * HDIM, (2 * GROUP + 1) * HDIM)
 
 
@@ -114,13 +110,12 @@
     return k_frame <= rows[FRAME_LANE : FRAME_LANE + 1, :]
 
 
-def stats_kernel(bias_ref, own, far, near, w2, w3, out_ref):
+def stats_kernel(bias_ref, tokens, own, near, w2, w3, out_ref):
     half = own.shape[0]
-    rows = both(own, far, META).astype(F32).T
-    mask = seen(rows, own)
+    mask = seen(tokens[:, META].astype(F32).T, own)
     out_ref[...] = jnp.zeros_like(out_ref)
     for head in range(GROUP):
-        queries = both(own, far, head_slice(head)).T
+        queries = tokens[:, head_slice(head)].T
         at = head_slice(2 * head)
         keys = [near[:, at], near[:, head_slice(2 * (GROUP + head))], w2[:, at], w3[:, at]]
         scores = jnp.dot(
@@ -148,165 +143,167 @@
     return pl.BlockSpec(memory_space=pltpu.VMEM)
 
 
-def stats(bias, own, far, near, w2, w3):
+def stats(name, bias, tokens, own, near, w2, w3):
     half = own.shape[0]
-    pairs = GROUP * 2 * half * 4 * half
+    pairs = GROUP * half * 4 * half
     return pl.pallas_call(
         stats_kernel,
-        out_shape=jax.ShapeDtypeStruct((16, 2 * half), F32),
+        out_shape=jax.ShapeDtypeStruct((16, half), F32),
         in_specs=[smem()] + [vmem()] * 5,
         out_specs=vmem(),
         compiler_params=params(),
-        cost_estimate=cost(4 * pairs * HDIM, 6 * half * GROUP * HDIM * 2, pairs),
-        name="stats",
-    )(bias, own, far, near, w2, w3)
-
-
-def log_total(own_stats, far_stats):
-    half = own_stats.shape[1] // 2
-    turned = jnp.concatenate([far_stats[:, half:], far_stats[:, :half]], axis=1)
-    own_peak, own_sum = own_stats[:8, :], own_stats[8:, :]
-    far_peak, far_sum = turned[:8], turned[8:]
-    peak = jnp.maximum(own_peak, far_peak)
-    own_part = own_sum * jnp.exp2(own_peak - peak)
-    return peak + jnp.log2(own_part + far_sum * jnp.exp2(far_peak - peak))
-
-
-def grads_kernel(roles, bias_ref, place, own_stats, far_stats, own, far, *rest):
+        cost_estimate=cost(4 * pairs * HDIM, 5 * half * GROUP * HDIM * 2, pairs),
+        name=name,
+    )(bias, tokens, own, near, w2, w3)
+
+
+def log_total(one, other):
+    one_peak, one_sum = one[:8, :], one[8:, :]
+    other_peak, other_sum = other[:8, :], other[8:, :]
+    peak = jnp.maximum(one_peak, other_peak)
+    one_part = one_sum * jnp.exp2(one_peak - peak)
+    return peak + jnp.log2(one_part + other_sum * jnp.exp2(other_peak - peak))
+
+
+def grads_kernel(roles, parts_in, dq_in, last, bias_ref, place, one, other, tokens, own, *rest):
     *rest, rows = rest
     blocks, rest = rest[: len(roles)], rest[len(roles) :]
-    if 3 in roles:
-        dq_out, *outs = rest
-    else:
-        dq_part, dq_out, *outs = rest
+    if parts_in:
+        parts, rest = rest[: len(roles)], rest[len(roles) :]
+    if dq_in:
+        dq_part, *rest = rest
+    dq_out, *outs = rest
     half = own.shape[0]
-    rows[...] = both(own, far, META).astype(F32).T
-    totals = log_total(own_stats, far_stats)
+    rows[...] = tokens[:, META].astype(F32).T
+    totals = log_total(one, other)
     for head in range(GROUP):
-        q_cols, g_cols = head_slice(head), head_slice(GROUP + head)
-        queries, grads = both(own, far, q_cols), both(own, far, g_cols)
+        q_cols = head_slice(head)
+        queries, grads = tokens[:, q_cols], tokens[:, head_slice(GROUP + head)]
         first = place[0] * GROUP + head
         dot = rows[pl.ds(first, 1), :] + rows[pl.ds(LOW_LANE + first, 1), :]
-        total = totals[head : head + 1]
         at = [2 * (GROUP + head) if role == 1 else 2 * head for role in roles]
         keys = jnp.concatenate([ref[:, head_slice(a)] for ref, a in zip(blocks, at)], axis=0)
         values = jnp.concatenate([ref[:, head_slice(a + 1)] for ref, a in zip(blocks, at)], axis=0)
         scores = jnp.dot(keys, queries.T, preferred_element_type=F32) * SCALE2
-        if 0 in roles:
-            scores = jnp.where(seen(rows, own), scores, NEG)
-        bounds = [total - bias_ref[role] for role in roles]
-        parts = [
-            jnp.exp2(scores[i * half : (i + 1) * half] - bound) for i, bound in enumerate(bounds)
-        ]
-        probs = jnp.concatenate(parts, axis=0)
+        pieces = []
+        for i, role in enumerate(roles):
+            piece = scores[i * half : (i + 1) * half]
+            if role == 0:
+                piece = jnp.where(seen(rows, own), piece, NEG)
+            pieces.append(jnp.exp2(piece - (totals[head : head + 1] - bias_ref[role])))
+        probs = jnp.concatenate(pieces, axis=0)
         dv = jnp.dot(probs.astype(BF16), grads, preferred_element_type=F32)
         dp = jnp.dot(values, grads.T, preferred_element_type=F32)
         ds = (probs * (dp - dot)).astype(BF16)
         dk = jnp.dot(ds, queries, preferred_element_type=F32) * FACTOR
         dq = jnp.dot(keys.T, ds, preferred_element_type=F32)
         for i, out in enumerate(outs):
-            out[:, head_slice(2 * head)] = dk[i * half : (i + 1) * half].astype(out.dtype)
-            out[:, head_slice(2 * head + 1)] = dv[i * half : (i + 1) * half].astype(out.dtype)
-        if 3 not in roles:
+            rows_of = slice(i * half, (i + 1) * half)
+            for cols, value in ((2 * head, dk[rows_of]), (2 * head + 1, dv[rows_of])):
+                if parts_in:
+                    value += parts[i][:, head_slice(cols)].astype(F32)
+                out[:, head_slice(cols)] = value.astype(out.dtype)
+        if dq_in:
             dq += dq_part[q_cols, :]
-        if 0 in roles:
-            turned = (dq * FACTOR).T.astype(BF16)
-            near_rows = pl.multiple_of(place[1] * half, half)
-            far_rows = pl.multiple_of((1 - place[1]) * half, half)
-            dq_out[pl.ds(near_rows, half), q_cols] = turned[:half]
-            dq_out[pl.ds(far_rows, half), q_cols] = turned[half:]
+        if last:
+            dq_out[:, q_cols] = (dq * FACTOR).T.astype(dq_out.dtype)
         else:
             dq_out[q_cols, :] = dq
 
 
-def grads(bias, place, own_stats, far_stats, own, far, roles, blocks, dq_part=None):
+def grads(name, common, tokens, own, blocks, kinds, parts=(), dq_part=None, dq_kind=None):
+    roles = tuple(blocks)
     half = own.shape[0]
     wide = GROUP * HDIM
-    pairs = GROUP * 2 * half * len(roles) * half
-    outs = [
-        jax.ShapeDtypeStruct((half, 2 * wide), F32 if role == 0 else BF16) for role in roles
-    ]
-    extra = [] if dq_part is None else [dq_part]
-    if 0 in roles:
-        dq_out = jax.ShapeDtypeStruct((2 * half, wide), BF16)
+    pairs = GROUP * half * len(roles) * half
+    extra = list(parts) + ([] if dq_part is None else [dq_part])
+    if dq_kind is None:
+        dq_out = jax.ShapeDtypeStruct((wide, half), F32)
     else:
-        dq_out = jax.ShapeDtypeStruct((wide, 2 * half), F32)
-    return pl.pallas_call(
-        functools.partial(grads_kernel, roles),
-        out_shape=[dq_out] + outs,
-        in_specs=[smem(), smem()] + [vmem()] * (4 + len(blocks) + len(extra)),
-        out_specs=[vmem()] * (1 + len(outs)),
-        scratch_shapes=[pltpu.VMEM((HDIM, 2 * half), F32)],
-        compiler_params=params(),
-        cost_estimate=cost(10 * pairs * HDIM, 18 * half * wide * 2, pairs),
-        name="grads" + "".join(str(role) for role in roles),
-    )(bias, place, own_stats, far_stats, own, far, *blocks, *extra)
-
-
-def fold_kernel(even_ref, d1, swapped, side, out):
+        dq_out = jax.ShapeDtypeStruct((half, wide), dq_kind)
+    return pl.pallas_call(
+        functools.partial(
+            grads_kernel, roles, bool(parts), dq_part is not None, dq_kind is not None
+        ),
+        out_shape=[dq_out] + [jax.ShapeDtypeStruct((half, 2 * wide), kind) for kind in kinds],
+        in_specs=[smem(), smem()] + [vmem()] * (4 + len(roles) + len(extra)),
+        out_specs=[vmem()] * (1 + len(kinds)),
+        scratch_shapes=[pltpu.VMEM((HDIM, half), F32)],
+        compiler_params=params(),
+        cost_estimate=cost(10 * pairs * HDIM, 12 * half * wide * 2, pairs),
+        name=name,
+    )(*common, tokens, own, *blocks.values(), *extra)
+
+
+def fold_kernel(even_ref, d1, swapped, side, dq_own, dq_back, out, dq_out):
     odd = 1.0 - even_ref[0].astype(F32)
     total = d1[...].astype(F32) + swapped[...].astype(F32) + side[...].astype(F32) * odd
     out[...] = total.astype(BF16)
-
-
-def fold(even, d1, swapped, side):
+    dq_out[...] = (dq_own[...] + dq_back[...].astype(F32)).astype(BF16)
+
+
+def fold(even, d1, swapped, side, dq_own, dq_back):
     return pl.pallas_call(
         fold_kernel,
-        out_shape=jax.ShapeDtypeStruct(d1.shape, BF16),
-        in_specs=[smem()] + [vmem()] * 3,
-        out_specs=vmem(),
+        out_shape=[
+            jax.ShapeDtypeStruct(d1.shape, BF16),
+            jax.ShapeDtypeStruct(dq_own.shape, BF16),
+        ],
+        in_specs=[smem()] + [vmem()] * 5,
+        out_specs=[vmem()] * 2,
         compiler_params=params(),
         cost_estimate=cost(3 * d1.size, 8 * d1.size),
         name="fold",
-    )(even, d1, swapped, side)
-
-
-def close_kernel(even_ref, d0, back, side, out):
+    )(even, d1, swapped, side, dq_own, dq_back)
+
+
+def close_kernel(even_ref, dq, d0, back, side, out):
     even = even_ref[0].astype(F32)
     tok = out.shape[1]
+    wide = dq.shape[1]
     for step in range(XN):
         rows = slice(step * tok, (step + 1) * tok)
         pair = d0[rows, :] + back[rows, :].astype(F32) + side[rows, :].astype(F32) * even
-        out[step] = pair.astype(BF16)
-
-
-def close(even, d0, back, side):
-    half, wide = d0.shape
+        out[step, :, :wide] = dq[rows, :]
+        out[step, :, wide:] = pair.astype(BF16)
+
+
+def close(even, dq, d0, back, side):
+    half, wide = dq.shape
     tok = half // XN
     return pl.pallas_call(
         close_kernel,
-        out_shape=jax.ShapeDtypeStruct((XN, tok, wide), BF16),
-        in_specs=[smem()] + [vmem()] * 3,
+        out_shape=jax.ShapeDtypeStruct((XN, tok, 3 * wide), BF16),
+        in_specs=[smem()] + [vmem()] * 4,
         out_specs=vmem(),
         compiler_params=params(),
-        cost_estimate=cost(3 * half * wide, 10 * half * wide),
+        cost_estimate=cost(6 * half * wide, 24 * half * wide),
         name="close",
-    )(even, d0, back, side)
-
-
-def unpack_kernel(parts, halves, dq, dk, dv):
+    )(even, dq, d0, back, side)
+
+
+def unpack_kernel(parts, dq, dk, dv):
     wide = GROUP * HDIM
     for group in range(XN):
-        total = halves[group].astype(F32) + halves[XN + group].astype(F32)
-        dq[:, group * wide : (group + 1) * wide] = total.astype(BF16)
+        dq[:, group * wide : (group + 1) * wide] = parts[group, :, :wide]
         for h in range(GROUP):
-            at = 2 * h * HDIM
+            at = wide + 2 * h * HDIM
             cols = slice((group * GROUP + h) * HDIM, (group * GROUP + h + 1) * HDIM)
             dk[:, cols] = parts[group, :, at : at + HDIM]
             dv[:, cols] = parts[group, :, at + HDIM : at + 2 * HDIM]
 
 
-def unpack(parts, halves):
+def unpack(parts):
     tok = parts.shape[1]
     return pl.pallas_call(
         unpack_kernel,
         out_shape=[jax.ShapeDtypeStruct((tok, HEADS * HDIM), BF16)] * 3,
-        in_specs=[vmem()] * 2,
+        in_specs=[vmem()],
         out_specs=[vmem()] * 3,
         compiler_params=params(),
-        cost_estimate=cost(0, 14 * tok * HEADS * HDIM),
+        cost_estimate=cost(0, 12 * tok * HEADS * HDIM),
         name="unpack",
-    )(parts, halves)
+    )(parts)
 
 
 def over_x(value):
@@ -357,18 +354,27 @@
     )
     bias = jnp.where(held, 0.0, NEG).astype(F32)
 
-    own_stats = stats(bias, own, far, near, w2, w3)
-    common = (bias, place, own_stats, across_z(own_stats), own, far)
-    dq_part, d2, d3 = grads(*common, (2, 3), (w2, w3))
+    window = (near, w2, w3)
+    own_near = stats("stats_own", bias, own, own, *window)
+    far_other = across_z(own_near)
+    far_near = stats("stats_far", bias, far, own, *window)
+    own_other = across_z(far_near)
+
+    common = (bias, place, far_near, far_other)
+    blocks = {0: near, 1: near, 2: w2, 3: w3}
+    dq_far, *parts = grads("grads_far", common, far, own, blocks, [BF16] * 4, dq_kind=BF16)
+    dq_back = across_z(dq_far)
+    common = (bias, place, own_near, own_other)
+    dq_part, d2, d3 = grads(
+        "grads_own23", common, own, own, {2: w2, 3: w3}, [BF16] * 2, parts[2:]
+    )
     side, swapped = along_row(d3, -1), in_chip(d2)
-    dq_part, d1 = grads(*common, (1,), (near,), dq_part)
-    held = fold(even, d1, swapped, side)
+    dq_own, d0, d1 = grads(
+        "grads_own01", common, own, own, {0: near, 1: near}, [F32, BF16], parts[:2], dq_part, F32
+    )
+    held, dq = fold(even, d1, swapped, side, dq_own, dq_back)
     back = along_row(held, -2)
-    dq_part, held = lax.optimization_barrier((dq_part, held))
-    dq, d0 = grads(*common, (0,), (near,), dq_part)
-    halves = lax.all_to_all(dq.reshape(-1, tok, GROUP * HDIM), "col", 0, 0)
-    back, halves = lax.optimization_barrier((back, halves))
-    return tuple(unpack(over_x(close(even, d0, back, side)), halves))
+    return tuple(unpack(over_x(close(even, dq, d0, back, side))))
 
 
 def solution(mesh):

time: 168 us -> 176 us (1.048)
  the two profiles are of different devices: /device:TPU:121 before, /device:TPU:240 now
where the time goes in v8:
time: 176 us; the launch traced here: 175 us
  waiting for transfers between devices  71.8 us (41%)
  starting transfers between devices  49.2 us (28%)
  Pallas kernels  24.1 us (14%)
  blocking collectives  19.8 us (11%)
  local copies, waits for them, and re-layouts  6.5 us (4%)
  other arithmetic  2.45 us (1%)
    ppermute x4, waiting for transfers between devices, along_row(): lax.ppermute(value, 'row', [(r, r + steps) for r in range(first, last)])  53.9 us
    ppermute x4, starting transfers between devices, across_z(): lax.ppermute(value, 'col', [(c, (c + XN) % count) for c in range(count)])  26.4 us
    all_to_all x1, blocking collectives, over_x(): return lax.all_to_all(value, 'col', 0, 0, axis_index_groups=groups)  19.8 us
    pallas_call x3, Pallas kernels, grads(): pl.pallas_call(functools.partial(grads_kernel, roles, bool(parts), dq_par...  12 us
    ppermute x4, starting transfers between devices, along_row(): lax.ppermute(value, 'row', [(r, r + steps) for r in range(first, last)])  11.1 us
    all_to_all x2, waiting for transfers between devices, over_x(): return lax.all_to_all(value, 'col', 0, 0, axis_index_groups=groups)  10.8 us
    all_to_all x2, starting transfers between devices, over_x(): return lax.all_to_all(value, 'col', 0, 0, axis_index_groups=groups)  7.84 us
    ppermute x4, waiting for transfers between devices, across_z(): lax.ppermute(value, 'col', [(c, (c + XN) % count) for c in range(count)])  7.12 us
  transfers between devices with their start and end apart: 12, of which 6 were waited for; matrix products, arithmetic and copies ran while one was open for 1% of the time, Pallas kernels for 10%

profile of v8, /device:TPU:240, one launch (start us, length us, event | category | flops | bytes accessed | tf_op | source)
XLA Modules:
  0.0 174.7 jit_solution(4640073982422437153)
XLA Ops:
  0.6 0.0 copy-start.6
  0.6 1.1 pad_maximum_fusion.near
  1.8 2.6 %collective-permute-start = (bf16[2,64,2560]{2,1,0:T(8,128)(2,1)S(1)}, bf16[2,64,2560]{2,1,0:T(8,128)(2,1)S(1)}, u32[]{:S(2)}, u32[]{:S(2)}) collective-permute-start(bf16[2,64,2560]{2,1,0:T(8,128)(2,1)S(1)} %pad_maximum_fusion.near), channel_id=1, source_target_pairs={{0,16},{8,24},{16,32},{24,40},{32,48},{40,56},{48,64},{56,72},{64,... | collective-permute-start | bytes 1966088 | tf_op jit(solution)/shard_map/ppermute | solution.py:322
  4.4 0.0 copy-done.6
  4.4 0.7 copy.9.f_ref
  5.1 3.1 %pack_queries.1 = bf16[4,64,1408]{2,1,0:T(8,128)(2,1)} custom-call(bf16[64,2560]{1,0:T(8,128)(2,1)} %q_any.1, bf16[64,2560]{1,0:T(8,128)(2,1)} %o_any.1, bf16[64,2560]{1,0:T(8,128)(2,1)} %g_any.1, s32[64,1]{1,0:T(8,128)} %copy.9.f_ref), custom_call_target="tpu_custom_call" | custom-call | flops 327680 | bytes 2293760 | tf_op jit(solution)/shard_map/pack_queries/pallas_call | solution.py:66
  8.2 4.3 %all-to-all-start = ((bf16[4,64,1408]{2,1,0:T(8,128)(2,1)}), bf16[4,64,1408]{2,1,0:T(8,128)(2,1)S(1)}, u32[]{:S(2)}, u32[]{:S(2)}) async-start(bf16[4,64,1408]{2,1,0:T(8,128)(2,1)} %pack_queries.1), calls=%async_computation | async-start | bytes 1441792 | tf_op jit(solution)/shard_map/all_to_all | solution.py:311
  12.5 7.6 %collective-permute-done.far = bf16[2,64,2560]{2,1,0:T(8,128)(2,1)S(1)} collective-permute-done((bf16[2,64,2560]{2,1,0:T(8,128)(2,1)S(1)}, bf16[2,64,2560]{2,1,0:T(8,128)(2,1)S(1)}, u32[]{:S(2)}, u32[]{:S(2)}) %collective-permute-start) | collective-permute-done | bytes 655392 | tf_op jit(solution)/shard_map/ppermute | solution.py:322
  20.1 1.3 pack_keys.1
  21.4 2.4 %all-to-all-done = bf16[4,64,1408]{2,1,0:T(8,128)(2,1)S(1)} async-done(((bf16[4,64,1408]{2,1,0:T(8,128)(2,1)}), bf16[4,64,1408]{2,1,0:T(8,128)(2,1)S(1)}, u32[]{:S(2)}, u32[]{:S(2)}) %all-to-all-start) | async-done | bytes 720928 | tf_op jit(solution)/shard_map/all_to_all | solution.py:311
  23.8 3.5 %all-to-all-start.1 = ((bf16[4,64,2560]{2,1,0:T(8,128)(2,1)}), bf16[4,64,2560]{2,1,0:T(8,128)(2,1)S(1)}, u32[]{:S(2)}, u32[]{:S(2)}) async-start(bf16[4,64,2560]{2,1,0:T(8,128)(2,1)} %pack_keys.1), calls=%async_computation.1 | async-start | bytes 2621440 | tf_op jit(solution)/shard_map/all_to_all | solution.py:311
  27.4 8.2 %collective-permute-start.3 = (bf16[256,1408]{1,0:T(8,128)(2,1)S(1)}, bf16[256,1408]{1,0:T(8,128)(2,1)}, u32[]{:S(2)}, u32[]{:S(2)}) collective-permute-start(bf16[256,1408]{1,0:T(8,128)(2,1)S(1)} %bitcast.19), channel_id=1, source_target_pairs={{0,4},{1,5},{2,6},{3,7},{4,0},{5,1},{6,2},{7,3},{8,12},{9,13},{10,... | collective-permute-start | bytes 2162696 | tf_op jit(solution)/shard_map/ppermute | solution.py:316
  35.6 8.4 %all-to-all-done.1 = bf16[4,64,2560]{2,1,0:T(8,128)(2,1)S(1)} async-done(((bf16[4,64,2560]{2,1,0:T(8,128)(2,1)}), bf16[4,64,2560]{2,1,0:T(8,128)(2,1)S(1)}, u32[]{:S(2)}, u32[]{:S(2)}) %all-to-all-start.1) | async-done | bytes 1310752 | tf_op jit(solution)/shard_map/all_to_all | solution.py:311
  44.0 1.2 slice_select_fusion
  45.2 1.9 %collective-permute-start.2 = (bf16[256,1280]{1,0:T(8,128)(2,1)}, bf16[256,1280]{1,0:T(8,128)(2,1)S(1)}, u32[]{:S(2)}, u32[]{:S(2)}) collective-permute-start(bf16[256,1280]{1,0:T(8,128)(2,1)} %get-tuple-element.29), channel_id=1, source_target_pairs={{0,8},{8,16},{16,24},{24,32},{32,40},{40,48},{48,56},{56,64},{64,7... | collective-permute-start | bytes 1966088 | tf_op jit(solution)/shard_map/ppermute | solution.py:322
  47.1 2.0 %collective-permute-start.1 = (bf16[256,1280]{1,0:T(8,128)(2,1)}, bf16[256,1280]{1,0:T(8,128)(2,1)S(1)}, u32[]{:S(2)}, u32[]{:S(2)}) collective-permute-start(bf16[256,1280]{1,0:T(8,128)(2,1)} %get-tuple-element.30), channel_id=1, source_target_pairs={{0,8},{8,0},{16,24},{24,16},{32,40},{40,32},{48,56},{56,48},{64,72... | collective-permute-start | bytes 1966088 | tf_op jit(solution)/shard_map/ppermute | solution.py:327
  49.1 0.1 pad_add_fusion.place
  49.2 0.1 add_select_fusion.bias_ref
  49.3 8.0 %collective-permute-done.2.w3.rest_3_.rest_1_ = bf16[256,1280]{1,0:T(8,128)(2,1)S(1)} collective-permute-done((bf16[256,1280]{1,0:T(8,128)(2,1)}, bf16[256,1280]{1,0:T(8,128)(2,1)S(1)}, u32[]{:S(2)}, u32[]{:S(2)}) %collective-permute-start.2) | collective-permute-done | bytes 655392 | tf_op jit(solution)/shard_map/ppermute | solution.py:322
  57.3 0.0 collective-permute-done.1.w2.rest_2_.rest_0_
  57.3 2.2 %stats_own.1.one = f32[16,256]{1,0:T(8,128)S(1)} custom-call(f32[4]{0:T(128)S(1)} %add_select_fusion.bias_ref, bf16[256,1408]{1,0:T(8,128)(2,1)S(1)} %bitcast.20, bf16[256,1408]{1,0:T(8,128)(2,1)S(1)} %bitcast.21, bf16[256,2560]{1,0:T(8,128)(2,1)S(1)} %bitcast.13, bf16[256,1280]{1,0:T(8,128)(2,1)S(1)} %collective-permute-done.1.w2.rest_2_.rest_0_, ...), custom_call_target="tpu_custom_call" | custom-call | flops 671088640 | bytes 1638400 | tf_op jit(solution)/shard_map/stats_own/pallas_call | solution.py:149
  59.5 8.2 %collective-permute-start.5 = (f32[16,256]{1,0:T(8,128)S(1)}, f32[16,256]{1,0:T(8,128)S(1)}, u32[]{:S(2)}, u32[]{:S(2)}) collective-permute-start(f32[16,256]{1,0:T(8,128)S(1)} %stats_own.1.one), channel_id=1, source_target_pairs={{0,4},{1,5},{2,6},{3,7},{4,0},{5,1},{6,2},{7,3},{8,12},{9,13},{10,... | collective-permute-start | bytes 49160 | tf_op jit(solution)/shard_map/ppermute | solution.py:316
  67.7 0.0 collective-permute-done.3.tokens
  67.7 2.8 %stats_far.1.one = f32[16,256]{1,0:T(8,128)S(1)} custom-call(f32[4]{0:T(128)S(1)} %add_select_fusion.bias_ref, bf16[256,1408]{1,0:T(8,128)(2,1)} %collective-permute-done.3.tokens, bf16[256,1408]{1,0:T(8,128)(2,1)S(1)} %bitcast.22, bf16[256,2560]{1,0:T(8,128)(2,1)S(1)} %bitcast.14, bf16[256,1280]{1,0:T(8,128)(2,1)S(1)} %collective-permute-done.1.w2.rest_2_.rest_0_, ...), custom_call_target="tpu_custom_call" | custom-call | flops 671088640 | bytes 1638400 | tf_op jit(solution)/shard_map/stats_far/pallas_call | solution.py:149
  70.6 3.9 %collective-permute-start.4 = (f32[16,256]{1,0:T(8,128)S(1)}, f32[16,256]{1,0:T(8,128)S(1)}, u32[]{:S(2)}, u32[]{:S(2)}) collective-permute-start(f32[16,256]{1,0:T(8,128)S(1)} %stats_far.1.one), channel_id=1, source_target_pairs={{0,4},{1,5},{2,6},{3,7},{4,0},{5,1},{6,2},{7,3},{8,12},{9,13},{10,... | collective-permute-start | bytes 49160 | tf_op jit(solution)/shard_map/ppermute | solution.py:316
  74.5 0.0 collective-permute-done.5.other
  74.5 5.5 %grads_far.1 = (bf16[256,640]{1,0:T(8,128)(2,1)}, bf16[256,1280]{1,0:T(8,128)(2,1)S(1)}, bf16[256,1280]{1,0:T(8,128)(2,1)S(1)}, bf16[256,1280]{1,0:T(8,128)(2,1)S(1)}, bf16[256,1280]{1,0:T(8,128)(2,1)S(1)}) custom-call(f32[4]{0:T(128)S(1)} %add_select_fusion.bias_ref, s32[2]{0:T(128)S(1)} %pad_add_fusion.place, f32[16,256]{1,0:T(8,128)S(1)} %stats_far.1.one, ...), custom_call_target="tpu_custom_call" | custom-call | flops 1677721600 | bytes 3932160 | tf_op jit(solution)/shard_map/grads_far/pallas_call | solution.py:224
  80.0 0.0 copy-start
  80.0 0.9 copy-done
  80.8 0.0 copy-start.2
  80.8 0.8 copy-done.2
  81.6 0.0 collective-permute-done.4.other
  81.7 3.7 %grads_own23.1 = (f32[640,256]{1,0:T(8,128)S(1)}, bf16[256,1280]{1,0:T(8,128)(2,1)}, bf16[256,1280]{1,0:T(8,128)(2,1)}) custom-call(f32[4]{0:T(128)S(1)} %add_select_fusion.bias_ref, s32[2]{0:T(128)S(1)} %pad_add_fusion.place, f32[16,256]{1,0:T(8,128)S(1)} %stats_own.1.one, f32[16,256]{1,0:T(8,128)S(1)} %collective-permute-done.4.other, ...), custom_call_target="tpu_custom_call" | custom-call | flops 838860800 | bytes 3932160 | tf_op jit(solution)/shard_map/grads_own23/pallas_call | solution.py:224
  85.4 0.0 copy-start.4
  85.4 0.8 copy-done.4
  86.2 1.9 %collective-permute-start.6 = (bf16[256,1280]{1,0:T(8,128)(2,1)}, bf16[256,1280]{1,0:T(8,128)(2,1)S(1)}, u32[]{:S(2)}, u32[]{:S(2)}) collective-permute-start(bf16[256,1280]{1,0:T(8,128)(2,1)} %get-tuple-element.22), channel_id=1, source_target_pairs={{0,8},{8,0},{16,24},{24,16},{32,40},{40,32},{48,56},{56,48},{64,72... | collective-permute-start | bytes 1966088 | tf_op jit(solution)/shard_map/ppermute | solution.py:327
  88.1 3.4 %collective-permute-start.7 = (bf16[256,1280]{1,0:T(8,128)(2,1)}, bf16[256,1280]{1,0:T(8,128)(2,1)S(1)}, u32[]{:S(2)}, u32[]{:S(2)}) collective-permute-start(bf16[256,1280]{1,0:T(8,128)(2,1)} %get-tuple-element.23), channel_id=1, source_target_pairs={{8,0},{16,8},{24,16},{32,24},{40,32},{48,40},{56,48},{64,56},{72,6... | collective-permute-start | bytes 1966088 | tf_op jit(solution)/shard_map/ppermute | solution.py:322
  91.5 6.0 %collective-permute-start.8 = (bf16[256,640]{1,0:T(8,128)(2,1)}, bf16[256,640]{1,0:T(8,128)(2,1)}, u32[]{:S(2)}, u32[]{:S(2)}) collective-permute-start(bf16[256,640]{1,0:T(8,128)(2,1)} %get-tuple-element.25), channel_id=1, source_target_pairs={{0,4},{1,5},{2,6},{3,7},{4,0},{5,1},{6,2},{7,3},{8,12},{9,13},{10,... | collective-permute-start | bytes 983048 | tf_op jit(solution)/shard_map/ppermute | solution.py:316
  97.6 0.0 copy-start.1
  97.6 1.1 copy-done.1
  98.6 0.0 copy-start.3
  98.6 1.1 copy-done.3
  99.7 0.0 copy-start.5
  99.7 1.1 copy-done.5
  100.8 2.8 %grads_own01.1 = (f32[256,640]{1,0:T(8,128)S(1)}, f32[256,1280]{1,0:T(8,128)S(1)}, bf16[256,1280]{1,0:T(8,128)(2,1)S(1)}) custom-call(f32[4]{0:T(128)S(1)} %add_select_fusion.bias_ref, s32[2]{0:T(128)S(1)} %pad_add_fusion.place, f32[16,256]{1,0:T(8,128)S(1)} %stats_own.1.one, f32[16,256]{1,0:T(8,128)S(1)} %collective-permute-done.4.other, ...), custom_call_target="tpu_custom_call" | custom-call | flops 838860800 | bytes 3932160 | tf_op jit(solution)/shard_map/grads_own01/pallas_call | solution.py:224
  103.6 7.1 %collective-permute-done.8.dq_back = bf16[256,640]{1,0:T(8,128)(2,1)} collective-permute-done((bf16[256,640]{1,0:T(8,128)(2,1)}, bf16[256,640]{1,0:T(8,128)(2,1)}, u32[]{:S(2)}, u32[]{:S(2)}) %collective-permute-start.8) | collective-permute-done | bytes 327712 | tf_op jit(solution)/shard_map/ppermute | solution.py:316
  110.8 0.0 collective-permute-done.6.swapped
  110.8 0.0 collective-permute-done.7.side
  110.8 1.3 fold.1
  112.1 3.3 %collective-permute-start.9 = (bf16[256,1280]{1,0:T(8,128)(2,1)S(1)}, bf16[256,1280]{1,0:T(8,128)(2,1)S(1)}, u32[]{:S(2)}, u32[]{:S(2)}) collective-permute-start(bf16[256,1280]{1,0:T(8,128)(2,1)S(1)} %get-tuple-element.28), channel_id=1, source_target_pairs={{16,0},{24,8},{32,16},{40,24},{48,32},{56,40},{64,48},{72,56},{80,... | collective-permute-start | bytes 1966088 | tf_op jit(solution)/shard_map/ppermute | solution.py:322
  115.4 38.3 %collective-permute-done.9.back = bf16[256,1280]{1,0:T(8,128)(2,1)S(1)} collective-permute-done((bf16[256,1280]{1,0:T(8,128)(2,1)S(1)}, bf16[256,1280]{1,0:T(8,128)(2,1)S(1)}, u32[]{:S(2)}, u32[]{:S(2)}) %collective-permute-start.9) | collective-permute-done | bytes 655392 | tf_op jit(solution)/shard_map/ppermute | solution.py:322
  153.6 0.2 close.1
  153.9 19.8 %all_to_all.15.parts = bf16[4,64,1920]{2,1,0:T(8,128)(2,1)S(1)} all-to-all(bf16[4,64,1920]{2,1,0:T(8,128)(2,1)S(1)} %close.1), channel_id=1, replica_groups={{0,1,2,3},{4,5,6,7},{8,9,10,11},{12,13,14,15},{16,17,18,19},{20,21,22,2..., dimensions={0} | all-to-all | bytes 1966080 | tf_op jit(solution)/shard_map/all_to_all | solution.py:311
  173.7 1.1 unpack.1
Async XLA Ops:
  0.6 3.7 %copy-start.6 = (s32[64]{0:T(128)S(1)}, s32[64]{0:T(128)}, u32[]{:S(2)}) copy-start(s32[64]{0:T(128)} %param.11) | copy-start | bytes 772
  1.8 18.4 %collective-permute-start = (bf16[2,64,2560]{2,1,0:T(8,128)(2,1)S(1)}, bf16[2,64,2560]{2,1,0:T(8,128)(2,1)S(1)}, u32[]{:S(2)}, u32[]{:S(2)}) collective-permute-start(bf16[2,64,2560]{2,1,0:T(8,128)(2,1)S(1)} %pad_maximum_fusion.near), channel_id=1, source_target_pairs={{0,16},{8,24},{16,32},{24,40},{32,48},{40,56},{48,64},{56,72},{64,... | collective-permute-start | bytes 1966088 | tf_op jit(solution)/shard_map/ppermute | solution.py:322
  8.2 15.6 %all-to-all-start = ((bf16[4,64,1408]{2,1,0:T(8,128)(2,1)}), bf16[4,64,1408]{2,1,0:T(8,128)(2,1)S(1)}, u32[]{:S(2)}, u32[]{:S(2)}) async-start(bf16[4,64,1408]{2,1,0:T(8,128)(2,1)} %pack_queries.1), calls=%async_computation | async-start | bytes 1441792 | tf_op jit(solution)/shard_map/all_to_all | solution.py:311
  23.8 20.2 %all-to-all-start.1 = ((bf16[4,64,2560]{2,1,0:T(8,128)(2,1)}), bf16[4,64,2560]{2,1,0:T(8,128)(2,1)S(1)}, u32[]{:S(2)}, u32[]{:S(2)}) async-start(bf16[4,64,2560]{2,1,0:T(8,128)(2,1)} %pack_keys.1), calls=%async_computation.1 | async-start | bytes 2621440 | tf_op jit(solution)/shard_map/all_to_all | solution.py:311
  27.4 40.4 %collective-permute-start.3 = (bf16[256,1408]{1,0:T(8,128)(2,1)S(1)}, bf16[256,1408]{1,0:T(8,128)(2,1)}, u32[]{:S(2)}, u32[]{:S(2)}) collective-permute-start(bf16[256,1408]{1,0:T(8,128)(2,1)S(1)} %bitcast.19), channel_id=1, source_target_pairs={{0,4},{1,5},{2,6},{3,7},{4,0},{5,1},{6,2},{7,3},{8,12},{9,13},{10,... | collective-permute-start | bytes 2162696 | tf_op jit(solution)/shard_map/ppermute | solution.py:316
  45.2 12.1 %collective-permute-start.2 = (bf16[256,1280]{1,0:T(8,128)(2,1)}, bf16[256,1280]{1,0:T(8,128)(2,1)S(1)}, u32[]{:S(2)}, u32[]{:S(2)}) collective-permute-start(bf16[256,1280]{1,0:T(8,128)(2,1)} %get-tuple-element.29), channel_id=1, source_target_pairs={{0,8},{8,16},{16,24},{24,32},{32,40},{40,48},{48,56},{56,64},{64,7... | collective-permute-start | bytes 1966088 | tf_op jit(solution)/shard_map/ppermute | solution.py:322
  47.1 10.2 %collective-permute-start.1 = (bf16[256,1280]{1,0:T(8,128)(2,1)}, bf16[256,1280]{1,0:T(8,128)(2,1)S(1)}, u32[]{:S(2)}, u32[]{:S(2)}) collective-permute-start(bf16[256,1280]{1,0:T(8,128)(2,1)} %get-tuple-element.30), channel_id=1, source_target_pairs={{0,8},{8,0},{16,24},{24,16},{32,40},{40,32},{48,56},{56,48},{64,72... | collective-permute-start | bytes 1966088 | tf_op jit(solution)/shard_map/ppermute | solution.py:327
  59.5 14.9 %collective-permute-start.5 = (f32[16,256]{1,0:T(8,128)S(1)}, f32[16,256]{1,0:T(8,128)S(1)}, u32[]{:S(2)}, u32[]{:S(2)}) collective-permute-start(f32[16,256]{1,0:T(8,128)S(1)} %stats_own.1.one), channel_id=1, source_target_pairs={{0,4},{1,5},{2,6},{3,7},{4,0},{5,1},{6,2},{7,3},{8,12},{9,13},{10,... | collective-permute-start | bytes 49160 | tf_op jit(solution)/shard_map/ppermute | solution.py:316
  70.6 11.1 %collective-permute-start.4 = (f32[16,256]{1,0:T(8,128)S(1)}, f32[16,256]{1,0:T(8,128)S(1)}, u32[]{:S(2)}, u32[]{:S(2)}) collective-permute-start(f32[16,256]{1,0:T(8,128)S(1)} %stats_far.1.one), channel_id=1, source_target_pairs={{0,4},{1,5},{2,6},{3,7},{4,0},{5,1},{6,2},{7,3},{8,12},{9,13},{10,... | collective-permute-start | bytes 49160 | tf_op jit(solution)/shard_map/ppermute | solution.py:316
  80.0 0.9 copy-start
  80.8 0.8 copy-start.2
  85.4 0.8 copy-start.4
  86.2 24.5 %collective-permute-start.6 = (bf16[256,1280]{1,0:T(8,128)(2,1)}, bf16[256,1280]{1,0:T(8,128)(2,1)S(1)}, u32[]{:S(2)}, u32[]{:S(2)}) collective-permute-start(bf16[256,1280]{1,0:T(8,128)(2,1)} %get-tuple-element.22), channel_id=1, source_target_pairs={{0,8},{8,0},{16,24},{24,16},{32,40},{40,32},{48,56},{56,48},{64,72... | collective-permute-start | bytes 1966088 | tf_op jit(solution)/shard_map/ppermute | solution.py:327
  88.1 22.6 %collective-permute-start.7 = (bf16[256,1280]{1,0:T(8,128)(2,1)}, bf16[256,1280]{1,0:T(8,128)(2,1)S(1)}, u32[]{:S(2)}, u32[]{:S(2)}) collective-permute-start(bf16[256,1280]{1,0:T(8,128)(2,1)} %get-tuple-element.23), channel_id=1, source_target_pairs={{8,0},{16,8},{24,16},{32,24},{40,32},{48,40},{56,48},{64,56},{72,6... | collective-permute-start | bytes 1966088 | tf_op jit(solution)/shard_map/ppermute | solution.py:322
  91.5 19.3 %collective-permute-start.8 = (bf16[256,640]{1,0:T(8,128)(2,1)}, bf16[256,640]{1,0:T(8,128)(2,1)}, u32[]{:S(2)}, u32[]{:S(2)}) collective-permute-start(bf16[256,640]{1,0:T(8,128)(2,1)} %get-tuple-element.25), channel_id=1, source_target_pairs={{0,4},{1,5},{2,6},{3,7},{4,0},{5,1},{6,2},{7,3},{8,12},{9,13},{10,... | collective-permute-start | bytes 983048 | tf_op jit(solution)/shard_map/ppermute | solution.py:316
  97.6 1.1 copy-start.1
  98.6 1.1 copy-start.3
  99.7 1.1 copy-start.5
  112.1 41.6 %collective-permute-start.9 = (bf16[256,1280]{1,0:T(8,128)(2,1)S(1)}, bf16[256,1280]{1,0:T(8,128)(2,1)S(1)}, u32[]{:S(2)}, u32[]{:S(2)}) collective-permute-start(bf16[256,1280]{1,0:T(8,128)(2,1)S(1)} %get-tuple-element.28), channel_id=1, source_target_pairs={{16,0},{24,8},{32,16},{40,24},{48,32},{56,40},{64,48},{72,56},{80,... | collective-permute-start | bytes 1966088 | tf_op jit(solution)/shard_map/ppermute | solution.py:322

commit v9 on v8

--- a/solution.py
+++ b/solution.py
@@ -75,27 +75,27 @@
     )(query, saved_out, grad_out, frames)
 
 
-def pack_keys_kernel(near, far, out):
+def pack_keys_kernel(k_any, v_any, out, held, sems):
+    load_all((k_any, v_any), held, sems)
     for head in range(HEADS):
         group, h = divmod(head, GROUP)
         cols = slice(head * HDIM, (head + 1) * HDIM)
-        for block, ref in enumerate((near, far)):
-            for at in range(2):
-                first = (2 * (block * GROUP + h) + at) * HDIM
-                out[group, :, first : first + HDIM] = ref[at, :, cols]
-
-
-def pack_keys(near, far):
-    _, tok, width = near.shape
+        for at in range(2):
+            out[group, :, (2 * h + at) * HDIM : (2 * h + at + 1) * HDIM] = held[at, :, cols]
+
+
+def pack_keys(key, value):
+    tok, width = key.shape
     return pl.pallas_call(
         pack_keys_kernel,
-        out_shape=jax.ShapeDtypeStruct((XN, tok, 4 * GROUP * HDIM), BF16),
-        in_specs=[vmem()] * 2,
-        out_specs=vmem(),
-        compiler_params=params(),
-        cost_estimate=cost(0, 16 * tok * width),
+        out_shape=jax.ShapeDtypeStruct((XN, tok, 2 * GROUP * HDIM), BF16),
+        in_specs=[pl.BlockSpec(memory_space=pl.ANY)] * 2,
+        out_specs=vmem(),
+        scratch_shapes=[pltpu.VMEM((2, tok, width), BF16), pltpu.SemaphoreType.DMA((2,))],
+        compiler_params=params(60),
+        cost_estimate=cost(0, 8 * tok * width),
         name="pack_keys",
-    )(near, far)
+    )(key, value)
 
 
 META = slice(2 * GROUP * HDIM, (2 * GROUP + 1) * HDIM)
@@ -110,14 +110,13 @@
     return k_frame <= rows[FRAME_LANE : FRAME_LANE + 1, :]
 
 
-def stats_kernel(bias_ref, tokens, own, near, w2, w3, out_ref):
+def stats_kernel(bias_ref, tokens, own, w0, w1, w2, w3, out_ref):
     half = own.shape[0]
     mask = seen(tokens[:, META].astype(F32).T, own)
     out_ref[...] = jnp.zeros_like(out_ref)
     for head in range(GROUP):
         queries = tokens[:, head_slice(head)].T
-        at = head_slice(2 * head)
-        keys = [near[:, at], near[:, head_slice(2 * (GROUP + head))], w2[:, at], w3[:, at]]
+        keys = [ref[:, head_slice(2 * head)] for ref in (w0, w1, w2, w3)]
         scores = jnp.dot(
             jnp.concatenate(keys, axis=0), queries, preferred_element_type=F32
         ) * SCALE2
@@ -143,18 +142,22 @@
     return pl.BlockSpec(memory_space=pltpu.VMEM)
 
 
-def stats(name, bias, tokens, own, near, w2, w3):
+def stats(name, bias, tokens, own, window):
     half = own.shape[0]
     pairs = GROUP * half * 4 * half
     return pl.pallas_call(
         stats_kernel,
         out_shape=jax.ShapeDtypeStruct((16, half), F32),
-        in_specs=[smem()] + [vmem()] * 5,
+        in_specs=[smem()] + [vmem()] * 6,
         out_specs=vmem(),
         compiler_params=params(),
         cost_estimate=cost(4 * pairs * HDIM, 5 * half * GROUP * HDIM * 2, pairs),
         name=name,
-    )(bias, tokens, own, near, w2, w3)
+    )(bias, tokens, own, *window)
+
+
+def shape_of(shape, kind, kept):
+    return pltpu.VMEM(shape, kind) if kept else jax.ShapeDtypeStruct(shape, kind)
 
 
 def log_total(one, other):
@@ -181,9 +184,8 @@
         queries, grads = tokens[:, q_cols], tokens[:, head_slice(GROUP + head)]
         first = place[0] * GROUP + head
         dot = rows[pl.ds(first, 1), :] + rows[pl.ds(LOW_LANE + first, 1), :]
-        at = [2 * (GROUP + head) if role == 1 else 2 * head for role in roles]
-        keys = jnp.concatenate([ref[:, head_slice(a)] for ref, a in zip(blocks, at)], axis=0)
-        values = jnp.concatenate([ref[:, head_slice(a + 1)] for ref, a in zip(blocks, at)], axis=0)
+        keys = jnp.concatenate([ref[:, head_slice(2 * head)] for ref in blocks], axis=0)
+        values = jnp.concatenate([ref[:, head_slice(2 * head + 1)] for ref in blocks], axis=0)
         scores = jnp.dot(keys, queries.T, preferred_element_type=F32) * SCALE2
         pieces = []
         for i, role in enumerate(roles):
@@ -211,75 +213,69 @@
             dq_out[q_cols, :] = dq
 
 
-def grads(name, common, tokens, own, blocks, kinds, parts=(), dq_part=None, dq_kind=None):
-    roles = tuple(blocks)
+def grads(name, common, tokens, own, window, roles, outs, parts=(), dq_part=None, dq_out=None):
     half = own.shape[0]
     wide = GROUP * HDIM
     pairs = GROUP * half * len(roles) * half
     extra = list(parts) + ([] if dq_part is None else [dq_part])
-    if dq_kind is None:
-        dq_out = jax.ShapeDtypeStruct((wide, half), F32)
+    last = dq_out is not None
+    if last:
+        dq_shape = shape_of((half, wide), *dq_out)
     else:
-        dq_out = jax.ShapeDtypeStruct((half, wide), dq_kind)
-    return pl.pallas_call(
-        functools.partial(
-            grads_kernel, roles, bool(parts), dq_part is not None, dq_kind is not None
-        ),
-        out_shape=[dq_out] + [jax.ShapeDtypeStruct((half, 2 * wide), kind) for kind in kinds],
+        dq_shape = shape_of((wide, half), F32, True)
+    return pl.pallas_call(
+        functools.partial(grads_kernel, roles, bool(parts), dq_part is not None, last),
+        out_shape=[dq_shape] + [shape_of((half, 2 * wide), *out) for out in outs],
         in_specs=[smem(), smem()] + [vmem()] * (4 + len(roles) + len(extra)),
-        out_specs=[vmem()] * (1 + len(kinds)),
+        out_specs=[vmem()] * (1 + len(outs)),
         scratch_shapes=[pltpu.VMEM((HDIM, half), F32)],
         compiler_params=params(),
         cost_estimate=cost(10 * pairs * HDIM, 12 * half * wide * 2, pairs),
         name=name,
-    )(*common, tokens, own, *blocks.values(), *extra)
-
-
-def fold_kernel(even_ref, d1, swapped, side, dq_own, dq_back, out, dq_out):
+    )(*common, tokens, own, *[window[role] for role in roles], *extra)
+
+
+def fold_kernel(even_ref, d1, swapped, side, out):
     odd = 1.0 - even_ref[0].astype(F32)
     total = d1[...].astype(F32) + swapped[...].astype(F32) + side[...].astype(F32) * odd
     out[...] = total.astype(BF16)
-    dq_out[...] = (dq_own[...] + dq_back[...].astype(F32)).astype(BF16)
-
-
-def fold(even, d1, swapped, side, dq_own, dq_back):
+
+
+def fold(even, d1, swapped, side):
     return pl.pallas_call(
         fold_kernel,
-        out_shape=[
-            jax.ShapeDtypeStruct(d1.shape, BF16),
-            jax.ShapeDtypeStruct(dq_own.shape, BF16),
-        ],
-        in_specs=[smem()] + [vmem()] * 5,
-        out_specs=[vmem()] * 2,
+        out_shape=jax.ShapeDtypeStruct(d1.shape, BF16),
+        in_specs=[smem()] + [vmem()] * 3,
+        out_specs=vmem(),
         compiler_params=params(),
         cost_estimate=cost(3 * d1.size, 8 * d1.size),
         name="fold",
-    )(even, d1, swapped, side, dq_own, dq_back)
-
-
-def close_kernel(even_ref, dq, d0, back, side, out):
+    )(even, d1, swapped, side)
+
+
+def close_kernel(even_ref, dq_own, dq_back, d0, back, side, out):
     even = even_ref[0].astype(F32)
     tok = out.shape[1]
-    wide = dq.shape[1]
+    wide = dq_own.shape[1]
     for step in range(XN):
         rows = slice(step * tok, (step + 1) * tok)
         pair = d0[rows, :] + back[rows, :].astype(F32) + side[rows, :].astype(F32) * even
-        out[step, :, :wide] = dq[rows, :]
+        out[step, :, :wide] = (dq_own[rows, :] + dq_back[rows, :].astype(F32)).astype(BF16)
         out[step, :, wide:] = pair.astype(BF16)
 
 
-def close(even, dq, d0, back, side):
-    half, wide = dq.shape
+def close(even, dq_own, dq_back, d0, back, side):
+    half, wide = dq_own.shape
     tok = half // XN
     return pl.pallas_call(
         close_kernel,
         out_shape=jax.ShapeDtypeStruct((XN, tok, 3 * wide), BF16),
-        in_specs=[smem()] + [vmem()] * 4,
+        in_specs=[smem()] + [vmem()] * 5,
         out_specs=vmem(),
         compiler_params=params(),
         cost_estimate=cost(6 * half * wide, 24 * half * wide),
         name="close",
-    )(even, dq, d0, back, side)
+    )(even, dq_own, dq_back, d0, back, side)
 
 
 def unpack_kernel(parts, dq, dk, dv):
@@ -334,14 +330,14 @@
     even = is_even.astype(jnp.int32).reshape(1)
     tok = query.shape[0]
     half = XN * tok
-    wide = 2 * GROUP * HDIM
-
-    kv = jnp.stack([key, value])
-    kv_far = along_row(kv, 2)
-    own = over_x(pack_queries(query, saved_out, grad_out, frame_ids[:, None])).reshape(half, -1)
+
+    qg = pack_queries(query, saved_out, grad_out, frame_ids[:, None])
+    w0 = over_x(pack_keys(key, value))
+    qg, w0 = lax.optimization_barrier((qg, w0))
+    w0 = w0.reshape(half, -1)
+    own = over_x(qg).reshape(half, -1)
     far = across_z(own)
-    near = over_x(pack_keys(kv, kv_far)).reshape(half, -1)
-    w0, w1 = near[:, :wide], near[:, wide:]
+    w1 = along_row(w0, 2)
     w3 = along_row(jnp.where(is_even, w0, w1), 1)
     w2 = in_chip(w1)
     held = jnp.stack(
@@ -354,27 +350,28 @@
     )
     bias = jnp.where(held, 0.0, NEG).astype(F32)
 
-    window = (near, w2, w3)
-    own_near = stats("stats_own", bias, own, own, *window)
+    window = (w0, w1, w2, w3)
+    own_near = stats("stats_own", bias, own, own, window)
     far_other = across_z(own_near)
-    far_near = stats("stats_far", bias, far, own, *window)
+    far_near = stats("stats_far", bias, far, own, window)
     own_other = across_z(far_near)
 
     common = (bias, place, far_near, far_other)
-    blocks = {0: near, 1: near, 2: w2, 3: w3}
-    dq_far, *parts = grads("grads_far", common, far, own, blocks, [BF16] * 4, dq_kind=BF16)
+    kept, sent, summed = (BF16, True), (BF16, False), (F32, True)
+    dq_far, *parts = grads(
+        "grads_far", common, far, own, window, (0, 1, 2, 3), [kept] * 4, dq_out=sent
+    )
     dq_back = across_z(dq_far)
     common = (bias, place, own_near, own_other)
     dq_part, d2, d3 = grads(
-        "grads_own23", common, own, own, {2: w2, 3: w3}, [BF16] * 2, parts[2:]
+        "grads_own23", common, own, own, window, (2, 3), [sent] * 2, parts[2:]
     )
     side, swapped = along_row(d3, -1), in_chip(d2)
     dq_own, d0, d1 = grads(
-        "grads_own01", common, own, own, {0: near, 1: near}, [F32, BF16], parts[:2], dq_part, F32
-    )
-    held, dq = fold(even, d1, swapped, side, dq_own, dq_back)
-    back = along_row(held, -2)
-    return tuple(unpack(over_x(close(even, dq, d0, back, side))))
+        "grads_own01", common, own, own, window, (0, 1), [summed, kept], parts[:2], dq_part, summed
+    )
+    back = along_row(fold(even, d1, swapped, side), -2)
+    return tuple(unpack(over_x(close(even, dq_own, dq_back, d0, back, side))))
 
 
 def solution(mesh):

time: 176 us -> 165 us (0.938)
  the two profiles are of different devices: /device:TPU:240 before, /device:TPU:248 now
where the time goes in v9:
time: 165 us; the launch traced here: 164 us
  waiting for transfers between devices  68.6 us (42%)
  starting transfers between devices  46.7 us (28%)
  Pallas kernels  23.2 us (14%)
  blocking collectives  17.3 us (10%)
  local copies, waits for them, and re-layouts  6.39 us (4%)
    ppermute x4, waiting for transfers between devices, across_z(): lax.ppermute(value, 'col', [(c, (c + XN) % count) for c in range(count)])  40.7 us
    ppermute x4, starting transfers between devices, across_z(): lax.ppermute(value, 'col', [(c, (c + XN) % count) for c in range(count)])  25.1 us
    all_to_all x2, waiting for transfers between devices, over_x(): return lax.all_to_all(value, 'col', 0, 0, axis_index_groups=groups)  17.7 us
    all_to_all x1, blocking collectives, over_x(): return lax.all_to_all(value, 'col', 0, 0, axis_index_groups=groups)  17.3 us
    pallas_call x3, Pallas kernels, grads(): pl.pallas_call(functools.partial(grads_kernel, roles, bool(parts), dq_par...  11.4 us
    ppermute x4, waiting for transfers between devices, along_row(): lax.ppermute(value, 'row', [(r, r + steps) for r in range(first, last)])  10.2 us
    ppermute x4, starting transfers between devices, along_row(): lax.ppermute(value, 'row', [(r, r + steps) for r in range(first, last)])  9.94 us
    all_to_all x2, starting transfers between devices, over_x(): return lax.all_to_all(value, 'col', 0, 0, axis_index_groups=groups)  7.8 us
  transfers between devices with their start and end apart: 12, of which 6 were waited for; matrix products, arithmetic and copies ran while one was open for 1% of the time, Pallas kernels for 10%

profile of v9, /device:TPU:248, one launch (start us, length us, event | category | flops | bytes accessed | tf_op | source)
XLA Modules:
  0.0 164.2 jit_solution(6514049962120844163)
XLA Ops:
  0.6 0.0 copy-start.8
  0.6 2.1 %pack_keys.1 = bf16[4,64,1280]{2,1,0:T(8,128)(2,1)} custom-call(bf16[64,2560]{1,0:T(8,128)(2,1)} %k_any.1, bf16[64,2560]{1,0:T(8,128)(2,1)} %v_any.1), custom_call_target="tpu_custom_call" | custom-call | bytes 1310720 | tf_op jit(solution)/shard_map/pack_keys/pallas_call | solution.py:89
  2.7 4.3 %all-to-all-start = ((bf16[4,64,1280]{2,1,0:T(8,128)(2,1)}), bf16[4,64,1280]{2,1,0:T(8,128)(2,1)S(1)}, u32[]{:S(2)}, u32[]{:S(2)}) async-start(bf16[4,64,1280]{2,1,0:T(8,128)(2,1)} %pack_keys.1), calls=%async_computation | async-start | bytes 1310720 | tf_op jit(solution)/shard_map/all_to_all | solution.py:307
  7.0 0.0 copy-done.8
  7.0 0.7 copy.9.f_ref
  7.7 3.1 %pack_queries.1 = bf16[4,64,1408]{2,1,0:T(8,128)(2,1)} custom-call(bf16[64,2560]{1,0:T(8,128)(2,1)} %q_any.1, bf16[64,2560]{1,0:T(8,128)(2,1)} %o_any.1, bf16[64,2560]{1,0:T(8,128)(2,1)} %g_any.1, s32[64,1]{1,0:T(8,128)} %copy.9.f_ref), custom_call_target="tpu_custom_call" | custom-call | flops 327680 | bytes 2293760 | tf_op jit(solution)/shard_map/pack_queries/pallas_call | solution.py:66
  10.8 7.1 %all-to-all-done = bf16[4,64,1280]{2,1,0:T(8,128)(2,1)S(1)} async-done(((bf16[4,64,1280]{2,1,0:T(8,128)(2,1)}), bf16[4,64,1280]{2,1,0:T(8,128)(2,1)S(1)}, u32[]{:S(2)}, u32[]{:S(2)}) %all-to-all-start) | async-done | bytes 655392 | tf_op jit(solution)/shard_map/all_to_all | solution.py:307
  17.9 1.3 collective-permute-start
  19.2 3.5 %all-to-all-start.1 = ((bf16[4,64,1408]{2,1,0:T(8,128)(2,1)}), bf16[4,64,1408]{2,1,0:T(8,128)(2,1)S(1)}, u32[]{:S(2)}, u32[]{:S(2)}) async-start(bf16[4,64,1408]{2,1,0:T(8,128)(2,1)} %pack_queries.1), calls=%async_computation.1 | async-start | bytes 1441792 | tf_op jit(solution)/shard_map/all_to_all | solution.py:307
  22.7 10.6 %all-to-all-done.1 = bf16[4,64,1408]{2,1,0:T(8,128)(2,1)S(1)} async-done(((bf16[4,64,1408]{2,1,0:T(8,128)(2,1)}), bf16[4,64,1408]{2,1,0:T(8,128)(2,1)S(1)}, u32[]{:S(2)}, u32[]{:S(2)}) %all-to-all-start.1) | async-done | bytes 720928 | tf_op jit(solution)/shard_map/all_to_all | solution.py:307
  33.4 8.2 %collective-permute-start.3 = (bf16[256,1408]{1,0:T(8,128)(2,1)S(1)}, bf16[256,1408]{1,0:T(8,128)(2,1)}, u32[]{:S(2)}, u32[]{:S(2)}) collective-permute-start(bf16[256,1408]{1,0:T(8,128)(2,1)S(1)} %bitcast.11), channel_id=1, source_target_pairs={{0,4},{1,5},{2,6},{3,7},{4,0},{5,1},{6,2},{7,3},{8,12},{9,13},{10,... | collective-permute-start | bytes 2162696 | tf_op jit(solution)/shard_map/ppermute | solution.py:312
  41.6 0.0 collective-permute-done.w1.rest_1_
  41.6 1.0 broadcast_select_fusion
  42.6 1.9 %collective-permute-start.2 = (bf16[256,1280]{1,0:T(8,128)(2,1)}, bf16[256,1280]{1,0:T(8,128)(2,1)S(1)}, u32[]{:S(2)}, u32[]{:S(2)}) collective-permute-start(bf16[256,1280]{1,0:T(8,128)(2,1)} %broadcast_select_fusion), channel_id=1, source_target_pairs={{0,8},{8,16},{16,24},{24,32},{32,40},{40,48},{48,56},{56,64},{64,7... | collective-permute-start | bytes 1966088 | tf_op jit(solution)/shard_map/ppermute | solution.py:318
  44.5 1.9 %collective-permute-start.1 = (bf16[256,1280]{1,0:T(8,128)(2,1)S(1)}, bf16[256,1280]{1,0:T(8,128)(2,1)S(1)}, u32[]{:S(2)}, u32[]{:S(2)}) collective-permute-start(bf16[256,1280]{1,0:T(8,128)(2,1)S(1)} %collective-permute-done.w1.rest_1_), channel_id=1, source_target_pairs={{0,8},{8,0},{16,24},{24,16},{32,40},{40,32},{48,56},{56,48},{64,72... | collective-permute-start | bytes 1966088 | tf_op jit(solution)/shard_map/ppermute | solution.py:323
  46.5 0.1 pad_add_fusion.place
  46.5 0.1 add_select_fusion.bias_ref
  46.6 8.1 %collective-permute-done.2.w3.rest_3_.rest_1_ = bf16[256,1280]{1,0:T(8,128)(2,1)S(1)} collective-permute-done((bf16[256,1280]{1,0:T(8,128)(2,1)}, bf16[256,1280]{1,0:T(8,128)(2,1)S(1)}, u32[]{:S(2)}, u32[]{:S(2)}) %collective-permute-start.2) | collective-permute-done | bytes 655392 | tf_op jit(solution)/shard_map/ppermute | solution.py:318
  54.7 0.0 collective-permute-done.1.w2.rest_2_.rest_0_
  54.7 2.2 %stats_own.1.one = f32[16,256]{1,0:T(8,128)S(1)} custom-call(f32[4]{0:T(128)S(1)} %add_select_fusion.bias_ref, bf16[256,1408]{1,0:T(8,128)(2,1)S(1)} %bitcast.12, bf16[256,1408]{1,0:T(8,128)(2,1)S(1)} %bitcast.13, bf16[256,1280]{1,0:T(8,128)(2,1)S(1)} %bitcast.21, bf16[256,1280]{1,0:T(8,128)(2,1)S(1)} %collective-permute-done.w1.rest_1_, ...), custom_call_target="tpu_custom_call" | custom-call | flops 671088640 | bytes 1638400 | tf_op jit(solution)/shard_map/stats_own/pallas_call | solution.py:148
  56.9 1.9 %collective-permute-start.5 = (f32[16,256]{1,0:T(8,128)S(1)}, f32[16,256]{1,0:T(8,128)S(1)}, u32[]{:S(2)}, u32[]{:S(2)}) collective-permute-start(f32[16,256]{1,0:T(8,128)S(1)} %stats_own.1.one), channel_id=1, source_target_pairs={{0,4},{1,5},{2,6},{3,7},{4,0},{5,1},{6,2},{7,3},{8,12},{9,13},{10,... | collective-permute-start | bytes 49160 | tf_op jit(solution)/shard_map/ppermute | solution.py:312
  58.8 7.4 %collective-permute-done.3.tokens = bf16[256,1408]{1,0:T(8,128)(2,1)} collective-permute-done((bf16[256,1408]{1,0:T(8,128)(2,1)S(1)}, bf16[256,1408]{1,0:T(8,128)(2,1)}, u32[]{:S(2)}, u32[]{:S(2)}) %collective-permute-start.3) | collective-permute-done | bytes 720928 | tf_op jit(solution)/shard_map/ppermute | solution.py:312
  66.2 2.8 %stats_far.1.one = f32[16,256]{1,0:T(8,128)S(1)} custom-call(f32[4]{0:T(128)S(1)} %add_select_fusion.bias_ref, bf16[256,1408]{1,0:T(8,128)(2,1)} %collective-permute-done.3.tokens, bf16[256,1408]{1,0:T(8,128)(2,1)S(1)} %bitcast.14, bf16[256,1280]{1,0:T(8,128)(2,1)S(1)} %bitcast.22, bf16[256,1280]{1,0:T(8,128)(2,1)S(1)} %collective-permute-done.w1.rest_1_, ...), custom_call_target="tpu_custom_call" | custom-call | flops 671088640 | bytes 1638400 | tf_op jit(solution)/shard_map/stats_far/pallas_call | solution.py:148
  69.0 11.8 %collective-permute-start.4 = (f32[16,256]{1,0:T(8,128)S(1)}, f32[16,256]{1,0:T(8,128)S(1)}, u32[]{:S(2)}, u32[]{:S(2)}) collective-permute-start(f32[16,256]{1,0:T(8,128)S(1)} %stats_far.1.one), channel_id=1, source_target_pairs={{0,4},{1,5},{2,6},{3,7},{4,0},{5,1},{6,2},{7,3},{8,12},{9,13},{10,... | collective-permute-start | bytes 49160 | tf_op jit(solution)/shard_map/ppermute | solution.py:312
  80.8 0.0 collective-permute-done.5.other
  80.8 4.8 %grads_far.1 = (bf16[256,640]{1,0:T(8,128)(2,1)S(1)}, bf16[256,1280]{1,0:T(8,128)(2,1)S(1)}, bf16[256,1280]{1,0:T(8,128)(2,1)S(1)}, bf16[256,1280]{1,0:T(8,128)(2,1)S(1)}, bf16[256,1280]{1,0:T(8,128)(2,1)S(1)}) custom-call(f32[4]{0:T(128)S(1)} %add_select_fusion.bias_ref, s32[2]{0:T(128)S(1)} %pad_add_fusion.place, f32[16,256]{1,0:T(8,128)S(1)} %stats_far.1.one, ...), custom_call_target="tpu_custom_call" | custom-call | flops 1677721600 | bytes 3932160 | tf_op jit(solution)/shard_map/grads_far/pallas_call | solution.py:226
  85.6 0.0 copy-start
  85.6 0.8 copy-done
  86.5 0.0 copy-start.6
  86.5 0.7 copy-done.6
  87.2 0.0 copy-start.2
  87.2 0.0 collective-permute-done.4.other
  87.2 3.7 %grads_own23.1 = (f32[640,256]{1,0:T(8,128)S(1)}, bf16[256,1280]{1,0:T(8,128)(2,1)}, bf16[256,1280]{1,0:T(8,128)(2,1)}) custom-call(f32[4]{0:T(128)S(1)} %add_select_fusion.bias_ref, s32[2]{0:T(128)S(1)} %pad_add_fusion.place, f32[16,256]{1,0:T(8,128)S(1)} %stats_own.1.one, f32[16,256]{1,0:T(8,128)S(1)} %collective-permute-done.4.other, ...), custom_call_target="tpu_custom_call" | custom-call | flops 838860800 | bytes 3932160 | tf_op jit(solution)/shard_map/grads_own23/pallas_call | solution.py:226
  90.9 0.0 copy-done.2
  90.9 0.0 copy-start.4
  90.9 0.8 copy-done.4
  91.8 1.9 %collective-permute-start.7 = (bf16[256,1280]{1,0:T(8,128)(2,1)}, bf16[256,1280]{1,0:T(8,128)(2,1)S(1)}, u32[]{:S(2)}, u32[]{:S(2)}) collective-permute-start(bf16[256,1280]{1,0:T(8,128)(2,1)} %get-tuple-element.27), channel_id=1, source_target_pairs={{0,8},{8,0},{16,24},{24,16},{32,40},{40,32},{48,56},{56,48},{64,72... | collective-permute-start | bytes 1966088 | tf_op jit(solution)/shard_map/ppermute | solution.py:323
  93.7 3.5 %collective-permute-start.8 = (bf16[256,1280]{1,0:T(8,128)(2,1)}, bf16[256,1280]{1,0:T(8,128)(2,1)S(1)}, u32[]{:S(2)}, u32[]{:S(2)}) collective-permute-start(bf16[256,1280]{1,0:T(8,128)(2,1)} %get-tuple-element.28), channel_id=1, source_target_pairs={{8,0},{16,8},{24,16},{32,24},{40,32},{48,40},{56,48},{64,56},{72,6... | collective-permute-start | bytes 1966088 | tf_op jit(solution)/shard_map/ppermute | solution.py:318
  97.2 0.0 copy-start.1
  97.2 1.1 copy-done.1
  98.2 0.0 copy-start.3
  98.3 1.1 copy-done.3
  99.3 0.0 copy-start.5
  99.3 1.1 copy-done.5
  100.4 2.9 %grads_own01.1 = (f32[256,640]{1,0:T(8,128)S(1)}, f32[256,1280]{1,0:T(8,128)S(1)}, bf16[256,1280]{1,0:T(8,128)(2,1)S(1)}) custom-call(f32[4]{0:T(128)S(1)} %add_select_fusion.bias_ref, s32[2]{0:T(128)S(1)} %pad_add_fusion.place, f32[16,256]{1,0:T(8,128)S(1)} %stats_own.1.one, f32[16,256]{1,0:T(8,128)S(1)} %collective-permute-done.4.other, ...), custom_call_target="tpu_custom_call" | custom-call | flops 838860800 | bytes 3932160 | tf_op jit(solution)/shard_map/grads_own01/pallas_call | solution.py:226
  103.3 0.0 collective-permute-done.7.swapped
  103.3 2.1 %collective-permute-done.8.side = bf16[256,1280]{1,0:T(8,128)(2,1)S(1)} collective-permute-done((bf16[256,1280]{1,0:T(8,128)(2,1)}, bf16[256,1280]{1,0:T(8,128)(2,1)S(1)}, u32[]{:S(2)}, u32[]{:S(2)}) %collective-permute-start.8) | collective-permute-done | bytes 655392 | tf_op jit(solution)/shard_map/ppermute | solution.py:318
  105.4 0.0 copy-start.7
  105.4 0.3 fold.1
  105.7 3.3 %collective-permute-start.9 = (bf16[256,1280]{1,0:T(8,128)(2,1)S(1)}, bf16[256,1280]{1,0:T(8,128)(2,1)S(1)}, u32[]{:S(2)}, u32[]{:S(2)}) collective-permute-start(bf16[256,1280]{1,0:T(8,128)(2,1)S(1)} %fold.1), channel_id=1, source_target_pairs={{16,0},{24,8},{32,16},{40,24},{48,32},{56,40},{64,48},{72,56},{80,... | collective-permute-start | bytes 1966088 | tf_op jit(solution)/shard_map/ppermute | solution.py:318
  109.0 0.0 copy-done.7
  109.0 3.2 %collective-permute-start.6 = (bf16[256,640]{1,0:T(8,128)(2,1)S(1)}, bf16[256,640]{1,0:T(8,128)(2,1)S(1)}, u32[]{:S(2)}, u32[]{:S(2)}) collective-permute-start(bf16[256,640]{1,0:T(8,128)(2,1)S(1)} %copy-done.7), channel_id=1, source_target_pairs={{0,4},{1,5},{2,6},{3,7},{4,0},{5,1},{6,2},{7,3},{8,12},{9,13},{10,... | collective-permute-start | bytes 983048 | tf_op jit(solution)/shard_map/ppermute | solution.py:312
  112.1 33.4 %collective-permute-done.6.dq_back = bf16[256,640]{1,0:T(8,128)(2,1)S(1)} collective-permute-done((bf16[256,640]{1,0:T(8,128)(2,1)S(1)}, bf16[256,640]{1,0:T(8,128)(2,1)S(1)}, u32[]{:S(2)}, u32[]{:S(2)}) %collective-permute-start.6) | collective-permute-done | bytes 327712 | tf_op jit(solution)/shard_map/ppermute | solution.py:312
  145.5 0.0 collective-permute-done.9.back
  145.5 0.3 close.1
  145.8 17.3 %all_to_all.15.parts = bf16[4,64,1920]{2,1,0:T(8,128)(2,1)S(1)} all-to-all(bf16[4,64,1920]{2,1,0:T(8,128)(2,1)S(1)} %close.1), channel_id=1, replica_groups={{0,1,2,3},{4,5,6,7},{8,9,10,11},{12,13,14,15},{16,17,18,19},{20,21,22,2..., dimensions={0} | all-to-all | bytes 1966080 | tf_op jit(solution)/shard_map/all_to_all | solution.py:307
  163.1 1.1 unpack.1
Async XLA Ops:
  0.6 6.4 %copy-start.8 = (s32[64]{0:T(128)S(1)}, s32[64]{0:T(128)}, u32[]{:S(2)}) copy-start(s32[64]{0:T(128)} %param.11) | copy-start | bytes 772
  2.7 15.2 %all-to-all-start = ((bf16[4,64,1280]{2,1,0:T(8,128)(2,1)}), bf16[4,64,1280]{2,1,0:T(8,128)(2,1)S(1)}, u32[]{:S(2)}, u32[]{:S(2)}) async-start(bf16[4,64,1280]{2,1,0:T(8,128)(2,1)} %pack_keys.1), calls=%async_computation | async-start | bytes 1310720 | tf_op jit(solution)/shard_map/all_to_all | solution.py:307
  17.9 23.7 %collective-permute-start = (bf16[256,1280]{1,0:T(8,128)(2,1)S(1)}, bf16[256,1280]{1,0:T(8,128)(2,1)S(1)}, u32[]{:S(2)}, u32[]{:S(2)}) collective-permute-start(bf16[256,1280]{1,0:T(8,128)(2,1)S(1)} %bitcast.20), channel_id=1, source_target_pairs={{0,16},{8,24},{16,32},{24,40},{32,48},{40,56},{48,64},{56,72},{64,... | collective-permute-start | bytes 1966088 | tf_op jit(solution)/shard_map/ppermute | solution.py:318
  19.2 14.1 %all-to-all-start.1 = ((bf16[4,64,1408]{2,1,0:T(8,128)(2,1)}), bf16[4,64,1408]{2,1,0:T(8,128)(2,1)S(1)}, u32[]{:S(2)}, u32[]{:S(2)}) async-start(bf16[4,64,1408]{2,1,0:T(8,128)(2,1)} %pack_queries.1), calls=%async_computation.1 | async-start | bytes 1441792 | tf_op jit(solution)/shard_map/all_to_all | solution.py:307
  33.4 32.9 %collective-permute-start.3 = (bf16[256,1408]{1,0:T(8,128)(2,1)S(1)}, bf16[256,1408]{1,0:T(8,128)(2,1)}, u32[]{:S(2)}, u32[]{:S(2)}) collective-permute-start(bf16[256,1408]{1,0:T(8,128)(2,1)S(1)} %bitcast.11), channel_id=1, source_target_pairs={{0,4},{1,5},{2,6},{3,7},{4,0},{5,1},{6,2},{7,3},{8,12},{9,13},{10,... | collective-permute-start | bytes 2162696 | tf_op jit(solution)/shard_map/ppermute | solution.py:312
  42.6 12.1 %collective-permute-start.2 = (bf16[256,1280]{1,0:T(8,128)(2,1)}, bf16[256,1280]{1,0:T(8,128)(2,1)S(1)}, u32[]{:S(2)}, u32[]{:S(2)}) collective-permute-start(bf16[256,1280]{1,0:T(8,128)(2,1)} %broadcast_select_fusion), channel_id=1, source_target_pairs={{0,8},{8,16},{16,24},{24,32},{32,40},{40,48},{48,56},{56,64},{64,7... | collective-permute-start | bytes 1966088 | tf_op jit(solution)/shard_map/ppermute | solution.py:318
  44.5 10.2 %collective-permute-start.1 = (bf16[256,1280]{1,0:T(8,128)(2,1)S(1)}, bf16[256,1280]{1,0:T(8,128)(2,1)S(1)}, u32[]{:S(2)}, u32[]{:S(2)}) collective-permute-start(bf16[256,1280]{1,0:T(8,128)(2,1)S(1)} %collective-permute-done.w1.rest_1_), channel_id=1, source_target_pairs={{0,8},{8,0},{16,24},{24,16},{32,40},{40,32},{48,56},{56,48},{64,72... | collective-permute-start | bytes 1966088 | tf_op jit(solution)/shard_map/ppermute | solution.py:323
  56.9 23.9 %collective-permute-start.5 = (f32[16,256]{1,0:T(8,128)S(1)}, f32[16,256]{1,0:T(8,128)S(1)}, u32[]{:S(2)}, u32[]{:S(2)}) collective-permute-start(f32[16,256]{1,0:T(8,128)S(1)} %stats_own.1.one), channel_id=1, source_target_pairs={{0,4},{1,5},{2,6},{3,7},{4,0},{5,1},{6,2},{7,3},{8,12},{9,13},{10,... | collective-permute-start | bytes 49160 | tf_op jit(solution)/shard_map/ppermute | solution.py:312
  69.0 18.2 %collective-permute-start.4 = (f32[16,256]{1,0:T(8,128)S(1)}, f32[16,256]{1,0:T(8,128)S(1)}, u32[]{:S(2)}, u32[]{:S(2)}) collective-permute-start(f32[16,256]{1,0:T(8,128)S(1)} %stats_far.1.one), channel_id=1, source_target_pairs={{0,4},{1,5},{2,6},{3,7},{4,0},{5,1},{6,2},{7,3},{8,12},{9,13},{10,... | collective-permute-start | bytes 49160 | tf_op jit(solution)/shard_map/ppermute | solution.py:312
  85.6 0.9 copy-start
  86.5 0.7 copy-start.6
  87.2 3.7 %copy-start.2 = (bf16[256,1280]{1,0:T(8,128)(2,1)}, bf16[256,1280]{1,0:T(8,128)(2,1)S(1)}, u32[]{:S(2)}) copy-start(bf16[256,1280]{1,0:T(8,128)(2,1)S(1)} %get-tuple-element.19.rest_3_) | copy-start | bytes 1966084
  90.9 0.8 copy-start.4
  91.8 11.5 %collective-permute-start.7 = (bf16[256,1280]{1,0:T(8,128)(2,1)}, bf16[256,1280]{1,0:T(8,128)(2,1)S(1)}, u32[]{:S(2)}, u32[]{:S(2)}) collective-permute-start(bf16[256,1280]{1,0:T(8,128)(2,1)} %get-tuple-element.27), channel_id=1, source_target_pairs={{0,8},{8,0},{16,24},{24,16},{32,40},{40,32},{48,56},{56,48},{64,72... | collective-permute-start | bytes 1966088 | tf_op jit(solution)/shard_map/ppermute | solution.py:323
  93.7 11.7 %collective-permute-start.8 = (bf16[256,1280]{1,0:T(8,128)(2,1)}, bf16[256,1280]{1,0:T(8,128)(2,1)S(1)}, u32[]{:S(2)}, u32[]{:S(2)}) collective-permute-start(bf16[256,1280]{1,0:T(8,128)(2,1)} %get-tuple-element.28), channel_id=1, source_target_pairs={{8,0},{16,8},{24,16},{32,24},{40,32},{48,40},{56,48},{64,56},{72,6... | collective-permute-start | bytes 1966088 | tf_op jit(solution)/shard_map/ppermute | solution.py:318
  97.2 1.1 copy-start.1
  98.2 1.1 copy-start.3
  99.3 1.1 copy-start.5
  105.4 3.6 %copy-start.7 = (bf16[256,640]{1,0:T(8,128)(2,1)S(1)}, bf16[256,640]{1,0:T(8,128)(2,1)}, u32[]{:S(2)}) copy-start(bf16[256,640]{1,0:T(8,128)(2,1)} %copy-done.6) | copy-start | bytes 983044
  105.7 39.8 %collective-permute-start.9 = (bf16[256,1280]{1,0:T(8,128)(2,1)S(1)}, bf16[256,1280]{1,0:T(8,128)(2,1)S(1)}, u32[]{:S(2)}, u32[]{:S(2)}) collective-permute-start(bf16[256,1280]{1,0:T(8,128)(2,1)S(1)} %fold.1), channel_id=1, source_target_pairs={{16,0},{24,8},{32,16},{40,24},{48,32},{56,40},{64,48},{72,56},{80,... | collective-permute-start | bytes 1966088 | tf_op jit(solution)/shard_map/ppermute | solution.py:318
  109.0 36.5 %collective-permute-start.6 = (bf16[256,640]{1,0:T(8,128)(2,1)S(1)}, bf16[256,640]{1,0:T(8,128)(2,1)S(1)}, u32[]{:S(2)}, u32[]{:S(2)}) collective-permute-start(bf16[256,640]{1,0:T(8,128)(2,1)S(1)} %copy-done.7), channel_id=1, source_target_pairs={{0,4},{1,5},{2,6},{3,7},{4,0},{5,1},{6,2},{7,3},{8,12},{9,13},{10,... | collective-permute-start | bytes 983048 | tf_op jit(solution)/shard_map/ppermute | solution.py:312

commit v10 on v9

--- a/solution.py
+++ b/solution.py
@@ -168,13 +168,11 @@
     return peak + jnp.log2(one_part + other_sum * jnp.exp2(other_peak - peak))
 
 
-def grads_kernel(roles, parts_in, dq_in, last, bias_ref, place, one, other, tokens, own, *rest):
+def grads_kernel(roles, parts_in, bias_ref, place, one, other, tokens, own, *rest):
     *rest, rows = rest
     blocks, rest = rest[: len(roles)], rest[len(roles) :]
     if parts_in:
         parts, rest = rest[: len(roles)], rest[len(roles) :]
-    if dq_in:
-        dq_part, *rest = rest
     dq_out, *outs = rest
     half = own.shape[0]
     rows[...] = tokens[:, META].astype(F32).T
@@ -205,34 +203,29 @@
                 if parts_in:
                     value += parts[i][:, head_slice(cols)].astype(F32)
                 out[:, head_slice(cols)] = value.astype(out.dtype)
-        if dq_in:
-            dq += dq_part[q_cols, :]
-        if last:
-            dq_out[:, q_cols] = (dq * FACTOR).T.astype(dq_out.dtype)
+        turned = (dq * FACTOR).T.astype(dq_out.dtype)
+        if parts_in:
+            dq_out[:, q_cols] = turned
         else:
-            dq_out[q_cols, :] = dq
-
-
-def grads(name, common, tokens, own, window, roles, outs, parts=(), dq_part=None, dq_out=None):
+            dq_out[0, :, q_cols] = turned
+            dq_out[1, :, q_cols] = turned
+
+
+def grads(name, common, tokens, own, window, roles, outs, parts=(), dq_out=None):
     half = own.shape[0]
     wide = GROUP * HDIM
     pairs = GROUP * half * len(roles) * half
-    extra = list(parts) + ([] if dq_part is None else [dq_part])
-    last = dq_out is not None
-    if last:
-        dq_shape = shape_of((half, wide), *dq_out)
-    else:
-        dq_shape = shape_of((wide, half), F32, True)
-    return pl.pallas_call(
-        functools.partial(grads_kernel, roles, bool(parts), dq_part is not None, last),
+    dq_shape = shape_of((half, wide) if parts else (2, half, wide), *dq_out)
+    return pl.pallas_call(
+        functools.partial(grads_kernel, roles, bool(parts)),
         out_shape=[dq_shape] + [shape_of((half, 2 * wide), *out) for out in outs],
-        in_specs=[smem(), smem()] + [vmem()] * (4 + len(roles) + len(extra)),
+        in_specs=[smem(), smem()] + [vmem()] * (4 + len(roles) + len(parts)),
         out_specs=[vmem()] * (1 + len(outs)),
         scratch_shapes=[pltpu.VMEM((HDIM, half), F32)],
         compiler_params=params(),
         cost_estimate=cost(10 * pairs * HDIM, 12 * half * wide * 2, pairs),
         name=name,
-    )(*common, tokens, own, *[window[role] for role in roles], *extra)
+    )(*common, tokens, own, *[window[role] for role in roles], *parts)
 
 
 def fold_kernel(even_ref, d1, swapped, side, out):
@@ -253,29 +246,29 @@
     )(even, d1, swapped, side)
 
 
-def close_kernel(even_ref, dq_own, dq_back, d0, back, side, out):
+def close_kernel(even_ref, place, dq_own, dq_back, d0, back, side, out):
     even = even_ref[0].astype(F32)
     tok = out.shape[1]
     wide = dq_own.shape[1]
     for step in range(XN):
         rows = slice(step * tok, (step + 1) * tok)
         pair = d0[rows, :] + back[rows, :].astype(F32) + side[rows, :].astype(F32) * even
-        out[step, :, :wide] = (dq_own[rows, :] + dq_back[rows, :].astype(F32)).astype(BF16)
+        out[step, :, :wide] = (dq_own[rows, :] + dq_back[1 - place[1], rows, :].astype(F32)).astype(BF16)
         out[step, :, wide:] = pair.astype(BF16)
 
 
-def close(even, dq_own, dq_back, d0, back, side):
+def close(even, place, dq_own, dq_back, d0, back, side):
     half, wide = dq_own.shape
     tok = half // XN
     return pl.pallas_call(
         close_kernel,
         out_shape=jax.ShapeDtypeStruct((XN, tok, 3 * wide), BF16),
-        in_specs=[smem()] + [vmem()] * 5,
+        in_specs=[smem(), smem()] + [vmem()] * 5,
         out_specs=vmem(),
         compiler_params=params(),
         cost_estimate=cost(6 * half * wide, 24 * half * wide),
         name="close",
-    )(even, dq_own, dq_back, d0, back, side)
+    )(even, place, dq_own, dq_back, d0, back, side)
 
 
 def unpack_kernel(parts, dq, dk, dv):
@@ -310,6 +303,12 @@
 def across_z(value):
     count = lax.axis_size("col")
     return lax.ppermute(value, "col", [(c, (c + XN) % count) for c in range(count)])
+
+
+def pair_swap(value):
+    half = lax.axis_size("col") // 2
+    groups = [[c, c + half] for c in range(half)]
+    return lax.all_to_all(value, "col", 0, 0, axis_index_groups=groups)
 
 
 def along_row(value, steps):
@@ -358,20 +357,17 @@
 
     common = (bias, place, far_near, far_other)
     kept, sent, summed = (BF16, True), (BF16, False), (F32, True)
-    dq_far, *parts = grads(
-        "grads_far", common, far, own, window, (0, 1, 2, 3), [kept] * 4, dq_out=sent
-    )
-    dq_back = across_z(dq_far)
+    roles = (0, 1, 2, 3)
+    dq_far, *parts = grads("grads_far", common, far, own, window, roles, [kept] * 4, dq_out=sent)
+    dq_back = pair_swap(dq_far)
     common = (bias, place, own_near, own_other)
-    dq_part, d2, d3 = grads(
-        "grads_own23", common, own, own, window, (2, 3), [sent] * 2, parts[2:]
+    outs = [summed, kept, sent, sent]
+    dq_own, d0, d1, d2, d3 = grads(
+        "grads_own", common, own, own, window, roles, outs, parts, dq_out=summed
     )
     side, swapped = along_row(d3, -1), in_chip(d2)
-    dq_own, d0, d1 = grads(
-        "grads_own01", common, own, own, window, (0, 1), [summed, kept], parts[:2], dq_part, summed
-    )
     back = along_row(fold(even, d1, swapped, side), -2)
-    return tuple(unpack(over_x(close(even, dq_own, dq_back, d0, back, side))))
+    return tuple(unpack(over_x(close(even, place, dq_own, dq_back, d0, back, side))))
 
 
 def solution(mesh):

time: 165 us -> 169 us (1.024)
  local copies, waits for them, and re-layouts: 6.39 us -> 9.3 us
    ppermute x4 -> x3, waiting for transfers between devices: 40.7 us -> 7.4 us  [across_z(): lax.ppermute(value, 'col', [(c, (c + XN) % count) for c in range(count)])]
    all_to_all x0 -> x1, waiting for transfers between devices: none -> 32.4 us  [pair_swap(): return lax.all_to_all(value, 'col', 0, 0, axis_index_groups=groups)]
    all_to_all x0 -> x1, starting transfers between devices: none -> 3.52 us  [pair_swap(): return lax.all_to_all(value, 'col', 0, 0, axis_index_groups=groups)]
    ppermute x4 -> x3, starting transfers between devices: 25.1 us -> 22.1 us  [across_z(): lax.ppermute(value, 'col', [(c, (c + XN) % count) for c in range(count)])]
    unnamed x18 -> x24, local copies, waits for them, and re-layouts: 5.68 us -> 8.59 us
    ppermute x4, waiting for transfers between devices: 10.2 us -> 12.1 us  [along_row(): lax.ppermute(value, 'row', [(r, r + steps) for r in range(first, last)])]
    pallas_call x3 -> x2, Pallas kernels: 11.4 us -> 9.9 us  [grads(): pl.pallas_call(functools.partial(grads_kernel, roles, bool(parts)), out_s...]
  transfers between devices with their start and end apart: 12 -> 12, of which waited for: 6 -> 6; matrix products, arithmetic and copies ran while one was open for 1% -> 1% of each run, Pallas kernels for 10% -> 8%
where the time goes in v10:
time: 169 us; the launch traced here: 168 us
  waiting for transfers between devices  69.6 us (41%)
  starting transfers between devices  47.2 us (28%)
  Pallas kernels  23.1 us (14%)
  blocking collectives  17.2 us (10%)
  local copies, waits for them, and re-layouts  9.3 us (6%)
    all_to_all x1, waiting for transfers between devices, pair_swap(): return lax.all_to_all(value, 'col', 0, 0, axis_index_groups=groups)  32.4 us
    ppermute x3, starting transfers between devices, across_z(): lax.ppermute(value, 'col', [(c, (c + XN) % count) for c in range(count)])  22.1 us
    all_to_all x2, waiting for transfers between devices, over_x(): return lax.all_to_all(value, 'col', 0, 0, axis_index_groups=groups)  17.7 us
    all_to_all x1, blocking collectives, over_x(): return lax.all_to_all(value, 'col', 0, 0, axis_index_groups=groups)  17.2 us
    ppermute x4, waiting for transfers between devices, along_row(): lax.ppermute(value, 'row', [(r, r + steps) for r in range(first, last)])  12.1 us
    pallas_call x2, Pallas kernels, grads(): pl.pallas_call(functools.partial(grads_kernel, roles, bool(parts)), out_s...  9.9 us
    ppermute x4, starting transfers between devices, along_row(): lax.ppermute(value, 'row', [(r, r + steps) for r in range(first, last)])  9.75 us
    unnamed x24, local copies, waits for them, and re-layouts  8.59 us
  transfers between devices with their start and end apart: 12, of which 6 were waited for; matrix products, arithmetic and copies ran while one was open for 1% of the time, Pallas kernels for 8%

profile of v10, /device:TPU:248, one launch (start us, length us, event | category | flops | bytes accessed | tf_op | source)
XLA Modules:
  0.0 168.4 jit_solution(4446976866859666539)
XLA Ops:
  0.6 0.0 copy-start.11
  0.6 2.1 %pack_keys.1 = bf16[4,64,1280]{2,1,0:T(8,128)(2,1)} custom-call(bf16[64,2560]{1,0:T(8,128)(2,1)} %k_any.1, bf16[64,2560]{1,0:T(8,128)(2,1)} %v_any.1), custom_call_target="tpu_custom_call" | custom-call | bytes 1310720 | tf_op jit(solution)/shard_map/pack_keys/pallas_call | solution.py:89
  2.7 4.3 %all-to-all-start = ((bf16[4,64,1280]{2,1,0:T(8,128)(2,1)}), bf16[4,64,1280]{2,1,0:T(8,128)(2,1)S(1)}, u32[]{:S(2)}, u32[]{:S(2)}) async-start(bf16[4,64,1280]{2,1,0:T(8,128)(2,1)} %pack_keys.1), calls=%async_computation | async-start | bytes 1310720 | tf_op jit(solution)/shard_map/all_to_all | solution.py:300
  7.0 0.0 copy-done.11
  7.0 0.7 copy.9.f_ref
  7.8 3.1 %pack_queries.1 = bf16[4,64,1408]{2,1,0:T(8,128)(2,1)} custom-call(bf16[64,2560]{1,0:T(8,128)(2,1)} %q_any.1, bf16[64,2560]{1,0:T(8,128)(2,1)} %o_any.1, bf16[64,2560]{1,0:T(8,128)(2,1)} %g_any.1, s32[64,1]{1,0:T(8,128)} %copy.9.f_ref), custom_call_target="tpu_custom_call" | custom-call | flops 327680 | bytes 2293760 | tf_op jit(solution)/shard_map/pack_queries/pallas_call | solution.py:66
  10.8 7.1 %all-to-all-done = bf16[4,64,1280]{2,1,0:T(8,128)(2,1)S(1)} async-done(((bf16[4,64,1280]{2,1,0:T(8,128)(2,1)}), bf16[4,64,1280]{2,1,0:T(8,128)(2,1)S(1)}, u32[]{:S(2)}, u32[]{:S(2)}) %all-to-all-start) | async-done | bytes 655392 | tf_op jit(solution)/shard_map/all_to_all | solution.py:300
  17.9 1.3 collective-permute-start
  19.2 3.5 %all-to-all-start.1 = ((bf16[4,64,1408]{2,1,0:T(8,128)(2,1)}), bf16[4,64,1408]{2,1,0:T(8,128)(2,1)S(1)}, u32[]{:S(2)}, u32[]{:S(2)}) async-start(bf16[4,64,1408]{2,1,0:T(8,128)(2,1)} %pack_queries.1), calls=%async_computation.1 | async-start | bytes 1441792 | tf_op jit(solution)/shard_map/all_to_all | solution.py:300
  22.7 10.6 %all-to-all-done.1 = bf16[4,64,1408]{2,1,0:T(8,128)(2,1)S(1)} async-done(((bf16[4,64,1408]{2,1,0:T(8,128)(2,1)}), bf16[4,64,1408]{2,1,0:T(8,128)(2,1)S(1)}, u32[]{:S(2)}, u32[]{:S(2)}) %all-to-all-start.1) | async-done | bytes 720928 | tf_op jit(solution)/shard_map/all_to_all | solution.py:300
  33.4 8.2 %collective-permute-start.3 = (bf16[256,1408]{1,0:T(8,128)(2,1)S(1)}, bf16[256,1408]{1,0:T(8,128)(2,1)}, u32[]{:S(2)}, u32[]{:S(2)}) collective-permute-start(bf16[256,1408]{1,0:T(8,128)(2,1)S(1)} %bitcast.11), channel_id=1, source_target_pairs={{0,4},{1,5},{2,6},{3,7},{4,0},{5,1},{6,2},{7,3},{8,12},{9,13},{10,... | collective-permute-start | bytes 2162696 | tf_op jit(solution)/shard_map/ppermute | solution.py:305
  41.6 0.0 collective-permute-done.w1.rest_1_
  41.6 1.0 broadcast_select_fusion
  42.6 1.9 %collective-permute-start.2 = (bf16[256,1280]{1,0:T(8,128)(2,1)}, bf16[256,1280]{1,0:T(8,128)(2,1)S(1)}, u32[]{:S(2)}, u32[]{:S(2)}) collective-permute-start(bf16[256,1280]{1,0:T(8,128)(2,1)} %broadcast_select_fusion), channel_id=1, source_target_pairs={{0,8},{8,16},{16,24},{24,32},{32,40},{40,48},{48,56},{56,64},{64,7... | collective-permute-start | bytes 1966088 | tf_op jit(solution)/shard_map/ppermute | solution.py:317
  44.5 1.9 %collective-permute-start.1 = (bf16[256,1280]{1,0:T(8,128)(2,1)S(1)}, bf16[256,1280]{1,0:T(8,128)(2,1)S(1)}, u32[]{:S(2)}, u32[]{:S(2)}) collective-permute-start(bf16[256,1280]{1,0:T(8,128)(2,1)S(1)} %collective-permute-done.w1.rest_1_), channel_id=1, source_target_pairs={{0,8},{8,0},{16,24},{24,16},{32,40},{40,32},{48,56},{56,48},{64,72... | collective-permute-start | bytes 1966088 | tf_op jit(solution)/shard_map/ppermute | solution.py:322
  46.5 0.1 pad_add_fusion.place
  46.5 0.1 add_select_fusion.bias_ref
  46.6 8.1 %collective-permute-done.2.w3.rest_3_ = bf16[256,1280]{1,0:T(8,128)(2,1)S(1)} collective-permute-done((bf16[256,1280]{1,0:T(8,128)(2,1)}, bf16[256,1280]{1,0:T(8,128)(2,1)S(1)}, u32[]{:S(2)}, u32[]{:S(2)}) %collective-permute-start.2) | collective-permute-done | bytes 655392 | tf_op jit(solution)/shard_map/ppermute | solution.py:317
  54.7 0.0 collective-permute-done.1.w2.rest_2_
  54.7 2.2 %stats_own.1.one = f32[16,256]{1,0:T(8,128)S(1)} custom-call(f32[4]{0:T(128)S(1)} %add_select_fusion.bias_ref, bf16[256,1408]{1,0:T(8,128)(2,1)S(1)} %bitcast.12, bf16[256,1408]{1,0:T(8,128)(2,1)S(1)} %bitcast.13, bf16[256,1280]{1,0:T(8,128)(2,1)S(1)} %bitcast.19, bf16[256,1280]{1,0:T(8,128)(2,1)S(1)} %collective-permute-done.w1.rest_1_, ...), custom_call_target="tpu_custom_call" | custom-call | flops 671088640 | bytes 1638400 | tf_op jit(solution)/shard_map/stats_own/pallas_call | solution.py:148
  56.9 1.9 %collective-permute-start.5 = (f32[16,256]{1,0:T(8,128)S(1)}, f32[16,256]{1,0:T(8,128)S(1)}, u32[]{:S(2)}, u32[]{:S(2)}) collective-permute-start(f32[16,256]{1,0:T(8,128)S(1)} %stats_own.1.one), channel_id=1, source_target_pairs={{0,4},{1,5},{2,6},{3,7},{4,0},{5,1},{6,2},{7,3},{8,12},{9,13},{10,... | collective-permute-start | bytes 49160 | tf_op jit(solution)/shard_map/ppermute | solution.py:305
  58.8 7.4 %collective-permute-done.3.tokens = bf16[256,1408]{1,0:T(8,128)(2,1)} collective-permute-done((bf16[256,1408]{1,0:T(8,128)(2,1)S(1)}, bf16[256,1408]{1,0:T(8,128)(2,1)}, u32[]{:S(2)}, u32[]{:S(2)}) %collective-permute-start.3) | collective-permute-done | bytes 720928 | tf_op jit(solution)/shard_map/ppermute | solution.py:305
  66.2 2.8 %stats_far.1.one = f32[16,256]{1,0:T(8,128)S(1)} custom-call(f32[4]{0:T(128)S(1)} %add_select_fusion.bias_ref, bf16[256,1408]{1,0:T(8,128)(2,1)} %collective-permute-done.3.tokens, bf16[256,1408]{1,0:T(8,128)(2,1)S(1)} %bitcast.14, bf16[256,1280]{1,0:T(8,128)(2,1)S(1)} %bitcast.20, bf16[256,1280]{1,0:T(8,128)(2,1)S(1)} %collective-permute-done.w1.rest_1_, ...), custom_call_target="tpu_custom_call" | custom-call | flops 671088640 | bytes 1638400 | tf_op jit(solution)/shard_map/stats_far/pallas_call | solution.py:148
  69.0 12.0 %collective-permute-start.4 = (f32[16,256]{1,0:T(8,128)S(1)}, f32[16,256]{1,0:T(8,128)S(1)}, u32[]{:S(2)}, u32[]{:S(2)}) collective-permute-start(f32[16,256]{1,0:T(8,128)S(1)} %stats_far.1.one), channel_id=1, source_target_pairs={{0,4},{1,5},{2,6},{3,7},{4,0},{5,1},{6,2},{7,3},{8,12},{9,13},{10,... | collective-permute-start | bytes 49160 | tf_op jit(solution)/shard_map/ppermute | solution.py:305
  81.0 0.0 collective-permute-done.5.other
  81.0 4.8 %grads_far.1 = (bf16[2,256,640]{2,1,0:T(8,128)(2,1)S(1)}, bf16[256,1280]{1,0:T(8,128)(2,1)S(1)}, bf16[256,1280]{1,0:T(8,128)(2,1)S(1)}, bf16[256,1280]{1,0:T(8,128)(2,1)S(1)}, bf16[256,1280]{1,0:T(8,128)(2,1)S(1)}) custom-call(f32[4]{0:T(128)S(1)} %add_select_fusion.bias_ref, s32[2]{0:T(128)S(1)} %pad_add_fusion.place, f32[16,256]{1,0:T(8,128)S(1)} %stats_far.1.one, ...), custom_call_target="tpu_custom_call" | custom-call | flops 1677721600 | bytes 3932160 | tf_op jit(solution)/shard_map/grads_far/pallas_call | solution.py:219
  85.8 0.0 copy-start.2
  85.8 0.9 copy-done.2
  86.7 0.0 collective-permute-done.4.other
  86.7 5.1 %grads_own.1 = (f32[256,640]{1,0:T(8,128)S(1)}, f32[256,1280]{1,0:T(8,128)S(1)}, bf16[256,1280]{1,0:T(8,128)(2,1)S(1)}, bf16[256,1280]{1,0:T(8,128)(2,1)}, bf16[256,1280]{1,0:T(8,128)(2,1)}) custom-call(f32[4]{0:T(128)S(1)} %add_select_fusion.bias_ref, s32[2]{0:T(128)S(1)} %pad_add_fusion.place, f32[16,256]{1,0:T(8,128)S(1)} %stats_own.1.one, ...), custom_call_target="tpu_custom_call" | custom-call | flops 1677721600 | bytes 3932160 | tf_op jit(solution)/shard_map/grads_own/pallas_call | solution.py:219
  91.8 0.0 copy-start
  91.8 1.1 copy-done
  92.9 0.0 copy-start.3
  92.9 0.8 copy-done.3
  93.7 0.0 copy-start.7
  93.7 0.8 copy-done.7
  94.6 0.0 copy-start.4
  94.6 2.0 %collective-permute-start.6 = (bf16[256,1280]{1,0:T(8,128)(2,1)}, bf16[256,1280]{1,0:T(8,128)(2,1)S(1)}, u32[]{:S(2)}, u32[]{:S(2)}) collective-permute-start(bf16[256,1280]{1,0:T(8,128)(2,1)} %get-tuple-element.25), channel_id=1, source_target_pairs={{0,8},{8,0},{16,24},{24,16},{32,40},{40,32},{48,56},{56,48},{64,72... | collective-permute-start | bytes 1966088 | tf_op jit(solution)/shard_map/ppermute | solution.py:322
  96.6 3.3 %collective-permute-start.7 = (bf16[256,1280]{1,0:T(8,128)(2,1)}, bf16[256,1280]{1,0:T(8,128)(2,1)S(1)}, u32[]{:S(2)}, u32[]{:S(2)}) collective-permute-start(bf16[256,1280]{1,0:T(8,128)(2,1)} %get-tuple-element.26), channel_id=1, source_target_pairs={{8,0},{16,8},{24,16},{32,24},{40,32},{48,40},{56,48},{64,56},{72,6... | collective-permute-start | bytes 1966088 | tf_op jit(solution)/shard_map/ppermute | solution.py:317
  99.9 3.5 %all-to-all-start.2 = ((bf16[2,256,640]{2,1,0:T(8,128)(2,1)}), bf16[2,256,640]{2,1,0:T(8,128)(2,1)S(1)}, u32[]{:S(2)}, u32[]{:S(2)}) async-start(bf16[2,256,640]{2,1,0:T(8,128)(2,1)} %copy-done.2), calls=%async_computation.2 | async-start | bytes 1310720 | tf_op jit(solution)/shard_map/all_to_all | solution.py:311
  103.4 0.0 collective-permute-done.6.swapped
  103.5 0.0 copy-start.5
  103.5 0.8 copy-done.5
  104.3 4.0 %collective-permute-done.7.side = bf16[256,1280]{1,0:T(8,128)(2,1)S(1)} collective-permute-done((bf16[256,1280]{1,0:T(8,128)(2,1)}, bf16[256,1280]{1,0:T(8,128)(2,1)S(1)}, u32[]{:S(2)}, u32[]{:S(2)}) %collective-permute-start.7) | collective-permute-done | bytes 655392 | tf_op jit(solution)/shard_map/ppermute | solution.py:317
  108.3 0.0 copy-done.4
  108.3 0.0 copy-start.6
  108.3 1.1 copy-done.6
  109.4 0.0 copy-start.1
  109.4 1.1 fold.1
  110.5 3.3 %collective-permute-start.8 = (bf16[256,1280]{1,0:T(8,128)(2,1)}, bf16[256,1280]{1,0:T(8,128)(2,1)S(1)}, u32[]{:S(2)}, u32[]{:S(2)}) collective-permute-start(bf16[256,1280]{1,0:T(8,128)(2,1)} %fold.1), channel_id=1, source_target_pairs={{16,0},{24,8},{32,16},{40,24},{48,32},{56,40},{64,48},{72,56},{80,... | collective-permute-start | bytes 1966088 | tf_op jit(solution)/shard_map/ppermute | solution.py:317
  113.8 32.4 %all-to-all-done.2.dq_back = bf16[2,256,640]{2,1,0:T(8,128)(2,1)S(1)} async-done(((bf16[2,256,640]{2,1,0:T(8,128)(2,1)}), bf16[2,256,640]{2,1,0:T(8,128)(2,1)S(1)}, u32[]{:S(2)}, u32[]{:S(2)}) %all-to-all-start.2) | async-done | bytes 655392 | tf_op jit(solution)/shard_map/all_to_all | solution.py:311
  146.2 0.0 collective-permute-done.8.back
  146.2 0.0 copy-start.9
  146.2 0.9 copy-done.9
  147.1 0.0 copy-done.1
  147.1 0.0 copy-start.8
  147.1 1.1 copy-done.8
  148.2 0.0 copy-start.10
  148.2 1.1 copy-done.10
  149.3 0.8 close.1
  150.1 17.2 %all_to_all.20.parts = bf16[4,64,1920]{2,1,0:T(8,128)(2,1)S(1)} all-to-all(bf16[4,64,1920]{2,1,0:T(8,128)(2,1)S(1)} %close.1), channel_id=1, replica_groups={{0,1,2,3},{4,5,6,7},{8,9,10,11},{12,13,14,15},{16,17,18,19},{20,21,22,2..., dimensions={0} | all-to-all | bytes 1966080 | tf_op jit(solution)/shard_map/all_to_all | solution.py:300
  167.3 1.1 unpack.1
Async XLA Ops:
  0.6 6.4 %copy-start.11 = (s32[64]{0:T(128)S(1)}, s32[64]{0:T(128)}, u32[]{:S(2)}) copy-start(s32[64]{0:T(128)} %param.11) | copy-start | bytes 772
  2.7 15.2 %all-to-all-start = ((bf16[4,64,1280]{2,1,0:T(8,128)(2,1)}), bf16[4,64,1280]{2,1,0:T(8,128)(2,1)S(1)}, u32[]{:S(2)}, u32[]{:S(2)}) async-start(bf16[4,64,1280]{2,1,0:T(8,128)(2,1)} %pack_keys.1), calls=%async_computation | async-start | bytes 1310720 | tf_op jit(solution)/shard_map/all_to_all | solution.py:300
  17.9 23.7 %collective-permute-start = (bf16[256,1280]{1,0:T(8,128)(2,1)S(1)}, bf16[256,1280]{1,0:T(8,128)(2,1)S(1)}, u32[]{:S(2)}, u32[]{:S(2)}) collective-permute-start(bf16[256,1280]{1,0:T(8,128)(2,1)S(1)} %bitcast.18), channel_id=1, source_target_pairs={{0,16},{8,24},{16,32},{24,40},{32,48},{40,56},{48,64},{56,72},{64,... | collective-permute-start | bytes 1966088 | tf_op jit(solution)/shard_map/ppermute | solution.py:317
  19.2 14.1 %all-to-all-start.1 = ((bf16[4,64,1408]{2,1,0:T(8,128)(2,1)}), bf16[4,64,1408]{2,1,0:T(8,128)(2,1)S(1)}, u32[]{:S(2)}, u32[]{:S(2)}) async-start(bf16[4,64,1408]{2,1,0:T(8,128)(2,1)} %pack_queries.1), calls=%async_computation.1 | async-start | bytes 1441792 | tf_op jit(solution)/shard_map/all_to_all | solution.py:300
  33.4 32.9 %collective-permute-start.3 = (bf16[256,1408]{1,0:T(8,128)(2,1)S(1)}, bf16[256,1408]{1,0:T(8,128)(2,1)}, u32[]{:S(2)}, u32[]{:S(2)}) collective-permute-start(bf16[256,1408]{1,0:T(8,128)(2,1)S(1)} %bitcast.11), channel_id=1, source_target_pairs={{0,4},{1,5},{2,6},{3,7},{4,0},{5,1},{6,2},{7,3},{8,12},{9,13},{10,... | collective-permute-start | bytes 2162696 | tf_op jit(solution)/shard_map/ppermute | solution.py:305
  42.6 12.1 %collective-permute-start.2 = (bf16[256,1280]{1,0:T(8,128)(2,1)}, bf16[256,1280]{1,0:T(8,128)(2,1)S(1)}, u32[]{:S(2)}, u32[]{:S(2)}) collective-permute-start(bf16[256,1280]{1,0:T(8,128)(2,1)} %broadcast_select_fusion), channel_id=1, source_target_pairs={{0,8},{8,16},{16,24},{24,32},{32,40},{40,48},{48,56},{56,64},{64,7... | collective-permute-start | bytes 1966088 | tf_op jit(solution)/shard_map/ppermute | solution.py:317
  44.5 10.2 %collective-permute-start.1 = (bf16[256,1280]{1,0:T(8,128)(2,1)S(1)}, bf16[256,1280]{1,0:T(8,128)(2,1)S(1)}, u32[]{:S(2)}, u32[]{:S(2)}) collective-permute-start(bf16[256,1280]{1,0:T(8,128)(2,1)S(1)} %collective-permute-done.w1.rest_1_), channel_id=1, source_target_pairs={{0,8},{8,0},{16,24},{24,16},{32,40},{40,32},{48,56},{56,48},{64,72... | collective-permute-start | bytes 1966088 | tf_op jit(solution)/shard_map/ppermute | solution.py:322
  56.9 24.1 %collective-permute-start.5 = (f32[16,256]{1,0:T(8,128)S(1)}, f32[16,256]{1,0:T(8,128)S(1)}, u32[]{:S(2)}, u32[]{:S(2)}) collective-permute-start(f32[16,256]{1,0:T(8,128)S(1)} %stats_own.1.one), channel_id=1, source_target_pairs={{0,4},{1,5},{2,6},{3,7},{4,0},{5,1},{6,2},{7,3},{8,12},{9,13},{10,... | collective-permute-start | bytes 49160 | tf_op jit(solution)/shard_map/ppermute | solution.py:305
  69.0 17.7 %collective-permute-start.4 = (f32[16,256]{1,0:T(8,128)S(1)}, f32[16,256]{1,0:T(8,128)S(1)}, u32[]{:S(2)}, u32[]{:S(2)}) collective-permute-start(f32[16,256]{1,0:T(8,128)S(1)} %stats_far.1.one), channel_id=1, source_target_pairs={{0,4},{1,5},{2,6},{3,7},{4,0},{5,1},{6,2},{7,3},{8,12},{9,13},{10,... | collective-permute-start | bytes 49160 | tf_op jit(solution)/shard_map/ppermute | solution.py:305
  85.8 0.9 copy-start.2
  91.8 1.1 copy-start
  92.9 0.8 copy-start.3
  93.7 0.8 copy-start.7
  94.6 13.7 %copy-start.4 = (bf16[256,1280]{1,0:T(8,128)(2,1)S(1)}, bf16[256,1280]{1,0:T(8,128)(2,1)}, u32[]{:S(2)}) copy-start(bf16[256,1280]{1,0:T(8,128)(2,1)} %copy-done.3) | copy-start | bytes 1966084
  94.6 8.9 %collective-permute-start.6 = (bf16[256,1280]{1,0:T(8,128)(2,1)}, bf16[256,1280]{1,0:T(8,128)(2,1)S(1)}, u32[]{:S(2)}, u32[]{:S(2)}) collective-permute-start(bf16[256,1280]{1,0:T(8,128)(2,1)} %get-tuple-element.25), channel_id=1, source_target_pairs={{0,8},{8,0},{16,24},{24,16},{32,40},{40,32},{48,56},{56,48},{64,72... | collective-permute-start | bytes 1966088 | tf_op jit(solution)/shard_map/ppermute | solution.py:322
  96.6 11.7 %collective-permute-start.7 = (bf16[256,1280]{1,0:T(8,128)(2,1)}, bf16[256,1280]{1,0:T(8,128)(2,1)S(1)}, u32[]{:S(2)}, u32[]{:S(2)}) collective-permute-start(bf16[256,1280]{1,0:T(8,128)(2,1)} %get-tuple-element.26), channel_id=1, source_target_pairs={{8,0},{16,8},{24,16},{32,24},{40,32},{48,40},{56,48},{64,56},{72,6... | collective-permute-start | bytes 1966088 | tf_op jit(solution)/shard_map/ppermute | solution.py:317
  99.9 46.3 %all-to-all-start.2 = ((bf16[2,256,640]{2,1,0:T(8,128)(2,1)}), bf16[2,256,640]{2,1,0:T(8,128)(2,1)S(1)}, u32[]{:S(2)}, u32[]{:S(2)}) async-start(bf16[2,256,640]{2,1,0:T(8,128)(2,1)} %copy-done.2), calls=%async_computation.2 | async-start | bytes 1310720 | tf_op jit(solution)/shard_map/all_to_all | solution.py:311
  103.5 0.8 copy-start.5
  108.3 1.1 copy-start.6
  109.4 37.7 %copy-start.1 = (f32[256,1280]{1,0:T(8,128)S(1)}, f32[256,1280]{1,0:T(8,128)}, u32[]{:S(2)}) copy-start(f32[256,1280]{1,0:T(8,128)} %copy-done) | copy-start | bytes 3932164
  110.5 35.7 %collective-permute-start.8 = (bf16[256,1280]{1,0:T(8,128)(2,1)}, bf16[256,1280]{1,0:T(8,128)(2,1)S(1)}, u32[]{:S(2)}, u32[]{:S(2)}) collective-permute-start(bf16[256,1280]{1,0:T(8,128)(2,1)} %fold.1), channel_id=1, source_target_pairs={{16,0},{24,8},{32,16},{40,24},{48,32},{56,40},{64,48},{72,56},{80,... | collective-permute-start | bytes 1966088 | tf_op jit(solution)/shard_map/ppermute | solution.py:317
  146.2 0.9 copy-start.9
  147.1 1.1 copy-start.8
  148.2 1.1 copy-start.10

commit v11 on v9

--- a/solution.py
+++ b/solution.py
@@ -10,6 +10,7 @@
 
 HEADS = 20
 HDIM = 128
+WBLK = 4
 XN = 4
 GROUP = HEADS // XN
 NEG = -1e30
@@ -156,10 +157,6 @@
     )(bias, tokens, own, *window)
 
 
-def shape_of(shape, kind, kept):
-    return pltpu.VMEM(shape, kind) if kept else jax.ShapeDtypeStruct(shape, kind)
-
-
 def log_total(one, other):
     one_peak, one_sum = one[:8, :], one[8:, :]
     other_peak, other_sum = other[:8, :], other[8:, :]
@@ -168,28 +165,33 @@
     return peak + jnp.log2(one_part + other_sum * jnp.exp2(other_peak - peak))
 
 
-def grads_kernel(roles, parts_in, dq_in, last, bias_ref, place, one, other, tokens, own, *rest):
-    *rest, rows = rest
-    blocks, rest = rest[: len(roles)], rest[len(roles) :]
+def grads_kernel(parts_in, bias_ref, place, one, other, tokens, own, w0, w1, w2, w3, *rest):
     if parts_in:
-        parts, rest = rest[: len(roles)], rest[len(roles) :]
-    if dq_in:
-        dq_part, *rest = rest
-    dq_out, *outs = rest
+        parts, rest = rest[:WBLK], rest[WBLK:]
+    dq_out, *outs = rest[: 1 + WBLK]
+    rows, acc, dq_acc, sems, *rest = rest[1 + WBLK :]
+    loads, stores = [], []
+    if parts_in:
+        held, load_sems = rest
+        for role, part in enumerate(parts):
+            loads.append(pltpu.make_async_copy(part, held.at[role], load_sems.at[role]))
+            loads[-1].start()
     half = own.shape[0]
     rows[...] = tokens[:, META].astype(F32).T
     totals = log_total(one, other)
+    window = (w0, w1, w2, w3)
     for head in range(GROUP):
         q_cols = head_slice(head)
+        pair = slice(2 * head * HDIM, 2 * (head + 1) * HDIM)
         queries, grads = tokens[:, q_cols], tokens[:, head_slice(GROUP + head)]
         first = place[0] * GROUP + head
         dot = rows[pl.ds(first, 1), :] + rows[pl.ds(LOW_LANE + first, 1), :]
-        keys = jnp.concatenate([ref[:, head_slice(2 * head)] for ref in blocks], axis=0)
-        values = jnp.concatenate([ref[:, head_slice(2 * head + 1)] for ref in blocks], axis=0)
+        keys = jnp.concatenate([ref[:, head_slice(2 * head)] for ref in window], axis=0)
+        values = jnp.concatenate([ref[:, head_slice(2 * head + 1)] for ref in window], axis=0)
         scores = jnp.dot(keys, queries.T, preferred_element_type=F32) * SCALE2
         pieces = []
-        for i, role in enumerate(roles):
-            piece = scores[i * half : (i + 1) * half]
+        for role in range(WBLK):
+            piece = scores[role * half : (role + 1) * half]
             if role == 0:
                 piece = jnp.where(seen(rows, own), piece, NEG)
             pieces.append(jnp.exp2(piece - (totals[head : head + 1] - bias_ref[role])))
@@ -199,40 +201,60 @@
         ds = (probs * (dp - dot)).astype(BF16)
         dk = jnp.dot(ds, queries, preferred_element_type=F32) * FACTOR
         dq = jnp.dot(keys.T, ds, preferred_element_type=F32)
-        for i, out in enumerate(outs):
-            rows_of = slice(i * half, (i + 1) * half)
-            for cols, value in ((2 * head, dk[rows_of]), (2 * head + 1, dv[rows_of])):
+        if parts_in and head == 0:
+            for load in loads:
+                load.wait()
+        for role in range(WBLK):
+            of = slice(role * half, (role + 1) * half)
+            for cols, value in ((2 * head, dk[of]), (2 * head + 1, dv[of])):
                 if parts_in:
-                    value += parts[i][:, head_slice(cols)].astype(F32)
-                out[:, head_slice(cols)] = value.astype(out.dtype)
-        if dq_in:
-            dq += dq_part[q_cols, :]
-        if last:
-            dq_out[:, q_cols] = (dq * FACTOR).T.astype(dq_out.dtype)
-        else:
-            dq_out[q_cols, :] = dq
-
-
-def grads(name, common, tokens, own, window, roles, outs, parts=(), dq_part=None, dq_out=None):
+                    value += held[role, :, head_slice(cols)].astype(F32)
+                acc[role, :, head_slice(cols)] = value.astype(BF16)
+            stores.append(
+                pltpu.make_async_copy(
+                    acc.at[role, :, pair], outs[role].at[:, pair], sems.at[role, head]
+                )
+            )
+            stores[-1].start()
+        dq_acc[:, q_cols] = (dq * FACTOR).T.astype(dq_acc.dtype)
+        stores.append(
+            pltpu.make_async_copy(
+                dq_acc.at[:, q_cols], dq_out.at[:, q_cols], sems.at[WBLK, head]
+            )
+        )
+        stores[-1].start()
+    for store in stores:
+        store.wait()
+
+
+def grads(name, common, tokens, own, window, dq_kind, parts=()):
     half = own.shape[0]
     wide = GROUP * HDIM
-    pairs = GROUP * half * len(roles) * half
-    extra = list(parts) + ([] if dq_part is None else [dq_part])
-    last = dq_out is not None
-    if last:
-        dq_shape = shape_of((half, wide), *dq_out)
-    else:
-        dq_shape = shape_of((wide, half), F32, True)
-    return pl.pallas_call(
-        functools.partial(grads_kernel, roles, bool(parts), dq_part is not None, last),
-        out_shape=[dq_shape] + [shape_of((half, 2 * wide), *out) for out in outs],
-        in_specs=[smem(), smem()] + [vmem()] * (4 + len(roles) + len(extra)),
-        out_specs=[vmem()] * (1 + len(outs)),
-        scratch_shapes=[pltpu.VMEM((HDIM, half), F32)],
+    pairs = GROUP * half * WBLK * half
+    hbm = pl.BlockSpec(memory_space=pl.ANY)
+    scratch = [
+        pltpu.VMEM((HDIM, half), F32),
+        pltpu.VMEM((WBLK, half, 2 * wide), BF16),
+        pltpu.VMEM((half, wide), dq_kind),
+        pltpu.SemaphoreType.DMA((WBLK + 1, GROUP)),
+    ]
+    if parts:
+        scratch += [pltpu.VMEM((WBLK, half, 2 * wide), BF16), pltpu.SemaphoreType.DMA((WBLK,))]
+    return pl.pallas_call(
+        functools.partial(grads_kernel, bool(parts)),
+        out_shape=[jax.ShapeDtypeStruct((half, wide), dq_kind)]
+        + [jax.ShapeDtypeStruct((half, 2 * wide), BF16)] * WBLK,
+        in_specs=[smem(), smem()] + [vmem()] * (4 + WBLK) + [hbm] * len(parts),
+        out_specs=[hbm] * (1 + WBLK),
+        scratch_shapes=scratch,
         compiler_params=params(),
         cost_estimate=cost(10 * pairs * HDIM, 12 * half * wide * 2, pairs),
         name=name,
-    )(*common, tokens, own, *[window[role] for role in roles], *extra)
+    )(*common, tokens, own, *window, *parts)
+
+
+def row_block(shape):
+    return pl.BlockSpec(shape, lambda step: (step, 0))
 
 
 def fold_kernel(even_ref, d1, swapped, side, out):
@@ -242,11 +264,13 @@
 
 
 def fold(even, d1, swapped, side):
+    block = row_block((d1.shape[0] // 2, d1.shape[1]))
     return pl.pallas_call(
         fold_kernel,
+        grid=(2,),
         out_shape=jax.ShapeDtypeStruct(d1.shape, BF16),
-        in_specs=[smem()] + [vmem()] * 3,
-        out_specs=vmem(),
+        in_specs=[smem()] + [block] * 3,
+        out_specs=block,
         compiler_params=params(),
         cost_estimate=cost(3 * d1.size, 8 * d1.size),
         name="fold",
@@ -255,23 +279,22 @@
 
 def close_kernel(even_ref, dq_own, dq_back, d0, back, side, out):
     even = even_ref[0].astype(F32)
-    tok = out.shape[1]
     wide = dq_own.shape[1]
-    for step in range(XN):
-        rows = slice(step * tok, (step + 1) * tok)
-        pair = d0[rows, :] + back[rows, :].astype(F32) + side[rows, :].astype(F32) * even
-        out[step, :, :wide] = (dq_own[rows, :] + dq_back[rows, :].astype(F32)).astype(BF16)
-        out[step, :, wide:] = pair.astype(BF16)
+    pair = d0[...].astype(F32) + back[...].astype(F32) + side[...].astype(F32) * even
+    out[0, :, :wide] = (dq_own[...] + dq_back[...].astype(F32)).astype(BF16)
+    out[0, :, wide:] = pair.astype(BF16)
 
 
 def close(even, dq_own, dq_back, d0, back, side):
     half, wide = dq_own.shape
     tok = half // XN
+    pair = row_block((tok, 2 * wide))
     return pl.pallas_call(
         close_kernel,
+        grid=(XN,),
         out_shape=jax.ShapeDtypeStruct((XN, tok, 3 * wide), BF16),
-        in_specs=[smem()] + [vmem()] * 5,
-        out_specs=vmem(),
+        in_specs=[smem(), row_block((tok, wide)), row_block((tok, wide)), pair, pair, pair],
+        out_specs=pl.BlockSpec((1, tok, 3 * wide), lambda step: (step, 0, 0)),
         compiler_params=params(),
         cost_estimate=cost(6 * half * wide, 24 * half * wide),
         name="close",
@@ -321,6 +344,19 @@
 def in_chip(value):
     count = lax.axis_size("row")
     return lax.ppermute(value, "row", [(r, r ^ 1) for r in range(count)])
+
+
+def own_grads(operands):
+    common, own, window, parts, even = operands
+    dq_own, d0, d1, d2, d3 = grads("grads_own", common, own, own, window, F32, parts)
+    side, swapped = along_row(d3, -1), in_chip(d2)
+    return dq_own, d0, along_row(fold(even, d1, swapped, side), -2), side
+
+
+def no_grads(operands):
+    own, window = operands[1:3]
+    empty = jnp.zeros_like(window[0])
+    return jnp.zeros((own.shape[0], GROUP * HDIM), F32), empty, empty, empty
 
 
 def per_device(query, key, value, saved_out, grad_out, frame_ids):
@@ -357,20 +393,13 @@
     own_other = across_z(far_near)
 
     common = (bias, place, far_near, far_other)
-    kept, sent, summed = (BF16, True), (BF16, False), (F32, True)
-    dq_far, *parts = grads(
-        "grads_far", common, far, own, window, (0, 1, 2, 3), [kept] * 4, dq_out=sent
-    )
+    dq_far, *parts = grads("grads_far", common, far, own, window, BF16)
+    dq_far, own_other = lax.optimization_barrier((dq_far, own_other))
     dq_back = across_z(dq_far)
     common = (bias, place, own_near, own_other)
-    dq_part, d2, d3 = grads(
-        "grads_own23", common, own, own, window, (2, 3), [sent] * 2, parts[2:]
+    dq_own, d0, back, side = lax.cond(
+        row < lax.axis_size("row"), own_grads, no_grads, (common, own, window, parts, even)
     )
-    side, swapped = along_row(d3, -1), in_chip(d2)
-    dq_own, d0, d1 = grads(
-        "grads_own01", common, own, own, window, (0, 1), [summed, kept], parts[:2], dq_part, summed
-    )
-    back = along_row(fold(even, d1, swapped, side), -2)
     return tuple(unpack(over_x(close(even, dq_own, dq_back, d0, back, side))))
 
 

time: 165 us -> 167 us (1.012)
  the two profiles are of different devices: /device:TPU:248 before, /device:TPU:129 now
where the time goes in v11:
time: 167 us; the launch traced here: 166 us
  waiting for transfers between devices  65.5 us (39%)
  starting transfers between devices  48.3 us (29%)
  Pallas kernels  30.8 us (18%)
  blocking collectives  19.2 us (11%)
    ppermute x4, waiting for transfers between devices, along_row(): lax.ppermute(value, 'row', [(r, r + steps) for r in range(first, last)])  28.8 us
    ppermute x4, waiting for transfers between devices, across_z(): lax.ppermute(value, 'col', [(c, (c + XN) % count) for c in range(count)])  21.7 us
    ppermute x4, starting transfers between devices, across_z(): lax.ppermute(value, 'col', [(c, (c + XN) % count) for c in range(count)])  21 us
    all_to_all x1, blocking collectives, over_x(): return lax.all_to_all(value, 'col', 0, 0, axis_index_groups=groups)  19.2 us
    ppermute x4, starting transfers between devices, along_row(): lax.ppermute(value, 'row', [(r, r + steps) for r in range(first, last)])  15.2 us
    pallas_call x2, Pallas kernels, grads(): pl.pallas_call(functools.partial(grads_kernel, bool(parts)), out_shape=[j...  14.9 us
    all_to_all x2, waiting for transfers between devices, over_x(): return lax.all_to_all(value, 'col', 0, 0, axis_index_groups=groups)  14.9 us
    all_to_all x2, starting transfers between devices, over_x(): return lax.all_to_all(value, 'col', 0, 0, axis_index_groups=groups)  7.52 us
  transfers between devices with their start and end apart: 12, of which 6 were waited for; matrix products, arithmetic and copies ran while one was open for 1% of the time, Pallas kernels for 15%

profile of v11, /device:TPU:129, one launch (start us, length us, event | category | flops | bytes accessed | tf_op | source)
XLA Modules:
  0.0 166.2 jit_solution(15160431803789691062)
XLA Ops:
  0.6 2.0 %pack_keys.1 = bf16[4,64,1280]{2,1,0:T(8,128)(2,1)} custom-call(bf16[64,2560]{1,0:T(8,128)(2,1)} %k_any.1, bf16[64,2560]{1,0:T(8,128)(2,1)} %v_any.1), custom_call_target="tpu_custom_call" | custom-call | bytes 1310720 | tf_op jit(solution)/shard_map/pack_keys/pallas_call | solution.py:90
  2.7 4.0 %all-to-all-start = ((bf16[4,64,1280]{2,1,0:T(8,128)(2,1)}), bf16[4,64,1280]{2,1,0:T(8,128)(2,1)S(1)}, u32[]{:S(2)}, u32[]{:S(2)}) async-start(bf16[4,64,1280]{2,1,0:T(8,128)(2,1)} %pack_keys.1), calls=%async_computation | async-start | bytes 1310720 | tf_op jit(solution)/shard_map/all_to_all | solution.py:330
  6.7 0.0 copy-start
  6.7 0.7 copy-done
  7.4 0.7 copy.9.f_ref
  8.1 3.1 %pack_queries.1 = bf16[4,64,1408]{2,1,0:T(8,128)(2,1)} custom-call(bf16[64,2560]{1,0:T(8,128)(2,1)} %q_any.1, bf16[64,2560]{1,0:T(8,128)(2,1)} %o_any.1, bf16[64,2560]{1,0:T(8,128)(2,1)} %g_any.1, s32[64,1]{1,0:T(8,128)} %copy.9.f_ref), custom_call_target="tpu_custom_call" | custom-call | flops 327680 | bytes 2293760 | tf_op jit(solution)/shard_map/pack_queries/pallas_call | solution.py:67
  11.2 5.5 %all-to-all-done = bf16[4,64,1280]{2,1,0:T(8,128)(2,1)S(1)} async-done(((bf16[4,64,1280]{2,1,0:T(8,128)(2,1)}), bf16[4,64,1280]{2,1,0:T(8,128)(2,1)S(1)}, u32[]{:S(2)}, u32[]{:S(2)}) %all-to-all-start) | async-done | bytes 655392 | tf_op jit(solution)/shard_map/all_to_all | solution.py:330
  16.7 3.2 %collective-permute-start.3 = (bf16[256,1280]{1,0:T(8,128)(2,1)S(1)}, bf16[256,1280]{1,0:T(8,128)(2,1)S(1)}, u32[]{:S(2)}, u32[]{:S(2)}) collective-permute-start(bf16[256,1280]{1,0:T(8,128)(2,1)S(1)} %bitcast.17), channel_id=1, source_target_pairs={{0,16},{8,24},{16,32},{24,40},{32,48},{40,56},{48,64},{56,72},{64,... | collective-permute-start | bytes 1966088 | tf_op jit(solution)/shard_map/ppermute | solution.py:341
  19.9 3.5 %all-to-all-start.1 = ((bf16[4,64,1408]{2,1,0:T(8,128)(2,1)}), bf16[4,64,1408]{2,1,0:T(8,128)(2,1)S(1)}, u32[]{:S(2)}, u32[]{:S(2)}) async-start(bf16[4,64,1408]{2,1,0:T(8,128)(2,1)} %pack_queries.1), calls=%async_computation.1 | async-start | bytes 1441792 | tf_op jit(solution)/shard_map/all_to_all | solution.py:330
  23.4 9.4 %all-to-all-done.1 = bf16[4,64,1408]{2,1,0:T(8,128)(2,1)S(1)} async-done(((bf16[4,64,1408]{2,1,0:T(8,128)(2,1)}), bf16[4,64,1408]{2,1,0:T(8,128)(2,1)S(1)}, u32[]{:S(2)}, u32[]{:S(2)}) %all-to-all-start.1) | async-done | bytes 720928 | tf_op jit(solution)/shard_map/all_to_all | solution.py:330
  32.8 8.8 %collective-permute-start.6 = (bf16[256,1408]{1,0:T(8,128)(2,1)S(1)}, bf16[256,1408]{1,0:T(8,128)(2,1)S(1)}, u32[]{:S(2)}, u32[]{:S(2)}) collective-permute-start(bf16[256,1408]{1,0:T(8,128)(2,1)S(1)} %bitcast.11), channel_id=1, source_target_pairs={{0,4},{1,5},{2,6},{3,7},{4,0},{5,1},{6,2},{7,3},{8,12},{9,13},{10,... | collective-permute-start | bytes 2162696 | tf_op jit(solution)/shard_map/ppermute | solution.py:335
  41.7 0.0 collective-permute-done.3.w1
  41.7 0.1 broadcast_select_fusion
  41.8 6.4 %collective-permute-start.5 = (bf16[256,1280]{1,0:T(8,128)(2,1)S(1)}, bf16[256,1280]{1,0:T(8,128)(2,1)}, u32[]{:S(2)}, u32[]{:S(2)}) collective-permute-start(bf16[256,1280]{1,0:T(8,128)(2,1)S(1)} %broadcast_select_fusion), channel_id=1, source_target_pairs={{0,8},{8,16},{16,24},{24,32},{32,40},{40,48},{48,56},{56,64},{64,7... | collective-permute-start | bytes 1966088 | tf_op jit(solution)/shard_map/ppermute | solution.py:341
  48.2 1.9 %collective-permute-start.4 = (bf16[256,1280]{1,0:T(8,128)(2,1)S(1)}, bf16[256,1280]{1,0:T(8,128)(2,1)}, u32[]{:S(2)}, u32[]{:S(2)}) collective-permute-start(bf16[256,1280]{1,0:T(8,128)(2,1)S(1)} %collective-permute-done.3.w1), channel_id=1, source_target_pairs={{0,8},{8,0},{16,24},{24,16},{32,40},{40,32},{48,56},{56,48},{64,72... | collective-permute-start | bytes 1966088 | tf_op jit(solution)/shard_map/ppermute | solution.py:346
  50.2 0.1 pad_add_fusion.place
  50.3 0.1 add_select_fusion.bias_ref
  50.4 5.4 %collective-permute-done.5.w3 = bf16[256,1280]{1,0:T(8,128)(2,1)} collective-permute-done((bf16[256,1280]{1,0:T(8,128)(2,1)S(1)}, bf16[256,1280]{1,0:T(8,128)(2,1)}, u32[]{:S(2)}, u32[]{:S(2)}) %collective-permute-start.5) | collective-permute-done | bytes 655392 | tf_op jit(solution)/shard_map/ppermute | solution.py:341
  55.7 0.0 collective-permute-done.4.w2
  55.7 3.0 %stats_own.1 = f32[16,256]{1,0:T(8,128)S(1)} custom-call(f32[4]{0:T(128)S(1)} %add_select_fusion.bias_ref, bf16[256,1408]{1,0:T(8,128)(2,1)S(1)} %bitcast.12, bf16[256,1408]{1,0:T(8,128)(2,1)S(1)} %bitcast.13, bf16[256,1280]{1,0:T(8,128)(2,1)S(1)} %bitcast.18, bf16[256,1280]{1,0:T(8,128)(2,1)S(1)} %collective-permute-done.3.w1, ...), custom_call_target="tpu_custom_call" | custom-call | flops 671088640 | bytes 1638400 | tf_op jit(solution)/shard_map/stats_own/pallas_call | solution.py:149
  58.7 1.9 %collective-permute-start.7 = (f32[16,256]{1,0:T(8,128)S(1)}, f32[16,256]{1,0:T(8,128)S(1)}, u32[]{:S(2)}, u32[]{:S(2)}) collective-permute-start(f32[16,256]{1,0:T(8,128)S(1)} %stats_own.1), channel_id=1, source_target_pairs={{0,4},{1,5},{2,6},{3,7},{4,0},{5,1},{6,2},{7,3},{8,12},{9,13},{10,... | collective-permute-start | bytes 49160 | tf_op jit(solution)/shard_map/ppermute | solution.py:335
  60.7 21.7 %collective-permute-done.6.tokens = bf16[256,1408]{1,0:T(8,128)(2,1)S(1)} collective-permute-done((bf16[256,1408]{1,0:T(8,128)(2,1)S(1)}, bf16[256,1408]{1,0:T(8,128)(2,1)S(1)}, u32[]{:S(2)}, u32[]{:S(2)}) %collective-permute-start.6) | collective-permute-done | bytes 720928 | tf_op jit(solution)/shard_map/ppermute | solution.py:335
  82.4 3.0 %stats_far.1.one = f32[16,256]{1,0:T(8,128)S(1)} custom-call(f32[4]{0:T(128)S(1)} %add_select_fusion.bias_ref, bf16[256,1408]{1,0:T(8,128)(2,1)S(1)} %collective-permute-done.6.tokens, bf16[256,1408]{1,0:T(8,128)(2,1)S(1)} %bitcast.14, bf16[256,1280]{1,0:T(8,128)(2,1)S(1)} %bitcast.19, bf16[256,1280]{1,0:T(8,128)(2,1)S(1)} %collective-permute-done.3.w1, ...), custom_call_target="tpu_custom_call" | custom-call | flops 671088640 | bytes 1638400 | tf_op jit(solution)/shard_map/stats_far/pallas_call | solution.py:149
  85.3 5.8 %collective-permute-start.8 = (f32[16,256]{1,0:T(8,128)S(1)}, f32[16,256]{1,0:T(8,128)S(1)}, u32[]{:S(2)}, u32[]{:S(2)}) collective-permute-start(f32[16,256]{1,0:T(8,128)S(1)} %stats_far.1.one), channel_id=1, source_target_pairs={{0,4},{1,5},{2,6},{3,7},{4,0},{5,1},{6,2},{7,3},{8,12},{9,13},{10,... | collective-permute-start | bytes 49160 | tf_op jit(solution)/shard_map/ppermute | solution.py:335
  91.2 0.0 collective-permute-done.7.other
  91.2 6.7 %grads_far.1 = (bf16[256,640]{1,0:T(8,128)(2,1)S(1)}, bf16[256,1280]{1,0:T(8,128)(2,1)}, bf16[256,1280]{1,0:T(8,128)(2,1)}, bf16[256,1280]{1,0:T(8,128)(2,1)}, bf16[256,1280]{1,0:T(8,128)(2,1)}) custom-call(f32[4]{0:T(128)S(1)} %add_select_fusion.bias_ref, s32[2]{0:T(128)S(1)} %pad_add_fusion.place, f32[16,256]{1,0:T(8,128)S(1)} %stats_far.1.one, ...), custom_call_target="tpu_custom_call" | custom-call | flops 1677721600 | bytes 3932160 | tf_op jit(solution)/shard_map/grads_far/pallas_call | solution.py:243
  97.9 0.0 collective-permute-done.8
  97.9 4.4 %collective-permute-start.9 = (bf16[256,640]{1,0:T(8,128)(2,1)S(1)}, bf16[256,640]{1,0:T(8,128)(2,1)S(1)}, u32[]{:S(2)}, u32[]{:S(2)}) collective-permute-start(bf16[256,640]{1,0:T(8,128)(2,1)S(1)} %get-tuple-element.72), channel_id=1, source_target_pairs={{0,4},{1,5},{2,6},{3,7},{4,0},{5,1},{6,2},{7,3},{8,12},{9,13},{10,... | collective-permute-start | bytes 983048 | tf_op jit(solution)/shard_map/ppermute | solution.py:335
  102.3 41.3 %conditional.1 = (f32[256,640]{1,0:T(8,128)S(1)}, bf16[256,1280]{1,0:T(8,128)(2,1)S(1)}, bf16[256,1280]{1,0:T(8,128)(2,1)}, bf16[256,1280]{1,0:T(8,128)(2,1)}) conditional(s32[]{:T(128)} %convert_element_type.4, () %tuple.17, (f32[4]{0:T(128)S(1)}, s32[2]{0:T(128)S(1)}, f32[16,256]{1,0:T(8,128)S(1)}, f32[16,256]{1,0:T(8,128)S(1)}, ...), branch_computations={%region_0.1_spmd, %region_1.2_spmd} | conditional | flops 1678704640 | bytes 14418072 | solution.py:400
  102.3 8.3 %grads_own.1 = (f32[256,640]{1,0:T(8,128)S(1)}, bf16[256,1280]{1,0:T(8,128)(2,1)S(1)}, bf16[256,1280]{1,0:T(8,128)(2,1)S(1)}, bf16[256,1280]{1,0:T(8,128)(2,1)S(1)}, bf16[256,1280]{1,0:T(8,128)(2,1)S(1)}) custom-call(f32[4]{0:T(128)S(1)} %get-tuple-element.28.bias_ref, s32[2]{0:T(128)S(1)} %get-tuple-element.29.place, f32[16,256]{1,0:T(8,128)S(1)} %get-tuple-element.30.one, ...), custom_call_target="tpu_custom_call" | custom-call | flops 1677721600 | bytes 3932160 | tf_op jit(solution)/shard_map/cond/branch_1_fun/grads_own/pallas_call | solution.py:243
  110.5 2.7 %collective-permute-start = (bf16[256,1280]{1,0:T(8,128)(2,1)S(1)}, bf16[256,1280]{1,0:T(8,128)(2,1)S(1)}, u32[]{:S(2)}, u32[]{:S(2)}) collective-permute-start(bf16[256,1280]{1,0:T(8,128)(2,1)S(1)} %get-tuple-element.45), channel_id=1, source_target_pairs={{0,8},{8,0},{16,24},{24,16},{32,40},{40,32},{48,56},{56,48},{64,72... | collective-permute-start | bytes 1966088 | tf_op jit(solution)/shard_map/cond/branch_1_fun/ppermute | solution.py:346
  113.2 1.9 %collective-permute-start.1 = (bf16[256,1280]{1,0:T(8,128)(2,1)S(1)}, bf16[256,1280]{1,0:T(8,128)(2,1)}, u32[]{:S(2)}, u32[]{:S(2)}) collective-permute-start(bf16[256,1280]{1,0:T(8,128)(2,1)S(1)} %get-tuple-element.46), channel_id=1, source_target_pairs={{8,0},{16,8},{24,16},{32,24},{40,32},{48,40},{56,48},{64,56},{72,6... | collective-permute-start | bytes 1966088 | tf_op jit(solution)/shard_map/cond/branch_1_fun/ppermute | solution.py:341
  115.2 0.0 collective-permute-done.swapped
  115.2 10.1 %collective-permute-done.1.side = bf16[256,1280]{1,0:T(8,128)(2,1)} collective-permute-done((bf16[256,1280]{1,0:T(8,128)(2,1)S(1)}, bf16[256,1280]{1,0:T(8,128)(2,1)}, u32[]{:S(2)}, u32[]{:S(2)}) %collective-permute-start.1) | collective-permute-done | bytes 655392 | tf_op jit(solution)/shard_map/cond/branch_1_fun/ppermute | solution.py:341
  125.2 1.3 fold.1
  126.5 3.6 %collective-permute-start.2 = (bf16[256,1280]{1,0:T(8,128)(2,1)S(1)}, bf16[256,1280]{1,0:T(8,128)(2,1)}, u32[]{:S(2)}, u32[]{:S(2)}) collective-permute-start(bf16[256,1280]{1,0:T(8,128)(2,1)S(1)} %fold.1), channel_id=1, source_target_pairs={{16,0},{24,8},{32,16},{40,24},{48,32},{56,40},{64,48},{72,56},{80,... | collective-permute-start | bytes 1966088 | tf_op jit(solution)/shard_map/cond/branch_1_fun/ppermute | solution.py:341
  130.2 13.4 %collective-permute-done.2 = bf16[256,1280]{1,0:T(8,128)(2,1)} collective-permute-done((bf16[256,1280]{1,0:T(8,128)(2,1)S(1)}, bf16[256,1280]{1,0:T(8,128)(2,1)}, u32[]{:S(2)}, u32[]{:S(2)}) %collective-permute-start.2) | collective-permute-done | bytes 655392 | tf_op jit(solution)/shard_map/cond/branch_1_fun/ppermute | solution.py:341
  143.6 0.0 collective-permute-done.9.dq_back
  143.6 2.4 %close.1 = bf16[4,64,1920]{2,1,0:T(8,128)(2,1)S(1)} custom-call(s32[1]{0:T(128)} %bitcast.even_ref, f32[256,640]{1,0:T(8,128)S(1)} %get-tuple-element.71.dq_own, bf16[256,640]{1,0:T(8,128)(2,1)S(1)} %collective-permute-done.9.dq_back, bf16[256,1280]{1,0:T(8,128)(2,1)S(1)} %get-tuple-element.73.d0, bf16[256,1280]{1,0:T(8,128)(2,1)} %get-tuple-element.74.back, ...), custom_call_target="tpu_custom_call" | custom-call | flops 983040 | bytes 3932160 | tf_op jit(solution)/shard_map/close/pallas_call | solution.py:292
  146.0 19.2 %all_to_all.15.parts = bf16[4,64,1920]{2,1,0:T(8,128)(2,1)S(1)} all-to-all(bf16[4,64,1920]{2,1,0:T(8,128)(2,1)S(1)} %close.1), channel_id=1, replica_groups={{0,1,2,3},{4,5,6,7},{8,9,10,11},{12,13,14,15},{16,17,18,19},{20,21,22,2..., dimensions={0} | all-to-all | bytes 1966080 | tf_op jit(solution)/shard_map/all_to_all | solution.py:330
  165.2 1.1 unpack.1
Async XLA Ops:
  2.7 14.0 %all-to-all-start = ((bf16[4,64,1280]{2,1,0:T(8,128)(2,1)}), bf16[4,64,1280]{2,1,0:T(8,128)(2,1)S(1)}, u32[]{:S(2)}, u32[]{:S(2)}) async-start(bf16[4,64,1280]{2,1,0:T(8,128)(2,1)} %pack_keys.1), calls=%async_computation | async-start | bytes 1310720 | tf_op jit(solution)/shard_map/all_to_all | solution.py:330
  6.7 0.7 copy-start
  16.7 25.0 %collective-permute-start.3 = (bf16[256,1280]{1,0:T(8,128)(2,1)S(1)}, bf16[256,1280]{1,0:T(8,128)(2,1)S(1)}, u32[]{:S(2)}, u32[]{:S(2)}) collective-permute-start(bf16[256,1280]{1,0:T(8,128)(2,1)S(1)} %bitcast.17), channel_id=1, source_target_pairs={{0,16},{8,24},{16,32},{24,40},{32,48},{40,56},{48,64},{56,72},{64,... | collective-permute-start | bytes 1966088 | tf_op jit(solution)/shard_map/ppermute | solution.py:341
  19.9 12.9 %all-to-all-start.1 = ((bf16[4,64,1408]{2,1,0:T(8,128)(2,1)}), bf16[4,64,1408]{2,1,0:T(8,128)(2,1)S(1)}, u32[]{:S(2)}, u32[]{:S(2)}) async-start(bf16[4,64,1408]{2,1,0:T(8,128)(2,1)} %pack_queries.1), calls=%async_computation.1 | async-start | bytes 1441792 | tf_op jit(solution)/shard_map/all_to_all | solution.py:330
  32.8 49.5 %collective-permute-start.6 = (bf16[256,1408]{1,0:T(8,128)(2,1)S(1)}, bf16[256,1408]{1,0:T(8,128)(2,1)S(1)}, u32[]{:S(2)}, u32[]{:S(2)}) collective-permute-start(bf16[256,1408]{1,0:T(8,128)(2,1)S(1)} %bitcast.11), channel_id=1, source_target_pairs={{0,4},{1,5},{2,6},{3,7},{4,0},{5,1},{6,2},{7,3},{8,12},{9,13},{10,... | collective-permute-start | bytes 2162696 | tf_op jit(solution)/shard_map/ppermute | solution.py:335
  41.8 14.0 %collective-permute-start.5 = (bf16[256,1280]{1,0:T(8,128)(2,1)S(1)}, bf16[256,1280]{1,0:T(8,128)(2,1)}, u32[]{:S(2)}, u32[]{:S(2)}) collective-permute-start(bf16[256,1280]{1,0:T(8,128)(2,1)S(1)} %broadcast_select_fusion), channel_id=1, source_target_pairs={{0,8},{8,16},{16,24},{24,32},{32,40},{40,48},{48,56},{56,64},{64,7... | collective-permute-start | bytes 1966088 | tf_op jit(solution)/shard_map/ppermute | solution.py:341
  48.2 7.5 %collective-permute-start.4 = (bf16[256,1280]{1,0:T(8,128)(2,1)S(1)}, bf16[256,1280]{1,0:T(8,128)(2,1)}, u32[]{:S(2)}, u32[]{:S(2)}) collective-permute-start(bf16[256,1280]{1,0:T(8,128)(2,1)S(1)} %collective-permute-done.3.w1), channel_id=1, source_target_pairs={{0,8},{8,0},{16,24},{24,16},{32,40},{40,32},{48,56},{56,48},{64,72... | collective-permute-start | bytes 1966088 | tf_op jit(solution)/shard_map/ppermute | solution.py:346
  58.7 32.4 %collective-permute-start.7 = (f32[16,256]{1,0:T(8,128)S(1)}, f32[16,256]{1,0:T(8,128)S(1)}, u32[]{:S(2)}, u32[]{:S(2)}) collective-permute-start(f32[16,256]{1,0:T(8,128)S(1)} %stats_own.1), channel_id=1, source_target_pairs={{0,4},{1,5},{2,6},{3,7},{4,0},{5,1},{6,2},{7,3},{8,12},{9,13},{10,... | collective-permute-start | bytes 49160 | tf_op jit(solution)/shard_map/ppermute | solution.py:335
  85.3 12.5 %collective-permute-start.8 = (f32[16,256]{1,0:T(8,128)S(1)}, f32[16,256]{1,0:T(8,128)S(1)}, u32[]{:S(2)}, u32[]{:S(2)}) collective-permute-start(f32[16,256]{1,0:T(8,128)S(1)} %stats_far.1.one), channel_id=1, source_target_pairs={{0,4},{1,5},{2,6},{3,7},{4,0},{5,1},{6,2},{7,3},{8,12},{9,13},{10,... | collective-permute-start | bytes 49160 | tf_op jit(solution)/shard_map/ppermute | solution.py:335
  97.9 45.7 %collective-permute-start.9 = (bf16[256,640]{1,0:T(8,128)(2,1)S(1)}, bf16[256,640]{1,0:T(8,128)(2,1)S(1)}, u32[]{:S(2)}, u32[]{:S(2)}) collective-permute-start(bf16[256,640]{1,0:T(8,128)(2,1)S(1)} %get-tuple-element.72), channel_id=1, source_target_pairs={{0,4},{1,5},{2,6},{3,7},{4,0},{5,1},{6,2},{7,3},{8,12},{9,13},{10,... | collective-permute-start | bytes 983048 | tf_op jit(solution)/shard_map/ppermute | solution.py:335
  110.5 4.6 %collective-permute-start = (bf16[256,1280]{1,0:T(8,128)(2,1)S(1)}, bf16[256,1280]{1,0:T(8,128)(2,1)S(1)}, u32[]{:S(2)}, u32[]{:S(2)}) collective-permute-start(bf16[256,1280]{1,0:T(8,128)(2,1)S(1)} %get-tuple-element.45), channel_id=1, source_target_pairs={{0,8},{8,0},{16,24},{24,16},{32,40},{40,32},{48,56},{56,48},{64,72... | collective-permute-start | bytes 1966088 | tf_op jit(solution)/shard_map/cond/branch_1_fun/ppermute | solution.py:346
  113.2 12.0 %collective-permute-start.1 = (bf16[256,1280]{1,0:T(8,128)(2,1)S(1)}, bf16[256,1280]{1,0:T(8,128)(2,1)}, u32[]{:S(2)}, u32[]{:S(2)}) collective-permute-start(bf16[256,1280]{1,0:T(8,128)(2,1)S(1)} %get-tuple-element.46), channel_id=1, source_target_pairs={{8,0},{16,8},{24,16},{32,24},{40,32},{48,40},{56,48},{64,56},{72,6... | collective-permute-start | bytes 1966088 | tf_op jit(solution)/shard_map/cond/branch_1_fun/ppermute | solution.py:341
  126.5 17.0 %collective-permute-start.2 = (bf16[256,1280]{1,0:T(8,128)(2,1)S(1)}, bf16[256,1280]{1,0:T(8,128)(2,1)}, u32[]{:S(2)}, u32[]{:S(2)}) collective-permute-start(bf16[256,1280]{1,0:T(8,128)(2,1)S(1)} %fold.1), channel_id=1, source_target_pairs={{16,0},{24,8},{32,16},{40,24},{48,32},{56,40},{64,48},{72,56},{80,... | collective-permute-start | bytes 1966088 | tf_op jit(solution)/shard_map/cond/branch_1_fun/ppermute | solution.py:341

commit v12 on v11

--- a/solution.py
+++ b/solution.py
@@ -40,7 +40,18 @@
         copy.wait()
 
 
-def pack_queries_kernel(q_any, o_any, g_any, f_ref, out, held, sems):
+def head_columns(place, step, h):
+    group = lax.rem(place[0] + step, XN)
+    return pl.ds(pl.multiple_of((group * GROUP + h) * HDIM, HDIM), HDIM)
+
+
+def group_columns(place, step):
+    group = lax.rem(place[0] + step, XN)
+    return pl.ds(pl.multiple_of(group * GROUP * HDIM, GROUP * HDIM), GROUP * HDIM)
+
+
+def pack_queries_kernel(place, q_any, o_any, g_any, f_ref, *rest):
+    outs, (held, sems) = rest[:XN], rest[XN:]
     load_all((q_any, o_any, g_any), held, sems)
     tok = held.shape[1]
     wide = GROUP * HDIM
@@ -54,49 +65,49 @@
         meta = jnp.where(lane == head, high, meta)
         meta = jnp.where(lane == LOW_LANE + head, dot - high, meta)
     meta = meta.astype(BF16)
-    for group in range(XN):
-        here = slice(group * wide, (group + 1) * wide)
-        out[group, :, :wide] = held[0, :, here]
-        out[group, :, wide : 2 * wide] = held[2, :, here]
-        out[group, :, 2 * wide :] = meta
-
-
-def pack_queries(query, saved_out, grad_out, frames):
+    for step, out in enumerate(outs):
+        here = group_columns(place, step)
+        out[:, :wide] = held[0, :, here]
+        out[:, wide : 2 * wide] = held[2, :, here]
+        out[:, 2 * wide :] = meta
+
+
+def pack_queries(place, query, saved_out, grad_out, frames):
     tok, width = query.shape
-    shape = (XN, tok, 2 * GROUP * HDIM + HDIM)
     return pl.pallas_call(
         pack_queries_kernel,
-        out_shape=jax.ShapeDtypeStruct(shape, BF16),
-        in_specs=[pl.BlockSpec(memory_space=pl.ANY)] * 3 + [vmem()],
-        out_specs=vmem(),
+        out_shape=[jax.ShapeDtypeStruct((tok, 2 * GROUP * HDIM + HDIM), BF16)] * XN,
+        in_specs=[smem()] + [pl.BlockSpec(memory_space=pl.ANY)] * 3 + [vmem()],
+        out_specs=[vmem()] * XN,
         scratch_shapes=[pltpu.VMEM((3, tok, width), BF16), pltpu.SemaphoreType.DMA((3,))],
         compiler_params=params(60),
         cost_estimate=cost(2 * tok * width, 14 * tok * width),
         name="pack_queries",
-    )(query, saved_out, grad_out, frames)
-
-
-def pack_keys_kernel(k_any, v_any, out, held, sems):
+    )(place, query, saved_out, grad_out, frames)
+
+
+def pack_keys_kernel(place, k_any, v_any, *rest):
+    outs, (held, sems) = rest[:XN], rest[XN:]
     load_all((k_any, v_any), held, sems)
-    for head in range(HEADS):
-        group, h = divmod(head, GROUP)
-        cols = slice(head * HDIM, (head + 1) * HDIM)
-        for at in range(2):
-            out[group, :, (2 * h + at) * HDIM : (2 * h + at + 1) * HDIM] = held[at, :, cols]
-
-
-def pack_keys(key, value):
+    for step, out in enumerate(outs):
+        for h in range(GROUP):
+            cols = head_columns(place, step, h)
+            for at in range(2):
+                out[:, (2 * h + at) * HDIM : (2 * h + at + 1) * HDIM] = held[at, :, cols]
+
+
+def pack_keys(place, key, value):
     tok, width = key.shape
     return pl.pallas_call(
         pack_keys_kernel,
-        out_shape=jax.ShapeDtypeStruct((XN, tok, 2 * GROUP * HDIM), BF16),
-        in_specs=[pl.BlockSpec(memory_space=pl.ANY)] * 2,
-        out_specs=vmem(),
+        out_shape=[jax.ShapeDtypeStruct((tok, 2 * GROUP * HDIM), BF16)] * XN,
+        in_specs=[smem()] + [pl.BlockSpec(memory_space=pl.ANY)] * 2,
+        out_specs=[vmem()] * XN,
         scratch_shapes=[pltpu.VMEM((2, tok, width), BF16), pltpu.SemaphoreType.DMA((2,))],
         compiler_params=params(60),
         cost_estimate=cost(0, 8 * tok * width),
         name="pack_keys",
-    )(key, value)
+    )(place, key, value)
 
 
 META = slice(2 * GROUP * HDIM, (2 * GROUP + 1) * HDIM)
@@ -169,13 +180,9 @@
     if parts_in:
         parts, rest = rest[:WBLK], rest[WBLK:]
     dq_out, *outs = rest[: 1 + WBLK]
-    rows, acc, dq_acc, sems, *rest = rest[1 + WBLK :]
-    loads, stores = [], []
-    if parts_in:
-        held, load_sems = rest
-        for role, part in enumerate(parts):
-            loads.append(pltpu.make_async_copy(part, held.at[role], load_sems.at[role]))
-            loads[-1].start()
+    rows, dq_acc, sems, *rest = rest[1 + WBLK :]
+    sums = [rest[0].at[role] for role in range(WBLK)] if parts_in else outs
+    stores = []
     half = own.shape[0]
     rows[...] = tokens[:, META].astype(F32).T
     totals = log_total(one, other)
@@ -201,21 +208,19 @@
         ds = (probs * (dp - dot)).astype(BF16)
         dk = jnp.dot(ds, queries, preferred_element_type=F32) * FACTOR
         dq = jnp.dot(keys.T, ds, preferred_element_type=F32)
-        if parts_in and head == 0:
-            for load in loads:
-                load.wait()
         for role in range(WBLK):
             of = slice(role * half, (role + 1) * half)
             for cols, value in ((2 * head, dk[of]), (2 * head + 1, dv[of])):
                 if parts_in:
-                    value += held[role, :, head_slice(cols)].astype(F32)
-                acc[role, :, head_slice(cols)] = value.astype(BF16)
-            stores.append(
-                pltpu.make_async_copy(
-                    acc.at[role, :, pair], outs[role].at[:, pair], sems.at[role, head]
+                    value += parts[role][:, head_slice(cols)].astype(F32)
+                sums[role][:, head_slice(cols)] = value.astype(BF16)
+            if parts_in:
+                stores.append(
+                    pltpu.make_async_copy(
+                        sums[role].at[:, pair], outs[role].at[:, pair], sems.at[role, head]
+                    )
                 )
-            )
-            stores[-1].start()
+                stores[-1].start()
         dq_acc[:, q_cols] = (dq * FACTOR).T.astype(dq_acc.dtype)
         stores.append(
             pltpu.make_async_copy(
@@ -234,18 +239,17 @@
     hbm = pl.BlockSpec(memory_space=pl.ANY)
     scratch = [
         pltpu.VMEM((HDIM, half), F32),
-        pltpu.VMEM((WBLK, half, 2 * wide), BF16),
         pltpu.VMEM((half, wide), dq_kind),
         pltpu.SemaphoreType.DMA((WBLK + 1, GROUP)),
     ]
     if parts:
-        scratch += [pltpu.VMEM((WBLK, half, 2 * wide), BF16), pltpu.SemaphoreType.DMA((WBLK,))]
+        scratch.append(pltpu.VMEM((WBLK, half, 2 * wide), BF16))
     return pl.pallas_call(
         functools.partial(grads_kernel, bool(parts)),
         out_shape=[jax.ShapeDtypeStruct((half, wide), dq_kind)]
         + [jax.ShapeDtypeStruct((half, 2 * wide), BF16)] * WBLK,
-        in_specs=[smem(), smem()] + [vmem()] * (4 + WBLK) + [hbm] * len(parts),
-        out_specs=[hbm] * (1 + WBLK),
+        in_specs=[smem(), smem()] + [vmem()] * (4 + WBLK + len(parts)),
+        out_specs=[hbm] + [hbm if parts else vmem()] * WBLK,
         scratch_shapes=scratch,
         compiler_params=params(),
         cost_estimate=cost(10 * pairs * HDIM, 12 * half * wide * 2, pairs),
@@ -277,15 +281,16 @@
     )(even, d1, swapped, side)
 
 
-def close_kernel(even_ref, dq_own, dq_back, d0, back, side, out):
+def close_kernel(even_ref, place, dq_own, dq_back, d0, back, side, out):
     even = even_ref[0].astype(F32)
     wide = dq_own.shape[1]
+    owner = pl.ds(lax.rem(place[0] + XN - pl.program_id(0), XN), 1)
     pair = d0[...].astype(F32) + back[...].astype(F32) + side[...].astype(F32) * even
-    out[0, :, :wide] = (dq_own[...] + dq_back[...].astype(F32)).astype(BF16)
-    out[0, :, wide:] = pair.astype(BF16)
-
-
-def close(even, dq_own, dq_back, d0, back, side):
+    out[owner, :, :wide] = (dq_own[...] + dq_back[...].astype(F32)).astype(BF16)[None]
+    out[owner, :, wide:] = pair.astype(BF16)[None]
+
+
+def close(even, place, dq_own, dq_back, d0, back, side):
     half, wide = dq_own.shape
     tok = half // XN
     pair = row_block((tok, 2 * wide))
@@ -293,12 +298,12 @@
         close_kernel,
         grid=(XN,),
         out_shape=jax.ShapeDtypeStruct((XN, tok, 3 * wide), BF16),
-        in_specs=[smem(), row_block((tok, wide)), row_block((tok, wide)), pair, pair, pair],
-        out_specs=pl.BlockSpec((1, tok, 3 * wide), lambda step: (step, 0, 0)),
+        in_specs=[smem(), smem(), row_block((tok, wide)), row_block((tok, wide)), pair, pair, pair],
+        out_specs=pl.BlockSpec((XN, tok, 3 * wide), lambda step: (0, 0, 0)),
         compiler_params=params(),
         cost_estimate=cost(6 * half * wide, 24 * half * wide),
         name="close",
-    )(even, dq_own, dq_back, d0, back, side)
+    )(even, place, dq_own, dq_back, d0, back, side)
 
 
 def unpack_kernel(parts, dq, dk, dv):
@@ -330,6 +335,15 @@
     return lax.all_to_all(value, "col", 0, 0, axis_index_groups=groups)
 
 
+def gathered_over_x(chunks):
+    count = lax.axis_size("col")
+    moved = [chunks[0]]
+    for step in range(1, XN):
+        pairs = [(c, c // XN * XN + (c + step) % XN) for c in range(count)]
+        moved.append(lax.ppermute(chunks[step], "col", pairs))
+    return jnp.concatenate(moved, axis=0)
+
+
 def across_z(value):
     count = lax.axis_size("col")
     return lax.ppermute(value, "col", [(c, (c + XN) % count) for c in range(count)])
@@ -364,14 +378,9 @@
     place = jnp.stack([col % XN, col // XN]).astype(jnp.int32)
     is_even = row % 2 == 0
     even = is_even.astype(jnp.int32).reshape(1)
-    tok = query.shape[0]
-    half = XN * tok
-
-    qg = pack_queries(query, saved_out, grad_out, frame_ids[:, None])
-    w0 = over_x(pack_keys(key, value))
-    qg, w0 = lax.optimization_barrier((qg, w0))
-    w0 = w0.reshape(half, -1)
-    own = over_x(qg).reshape(half, -1)
+
+    own = gathered_over_x(pack_queries(place, query, saved_out, grad_out, frame_ids[:, None]))
+    w0 = gathered_over_x(pack_keys(place, key, value))
     far = across_z(own)
     w1 = along_row(w0, 2)
     w3 = along_row(jnp.where(is_even, w0, w1), 1)
@@ -400,7 +409,7 @@
     dq_own, d0, back, side = lax.cond(
         row < lax.axis_size("row"), own_grads, no_grads, (common, own, window, parts, even)
     )
-    return tuple(unpack(over_x(close(even, dq_own, dq_back, d0, back, side))))
+    return tuple(unpack(over_x(close(even, place, dq_own, dq_back, d0, back, side))))
 
 
 def solution(mesh):

time: 167 us -> 180 us (1.078)
  the two profiles are of different devices: /device:TPU:129 before, /device:TPU:1 now
where the time goes in v12:
time: 180 us; the launch traced here: 179 us
  starting transfers between devices  70.1 us (39%)
  waiting for transfers between devices  54.6 us (30%)
  Pallas kernels  31.9 us (18%)
  blocking collectives  18.3 us (10%)
    ppermute x4, starting transfers between devices, across_z(): lax.ppermute(value, 'col', [(c, (c + XN) % count) for c in range(count)])  32.8 us
    ppermute x4, waiting for transfers between devices, along_row(): lax.ppermute(value, 'row', [(r, r + steps) for r in range(first, last)])  31.6 us
    ppermute x4, waiting for transfers between devices, across_z(): lax.ppermute(value, 'col', [(c, (c + XN) % count) for c in range(count)])  23 us
    ppermute x6, starting transfers between devices, gathered_over_x(): moved.append(lax.ppermute(chunks[step], 'col', pairs))  19.9 us
    all_to_all x1, blocking collectives, over_x(): return lax.all_to_all(value, 'col', 0, 0, axis_index_groups=groups)  18.3 us
    pallas_call x2, Pallas kernels, grads(): pl.pallas_call(functools.partial(grads_kernel, bool(parts)), out_shape=[j...  15.5 us
    ppermute x4, starting transfers between devices, along_row(): lax.ppermute(value, 'row', [(r, r + steps) for r in range(first, last)])  12.4 us
    pallas_call x2, Pallas kernels, stats(): pl.pallas_call(stats_kernel, out_shape=jax.ShapeDtypeStruct((16, half), F...  5.96 us
  transfers between devices with their start and end apart: 16, of which 4 were waited for; matrix products, arithmetic and copies ran while one was open for 1% of the time, Pallas kernels for 14%

profile of v12, /device:TPU:1, one launch (start us, length us, event | category | flops | bytes accessed | tf_op | source)
XLA Modules:
  0.0 178.8 jit_solution(15653689745471524183)
XLA Ops:
  0.7 0.1 pad_add_fusion.place
  0.7 2.6 %pack_keys.1 = (bf16[64,1280]{1,0:T(8,128)(2,1)}, bf16[64,1280]{1,0:T(8,128)(2,1)}, bf16[64,1280]{1,0:T(8,128)(2,1)}, bf16[64,1280]{1,0:T(8,128)(2,1)}) custom-call(s32[2]{0:T(128)S(1)} %pad_add_fusion.place, bf16[64,2560]{1,0:T(8,128)(2,1)} %k_any.1, bf16[64,2560]{1,0:T(8,128)(2,1)} %v_any.1), custom_call_target="tpu_custom_call" | custom-call | bytes 1310720 | tf_op jit(solution)/shard_map/pack_keys/pallas_call | solution.py:101
  3.3 3.9 %collective-permute-start.6 = (bf16[64,1280]{1,0:T(8,128)(2,1)}, bf16[64,1280]{1,0:T(8,128)(2,1)S(1)}, u32[]{:S(2)}, u32[]{:S(2)}) collective-permute-start(bf16[64,1280]{1,0:T(8,128)(2,1)} %get-tuple-element.74), channel_id=1, source_target_pairs={{0,1},{1,2},{2,3},{3,0},{4,5},{5,6},{6,7},{7,4},{8,9},{9,10},{10,1... | collective-permute-start | bytes 491528 | tf_op jit(solution)/shard_map/ppermute | solution.py:343
  7.3 4.4 %collective-permute-start.7 = (bf16[64,1280]{1,0:T(8,128)(2,1)}, bf16[64,1280]{1,0:T(8,128)(2,1)S(1)}, u32[]{:S(2)}, u32[]{:S(2)}) collective-permute-start(bf16[64,1280]{1,0:T(8,128)(2,1)} %get-tuple-element.75), channel_id=1, source_target_pairs={{0,2},{1,3},{2,0},{3,1},{4,6},{5,7},{6,4},{7,5},{8,10},{9,11},{10,... | collective-permute-start | bytes 491528 | tf_op jit(solution)/shard_map/ppermute | solution.py:343
  11.6 0.0 copy-start.2
  11.6 3.1 %collective-permute-start.8 = (bf16[64,1280]{1,0:T(8,128)(2,1)}, bf16[64,1280]{1,0:T(8,128)(2,1)S(1)}, u32[]{:S(2)}, u32[]{:S(2)}) collective-permute-start(bf16[64,1280]{1,0:T(8,128)(2,1)} %get-tuple-element.76), channel_id=1, source_target_pairs={{0,3},{1,0},{2,1},{3,2},{4,7},{5,4},{6,5},{7,6},{8,11},{9,8},{10,9... | collective-permute-start | bytes 491528 | tf_op jit(solution)/shard_map/ppermute | solution.py:343
  14.7 0.0 copy-done.2
  14.7 0.7 copy.9.f_ref
  15.4 0.0 copy-start.1
  15.4 3.1 %pack_queries.1 = (bf16[64,1408]{1,0:T(8,128)(2,1)}, bf16[64,1408]{1,0:T(8,128)(2,1)}, bf16[64,1408]{1,0:T(8,128)(2,1)}, bf16[64,1408]{1,0:T(8,128)(2,1)}) custom-call(s32[2]{0:T(128)S(1)} %pad_add_fusion.place, bf16[64,2560]{1,0:T(8,128)(2,1)} %q_any.1, bf16[64,2560]{1,0:T(8,128)(2,1)} %o_any.1, bf16[64,2560]{1,0:T(8,128)(2,1)} %g_any.1, s32[64,1]{1,0:T(8,128)} %copy.9.f_ref), custom_call_target="tpu_custom_call" | custom-call | flops 327680 | bytes 2293760 | tf_op jit(solution)/shard_map/pack_queries/pallas_call | solution.py:77
  18.6 2.2 %collective-permute-start.3 = (bf16[64,1408]{1,0:T(8,128)(2,1)}, bf16[64,1408]{1,0:T(8,128)(2,1)S(1)}, u32[]{:S(2)}, u32[]{:S(2)}) collective-permute-start(bf16[64,1408]{1,0:T(8,128)(2,1)} %get-tuple-element.70), channel_id=1, source_target_pairs={{0,1},{1,2},{2,3},{3,0},{4,5},{5,6},{6,7},{7,4},{8,9},{9,10},{10,1... | collective-permute-start | bytes 540680 | tf_op jit(solution)/shard_map/ppermute | solution.py:343
  20.8 0.0 copy-start
  20.8 2.9 %collective-permute-start.4 = (bf16[64,1408]{1,0:T(8,128)(2,1)}, bf16[64,1408]{1,0:T(8,128)(2,1)S(1)}, u32[]{:S(2)}, u32[]{:S(2)}) collective-permute-start(bf16[64,1408]{1,0:T(8,128)(2,1)} %get-tuple-element.71), channel_id=1, source_target_pairs={{0,2},{1,3},{2,0},{3,1},{4,6},{5,7},{6,4},{7,5},{8,10},{9,11},{10,... | collective-permute-start | bytes 540680 | tf_op jit(solution)/shard_map/ppermute | solution.py:343
  23.8 0.0 copy-done.1
  23.8 0.0 copy-done
  23.8 0.0 copy-start.3
  23.8 0.0 collective-permute-done.6
  23.8 0.9 copy-done.3
  24.7 3.4 %collective-permute-start.5 = (bf16[64,1408]{1,0:T(8,128)(2,1)S(1)}, bf16[64,1408]{1,0:T(8,128)(2,1)S(1)}, u32[]{:S(2)}, u32[]{:S(2)}) collective-permute-start(bf16[64,1408]{1,0:T(8,128)(2,1)S(1)} %copy-done.3), channel_id=1, source_target_pairs={{0,3},{1,0},{2,1},{3,2},{4,7},{5,4},{6,5},{7,6},{8,11},{9,8},{10,9... | collective-permute-start | bytes 540680 | tf_op jit(solution)/shard_map/ppermute | solution.py:343
  28.2 0.0 collective-permute-done.7
  28.2 0.0 collective-permute-done.8
  28.2 3.2 %collective-permute-start.9 = (bf16[256,1280]{1,0:T(8,128)(2,1)S(1)}, bf16[256,1280]{1,0:T(8,128)(2,1)S(1)}, u32[]{:S(2)}, u32[]{:S(2)}) collective-permute-start(bf16[256,1280]{1,0:T(8,128)(2,1)S(1)} %constant_dynamic-update-slice_fusion.4.w0), channel_id=1, source_target_pairs={{0,16},{8,24},{16,32},{24,40},{32,48},{40,56},{48,64},{56,72},{64,... | collective-permute-start | bytes 1966088 | tf_op jit(solution)/shard_map/ppermute | solution.py:355
  31.5 0.0 collective-permute-done.3
  31.5 0.0 collective-permute-done.4
  31.6 0.0 collective-permute-done.5
  31.6 12.8 %collective-permute-start.12 = (bf16[256,1408]{1,0:T(8,128)(2,1)S(1)}, bf16[256,1408]{1,0:T(8,128)(2,1)S(1)}, u32[]{:S(2)}, u32[]{:S(2)}) collective-permute-start(bf16[256,1408]{1,0:T(8,128)(2,1)S(1)} %constant_dynamic-update-slice_fusion.tokens.own), channel_id=1, source_target_pairs={{0,4},{1,5},{2,6},{3,7},{4,0},{5,1},{6,2},{7,3},{8,12},{9,13},{10,... | collective-permute-start | bytes 2162696 | tf_op jit(solution)/shard_map/ppermute | solution.py:349
  44.4 0.0 collective-permute-done.9.w1
  44.4 0.9 broadcast_select_fusion
  45.3 6.0 %collective-permute-start.11 = (bf16[256,1280]{1,0:T(8,128)(2,1)}, bf16[256,1280]{1,0:T(8,128)(2,1)}, u32[]{:S(2)}, u32[]{:S(2)}) collective-permute-start(bf16[256,1280]{1,0:T(8,128)(2,1)} %broadcast_select_fusion), channel_id=1, source_target_pairs={{0,8},{8,16},{16,24},{24,32},{32,40},{40,48},{48,56},{56,64},{64,7... | collective-permute-start | bytes 1966088 | tf_op jit(solution)/shard_map/ppermute | solution.py:355
  51.3 1.9 %collective-permute-start.10 = (bf16[256,1280]{1,0:T(8,128)(2,1)S(1)}, bf16[256,1280]{1,0:T(8,128)(2,1)}, u32[]{:S(2)}, u32[]{:S(2)}) collective-permute-start(bf16[256,1280]{1,0:T(8,128)(2,1)S(1)} %collective-permute-done.9.w1), channel_id=1, source_target_pairs={{0,8},{8,0},{16,24},{24,16},{32,40},{40,32},{48,56},{56,48},{64,72... | collective-permute-start | bytes 1966088 | tf_op jit(solution)/shard_map/ppermute | solution.py:360
  53.2 0.1 add_select_fusion.bias_ref
  53.3 5.8 %collective-permute-done.11.w3 = bf16[256,1280]{1,0:T(8,128)(2,1)} collective-permute-done((bf16[256,1280]{1,0:T(8,128)(2,1)}, bf16[256,1280]{1,0:T(8,128)(2,1)}, u32[]{:S(2)}, u32[]{:S(2)}) %collective-permute-start.11) | collective-permute-done | bytes 655392 | tf_op jit(solution)/shard_map/ppermute | solution.py:355
  59.1 0.0 collective-permute-done.10.w2
  59.1 3.0 %stats_own.1 = f32[16,256]{1,0:T(8,128)S(1)} custom-call(f32[4]{0:T(128)S(1)} %add_select_fusion.bias_ref, bf16[256,1408]{1,0:T(8,128)(2,1)S(1)} %constant_dynamic-update-slice_fusion.tokens.own, bf16[256,1408]{1,0:T(8,128)(2,1)S(1)} %constant_dynamic-update-slice_fusion.tokens.own, bf16[256,1280]{1,0:T(8,128)(2,1)S(1)} %constant_dynamic-update-slice_fusion.4.w0, ...), custom_call_target="tpu_custom_call" | custom-call | flops 671088640 | bytes 1638400 | tf_op jit(solution)/shard_map/stats_own/pallas_call | solution.py:160
  62.1 10.6 %collective-permute-start.13 = (f32[16,256]{1,0:T(8,128)S(1)}, f32[16,256]{1,0:T(8,128)S(1)}, u32[]{:S(2)}, u32[]{:S(2)}) collective-permute-start(f32[16,256]{1,0:T(8,128)S(1)} %stats_own.1), channel_id=1, source_target_pairs={{0,4},{1,5},{2,6},{3,7},{4,0},{5,1},{6,2},{7,3},{8,12},{9,13},{10,... | collective-permute-start | bytes 49160 | tf_op jit(solution)/shard_map/ppermute | solution.py:349
  72.7 23.0 %collective-permute-done.12.tokens = bf16[256,1408]{1,0:T(8,128)(2,1)S(1)} collective-permute-done((bf16[256,1408]{1,0:T(8,128)(2,1)S(1)}, bf16[256,1408]{1,0:T(8,128)(2,1)S(1)}, u32[]{:S(2)}, u32[]{:S(2)}) %collective-permute-start.12) | collective-permute-done | bytes 720928 | tf_op jit(solution)/shard_map/ppermute | solution.py:349
  95.7 3.0 %stats_far.1.one = f32[16,256]{1,0:T(8,128)S(1)} custom-call(f32[4]{0:T(128)S(1)} %add_select_fusion.bias_ref, bf16[256,1408]{1,0:T(8,128)(2,1)S(1)} %collective-permute-done.12.tokens, bf16[256,1408]{1,0:T(8,128)(2,1)S(1)} %constant_dynamic-update-slice_fusion.tokens.own, bf16[256,1280]{1,0:T(8,128)(2,1)S(1)} %constant_dynamic-update-slice_fusion.4.w0, ...), custom_call_target="tpu_custom_call" | custom-call | flops 671088640 | bytes 1638400 | tf_op jit(solution)/shard_map/stats_far/pallas_call | solution.py:160
  98.7 1.9 %collective-permute-start.14 = (f32[16,256]{1,0:T(8,128)S(1)}, f32[16,256]{1,0:T(8,128)S(1)}, u32[]{:S(2)}, u32[]{:S(2)}) collective-permute-start(f32[16,256]{1,0:T(8,128)S(1)} %stats_far.1.one), channel_id=1, source_target_pairs={{0,4},{1,5},{2,6},{3,7},{4,0},{5,1},{6,2},{7,3},{8,12},{9,13},{10,... | collective-permute-start | bytes 49160 | tf_op jit(solution)/shard_map/ppermute | solution.py:349
  100.6 0.0 collective-permute-done.13.other
  100.6 7.6 %grads_far.1 = (bf16[256,640]{1,0:T(8,128)(2,1)S(1)}, bf16[256,1280]{1,0:T(8,128)(2,1)}, bf16[256,1280]{1,0:T(8,128)(2,1)}, bf16[256,1280]{1,0:T(8,128)(2,1)}, bf16[256,1280]{1,0:T(8,128)(2,1)}) custom-call(f32[4]{0:T(128)S(1)} %add_select_fusion.bias_ref, s32[2]{0:T(128)S(1)} %pad_add_fusion.place, f32[16,256]{1,0:T(8,128)S(1)} %stats_far.1.one, ...), custom_call_target="tpu_custom_call" | custom-call | flops 1677721600 | bytes 3932160 | tf_op jit(solution)/shard_map/grads_far/pallas_call | solution.py:247
  108.3 0.0 collective-permute-done.14
  108.3 7.5 %collective-permute-start.15 = (bf16[256,640]{1,0:T(8,128)(2,1)S(1)}, bf16[256,640]{1,0:T(8,128)(2,1)S(1)}, u32[]{:S(2)}, u32[]{:S(2)}) collective-permute-start(bf16[256,640]{1,0:T(8,128)(2,1)S(1)} %get-tuple-element.84), channel_id=1, source_target_pairs={{0,4},{1,5},{2,6},{3,7},{4,0},{5,1},{6,2},{7,3},{8,12},{9,13},{10,... | collective-permute-start | bytes 983048 | tf_op jit(solution)/shard_map/ppermute | solution.py:349
  115.7 41.3 %conditional.1 = (f32[256,640]{1,0:T(8,128)S(1)}, bf16[256,1280]{1,0:T(8,128)(2,1)S(1)}, bf16[256,1280]{1,0:T(8,128)(2,1)}, bf16[256,1280]{1,0:T(8,128)(2,1)}) conditional(s32[]{:T(128)} %convert_element_type.4, () %tuple.16, (f32[4]{0:T(128)S(1)}, s32[2]{0:T(128)S(1)}, f32[16,256]{1,0:T(8,128)S(1)}, f32[16,256]{1,0:T(8,128)S(1)}, ...), branch_computations={%region_0.1_spmd, %region_1.2_spmd} | conditional | flops 1678704640 | bytes 14418072 | solution.py:409
  115.7 7.8 %grads_own.1 = (f32[256,640]{1,0:T(8,128)S(1)}, bf16[256,1280]{1,0:T(8,128)(2,1)S(1)}, bf16[256,1280]{1,0:T(8,128)(2,1)S(1)}, bf16[256,1280]{1,0:T(8,128)(2,1)S(1)}, bf16[256,1280]{1,0:T(8,128)(2,1)S(1)}) custom-call(f32[4]{0:T(128)S(1)} %get-tuple-element.28.bias_ref, s32[2]{0:T(128)S(1)} %get-tuple-element.29.place, f32[16,256]{1,0:T(8,128)S(1)} %get-tuple-element.30.one, ...), custom_call_target="tpu_custom_call" | custom-call | flops 1677721600 | bytes 3932160 | tf_op jit(solution)/shard_map/cond/branch_1_fun/grads_own/pallas_call | solution.py:247
  123.6 3.1 %collective-permute-start = (bf16[256,1280]{1,0:T(8,128)(2,1)S(1)}, bf16[256,1280]{1,0:T(8,128)(2,1)S(1)}, u32[]{:S(2)}, u32[]{:S(2)}) collective-permute-start(bf16[256,1280]{1,0:T(8,128)(2,1)S(1)} %get-tuple-element.45), channel_id=1, source_target_pairs={{0,8},{8,0},{16,24},{24,16},{32,40},{40,32},{48,56},{56,48},{64,72... | collective-permute-start | bytes 1966088 | tf_op jit(solution)/shard_map/cond/branch_1_fun/ppermute | solution.py:360
  126.7 1.9 %collective-permute-start.1 = (bf16[256,1280]{1,0:T(8,128)(2,1)S(1)}, bf16[256,1280]{1,0:T(8,128)(2,1)}, u32[]{:S(2)}, u32[]{:S(2)}) collective-permute-start(bf16[256,1280]{1,0:T(8,128)(2,1)S(1)} %get-tuple-element.46), channel_id=1, source_target_pairs={{8,0},{16,8},{24,16},{32,24},{40,32},{48,40},{56,48},{64,56},{72,6... | collective-permute-start | bytes 1966088 | tf_op jit(solution)/shard_map/cond/branch_1_fun/ppermute | solution.py:355
  128.6 0.0 collective-permute-done.swapped
  128.6 10.1 %collective-permute-done.1.side = bf16[256,1280]{1,0:T(8,128)(2,1)} collective-permute-done((bf16[256,1280]{1,0:T(8,128)(2,1)S(1)}, bf16[256,1280]{1,0:T(8,128)(2,1)}, u32[]{:S(2)}, u32[]{:S(2)}) %collective-permute-start.1) | collective-permute-done | bytes 655392 | tf_op jit(solution)/shard_map/cond/branch_1_fun/ppermute | solution.py:355
  138.7 1.3 fold.1
  140.0 1.3 collective-permute-start.2
  141.3 15.7 %collective-permute-done.2 = bf16[256,1280]{1,0:T(8,128)(2,1)} collective-permute-done((bf16[256,1280]{1,0:T(8,128)(2,1)S(1)}, bf16[256,1280]{1,0:T(8,128)(2,1)}, u32[]{:S(2)}, u32[]{:S(2)}) %collective-permute-start.2) | collective-permute-done | bytes 655392 | tf_op jit(solution)/shard_map/cond/branch_1_fun/ppermute | solution.py:355
  157.0 0.0 collective-permute-done.15.dq_back
  157.0 2.4 %close.1 = bf16[4,64,1920]{2,1,0:T(8,128)(2,1)S(1)} custom-call(s32[1]{0:T(128)} %bitcast.even_ref, s32[2]{0:T(128)S(1)} %pad_add_fusion.place, f32[256,640]{1,0:T(8,128)S(1)} %get-tuple-element.83.dq_own, bf16[256,640]{1,0:T(8,128)(2,1)S(1)} %collective-permute-done.15.dq_back, bf16[256,1280]{1,0:T(8,128)(2,1)S(1)} %get-tuple-element.85.d0, ...), custom_call_target="tpu_custom_call" | custom-call | flops 983040 | bytes 3932160 | tf_op jit(solution)/shard_map/close/pallas_call | solution.py:297
  159.5 18.3 %all_to_all.5.parts = bf16[4,64,1920]{2,1,0:T(8,128)(2,1)S(1)} all-to-all(bf16[4,64,1920]{2,1,0:T(8,128)(2,1)S(1)} %close.1), channel_id=1, replica_groups={{0,1,2,3},{4,5,6,7},{8,9,10,11},{12,13,14,15},{16,17,18,19},{20,21,22,2..., dimensions={0} | all-to-all | bytes 1966080 | tf_op jit(solution)/shard_map/all_to_all | solution.py:335
  177.7 1.1 unpack.1
  (8 shorter events, 0.1 us)
Async XLA Ops:
  3.3 20.5 %collective-permute-start.6 = (bf16[64,1280]{1,0:T(8,128)(2,1)}, bf16[64,1280]{1,0:T(8,128)(2,1)S(1)}, u32[]{:S(2)}, u32[]{:S(2)}) collective-permute-start(bf16[64,1280]{1,0:T(8,128)(2,1)} %get-tuple-element.74), channel_id=1, source_target_pairs={{0,1},{1,2},{2,3},{3,0},{4,5},{5,6},{6,7},{7,4},{8,9},{9,10},{10,1... | collective-permute-start | bytes 491528 | tf_op jit(solution)/shard_map/ppermute | solution.py:343
  7.3 20.9 %collective-permute-start.7 = (bf16[64,1280]{1,0:T(8,128)(2,1)}, bf16[64,1280]{1,0:T(8,128)(2,1)S(1)}, u32[]{:S(2)}, u32[]{:S(2)}) collective-permute-start(bf16[64,1280]{1,0:T(8,128)(2,1)} %get-tuple-element.75), channel_id=1, source_target_pairs={{0,2},{1,3},{2,0},{3,1},{4,6},{5,7},{6,4},{7,5},{8,10},{9,11},{10,... | collective-permute-start | bytes 491528 | tf_op jit(solution)/shard_map/ppermute | solution.py:343
  11.6 3.1 %copy-start.2 = (s32[64]{0:T(128)S(1)}, s32[64]{0:T(128)}, u32[]{:S(2)}) copy-start(s32[64]{0:T(128)} %param.13) | copy-start | bytes 772
  11.6 16.6 %collective-permute-start.8 = (bf16[64,1280]{1,0:T(8,128)(2,1)}, bf16[64,1280]{1,0:T(8,128)(2,1)S(1)}, u32[]{:S(2)}, u32[]{:S(2)}) collective-permute-start(bf16[64,1280]{1,0:T(8,128)(2,1)} %get-tuple-element.76), channel_id=1, source_target_pairs={{0,3},{1,0},{2,1},{3,2},{4,7},{5,4},{6,5},{7,6},{8,11},{9,8},{10,9... | collective-permute-start | bytes 491528 | tf_op jit(solution)/shard_map/ppermute | solution.py:343
  15.4 8.3 %copy-start.1 = (bf16[64,1280]{1,0:T(8,128)(2,1)S(1)}, bf16[64,1280]{1,0:T(8,128)(2,1)}, u32[]{:S(2)}) copy-start(bf16[64,1280]{1,0:T(8,128)(2,1)} %get-tuple-element.73) | copy-start | bytes 491524
  18.6 12.9 %collective-permute-start.3 = (bf16[64,1408]{1,0:T(8,128)(2,1)}, bf16[64,1408]{1,0:T(8,128)(2,1)S(1)}, u32[]{:S(2)}, u32[]{:S(2)}) collective-permute-start(bf16[64,1408]{1,0:T(8,128)(2,1)} %get-tuple-element.70), channel_id=1, source_target_pairs={{0,1},{1,2},{2,3},{3,0},{4,5},{5,6},{6,7},{7,4},{8,9},{9,10},{10,1... | collective-permute-start | bytes 540680 | tf_op jit(solution)/shard_map/ppermute | solution.py:343
  20.8 3.0 %copy-start = (bf16[64,1408]{1,0:T(8,128)(2,1)S(1)}, bf16[64,1408]{1,0:T(8,128)(2,1)}, u32[]{:S(2)}) copy-start(bf16[64,1408]{1,0:T(8,128)(2,1)} %get-tuple-element.69) | copy-start | bytes 540676
  20.8 10.7 %collective-permute-start.4 = (bf16[64,1408]{1,0:T(8,128)(2,1)}, bf16[64,1408]{1,0:T(8,128)(2,1)S(1)}, u32[]{:S(2)}, u32[]{:S(2)}) collective-permute-start(bf16[64,1408]{1,0:T(8,128)(2,1)} %get-tuple-element.71), channel_id=1, source_target_pairs={{0,2},{1,3},{2,0},{3,1},{4,6},{5,7},{6,4},{7,5},{8,10},{9,11},{10,... | collective-permute-start | bytes 540680 | tf_op jit(solution)/shard_map/ppermute | solution.py:343
  23.8 0.9 copy-start.3
  24.7 6.8 %collective-permute-start.5 = (bf16[64,1408]{1,0:T(8,128)(2,1)S(1)}, bf16[64,1408]{1,0:T(8,128)(2,1)S(1)}, u32[]{:S(2)}, u32[]{:S(2)}) collective-permute-start(bf16[64,1408]{1,0:T(8,128)(2,1)S(1)} %copy-done.3), channel_id=1, source_target_pairs={{0,3},{1,0},{2,1},{3,2},{4,7},{5,4},{6,5},{7,6},{8,11},{9,8},{10,9... | collective-permute-start | bytes 540680 | tf_op jit(solution)/shard_map/ppermute | solution.py:343
  28.2 16.1 %collective-permute-start.9 = (bf16[256,1280]{1,0:T(8,128)(2,1)S(1)}, bf16[256,1280]{1,0:T(8,128)(2,1)S(1)}, u32[]{:S(2)}, u32[]{:S(2)}) collective-permute-start(bf16[256,1280]{1,0:T(8,128)(2,1)S(1)} %constant_dynamic-update-slice_fusion.4.w0), channel_id=1, source_target_pairs={{0,16},{8,24},{16,32},{24,40},{32,48},{40,56},{48,64},{56,72},{64,... | collective-permute-start | bytes 1966088 | tf_op jit(solution)/shard_map/ppermute | solution.py:355
  31.6 64.1 %collective-permute-start.12 = (bf16[256,1408]{1,0:T(8,128)(2,1)S(1)}, bf16[256,1408]{1,0:T(8,128)(2,1)S(1)}, u32[]{:S(2)}, u32[]{:S(2)}) collective-permute-start(bf16[256,1408]{1,0:T(8,128)(2,1)S(1)} %constant_dynamic-update-slice_fusion.tokens.own), channel_id=1, source_target_pairs={{0,4},{1,5},{2,6},{3,7},{4,0},{5,1},{6,2},{7,3},{8,12},{9,13},{10,... | collective-permute-start | bytes 2162696 | tf_op jit(solution)/shard_map/ppermute | solution.py:349
  45.3 13.8 %collective-permute-start.11 = (bf16[256,1280]{1,0:T(8,128)(2,1)}, bf16[256,1280]{1,0:T(8,128)(2,1)}, u32[]{:S(2)}, u32[]{:S(2)}) collective-permute-start(bf16[256,1280]{1,0:T(8,128)(2,1)} %broadcast_select_fusion), channel_id=1, source_target_pairs={{0,8},{8,16},{16,24},{24,32},{32,40},{40,48},{48,56},{56,64},{64,7... | collective-permute-start | bytes 1966088 | tf_op jit(solution)/shard_map/ppermute | solution.py:355
  51.3 7.8 %collective-permute-start.10 = (bf16[256,1280]{1,0:T(8,128)(2,1)S(1)}, bf16[256,1280]{1,0:T(8,128)(2,1)}, u32[]{:S(2)}, u32[]{:S(2)}) collective-permute-start(bf16[256,1280]{1,0:T(8,128)(2,1)S(1)} %collective-permute-done.9.w1), channel_id=1, source_target_pairs={{0,8},{8,0},{16,24},{24,16},{32,40},{40,32},{48,56},{56,48},{64,72... | collective-permute-start | bytes 1966088 | tf_op jit(solution)/shard_map/ppermute | solution.py:360
  62.1 38.5 %collective-permute-start.13 = (f32[16,256]{1,0:T(8,128)S(1)}, f32[16,256]{1,0:T(8,128)S(1)}, u32[]{:S(2)}, u32[]{:S(2)}) collective-permute-start(f32[16,256]{1,0:T(8,128)S(1)} %stats_own.1), channel_id=1, source_target_pairs={{0,4},{1,5},{2,6},{3,7},{4,0},{5,1},{6,2},{7,3},{8,12},{9,13},{10,... | collective-permute-start | bytes 49160 | tf_op jit(solution)/shard_map/ppermute | solution.py:349
  98.7 9.6 %collective-permute-start.14 = (f32[16,256]{1,0:T(8,128)S(1)}, f32[16,256]{1,0:T(8,128)S(1)}, u32[]{:S(2)}, u32[]{:S(2)}) collective-permute-start(f32[16,256]{1,0:T(8,128)S(1)} %stats_far.1.one), channel_id=1, source_target_pairs={{0,4},{1,5},{2,6},{3,7},{4,0},{5,1},{6,2},{7,3},{8,12},{9,13},{10,... | collective-permute-start | bytes 49160 | tf_op jit(solution)/shard_map/ppermute | solution.py:349
  108.3 48.8 %collective-permute-start.15 = (bf16[256,640]{1,0:T(8,128)(2,1)S(1)}, bf16[256,640]{1,0:T(8,128)(2,1)S(1)}, u32[]{:S(2)}, u32[]{:S(2)}) collective-permute-start(bf16[256,640]{1,0:T(8,128)(2,1)S(1)} %get-tuple-element.84), channel_id=1, source_target_pairs={{0,4},{1,5},{2,6},{3,7},{4,0},{5,1},{6,2},{7,3},{8,12},{9,13},{10,... | collective-permute-start | bytes 983048 | tf_op jit(solution)/shard_map/ppermute | solution.py:349
  123.6 5.0 %collective-permute-start = (bf16[256,1280]{1,0:T(8,128)(2,1)S(1)}, bf16[256,1280]{1,0:T(8,128)(2,1)S(1)}, u32[]{:S(2)}, u32[]{:S(2)}) collective-permute-start(bf16[256,1280]{1,0:T(8,128)(2,1)S(1)} %get-tuple-element.45), channel_id=1, source_target_pairs={{0,8},{8,0},{16,24},{24,16},{32,40},{40,32},{48,56},{56,48},{64,72... | collective-permute-start | bytes 1966088 | tf_op jit(solution)/shard_map/cond/branch_1_fun/ppermute | solution.py:360
  126.7 12.0 %collective-permute-start.1 = (bf16[256,1280]{1,0:T(8,128)(2,1)S(1)}, bf16[256,1280]{1,0:T(8,128)(2,1)}, u32[]{:S(2)}, u32[]{:S(2)}) collective-permute-start(bf16[256,1280]{1,0:T(8,128)(2,1)S(1)} %get-tuple-element.46), channel_id=1, source_target_pairs={{8,0},{16,8},{24,16},{32,24},{40,32},{48,40},{56,48},{64,56},{72,6... | collective-permute-start | bytes 1966088 | tf_op jit(solution)/shard_map/cond/branch_1_fun/ppermute | solution.py:355
  140.0 17.0 %collective-permute-start.2 = (bf16[256,1280]{1,0:T(8,128)(2,1)S(1)}, bf16[256,1280]{1,0:T(8,128)(2,1)}, u32[]{:S(2)}, u32[]{:S(2)}) collective-permute-start(bf16[256,1280]{1,0:T(8,128)(2,1)S(1)} %fold.1), channel_id=1, source_target_pairs={{16,0},{24,8},{32,16},{40,24},{48,32},{56,40},{64,48},{72,56},{80,... | collective-permute-start | bytes 1966088 | tf_op jit(solution)/shard_map/cond/branch_1_fun/ppermute | solution.py:355

commit v13 on v11

--- a/solution.py
+++ b/solution.py
@@ -76,27 +76,27 @@
     )(query, saved_out, grad_out, frames)
 
 
-def pack_keys_kernel(k_any, v_any, out, held, sems):
-    load_all((k_any, v_any), held, sems)
+def pack_keys_kernel(near, far, out):
     for head in range(HEADS):
         group, h = divmod(head, GROUP)
         cols = slice(head * HDIM, (head + 1) * HDIM)
-        for at in range(2):
-            out[group, :, (2 * h + at) * HDIM : (2 * h + at + 1) * HDIM] = held[at, :, cols]
-
-
-def pack_keys(key, value):
-    tok, width = key.shape
+        for block, ref in enumerate((near, far)):
+            for at in range(2):
+                first = (2 * (block * GROUP + h) + at) * HDIM
+                out[group, :, first : first + HDIM] = ref[at, :, cols]
+
+
+def pack_keys(near, far):
+    _, tok, width = near.shape
     return pl.pallas_call(
         pack_keys_kernel,
-        out_shape=jax.ShapeDtypeStruct((XN, tok, 2 * GROUP * HDIM), BF16),
-        in_specs=[pl.BlockSpec(memory_space=pl.ANY)] * 2,
+        out_shape=jax.ShapeDtypeStruct((XN, tok, 4 * GROUP * HDIM), BF16),
+        in_specs=[vmem()] * 2,
         out_specs=vmem(),
-        scratch_shapes=[pltpu.VMEM((2, tok, width), BF16), pltpu.SemaphoreType.DMA((2,))],
-        compiler_params=params(60),
-        cost_estimate=cost(0, 8 * tok * width),
+        compiler_params=params(),
+        cost_estimate=cost(0, 16 * tok * width),
         name="pack_keys",
-    )(key, value)
+    )(near, far)
 
 
 META = slice(2 * GROUP * HDIM, (2 * GROUP + 1) * HDIM)
@@ -106,18 +106,19 @@
     return slice(at * HDIM, (at + 1) * HDIM)
 
 
-def seen(rows, own):
-    k_frame = own[:, META].astype(F32)[:, FRAME_LANE : FRAME_LANE + 1]
+def seen(rows, own_meta):
+    k_frame = own_meta.astype(F32)[:, FRAME_LANE : FRAME_LANE + 1]
     return k_frame <= rows[FRAME_LANE : FRAME_LANE + 1, :]
 
 
-def stats_kernel(bias_ref, tokens, own, w0, w1, w2, w3, out_ref):
+def stats_kernel(bias_ref, tokens, own, near, w2, w3, out_ref):
     half = own.shape[0]
-    mask = seen(tokens[:, META].astype(F32).T, own)
+    mask = seen(tokens[:, META].astype(F32).T, own[:, META])
     out_ref[...] = jnp.zeros_like(out_ref)
     for head in range(GROUP):
         queries = tokens[:, head_slice(head)].T
-        keys = [ref[:, head_slice(2 * head)] for ref in (w0, w1, w2, w3)]
+        at = head_slice(2 * head)
+        keys = [near[:, at], near[:, head_slice(2 * (GROUP + head))], w2[:, at], w3[:, at]]
         scores = jnp.dot(
             jnp.concatenate(keys, axis=0), queries, preferred_element_type=F32
         ) * SCALE2
@@ -149,7 +150,7 @@
     return pl.pallas_call(
         stats_kernel,
         out_shape=jax.ShapeDtypeStruct((16, half), F32),
-        in_specs=[smem()] + [vmem()] * 6,
+        in_specs=[smem()] + [vmem()] * 5,
         out_specs=vmem(),
         compiler_params=params(),
         cost_estimate=cost(4 * pairs * HDIM, 5 * half * GROUP * HDIM * 2, pairs),
@@ -165,35 +166,65 @@
     return peak + jnp.log2(one_part + other_sum * jnp.exp2(other_peak - peak))
 
 
-def grads_kernel(parts_in, bias_ref, place, one, other, tokens, own, w0, w1, w2, w3, *rest):
+def pair_slice(head):
+    return slice(2 * head * HDIM, 2 * (head + 1) * HDIM)
+
+
+def grads_kernel(parts_in, bias_ref, place, one, other, tokens, own, near, w2, w3, *rest):
     if parts_in:
         parts, rest = rest[:WBLK], rest[WBLK:]
     dq_out, *outs = rest[: 1 + WBLK]
-    rows, acc, dq_acc, sems, *rest = rest[1 + WBLK :]
-    loads, stores = [], []
-    if parts_in:
-        held, load_sems = rest
-        for role, part in enumerate(parts):
-            loads.append(pltpu.make_async_copy(part, held.at[role], load_sems.at[role]))
-            loads[-1].start()
-    half = own.shape[0]
-    rows[...] = tokens[:, META].astype(F32).T
+    rest = rest[1 + WBLK :]
+    rows, dq_acc, sums, window, held, k_meta, load_sems, sems, *rest = rest
+    half = rows.shape[1]
+
+    metas = [
+        pltpu.make_async_copy(tokens.at[:, META], held.at[:, META], load_sems.at[GROUP, 0]),
+        pltpu.make_async_copy(own.at[:, META], k_meta, load_sems.at[GROUP, 1]),
+    ]
+    loads = []
+    for head in range(GROUP):
+        at = pair_slice(head)
+        moves = [
+            (near.at[:, at], window.at[0, :, at]),
+            (near.at[:, pair_slice(GROUP + head)], window.at[1, :, at]),
+            (w2.at[:, at], window.at[2, :, at]),
+            (w3.at[:, at], window.at[3, :, at]),
+        ]
+        for cols in (head_slice(head), head_slice(GROUP + head)):
+            moves.append((tokens.at[:, cols], held.at[:, cols]))
+        if parts_in:
+            moves += [(part.at[:, at], rest[0].at[role, :, at]) for role, part in enumerate(parts)]
+        loads.append(
+            [
+                pltpu.make_async_copy(src, dst, load_sems.at[head, i])
+                for i, (src, dst) in enumerate(moves)
+            ]
+        )
+    for copy in metas + sum(loads, []):
+        copy.start()
+    for copy in metas:
+        copy.wait()
+
+    rows[...] = held[:, META].astype(F32).T
+    mask = seen(rows, k_meta[...])
     totals = log_total(one, other)
-    window = (w0, w1, w2, w3)
+    stores = []
     for head in range(GROUP):
+        for copy in loads[head]:
+            copy.wait()
         q_cols = head_slice(head)
-        pair = slice(2 * head * HDIM, 2 * (head + 1) * HDIM)
-        queries, grads = tokens[:, q_cols], tokens[:, head_slice(GROUP + head)]
+        queries, grads = held[:, q_cols], held[:, head_slice(GROUP + head)]
         first = place[0] * GROUP + head
         dot = rows[pl.ds(first, 1), :] + rows[pl.ds(LOW_LANE + first, 1), :]
-        keys = jnp.concatenate([ref[:, head_slice(2 * head)] for ref in window], axis=0)
-        values = jnp.concatenate([ref[:, head_slice(2 * head + 1)] for ref in window], axis=0)
+        keys = window[:, :, head_slice(2 * head)].reshape(WBLK * half, HDIM)
+        values = window[:, :, head_slice(2 * head + 1)].reshape(WBLK * half, HDIM)
         scores = jnp.dot(keys, queries.T, preferred_element_type=F32) * SCALE2
         pieces = []
         for role in range(WBLK):
             piece = scores[role * half : (role + 1) * half]
             if role == 0:
-                piece = jnp.where(seen(rows, own), piece, NEG)
+                piece = jnp.where(mask, piece, NEG)
             pieces.append(jnp.exp2(piece - (totals[head : head + 1] - bias_ref[role])))
         probs = jnp.concatenate(pieces, axis=0)
         dv = jnp.dot(probs.astype(BF16), grads, preferred_element_type=F32)
@@ -201,25 +232,23 @@
         ds = (probs * (dp - dot)).astype(BF16)
         dk = jnp.dot(ds, queries, preferred_element_type=F32) * FACTOR
         dq = jnp.dot(keys.T, ds, preferred_element_type=F32)
-        if parts_in and head == 0:
-            for load in loads:
-                load.wait()
         for role in range(WBLK):
             of = slice(role * half, (role + 1) * half)
             for cols, value in ((2 * head, dk[of]), (2 * head + 1, dv[of])):
                 if parts_in:
-                    value += held[role, :, head_slice(cols)].astype(F32)
-                acc[role, :, head_slice(cols)] = value.astype(BF16)
+                    value += rest[0][role, :, head_slice(cols)].astype(F32)
+                sums[role, :, head_slice(cols)] = value.astype(BF16)
+            at = pair_slice(head)
             stores.append(
                 pltpu.make_async_copy(
-                    acc.at[role, :, pair], outs[role].at[:, pair], sems.at[role, head]
+                    sums.at[role, :, at], outs[role].at[:, at], sems.at[head, role]
                 )
             )
             stores[-1].start()
         dq_acc[:, q_cols] = (dq * FACTOR).T.astype(dq_acc.dtype)
         stores.append(
             pltpu.make_async_copy(
-                dq_acc.at[:, q_cols], dq_out.at[:, q_cols], sems.at[WBLK, head]
+                dq_acc.at[:, q_cols], dq_out.at[:, q_cols], sems.at[head, WBLK]
             )
         )
         stores[-1].start()
@@ -232,22 +261,25 @@
     wide = GROUP * HDIM
     pairs = GROUP * half * WBLK * half
     hbm = pl.BlockSpec(memory_space=pl.ANY)
+    blocks = pltpu.VMEM((WBLK, half, 2 * wide), BF16)
     scratch = [
         pltpu.VMEM((HDIM, half), F32),
-        pltpu.VMEM((WBLK, half, 2 * wide), BF16),
         pltpu.VMEM((half, wide), dq_kind),
-        pltpu.SemaphoreType.DMA((WBLK + 1, GROUP)),
+        blocks,
+        blocks,
+        pltpu.VMEM(tokens.shape, BF16),
+        pltpu.VMEM((half, HDIM), BF16),
+        pltpu.SemaphoreType.DMA((GROUP + 1, 2 * WBLK + 2)),
+        pltpu.SemaphoreType.DMA((GROUP, WBLK + 1)),
     ]
-    if parts:
-        scratch += [pltpu.VMEM((WBLK, half, 2 * wide), BF16), pltpu.SemaphoreType.DMA((WBLK,))]
     return pl.pallas_call(
         functools.partial(grads_kernel, bool(parts)),
         out_shape=[jax.ShapeDtypeStruct((half, wide), dq_kind)]
         + [jax.ShapeDtypeStruct((half, 2 * wide), BF16)] * WBLK,
-        in_specs=[smem(), smem()] + [vmem()] * (4 + WBLK) + [hbm] * len(parts),
+        in_specs=[smem(), smem(), vmem(), vmem()] + [hbm] * (5 + len(parts)),
         out_specs=[hbm] * (1 + WBLK),
-        scratch_shapes=scratch,
-        compiler_params=params(),
+        scratch_shapes=scratch + [blocks] * bool(parts),
+        compiler_params=params(28),
         cost_estimate=cost(10 * pairs * HDIM, 12 * half * wide * 2, pairs),
         name=name,
     )(*common, tokens, own, *window, *parts)
@@ -355,7 +387,7 @@
 
 def no_grads(operands):
     own, window = operands[1:3]
-    empty = jnp.zeros_like(window[0])
+    empty = jnp.zeros_like(window[1])
     return jnp.zeros((own.shape[0], GROUP * HDIM), F32), empty, empty, empty
 
 
@@ -366,14 +398,14 @@
     even = is_even.astype(jnp.int32).reshape(1)
     tok = query.shape[0]
     half = XN * tok
-
-    qg = pack_queries(query, saved_out, grad_out, frame_ids[:, None])
-    w0 = over_x(pack_keys(key, value))
-    qg, w0 = lax.optimization_barrier((qg, w0))
-    w0 = w0.reshape(half, -1)
-    own = over_x(qg).reshape(half, -1)
+    wide = 2 * GROUP * HDIM
+
+    kv = jnp.stack([key, value])
+    kv_far = along_row(kv, 2)
+    own = over_x(pack_queries(query, saved_out, grad_out, frame_ids[:, None])).reshape(half, -1)
     far = across_z(own)
-    w1 = along_row(w0, 2)
+    near = over_x(pack_keys(kv, kv_far)).reshape(half, -1)
+    w0, w1 = near[:, :wide], near[:, wide:]
     w3 = along_row(jnp.where(is_even, w0, w1), 1)
     w2 = in_chip(w1)
     held = jnp.stack(
@@ -386,7 +418,7 @@
     )
     bias = jnp.where(held, 0.0, NEG).astype(F32)
 
-    window = (w0, w1, w2, w3)
+    window = (near, w2, w3)
     own_near = stats("stats_own", bias, own, own, window)
     far_other = across_z(own_near)
     far_near = stats("stats_far", bias, far, own, window)

time: 167 us -> 164 us (0.982)
  the two profiles are of different devices: /device:TPU:129 before, /device:TPU:1 now
where the time goes in v13:
time: 164 us; the launch traced here: 163 us
  starting transfers between devices  63.2 us (39%)
  waiting for transfers between devices  39.5 us (24%)
  Pallas kernels  30.8 us (19%)
  blocking collectives  25.6 us (16%)
  other arithmetic  2.22 us (1%)
    ppermute x4, waiting for transfers between devices, along_row(): lax.ppermute(value, 'row', [(r, r + steps) for r in range(first, last)])  33.5 us
    ppermute x4, starting transfers between devices, across_z(): lax.ppermute(value, 'col', [(c, (c + XN) % count) for c in range(count)])  32.8 us
    all_to_all x1, blocking collectives, over_x(): return lax.all_to_all(value, 'col', 0, 0, axis_index_groups=groups)  25.6 us
    ppermute x4, starting transfers between devices, along_row(): lax.ppermute(value, 'row', [(r, r + steps) for r in range(first, last)])  19 us
    pallas_call x2, Pallas kernels, grads(): pl.pallas_call(functools.partial(grads_kernel, bool(parts)), out_shape=[j...  15.7 us
    all_to_all x2, starting transfers between devices, over_x(): return lax.all_to_all(value, 'col', 0, 0, axis_index_groups=groups)  7.56 us
    pallas_call x2, Pallas kernels, stats(): pl.pallas_call(stats_kernel, out_shape=jax.ShapeDtypeStruct((16, half), F...  5.96 us
    all_to_all x2, waiting for transfers between devices, over_x(): return lax.all_to_all(value, 'col', 0, 0, axis_index_groups=groups)  4.42 us
  transfers between devices with their start and end apart: 12, of which 6 were waited for; matrix products, arithmetic and copies ran while one was open for 1% of the time, Pallas kernels for 17%

profile of v13, /device:TPU:1, one launch (start us, length us, event | category | flops | bytes accessed | tf_op | source)
XLA Modules:
  0.0 163.0 jit_solution(16452889530134282899)
XLA Ops:
  0.6 0.0 copy-start
  0.6 1.1 pad_maximum_fusion.near
  1.8 4.1 %collective-permute-start.3 = (bf16[2,64,2560]{2,1,0:T(8,128)(2,1)S(1)}, bf16[2,64,2560]{2,1,0:T(8,128)(2,1)S(1)}, u32[]{:S(2)}, u32[]{:S(2)}) collective-permute-start(bf16[2,64,2560]{2,1,0:T(8,128)(2,1)S(1)} %pad_maximum_fusion.near), channel_id=1, source_target_pairs={{0,16},{8,24},{16,32},{24,40},{32,48},{40,56},{48,64},{56,72},{64,... | collective-permute-start | bytes 1966088 | tf_op jit(solution)/shard_map/ppermute | solution.py:373
  5.9 0.0 copy-done
  5.9 0.7 copy.9.f_ref
  6.6 3.1 %pack_queries.1 = bf16[4,64,1408]{2,1,0:T(8,128)(2,1)} custom-call(bf16[64,2560]{1,0:T(8,128)(2,1)} %q_any.1, bf16[64,2560]{1,0:T(8,128)(2,1)} %o_any.1, bf16[64,2560]{1,0:T(8,128)(2,1)} %g_any.1, s32[64,1]{1,0:T(8,128)} %copy.9.f_ref), custom_call_target="tpu_custom_call" | custom-call | flops 327680 | bytes 2293760 | tf_op jit(solution)/shard_map/pack_queries/pallas_call | solution.py:67
  9.7 4.0 %all-to-all-start = ((bf16[4,64,1408]{2,1,0:T(8,128)(2,1)}), bf16[4,64,1408]{2,1,0:T(8,128)(2,1)S(1)}, u32[]{:S(2)}, u32[]{:S(2)}) async-start(bf16[4,64,1408]{2,1,0:T(8,128)(2,1)} %pack_queries.1), calls=%async_computation | async-start | bytes 1441792 | tf_op jit(solution)/shard_map/all_to_all | solution.py:362
  13.7 2.3 %collective-permute-done.3.far = bf16[2,64,2560]{2,1,0:T(8,128)(2,1)S(1)} collective-permute-done((bf16[2,64,2560]{2,1,0:T(8,128)(2,1)S(1)}, bf16[2,64,2560]{2,1,0:T(8,128)(2,1)S(1)}, u32[]{:S(2)}, u32[]{:S(2)}) %collective-permute-start.3) | collective-permute-done | bytes 655392 | tf_op jit(solution)/shard_map/ppermute | solution.py:373
  16.0 1.3 pack_keys.1
  17.3 4.4 %all-to-all-done = bf16[4,64,1408]{2,1,0:T(8,128)(2,1)S(1)} async-done(((bf16[4,64,1408]{2,1,0:T(8,128)(2,1)}), bf16[4,64,1408]{2,1,0:T(8,128)(2,1)S(1)}, u32[]{:S(2)}, u32[]{:S(2)}) %all-to-all-start) | async-done | bytes 720928 | tf_op jit(solution)/shard_map/all_to_all | solution.py:362
  21.7 3.5 %all-to-all-start.1 = ((bf16[4,64,2560]{2,1,0:T(8,128)(2,1)}), bf16[4,64,2560]{2,1,0:T(8,128)(2,1)S(1)}, u32[]{:S(2)}, u32[]{:S(2)}) async-start(bf16[4,64,2560]{2,1,0:T(8,128)(2,1)} %pack_keys.1), calls=%async_computation.1 | async-start | bytes 2621440 | tf_op jit(solution)/shard_map/all_to_all | solution.py:362
  25.3 13.0 %collective-permute-start.6 = (bf16[256,1408]{1,0:T(8,128)(2,1)S(1)}, bf16[256,1408]{1,0:T(8,128)(2,1)S(1)}, u32[]{:S(2)}, u32[]{:S(2)}) collective-permute-start(bf16[256,1408]{1,0:T(8,128)(2,1)S(1)} %bitcast.17), channel_id=1, source_target_pairs={{0,4},{1,5},{2,6},{3,7},{4,0},{5,1},{6,2},{7,3},{8,12},{9,13},{10,... | collective-permute-start | bytes 2162696 | tf_op jit(solution)/shard_map/ppermute | solution.py:367
  38.3 0.0 all-to-all-done.1
  38.3 0.9 slice_select_fusion
  39.2 11.2 %collective-permute-start.5 = (bf16[256,1280]{1,0:T(8,128)(2,1)}, bf16[256,1280]{1,0:T(8,128)(2,1)}, u32[]{:S(2)}, u32[]{:S(2)}) collective-permute-start(bf16[256,1280]{1,0:T(8,128)(2,1)} %get-tuple-element.69), channel_id=1, source_target_pairs={{0,8},{8,16},{16,24},{24,32},{32,40},{40,48},{48,56},{56,64},{64,7... | collective-permute-start | bytes 1966088 | tf_op jit(solution)/shard_map/ppermute | solution.py:373
  50.4 1.9 %collective-permute-start.4 = (bf16[256,1280]{1,0:T(8,128)(2,1)S(1)}, bf16[256,1280]{1,0:T(8,128)(2,1)}, u32[]{:S(2)}, u32[]{:S(2)}) collective-permute-start(bf16[256,1280]{1,0:T(8,128)(2,1)S(1)} %get-tuple-element.70), channel_id=1, source_target_pairs={{0,8},{8,0},{16,24},{24,16},{32,40},{40,32},{48,56},{56,48},{64,72... | collective-permute-start | bytes 1966088 | tf_op jit(solution)/shard_map/ppermute | solution.py:378
  52.4 0.1 pad_add_fusion.place
  52.5 0.1 add_select_fusion.bias_ref
  52.6 5.7 %collective-permute-done.5.w3 = bf16[256,1280]{1,0:T(8,128)(2,1)} collective-permute-done((bf16[256,1280]{1,0:T(8,128)(2,1)}, bf16[256,1280]{1,0:T(8,128)(2,1)}, u32[]{:S(2)}, u32[]{:S(2)}) %collective-permute-start.5) | collective-permute-done | bytes 655392 | tf_op jit(solution)/shard_map/ppermute | solution.py:373
  58.3 0.0 collective-permute-done.4.w2
  58.3 3.0 %stats_own.1 = f32[16,256]{1,0:T(8,128)S(1)} custom-call(f32[4]{0:T(128)S(1)} %add_select_fusion.bias_ref, bf16[256,1408]{1,0:T(8,128)(2,1)S(1)} %bitcast.18, bf16[256,1408]{1,0:T(8,128)(2,1)S(1)} %bitcast.19, bf16[256,2560]{1,0:T(8,128)(2,1)S(1)} %bitcast.13, bf16[256,1280]{1,0:T(8,128)(2,1)} %collective-permute-done.4.w2, ...), custom_call_target="tpu_custom_call" | custom-call | flops 671088640 | bytes 1638400 | tf_op jit(solution)/shard_map/stats_own/pallas_call | solution.py:150
  61.2 10.6 %collective-permute-start.7 = (f32[16,256]{1,0:T(8,128)S(1)}, f32[16,256]{1,0:T(8,128)S(1)}, u32[]{:S(2)}, u32[]{:S(2)}) collective-permute-start(f32[16,256]{1,0:T(8,128)S(1)} %stats_own.1), channel_id=1, source_target_pairs={{0,4},{1,5},{2,6},{3,7},{4,0},{5,1},{6,2},{7,3},{8,12},{9,13},{10,... | collective-permute-start | bytes 49160 | tf_op jit(solution)/shard_map/ppermute | solution.py:367
  71.9 0.0 collective-permute-done.6.tokens
  71.9 3.0 %stats_far.1.one = f32[16,256]{1,0:T(8,128)S(1)} custom-call(f32[4]{0:T(128)S(1)} %add_select_fusion.bias_ref, bf16[256,1408]{1,0:T(8,128)(2,1)S(1)} %collective-permute-done.6.tokens, bf16[256,1408]{1,0:T(8,128)(2,1)S(1)} %bitcast.20, bf16[256,2560]{1,0:T(8,128)(2,1)S(1)} %bitcast.14, bf16[256,1280]{1,0:T(8,128)(2,1)} %collective-permute-done.4.w2, ...), custom_call_target="tpu_custom_call" | custom-call | flops 671088640 | bytes 1638400 | tf_op jit(solution)/shard_map/stats_far/pallas_call | solution.py:150
  74.9 1.9 %collective-permute-start.8 = (f32[16,256]{1,0:T(8,128)S(1)}, f32[16,256]{1,0:T(8,128)S(1)}, u32[]{:S(2)}, u32[]{:S(2)}) collective-permute-start(f32[16,256]{1,0:T(8,128)S(1)} %stats_far.1.one), channel_id=1, source_target_pairs={{0,4},{1,5},{2,6},{3,7},{4,0},{5,1},{6,2},{7,3},{8,12},{9,13},{10,... | collective-permute-start | bytes 49160 | tf_op jit(solution)/shard_map/ppermute | solution.py:367
  76.8 1.6 collective-permute-done.7.other
  78.4 7.6 %grads_far.1 = (bf16[256,640]{1,0:T(8,128)(2,1)S(1)}, bf16[256,1280]{1,0:T(8,128)(2,1)}, bf16[256,1280]{1,0:T(8,128)(2,1)}, bf16[256,1280]{1,0:T(8,128)(2,1)}, bf16[256,1280]{1,0:T(8,128)(2,1)}) custom-call(f32[4]{0:T(128)S(1)} %add_select_fusion.bias_ref, s32[2]{0:T(128)S(1)} %pad_add_fusion.place, f32[16,256]{1,0:T(8,128)S(1)} %stats_far.1.one, ...), custom_call_target="tpu_custom_call" | custom-call | flops 1677721600 | bytes 3932160 | tf_op jit(solution)/shard_map/grads_far/pallas_call | solution.py:275
  86.0 0.0 collective-permute-done.8
  86.0 7.3 %collective-permute-start.9 = (bf16[256,640]{1,0:T(8,128)(2,1)S(1)}, bf16[256,640]{1,0:T(8,128)(2,1)S(1)}, u32[]{:S(2)}, u32[]{:S(2)}) collective-permute-start(bf16[256,640]{1,0:T(8,128)(2,1)S(1)} %get-tuple-element.65), channel_id=1, source_target_pairs={{0,4},{1,5},{2,6},{3,7},{4,0},{5,1},{6,2},{7,3},{8,12},{9,13},{10,... | collective-permute-start | bytes 983048 | tf_op jit(solution)/shard_map/ppermute | solution.py:367
  93.3 40.6 %conditional.1 = (f32[256,640]{1,0:T(8,128)S(1)}, bf16[256,1280]{1,0:T(8,128)(2,1)S(1)}, bf16[256,1280]{1,0:T(8,128)(2,1)}, bf16[256,1280]{1,0:T(8,128)(2,1)}) conditional(s32[]{:T(128)} %convert_element_type.4, () %tuple.16, (f32[4]{0:T(128)S(1)}, s32[2]{0:T(128)S(1)}, f32[16,256]{1,0:T(8,128)S(1)}, f32[16,256]{1,0:T(8,128)S(1)}, ...), branch_computations={%region_0.1_spmd, %region_1.2_spmd} | conditional | flops 1678704640 | bytes 14418072 | solution.py:432
  93.3 8.1 %grads_own.1 = (f32[256,640]{1,0:T(8,128)S(1)}, bf16[256,1280]{1,0:T(8,128)(2,1)S(1)}, bf16[256,1280]{1,0:T(8,128)(2,1)S(1)}, bf16[256,1280]{1,0:T(8,128)(2,1)S(1)}, bf16[256,1280]{1,0:T(8,128)(2,1)S(1)}) custom-call(f32[4]{0:T(128)S(1)} %get-tuple-element.26.bias_ref, s32[2]{0:T(128)S(1)} %get-tuple-element.27.place, f32[16,256]{1,0:T(8,128)S(1)} %get-tuple-element.28.one, ...), custom_call_target="tpu_custom_call" | custom-call | flops 1677721600 | bytes 3932160 | tf_op jit(solution)/shard_map/cond/branch_1_fun/grads_own/pallas_call | solution.py:275
  101.4 1.9 %collective-permute-start = (bf16[256,1280]{1,0:T(8,128)(2,1)S(1)}, bf16[256,1280]{1,0:T(8,128)(2,1)S(1)}, u32[]{:S(2)}, u32[]{:S(2)}) collective-permute-start(bf16[256,1280]{1,0:T(8,128)(2,1)S(1)} %get-tuple-element.42), channel_id=1, source_target_pairs={{0,8},{8,0},{16,24},{24,16},{32,40},{40,32},{48,56},{56,48},{64,72... | collective-permute-start | bytes 1966088 | tf_op jit(solution)/shard_map/cond/branch_1_fun/ppermute | solution.py:378
  103.3 2.4 %collective-permute-start.1 = (bf16[256,1280]{1,0:T(8,128)(2,1)S(1)}, bf16[256,1280]{1,0:T(8,128)(2,1)}, u32[]{:S(2)}, u32[]{:S(2)}) collective-permute-start(bf16[256,1280]{1,0:T(8,128)(2,1)S(1)} %get-tuple-element.43), channel_id=1, source_target_pairs={{8,0},{16,8},{24,16},{32,24},{40,32},{48,40},{56,48},{64,56},{72,6... | collective-permute-start | bytes 1966088 | tf_op jit(solution)/shard_map/cond/branch_1_fun/ppermute | solution.py:373
  105.7 0.0 collective-permute-done.swapped
  105.8 9.8 %collective-permute-done.1.side = bf16[256,1280]{1,0:T(8,128)(2,1)} collective-permute-done((bf16[256,1280]{1,0:T(8,128)(2,1)S(1)}, bf16[256,1280]{1,0:T(8,128)(2,1)}, u32[]{:S(2)}, u32[]{:S(2)}) %collective-permute-start.1) | collective-permute-done | bytes 655392 | tf_op jit(solution)/shard_map/cond/branch_1_fun/ppermute | solution.py:373
  115.5 1.3 fold.1
  116.8 1.3 collective-permute-start.2
  118.1 15.7 %collective-permute-done.2 = bf16[256,1280]{1,0:T(8,128)(2,1)} collective-permute-done((bf16[256,1280]{1,0:T(8,128)(2,1)S(1)}, bf16[256,1280]{1,0:T(8,128)(2,1)}, u32[]{:S(2)}, u32[]{:S(2)}) %collective-permute-start.2) | collective-permute-done | bytes 655392 | tf_op jit(solution)/shard_map/cond/branch_1_fun/ppermute | solution.py:373
  133.9 0.0 collective-permute-done.9.dq_back
  133.9 2.4 %close.1 = bf16[4,64,1920]{2,1,0:T(8,128)(2,1)S(1)} custom-call(s32[1]{0:T(128)} %bitcast.even_ref, f32[256,640]{1,0:T(8,128)S(1)} %get-tuple-element.64.dq_own, bf16[256,640]{1,0:T(8,128)(2,1)S(1)} %collective-permute-done.9.dq_back, bf16[256,1280]{1,0:T(8,128)(2,1)S(1)} %get-tuple-element.66.d0, bf16[256,1280]{1,0:T(8,128)(2,1)} %get-tuple-element.67.back, ...), custom_call_target="tpu_custom_call" | custom-call | flops 983040 | bytes 3932160 | tf_op jit(solution)/shard_map/close/pallas_call | solution.py:324
  136.3 25.6 %all_to_all.15.parts = bf16[4,64,1920]{2,1,0:T(8,128)(2,1)S(1)} all-to-all(bf16[4,64,1920]{2,1,0:T(8,128)(2,1)S(1)} %close.1), channel_id=1, replica_groups={{0,1,2,3},{4,5,6,7},{8,9,10,11},{12,13,14,15},{16,17,18,19},{20,21,22,2..., dimensions={0} | all-to-all | bytes 1966080 | tf_op jit(solution)/shard_map/all_to_all | solution.py:362
  161.9 1.1 unpack.1
Async XLA Ops:
  0.6 5.2 %copy-start = (s32[64]{0:T(128)S(1)}, s32[64]{0:T(128)}, u32[]{:S(2)}) copy-start(s32[64]{0:T(128)} %param.13) | copy-start | bytes 772
  1.8 14.2 %collective-permute-start.3 = (bf16[2,64,2560]{2,1,0:T(8,128)(2,1)S(1)}, bf16[2,64,2560]{2,1,0:T(8,128)(2,1)S(1)}, u32[]{:S(2)}, u32[]{:S(2)}) collective-permute-start(bf16[2,64,2560]{2,1,0:T(8,128)(2,1)S(1)} %pad_maximum_fusion.near), channel_id=1, source_target_pairs={{0,16},{8,24},{16,32},{24,40},{32,48},{40,56},{48,64},{56,72},{64,... | collective-permute-start | bytes 1966088 | tf_op jit(solution)/shard_map/ppermute | solution.py:373
  9.7 12.0 %all-to-all-start = ((bf16[4,64,1408]{2,1,0:T(8,128)(2,1)}), bf16[4,64,1408]{2,1,0:T(8,128)(2,1)S(1)}, u32[]{:S(2)}, u32[]{:S(2)}) async-start(bf16[4,64,1408]{2,1,0:T(8,128)(2,1)} %pack_queries.1), calls=%async_computation | async-start | bytes 1441792 | tf_op jit(solution)/shard_map/all_to_all | solution.py:362
  21.7 16.6 %all-to-all-start.1 = ((bf16[4,64,2560]{2,1,0:T(8,128)(2,1)}), bf16[4,64,2560]{2,1,0:T(8,128)(2,1)S(1)}, u32[]{:S(2)}, u32[]{:S(2)}) async-start(bf16[4,64,2560]{2,1,0:T(8,128)(2,1)} %pack_keys.1), calls=%async_computation.1 | async-start | bytes 2621440 | tf_op jit(solution)/shard_map/all_to_all | solution.py:362
  25.3 46.6 %collective-permute-start.6 = (bf16[256,1408]{1,0:T(8,128)(2,1)S(1)}, bf16[256,1408]{1,0:T(8,128)(2,1)S(1)}, u32[]{:S(2)}, u32[]{:S(2)}) collective-permute-start(bf16[256,1408]{1,0:T(8,128)(2,1)S(1)} %bitcast.17), channel_id=1, source_target_pairs={{0,4},{1,5},{2,6},{3,7},{4,0},{5,1},{6,2},{7,3},{8,12},{9,13},{10,... | collective-permute-start | bytes 2162696 | tf_op jit(solution)/shard_map/ppermute | solution.py:367
  39.2 19.0 %collective-permute-start.5 = (bf16[256,1280]{1,0:T(8,128)(2,1)}, bf16[256,1280]{1,0:T(8,128)(2,1)}, u32[]{:S(2)}, u32[]{:S(2)}) collective-permute-start(bf16[256,1280]{1,0:T(8,128)(2,1)} %get-tuple-element.69), channel_id=1, source_target_pairs={{0,8},{8,16},{16,24},{24,32},{32,40},{40,48},{48,56},{56,64},{64,7... | collective-permute-start | bytes 1966088 | tf_op jit(solution)/shard_map/ppermute | solution.py:373
  50.4 7.8 %collective-permute-start.4 = (bf16[256,1280]{1,0:T(8,128)(2,1)S(1)}, bf16[256,1280]{1,0:T(8,128)(2,1)}, u32[]{:S(2)}, u32[]{:S(2)}) collective-permute-start(bf16[256,1280]{1,0:T(8,128)(2,1)S(1)} %get-tuple-element.70), channel_id=1, source_target_pairs={{0,8},{8,0},{16,24},{24,16},{32,40},{40,32},{48,56},{56,48},{64,72... | collective-permute-start | bytes 1966088 | tf_op jit(solution)/shard_map/ppermute | solution.py:378
  61.2 17.2 %collective-permute-start.7 = (f32[16,256]{1,0:T(8,128)S(1)}, f32[16,256]{1,0:T(8,128)S(1)}, u32[]{:S(2)}, u32[]{:S(2)}) collective-permute-start(f32[16,256]{1,0:T(8,128)S(1)} %stats_own.1), channel_id=1, source_target_pairs={{0,4},{1,5},{2,6},{3,7},{4,0},{5,1},{6,2},{7,3},{8,12},{9,13},{10,... | collective-permute-start | bytes 49160 | tf_op jit(solution)/shard_map/ppermute | solution.py:367
  74.9 11.1 %collective-permute-start.8 = (f32[16,256]{1,0:T(8,128)S(1)}, f32[16,256]{1,0:T(8,128)S(1)}, u32[]{:S(2)}, u32[]{:S(2)}) collective-permute-start(f32[16,256]{1,0:T(8,128)S(1)} %stats_far.1.one), channel_id=1, source_target_pairs={{0,4},{1,5},{2,6},{3,7},{4,0},{5,1},{6,2},{7,3},{8,12},{9,13},{10,... | collective-permute-start | bytes 49160 | tf_op jit(solution)/shard_map/ppermute | solution.py:367
  86.0 47.9 %collective-permute-start.9 = (bf16[256,640]{1,0:T(8,128)(2,1)S(1)}, bf16[256,640]{1,0:T(8,128)(2,1)S(1)}, u32[]{:S(2)}, u32[]{:S(2)}) collective-permute-start(bf16[256,640]{1,0:T(8,128)(2,1)S(1)} %get-tuple-element.65), channel_id=1, source_target_pairs={{0,4},{1,5},{2,6},{3,7},{4,0},{5,1},{6,2},{7,3},{8,12},{9,13},{10,... | collective-permute-start | bytes 983048 | tf_op jit(solution)/shard_map/ppermute | solution.py:367
  101.4 4.3 %collective-permute-start = (bf16[256,1280]{1,0:T(8,128)(2,1)S(1)}, bf16[256,1280]{1,0:T(8,128)(2,1)S(1)}, u32[]{:S(2)}, u32[]{:S(2)}) collective-permute-start(bf16[256,1280]{1,0:T(8,128)(2,1)S(1)} %get-tuple-element.42), channel_id=1, source_target_pairs={{0,8},{8,0},{16,24},{24,16},{32,40},{40,32},{48,56},{56,48},{64,72... | collective-permute-start | bytes 1966088 | tf_op jit(solution)/shard_map/cond/branch_1_fun/ppermute | solution.py:378
  103.3 12.2 %collective-permute-start.1 = (bf16[256,1280]{1,0:T(8,128)(2,1)S(1)}, bf16[256,1280]{1,0:T(8,128)(2,1)}, u32[]{:S(2)}, u32[]{:S(2)}) collective-permute-start(bf16[256,1280]{1,0:T(8,128)(2,1)S(1)} %get-tuple-element.43), channel_id=1, source_target_pairs={{8,0},{16,8},{24,16},{32,24},{40,32},{48,40},{56,48},{64,56},{72,6... | collective-permute-start | bytes 1966088 | tf_op jit(solution)/shard_map/cond/branch_1_fun/ppermute | solution.py:373
  116.8 17.0 %collective-permute-start.2 = (bf16[256,1280]{1,0:T(8,128)(2,1)S(1)}, bf16[256,1280]{1,0:T(8,128)(2,1)}, u32[]{:S(2)}, u32[]{:S(2)}) collective-permute-start(bf16[256,1280]{1,0:T(8,128)(2,1)S(1)} %fold.1), channel_id=1, source_target_pairs={{16,0},{24,8},{32,16},{40,24},{48,32},{56,40},{64,48},{72,56},{80,... | collective-permute-start | bytes 1966088 | tf_op jit(solution)/shard_map/cond/branch_1_fun/ppermute | solution.py:373

commit v14 on v13

--- a/solution.py
+++ b/solution.py
@@ -45,7 +45,10 @@
     tok = held.shape[1]
     wide = GROUP * HDIM
     lane = lax.broadcasted_iota(jnp.int32, (tok, HDIM), 1)
-    meta = jnp.where(lane == FRAME_LANE, f_ref[...].astype(F32), 0.0)
+    here = lax.broadcasted_iota(jnp.int32, (tok, tok), 0)
+    same = here == lax.broadcasted_iota(jnp.int32, (tok, tok), 1)
+    frame = jnp.sum(jnp.where(same, f_ref[...].astype(F32), 0.0), axis=1, keepdims=True)
+    meta = jnp.where(lane == FRAME_LANE, frame, 0.0)
     for head in range(HEADS):
         cols = slice(head * HDIM, (head + 1) * HDIM)
         product = held[2, :, cols].astype(F32) * held[1, :, cols].astype(F32)
@@ -166,10 +169,6 @@
     return peak + jnp.log2(one_part + other_sum * jnp.exp2(other_peak - peak))
 
 
-def pair_slice(head):
-    return slice(2 * head * HDIM, 2 * (head + 1) * HDIM)
-
-
 def grads_kernel(parts_in, bias_ref, place, one, other, tokens, own, near, w2, w3, *rest):
     if parts_in:
         parts, rest = rest[:WBLK], rest[WBLK:]
@@ -178,41 +177,28 @@
     rows, dq_acc, sums, window, held, k_meta, load_sems, sems, *rest = rest
     half = rows.shape[1]
 
-    metas = [
-        pltpu.make_async_copy(tokens.at[:, META], held.at[:, META], load_sems.at[GROUP, 0]),
-        pltpu.make_async_copy(own.at[:, META], k_meta, load_sems.at[GROUP, 1]),
+    moves = [
+        (own.at[:, META], k_meta),
+        (tokens, held),
+        (near.at[:, : 2 * GROUP * HDIM], window.at[0]),
+        (near.at[:, 2 * GROUP * HDIM :], window.at[1]),
+        (w2, window.at[2]),
+        (w3, window.at[3]),
     ]
-    loads = []
-    for head in range(GROUP):
-        at = pair_slice(head)
-        moves = [
-            (near.at[:, at], window.at[0, :, at]),
-            (near.at[:, pair_slice(GROUP + head)], window.at[1, :, at]),
-            (w2.at[:, at], window.at[2, :, at]),
-            (w3.at[:, at], window.at[3, :, at]),
-        ]
-        for cols in (head_slice(head), head_slice(GROUP + head)):
-            moves.append((tokens.at[:, cols], held.at[:, cols]))
-        if parts_in:
-            moves += [(part.at[:, at], rest[0].at[role, :, at]) for role, part in enumerate(parts)]
-        loads.append(
-            [
-                pltpu.make_async_copy(src, dst, load_sems.at[head, i])
-                for i, (src, dst) in enumerate(moves)
-            ]
-        )
-    for copy in metas + sum(loads, []):
-        copy.start()
-    for copy in metas:
-        copy.wait()
+    if parts_in:
+        moves += [(part, rest[0].at[role]) for role, part in enumerate(parts)]
+    loads = [
+        pltpu.make_async_copy(src, dst, load_sems.at[i]) for i, (src, dst) in enumerate(moves)
+    ]
+    for load in loads:
+        load.start()
+    for load in loads:
+        load.wait()
 
     rows[...] = held[:, META].astype(F32).T
     mask = seen(rows, k_meta[...])
     totals = log_total(one, other)
-    stores = []
     for head in range(GROUP):
-        for copy in loads[head]:
-            copy.wait()
         q_cols = head_slice(head)
         queries, grads = held[:, q_cols], held[:, head_slice(GROUP + head)]
         first = place[0] * GROUP + head
@@ -238,20 +224,12 @@
                 if parts_in:
                     value += rest[0][role, :, head_slice(cols)].astype(F32)
                 sums[role, :, head_slice(cols)] = value.astype(BF16)
-            at = pair_slice(head)
-            stores.append(
-                pltpu.make_async_copy(
-                    sums.at[role, :, at], outs[role].at[:, at], sems.at[head, role]
-                )
-            )
-            stores[-1].start()
         dq_acc[:, q_cols] = (dq * FACTOR).T.astype(dq_acc.dtype)
-        stores.append(
-            pltpu.make_async_copy(
-                dq_acc.at[:, q_cols], dq_out.at[:, q_cols], sems.at[head, WBLK]
-            )
-        )
-        stores[-1].start()
+    stores = [pltpu.make_async_copy(dq_acc, dq_out, sems.at[WBLK])]
+    for role in range(WBLK):
+        stores.append(pltpu.make_async_copy(sums.at[role], outs[role], sems.at[role]))
+    for store in stores:
+        store.start()
     for store in stores:
         store.wait()
 
@@ -269,8 +247,8 @@
         blocks,
         pltpu.VMEM(tokens.shape, BF16),
         pltpu.VMEM((half, HDIM), BF16),
-        pltpu.SemaphoreType.DMA((GROUP + 1, 2 * WBLK + 2)),
-        pltpu.SemaphoreType.DMA((GROUP, WBLK + 1)),
+        pltpu.SemaphoreType.DMA((2 * WBLK + 2,)),
+        pltpu.SemaphoreType.DMA((WBLK + 1,)),
     ]
     return pl.pallas_call(
         functools.partial(grads_kernel, bool(parts)),
@@ -309,24 +287,39 @@
     )(even, d1, swapped, side)
 
 
-def close_kernel(even_ref, dq_own, dq_back, d0, back, side, out):
+def close_kernel(even_ref, dq_own, dq_back, d0, back, side, out, mine, theirs, pairs, sems):
     even = even_ref[0].astype(F32)
-    wide = dq_own.shape[1]
-    pair = d0[...].astype(F32) + back[...].astype(F32) + side[...].astype(F32) * even
-    out[0, :, :wide] = (dq_own[...] + dq_back[...].astype(F32)).astype(BF16)
-    out[0, :, wide:] = pair.astype(BF16)
+    moves = [(dq_own, mine), (dq_back, theirs)]
+    moves += [(src, pairs.at[at]) for at, src in enumerate((d0, back, side))]
+    loads = [pltpu.make_async_copy(src, dst, sems.at[i]) for i, (src, dst) in enumerate(moves)]
+    for load in loads:
+        load.start()
+    for load in loads:
+        load.wait()
+    tok = out.shape[1]
+    wide = mine.shape[1]
+    for step in range(XN):
+        rows = slice(step * tok, (step + 1) * tok)
+        pair = pairs[0, rows, :].astype(F32) + pairs[1, rows, :].astype(F32)
+        pair += pairs[2, rows, :].astype(F32) * even
+        out[step, :, :wide] = (mine[rows, :] + theirs[rows, :].astype(F32)).astype(BF16)
+        out[step, :, wide:] = pair.astype(BF16)
 
 
 def close(even, dq_own, dq_back, d0, back, side):
     half, wide = dq_own.shape
     tok = half // XN
-    pair = row_block((tok, 2 * wide))
     return pl.pallas_call(
         close_kernel,
-        grid=(XN,),
         out_shape=jax.ShapeDtypeStruct((XN, tok, 3 * wide), BF16),
-        in_specs=[smem(), row_block((tok, wide)), row_block((tok, wide)), pair, pair, pair],
-        out_specs=pl.BlockSpec((1, tok, 3 * wide), lambda step: (step, 0, 0)),
+        in_specs=[smem()] + [pl.BlockSpec(memory_space=pl.ANY)] * 5,
+        out_specs=vmem(),
+        scratch_shapes=[
+            pltpu.VMEM((half, wide), F32),
+            pltpu.VMEM((half, wide), BF16),
+            pltpu.VMEM((3, half, 2 * wide), BF16),
+            pltpu.SemaphoreType.DMA((5,)),
+        ],
         compiler_params=params(),
         cost_estimate=cost(6 * half * wide, 24 * half * wide),
         name="close",
@@ -402,7 +395,7 @@
 
     kv = jnp.stack([key, value])
     kv_far = along_row(kv, 2)
-    own = over_x(pack_queries(query, saved_out, grad_out, frame_ids[:, None])).reshape(half, -1)
+    own = over_x(pack_queries(query, saved_out, grad_out, frame_ids[None, :])).reshape(half, -1)
     far = across_z(own)
     near = over_x(pack_keys(kv, kv_far)).reshape(half, -1)
     w0, w1 = near[:, :wide], near[:, wide:]

time: 164 us -> 160 us (0.976)
  the two profiles are of different devices: /device:TPU:1 before, /device:TPU:129 now
where the time goes in v14:
time: 160 us; the launch traced here: 159 us
  starting transfers between devices  53.8 us (34%)
  waiting for transfers between devices  53.8 us (34%)
  Pallas kernels  30.2 us (19%)
  blocking collectives  18.3 us (11%)
  other arithmetic  2.22 us (1%)
    ppermute x4, waiting for transfers between devices, along_row(): lax.ppermute(value, 'row', [(r, r + steps) for r in range(first, last)])  38.5 us
    ppermute x4, starting transfers between devices, across_z(): lax.ppermute(value, 'col', [(c, (c + XN) % count) for c in range(count)])  27 us
    all_to_all x1, blocking collectives, over_x(): return lax.all_to_all(value, 'col', 0, 0, axis_index_groups=groups)  18.3 us
    pallas_call x2, Pallas kernels, grads(): pl.pallas_call(functools.partial(grads_kernel, bool(parts)), out_shape=[j...  15.4 us
    ppermute x4, starting transfers between devices, along_row(): lax.ppermute(value, 'row', [(r, r + steps) for r in range(first, last)])  13.8 us
    all_to_all x2, starting transfers between devices, over_x(): return lax.all_to_all(value, 'col', 0, 0, axis_index_groups=groups)  8.04 us
    ppermute x4, waiting for transfers between devices, across_z(): lax.ppermute(value, 'col', [(c, (c + XN) % count) for c in range(count)])  7.99 us
    all_to_all x2, waiting for transfers between devices, over_x(): return lax.all_to_all(value, 'col', 0, 0, axis_index_groups=groups)  7.28 us
  transfers between devices with their start and end apart: 12, of which 6 were waited for; matrix products, arithmetic and copies ran while one was open for 1% of the time, Pallas kernels for 17%

profile of v14, /device:TPU:129, one launch (start us, length us, event | category | flops | bytes accessed | tf_op | source)
XLA Modules:
  0.0 159.1 jit_solution(2640133417520964327)
XLA Ops:
  0.6 1.1 pad_maximum_fusion.near
  1.8 3.2 %collective-permute-start.3 = (bf16[2,64,2560]{2,1,0:T(8,128)(2,1)S(1)}, bf16[2,64,2560]{2,1,0:T(8,128)(2,1)S(1)}, u32[]{:S(2)}, u32[]{:S(2)}) collective-permute-start(bf16[2,64,2560]{2,1,0:T(8,128)(2,1)S(1)} %pad_maximum_fusion.near), channel_id=1, source_target_pairs={{0,16},{8,24},{16,32},{24,40},{32,48},{40,56},{48,64},{56,72},{64,... | collective-permute-start | bytes 1966088 | tf_op jit(solution)/shard_map/ppermute | solution.py:366
  5.0 3.0 %pack_queries.1 = bf16[4,64,1408]{2,1,0:T(8,128)(2,1)} custom-call(bf16[64,2560]{1,0:T(8,128)(2,1)} %q_any.1, bf16[64,2560]{1,0:T(8,128)(2,1)} %o_any.1, bf16[64,2560]{1,0:T(8,128)(2,1)} %g_any.1, s32[1,64]{1,0:T(1,128)} %bitcast.25), custom_call_target="tpu_custom_call" | custom-call | flops 327680 | bytes 2293760 | tf_op jit(solution)/shard_map/pack_queries/pallas_call | solution.py:70
  8.0 4.0 %all-to-all-start = ((bf16[4,64,1408]{2,1,0:T(8,128)(2,1)}), bf16[4,64,1408]{2,1,0:T(8,128)(2,1)S(1)}, u32[]{:S(2)}, u32[]{:S(2)}) async-start(bf16[4,64,1408]{2,1,0:T(8,128)(2,1)} %pack_queries.1), calls=%async_computation | async-start | bytes 1441792 | tf_op jit(solution)/shard_map/all_to_all | solution.py:355
  12.0 9.4 %collective-permute-done.3.far = bf16[2,64,2560]{2,1,0:T(8,128)(2,1)S(1)} collective-permute-done((bf16[2,64,2560]{2,1,0:T(8,128)(2,1)S(1)}, bf16[2,64,2560]{2,1,0:T(8,128)(2,1)S(1)}, u32[]{:S(2)}, u32[]{:S(2)}) %collective-permute-start.3) | collective-permute-done | bytes 655392 | tf_op jit(solution)/shard_map/ppermute | solution.py:366
  21.4 1.3 pack_keys.1
  22.7 0.0 all-to-all-done
  22.7 4.0 %all-to-all-start.1 = ((bf16[4,64,2560]{2,1,0:T(8,128)(2,1)}), bf16[4,64,2560]{2,1,0:T(8,128)(2,1)S(1)}, u32[]{:S(2)}, u32[]{:S(2)}) async-start(bf16[4,64,2560]{2,1,0:T(8,128)(2,1)} %pack_keys.1), calls=%async_computation.1 | async-start | bytes 2621440 | tf_op jit(solution)/shard_map/all_to_all | solution.py:355
  26.7 8.8 %collective-permute-start.6 = (bf16[256,1408]{1,0:T(8,128)(2,1)S(1)}, bf16[256,1408]{1,0:T(8,128)(2,1)S(1)}, u32[]{:S(2)}, u32[]{:S(2)}) collective-permute-start(bf16[256,1408]{1,0:T(8,128)(2,1)S(1)} %bitcast.17), channel_id=1, source_target_pairs={{0,4},{1,5},{2,6},{3,7},{4,0},{5,1},{6,2},{7,3},{8,12},{9,13},{10,... | collective-permute-start | bytes 2162696 | tf_op jit(solution)/shard_map/ppermute | solution.py:360
  35.5 7.3 %all-to-all-done.1 = bf16[4,64,2560]{2,1,0:T(8,128)(2,1)S(1)} async-done(((bf16[4,64,2560]{2,1,0:T(8,128)(2,1)}), bf16[4,64,2560]{2,1,0:T(8,128)(2,1)S(1)}, u32[]{:S(2)}, u32[]{:S(2)}) %all-to-all-start.1) | async-done | bytes 1310752 | tf_op jit(solution)/shard_map/all_to_all | solution.py:355
  42.8 0.9 slice_select_fusion
  43.8 5.0 %collective-permute-start.5 = (bf16[256,1280]{1,0:T(8,128)(2,1)}, bf16[256,1280]{1,0:T(8,128)(2,1)}, u32[]{:S(2)}, u32[]{:S(2)}) collective-permute-start(bf16[256,1280]{1,0:T(8,128)(2,1)} %get-tuple-element.69), channel_id=1, source_target_pairs={{0,8},{8,16},{16,24},{24,32},{32,40},{40,48},{48,56},{56,64},{64,7... | collective-permute-start | bytes 1966088 | tf_op jit(solution)/shard_map/ppermute | solution.py:366
  48.8 1.9 %collective-permute-start.4 = (bf16[256,1280]{1,0:T(8,128)(2,1)S(1)}, bf16[256,1280]{1,0:T(8,128)(2,1)}, u32[]{:S(2)}, u32[]{:S(2)}) collective-permute-start(bf16[256,1280]{1,0:T(8,128)(2,1)S(1)} %get-tuple-element.70), channel_id=1, source_target_pairs={{0,8},{8,0},{16,24},{24,16},{32,40},{40,32},{48,56},{56,48},{64,72... | collective-permute-start | bytes 1966088 | tf_op jit(solution)/shard_map/ppermute | solution.py:371
  50.7 0.1 pad_add_fusion.place
  50.8 0.1 add_select_fusion.bias_ref
  50.9 5.7 %collective-permute-done.5.w3 = bf16[256,1280]{1,0:T(8,128)(2,1)} collective-permute-done((bf16[256,1280]{1,0:T(8,128)(2,1)}, bf16[256,1280]{1,0:T(8,128)(2,1)}, u32[]{:S(2)}, u32[]{:S(2)}) %collective-permute-start.5) | collective-permute-done | bytes 655392 | tf_op jit(solution)/shard_map/ppermute | solution.py:366
  56.6 0.0 collective-permute-done.4.w2
  56.6 3.0 %stats_own.1 = f32[16,256]{1,0:T(8,128)S(1)} custom-call(f32[4]{0:T(128)S(1)} %add_select_fusion.bias_ref, bf16[256,1408]{1,0:T(8,128)(2,1)S(1)} %bitcast.18, bf16[256,1408]{1,0:T(8,128)(2,1)S(1)} %bitcast.19, bf16[256,2560]{1,0:T(8,128)(2,1)S(1)} %bitcast.13, bf16[256,1280]{1,0:T(8,128)(2,1)} %collective-permute-done.4.w2, ...), custom_call_target="tpu_custom_call" | custom-call | flops 671088640 | bytes 1638400 | tf_op jit(solution)/shard_map/stats_own/pallas_call | solution.py:153
  59.6 8.8 %collective-permute-start.7 = (f32[16,256]{1,0:T(8,128)S(1)}, f32[16,256]{1,0:T(8,128)S(1)}, u32[]{:S(2)}, u32[]{:S(2)}) collective-permute-start(f32[16,256]{1,0:T(8,128)S(1)} %stats_own.1), channel_id=1, source_target_pairs={{0,4},{1,5},{2,6},{3,7},{4,0},{5,1},{6,2},{7,3},{8,12},{9,13},{10,... | collective-permute-start | bytes 49160 | tf_op jit(solution)/shard_map/ppermute | solution.py:360
  68.4 8.0 %collective-permute-done.6.tokens = bf16[256,1408]{1,0:T(8,128)(2,1)S(1)} collective-permute-done((bf16[256,1408]{1,0:T(8,128)(2,1)S(1)}, bf16[256,1408]{1,0:T(8,128)(2,1)S(1)}, u32[]{:S(2)}, u32[]{:S(2)}) %collective-permute-start.6) | collective-permute-done | bytes 720928 | tf_op jit(solution)/shard_map/ppermute | solution.py:360
  76.4 3.0 %stats_far.1.one = f32[16,256]{1,0:T(8,128)S(1)} custom-call(f32[4]{0:T(128)S(1)} %add_select_fusion.bias_ref, bf16[256,1408]{1,0:T(8,128)(2,1)S(1)} %collective-permute-done.6.tokens, bf16[256,1408]{1,0:T(8,128)(2,1)S(1)} %bitcast.20, bf16[256,2560]{1,0:T(8,128)(2,1)S(1)} %bitcast.14, bf16[256,1280]{1,0:T(8,128)(2,1)} %collective-permute-done.4.w2, ...), custom_call_target="tpu_custom_call" | custom-call | flops 671088640 | bytes 1638400 | tf_op jit(solution)/shard_map/stats_far/pallas_call | solution.py:153
  79.4 5.9 %collective-permute-start.8 = (f32[16,256]{1,0:T(8,128)S(1)}, f32[16,256]{1,0:T(8,128)S(1)}, u32[]{:S(2)}, u32[]{:S(2)}) collective-permute-start(f32[16,256]{1,0:T(8,128)S(1)} %stats_far.1.one), channel_id=1, source_target_pairs={{0,4},{1,5},{2,6},{3,7},{4,0},{5,1},{6,2},{7,3},{8,12},{9,13},{10,... | collective-permute-start | bytes 49160 | tf_op jit(solution)/shard_map/ppermute | solution.py:360
  85.3 0.0 collective-permute-done.7.other
  85.3 7.6 %grads_far.1 = (bf16[256,640]{1,0:T(8,128)(2,1)S(1)}, bf16[256,1280]{1,0:T(8,128)(2,1)}, bf16[256,1280]{1,0:T(8,128)(2,1)}, bf16[256,1280]{1,0:T(8,128)(2,1)}, bf16[256,1280]{1,0:T(8,128)(2,1)}) custom-call(f32[4]{0:T(128)S(1)} %add_select_fusion.bias_ref, s32[2]{0:T(128)S(1)} %pad_add_fusion.place, f32[16,256]{1,0:T(8,128)S(1)} %stats_far.1.one, ...), custom_call_target="tpu_custom_call" | custom-call | flops 1677721600 | bytes 3932160 | tf_op jit(solution)/shard_map/grads_far/pallas_call | solution.py:253
  92.8 0.0 collective-permute-done.8
  92.9 3.5 %collective-permute-start.9 = (bf16[256,640]{1,0:T(8,128)(2,1)S(1)}, bf16[256,640]{1,0:T(8,128)(2,1)S(1)}, u32[]{:S(2)}, u32[]{:S(2)}) collective-permute-start(bf16[256,640]{1,0:T(8,128)(2,1)S(1)} %get-tuple-element.65), channel_id=1, source_target_pairs={{0,4},{1,5},{2,6},{3,7},{4,0},{5,1},{6,2},{7,3},{8,12},{9,13},{10,... | collective-permute-start | bytes 983048 | tf_op jit(solution)/shard_map/ppermute | solution.py:360
  96.3 41.2 %conditional.1 = (f32[256,640]{1,0:T(8,128)S(1)}, bf16[256,1280]{1,0:T(8,128)(2,1)S(1)}, bf16[256,1280]{1,0:T(8,128)(2,1)}, bf16[256,1280]{1,0:T(8,128)(2,1)}) conditional(s32[]{:T(128)} %convert_element_type.4, () %tuple.16, (f32[4]{0:T(128)S(1)}, s32[2]{0:T(128)S(1)}, f32[16,256]{1,0:T(8,128)S(1)}, f32[16,256]{1,0:T(8,128)S(1)}, ...), branch_computations={%region_0.1_spmd, %region_1.2_spmd} | conditional | flops 1678704640 | bytes 14418072 | solution.py:425
  96.3 7.8 %grads_own.1 = (f32[256,640]{1,0:T(8,128)S(1)}, bf16[256,1280]{1,0:T(8,128)(2,1)S(1)}, bf16[256,1280]{1,0:T(8,128)(2,1)S(1)}, bf16[256,1280]{1,0:T(8,128)(2,1)S(1)}, bf16[256,1280]{1,0:T(8,128)(2,1)S(1)}) custom-call(f32[4]{0:T(128)S(1)} %get-tuple-element.26.bias_ref, s32[2]{0:T(128)S(1)} %get-tuple-element.27.place, f32[16,256]{1,0:T(8,128)S(1)} %get-tuple-element.28.one, ...), custom_call_target="tpu_custom_call" | custom-call | flops 1677721600 | bytes 3932160 | tf_op jit(solution)/shard_map/cond/branch_1_fun/grads_own/pallas_call | solution.py:253
  104.2 3.1 %collective-permute-start = (bf16[256,1280]{1,0:T(8,128)(2,1)S(1)}, bf16[256,1280]{1,0:T(8,128)(2,1)S(1)}, u32[]{:S(2)}, u32[]{:S(2)}) collective-permute-start(bf16[256,1280]{1,0:T(8,128)(2,1)S(1)} %get-tuple-element.42), channel_id=1, source_target_pairs={{0,8},{8,0},{16,24},{24,16},{32,40},{40,32},{48,56},{56,48},{64,72... | collective-permute-start | bytes 1966088 | tf_op jit(solution)/shard_map/cond/branch_1_fun/ppermute | solution.py:371
  107.2 1.9 %collective-permute-start.1 = (bf16[256,1280]{1,0:T(8,128)(2,1)S(1)}, bf16[256,1280]{1,0:T(8,128)(2,1)}, u32[]{:S(2)}, u32[]{:S(2)}) collective-permute-start(bf16[256,1280]{1,0:T(8,128)(2,1)S(1)} %get-tuple-element.43), channel_id=1, source_target_pairs={{8,0},{16,8},{24,16},{32,24},{40,32},{48,40},{56,48},{64,56},{72,6... | collective-permute-start | bytes 1966088 | tf_op jit(solution)/shard_map/cond/branch_1_fun/ppermute | solution.py:366
  109.2 0.0 collective-permute-done.swapped
  109.2 10.1 %collective-permute-done.1.side = bf16[256,1280]{1,0:T(8,128)(2,1)} collective-permute-done((bf16[256,1280]{1,0:T(8,128)(2,1)S(1)}, bf16[256,1280]{1,0:T(8,128)(2,1)}, u32[]{:S(2)}, u32[]{:S(2)}) %collective-permute-start.1) | collective-permute-done | bytes 655392 | tf_op jit(solution)/shard_map/cond/branch_1_fun/ppermute | solution.py:366
  119.3 1.3 fold.1
  120.6 3.6 %collective-permute-start.2 = (bf16[256,1280]{1,0:T(8,128)(2,1)S(1)}, bf16[256,1280]{1,0:T(8,128)(2,1)}, u32[]{:S(2)}, u32[]{:S(2)}) collective-permute-start(bf16[256,1280]{1,0:T(8,128)(2,1)S(1)} %fold.1), channel_id=1, source_target_pairs={{16,0},{24,8},{32,16},{40,24},{48,32},{56,40},{64,48},{72,56},{80,... | collective-permute-start | bytes 1966088 | tf_op jit(solution)/shard_map/cond/branch_1_fun/ppermute | solution.py:366
  124.2 13.4 %collective-permute-done.2 = bf16[256,1280]{1,0:T(8,128)(2,1)} collective-permute-done((bf16[256,1280]{1,0:T(8,128)(2,1)S(1)}, bf16[256,1280]{1,0:T(8,128)(2,1)}, u32[]{:S(2)}, u32[]{:S(2)}) %collective-permute-start.2) | collective-permute-done | bytes 655392 | tf_op jit(solution)/shard_map/cond/branch_1_fun/ppermute | solution.py:366
  137.6 0.0 collective-permute-done.9.dq_back
  137.6 2.2 %close.1 = bf16[4,64,1920]{2,1,0:T(8,128)(2,1)S(1)} custom-call(s32[1]{0:T(128)} %bitcast.even_ref, f32[256,640]{1,0:T(8,128)S(1)} %get-tuple-element.64.dq_own, bf16[256,640]{1,0:T(8,128)(2,1)S(1)} %collective-permute-done.9.dq_back, bf16[256,1280]{1,0:T(8,128)(2,1)S(1)} %get-tuple-element.66.d0, bf16[256,1280]{1,0:T(8,128)(2,1)} %get-tuple-element.67.back, ...), custom_call_target="tpu_custom_call" | custom-call | flops 983040 | bytes 3932160 | tf_op jit(solution)/shard_map/close/pallas_call | solution.py:312
  139.8 18.3 %all_to_all.15.parts = bf16[4,64,1920]{2,1,0:T(8,128)(2,1)S(1)} all-to-all(bf16[4,64,1920]{2,1,0:T(8,128)(2,1)S(1)} %close.1), channel_id=1, replica_groups={{0,1,2,3},{4,5,6,7},{8,9,10,11},{12,13,14,15},{16,17,18,19},{20,21,22,2..., dimensions={0} | all-to-all | bytes 1966080 | tf_op jit(solution)/shard_map/all_to_all | solution.py:355
  158.1 1.1 unpack.1
Async XLA Ops:
  1.8 19.6 %collective-permute-start.3 = (bf16[2,64,2560]{2,1,0:T(8,128)(2,1)S(1)}, bf16[2,64,2560]{2,1,0:T(8,128)(2,1)S(1)}, u32[]{:S(2)}, u32[]{:S(2)}) collective-permute-start(bf16[2,64,2560]{2,1,0:T(8,128)(2,1)S(1)} %pad_maximum_fusion.near), channel_id=1, source_target_pairs={{0,16},{8,24},{16,32},{24,40},{32,48},{40,56},{48,64},{56,72},{64,... | collective-permute-start | bytes 1966088 | tf_op jit(solution)/shard_map/ppermute | solution.py:366
  8.0 14.7 %all-to-all-start = ((bf16[4,64,1408]{2,1,0:T(8,128)(2,1)}), bf16[4,64,1408]{2,1,0:T(8,128)(2,1)S(1)}, u32[]{:S(2)}, u32[]{:S(2)}) async-start(bf16[4,64,1408]{2,1,0:T(8,128)(2,1)} %pack_queries.1), calls=%async_computation | async-start | bytes 1441792 | tf_op jit(solution)/shard_map/all_to_all | solution.py:355
  22.7 20.1 %all-to-all-start.1 = ((bf16[4,64,2560]{2,1,0:T(8,128)(2,1)}), bf16[4,64,2560]{2,1,0:T(8,128)(2,1)S(1)}, u32[]{:S(2)}, u32[]{:S(2)}) async-start(bf16[4,64,2560]{2,1,0:T(8,128)(2,1)} %pack_keys.1), calls=%async_computation.1 | async-start | bytes 2621440 | tf_op jit(solution)/shard_map/all_to_all | solution.py:355
  26.7 49.7 %collective-permute-start.6 = (bf16[256,1408]{1,0:T(8,128)(2,1)S(1)}, bf16[256,1408]{1,0:T(8,128)(2,1)S(1)}, u32[]{:S(2)}, u32[]{:S(2)}) collective-permute-start(bf16[256,1408]{1,0:T(8,128)(2,1)S(1)} %bitcast.17), channel_id=1, source_target_pairs={{0,4},{1,5},{2,6},{3,7},{4,0},{5,1},{6,2},{7,3},{8,12},{9,13},{10,... | collective-permute-start | bytes 2162696 | tf_op jit(solution)/shard_map/ppermute | solution.py:360
  43.8 12.8 %collective-permute-start.5 = (bf16[256,1280]{1,0:T(8,128)(2,1)}, bf16[256,1280]{1,0:T(8,128)(2,1)}, u32[]{:S(2)}, u32[]{:S(2)}) collective-permute-start(bf16[256,1280]{1,0:T(8,128)(2,1)} %get-tuple-element.69), channel_id=1, source_target_pairs={{0,8},{8,16},{16,24},{24,32},{32,40},{40,48},{48,56},{56,64},{64,7... | collective-permute-start | bytes 1966088 | tf_op jit(solution)/shard_map/ppermute | solution.py:366
  48.8 7.8 %collective-permute-start.4 = (bf16[256,1280]{1,0:T(8,128)(2,1)S(1)}, bf16[256,1280]{1,0:T(8,128)(2,1)}, u32[]{:S(2)}, u32[]{:S(2)}) collective-permute-start(bf16[256,1280]{1,0:T(8,128)(2,1)S(1)} %get-tuple-element.70), channel_id=1, source_target_pairs={{0,8},{8,0},{16,24},{24,16},{32,40},{40,32},{48,56},{56,48},{64,72... | collective-permute-start | bytes 1966088 | tf_op jit(solution)/shard_map/ppermute | solution.py:371
  59.6 25.7 %collective-permute-start.7 = (f32[16,256]{1,0:T(8,128)S(1)}, f32[16,256]{1,0:T(8,128)S(1)}, u32[]{:S(2)}, u32[]{:S(2)}) collective-permute-start(f32[16,256]{1,0:T(8,128)S(1)} %stats_own.1), channel_id=1, source_target_pairs={{0,4},{1,5},{2,6},{3,7},{4,0},{5,1},{6,2},{7,3},{8,12},{9,13},{10,... | collective-permute-start | bytes 49160 | tf_op jit(solution)/shard_map/ppermute | solution.py:360
  79.4 13.5 %collective-permute-start.8 = (f32[16,256]{1,0:T(8,128)S(1)}, f32[16,256]{1,0:T(8,128)S(1)}, u32[]{:S(2)}, u32[]{:S(2)}) collective-permute-start(f32[16,256]{1,0:T(8,128)S(1)} %stats_far.1.one), channel_id=1, source_target_pairs={{0,4},{1,5},{2,6},{3,7},{4,0},{5,1},{6,2},{7,3},{8,12},{9,13},{10,... | collective-permute-start | bytes 49160 | tf_op jit(solution)/shard_map/ppermute | solution.py:360
  92.9 44.7 %collective-permute-start.9 = (bf16[256,640]{1,0:T(8,128)(2,1)S(1)}, bf16[256,640]{1,0:T(8,128)(2,1)S(1)}, u32[]{:S(2)}, u32[]{:S(2)}) collective-permute-start(bf16[256,640]{1,0:T(8,128)(2,1)S(1)} %get-tuple-element.65), channel_id=1, source_target_pairs={{0,4},{1,5},{2,6},{3,7},{4,0},{5,1},{6,2},{7,3},{8,12},{9,13},{10,... | collective-permute-start | bytes 983048 | tf_op jit(solution)/shard_map/ppermute | solution.py:360
  104.2 5.0 %collective-permute-start = (bf16[256,1280]{1,0:T(8,128)(2,1)S(1)}, bf16[256,1280]{1,0:T(8,128)(2,1)S(1)}, u32[]{:S(2)}, u32[]{:S(2)}) collective-permute-start(bf16[256,1280]{1,0:T(8,128)(2,1)S(1)} %get-tuple-element.42), channel_id=1, source_target_pairs={{0,8},{8,0},{16,24},{24,16},{32,40},{40,32},{48,56},{56,48},{64,72... | collective-permute-start | bytes 1966088 | tf_op jit(solution)/shard_map/cond/branch_1_fun/ppermute | solution.py:371
  107.2 12.0 %collective-permute-start.1 = (bf16[256,1280]{1,0:T(8,128)(2,1)S(1)}, bf16[256,1280]{1,0:T(8,128)(2,1)}, u32[]{:S(2)}, u32[]{:S(2)}) collective-permute-start(bf16[256,1280]{1,0:T(8,128)(2,1)S(1)} %get-tuple-element.43), channel_id=1, source_target_pairs={{8,0},{16,8},{24,16},{32,24},{40,32},{48,40},{56,48},{64,56},{72,6... | collective-permute-start | bytes 1966088 | tf_op jit(solution)/shard_map/cond/branch_1_fun/ppermute | solution.py:366
  120.6 17.0 %collective-permute-start.2 = (bf16[256,1280]{1,0:T(8,128)(2,1)S(1)}, bf16[256,1280]{1,0:T(8,128)(2,1)}, u32[]{:S(2)}, u32[]{:S(2)}) collective-permute-start(bf16[256,1280]{1,0:T(8,128)(2,1)S(1)} %fold.1), channel_id=1, source_target_pairs={{16,0},{24,8},{32,16},{40,24},{48,32},{56,40},{64,48},{72,56},{80,... | collective-permute-start | bytes 1966088 | tf_op jit(solution)/shard_map/cond/branch_1_fun/ppermute | solution.py:366

commit v15 on v14

--- a/solution.py
+++ b/solution.py
@@ -169,24 +169,25 @@
     return peak + jnp.log2(one_part + other_sum * jnp.exp2(other_peak - peak))
 
 
-def grads_kernel(parts_in, bias_ref, place, one, other, tokens, own, near, w2, w3, *rest):
+def grads_kernel(roles, parts_in, dq_in, bias_ref, place, one, other, tokens, own, *rest):
+    count = len(roles)
+    sources, rest = rest[: 1 + (2 in roles) * 2], rest[1 + (2 in roles) * 2 :]
     if parts_in:
-        parts, rest = rest[:WBLK], rest[WBLK:]
-    dq_out, *outs = rest[: 1 + WBLK]
-    rest = rest[1 + WBLK :]
-    rows, dq_acc, sums, window, held, k_meta, load_sems, sems, *rest = rest
+        parts, rest = rest[:count], rest[count:]
+    if dq_in:
+        dq_part, *rest = rest
+    dq_out, *outs = rest[: 1 + count]
+    rows, dq_acc, sums, window, held, k_meta, load_sems, sems, *rest = rest[1 + count :]
     half = rows.shape[1]
-
-    moves = [
-        (own.at[:, META], k_meta),
-        (tokens, held),
-        (near.at[:, : 2 * GROUP * HDIM], window.at[0]),
-        (near.at[:, 2 * GROUP * HDIM :], window.at[1]),
-        (w2, window.at[2]),
-        (w3, window.at[3]),
-    ]
+    near, *others = sources
+    blocks = [near.at[:, : 2 * GROUP * HDIM], near.at[:, 2 * GROUP * HDIM :], *others]
+
+    moves = [(own.at[:, META], k_meta), (tokens, held)]
+    moves += [(blocks[role], window.at[at]) for at, role in enumerate(roles)]
     if parts_in:
-        moves += [(part, rest[0].at[role]) for role, part in enumerate(parts)]
+        moves += [(part, rest[0].at[at]) for at, part in enumerate(parts)]
+    if dq_in:
+        moves.append((dq_part, rest[1]))
     loads = [
         pltpu.make_async_copy(src, dst, load_sems.at[i]) for i, (src, dst) in enumerate(moves)
     ]
@@ -196,21 +197,20 @@
         load.wait()
 
     rows[...] = held[:, META].astype(F32).T
-    mask = seen(rows, k_meta[...])
     totals = log_total(one, other)
     for head in range(GROUP):
         q_cols = head_slice(head)
         queries, grads = held[:, q_cols], held[:, head_slice(GROUP + head)]
         first = place[0] * GROUP + head
         dot = rows[pl.ds(first, 1), :] + rows[pl.ds(LOW_LANE + first, 1), :]
-        keys = window[:, :, head_slice(2 * head)].reshape(WBLK * half, HDIM)
-        values = window[:, :, head_slice(2 * head + 1)].reshape(WBLK * half, HDIM)
+        keys = window[:, :, head_slice(2 * head)].reshape(count * half, HDIM)
+        values = window[:, :, head_slice(2 * head + 1)].reshape(count * half, HDIM)
         scores = jnp.dot(keys, queries.T, preferred_element_type=F32) * SCALE2
         pieces = []
-        for role in range(WBLK):
-            piece = scores[role * half : (role + 1) * half]
+        for at, role in enumerate(roles):
+            piece = scores[at * half : (at + 1) * half]
             if role == 0:
-                piece = jnp.where(mask, piece, NEG)
+                piece = jnp.where(seen(rows, k_meta[...]), piece, NEG)
             pieces.append(jnp.exp2(piece - (totals[head : head + 1] - bias_ref[role])))
         probs = jnp.concatenate(pieces, axis=0)
         dv = jnp.dot(probs.astype(BF16), grads, preferred_element_type=F32)
@@ -218,28 +218,33 @@
         ds = (probs * (dp - dot)).astype(BF16)
         dk = jnp.dot(ds, queries, preferred_element_type=F32) * FACTOR
         dq = jnp.dot(keys.T, ds, preferred_element_type=F32)
-        for role in range(WBLK):
-            of = slice(role * half, (role + 1) * half)
+        for at in range(count):
+            of = slice(at * half, (at + 1) * half)
             for cols, value in ((2 * head, dk[of]), (2 * head + 1, dv[of])):
                 if parts_in:
-                    value += rest[0][role, :, head_slice(cols)].astype(F32)
-                sums[role, :, head_slice(cols)] = value.astype(BF16)
-        dq_acc[:, q_cols] = (dq * FACTOR).T.astype(dq_acc.dtype)
-    stores = [pltpu.make_async_copy(dq_acc, dq_out, sems.at[WBLK])]
-    for role in range(WBLK):
-        stores.append(pltpu.make_async_copy(sums.at[role], outs[role], sems.at[role]))
+                    value += rest[0][at, :, head_slice(cols)].astype(F32)
+                sums[at, :, head_slice(cols)] = value.astype(BF16)
+        turned = (dq * FACTOR).T
+        if dq_in:
+            turned += rest[1][:, q_cols]
+        dq_acc[:, q_cols] = turned.astype(dq_acc.dtype)
+    stores = [pltpu.make_async_copy(dq_acc, dq_out, sems.at[count])]
+    for at in range(count):
+        stores.append(pltpu.make_async_copy(sums.at[at], outs[at], sems.at[at]))
     for store in stores:
         store.start()
     for store in stores:
         store.wait()
 
 
-def grads(name, common, tokens, own, window, dq_kind, parts=()):
+def grads(name, common, tokens, own, roles, sources, dq_kind, parts=(), dq_part=None):
     half = own.shape[0]
     wide = GROUP * HDIM
-    pairs = GROUP * half * WBLK * half
+    count = len(roles)
+    pairs = GROUP * half * count * half
     hbm = pl.BlockSpec(memory_space=pl.ANY)
-    blocks = pltpu.VMEM((WBLK, half, 2 * wide), BF16)
+    blocks = pltpu.VMEM((count, half, 2 * wide), BF16)
+    extra = list(parts) + ([] if dq_part is None else [dq_part])
     scratch = [
         pltpu.VMEM((HDIM, half), F32),
         pltpu.VMEM((half, wide), dq_kind),
@@ -247,20 +252,24 @@
         blocks,
         pltpu.VMEM(tokens.shape, BF16),
         pltpu.VMEM((half, HDIM), BF16),
-        pltpu.SemaphoreType.DMA((2 * WBLK + 2,)),
+        pltpu.SemaphoreType.DMA((2 * WBLK + 3,)),
         pltpu.SemaphoreType.DMA((WBLK + 1,)),
     ]
-    return pl.pallas_call(
-        functools.partial(grads_kernel, bool(parts)),
+    if parts:
+        scratch.append(blocks)
+    if dq_part is not None:
+        scratch.append(pltpu.VMEM((half, wide), F32))
+    return pl.pallas_call(
+        functools.partial(grads_kernel, roles, bool(parts), dq_part is not None),
         out_shape=[jax.ShapeDtypeStruct((half, wide), dq_kind)]
-        + [jax.ShapeDtypeStruct((half, 2 * wide), BF16)] * WBLK,
-        in_specs=[smem(), smem(), vmem(), vmem()] + [hbm] * (5 + len(parts)),
-        out_specs=[hbm] * (1 + WBLK),
-        scratch_shapes=scratch + [blocks] * bool(parts),
+        + [jax.ShapeDtypeStruct((half, 2 * wide), BF16)] * count,
+        in_specs=[smem(), smem(), vmem(), vmem()] + [hbm] * (2 + len(sources) + len(extra)),
+        out_specs=[hbm] * (1 + count),
+        scratch_shapes=scratch,
         compiler_params=params(28),
         cost_estimate=cost(10 * pairs * HDIM, 12 * half * wide * 2, pairs),
         name=name,
-    )(*common, tokens, own, *window, *parts)
+    )(*common, tokens, own, *sources, *extra)
 
 
 def row_block(shape):
@@ -373,8 +382,12 @@
 
 def own_grads(operands):
     common, own, window, parts, even = operands
-    dq_own, d0, d1, d2, d3 = grads("grads_own", common, own, own, window, F32, parts)
+    near = window[:1]
+    dq_part, d2, d3 = grads("grads_own23", common, own, own, (2, 3), window, F32, parts[2:])
     side, swapped = along_row(d3, -1), in_chip(d2)
+    dq_own, d0, d1 = grads(
+        "grads_own01", common, own, own, (0, 1), near, F32, parts[:2], dq_part
+    )
     return dq_own, d0, along_row(fold(even, d1, swapped, side), -2), side
 
 
@@ -418,7 +431,7 @@
     own_other = across_z(far_near)
 
     common = (bias, place, far_near, far_other)
-    dq_far, *parts = grads("grads_far", common, far, own, window, BF16)
+    dq_far, *parts = grads("grads_far", common, far, own, (0, 1, 2, 3), window, BF16)
     dq_far, own_other = lax.optimization_barrier((dq_far, own_other))
     dq_back = across_z(dq_far)
     common = (bias, place, own_near, own_other)

time: 160 us -> 157 us (0.981)
  waiting for transfers between devices: 53.8 us -> 49 us
  Pallas kernels: 30.2 us -> 32.5 us
    ppermute x4, waiting for transfers between devices: 38.5 us -> 33.7 us  [along_row(): lax.ppermute(value, 'row', [(r, r + steps) for r in range(first, last)])]
    pallas_call x2 -> x3, Pallas kernels: 15.4 us -> 17.7 us  [grads(): pl.pallas_call(functools.partial(grads_kernel, roles, bool(parts), dq_par...]
  transfers between devices with their start and end apart: 12 -> 12, of which waited for: 6 -> 6; matrix products, arithmetic and copies ran while one was open for 1% -> 1% of each run, Pallas kernels for 17% -> 19%
where the time goes in v15:
time: 157 us
  starting transfers between devices  53.9 us (34%)
  waiting for transfers between devices  49 us (31%)
  Pallas kernels  32.5 us (21%)
  blocking collectives  18.3 us (12%)
  other arithmetic  2.22 us (1%)
    ppermute x4, waiting for transfers between devices, along_row(): lax.ppermute(value, 'row', [(r, r + steps) for r in range(first, last)])  33.7 us
    ppermute x4, starting transfers between devices, across_z(): lax.ppermute(value, 'col', [(c, (c + XN) % count) for c in range(count)])  26.9 us
    all_to_all x1, blocking collectives, over_x(): return lax.all_to_all(value, 'col', 0, 0, axis_index_groups=groups)  18.3 us
    pallas_call x3, Pallas kernels, grads(): pl.pallas_call(functools.partial(grads_kernel, roles, bool(parts), dq_par...  17.7 us
    ppermute x4, starting transfers between devices, along_row(): lax.ppermute(value, 'row', [(r, r + steps) for r in range(first, last)])  14 us
    all_to_all x2, starting transfers between devices, over_x(): return lax.all_to_all(value, 'col', 0, 0, axis_index_groups=groups)  8.04 us
    ppermute x4, waiting for transfers between devices, across_z(): lax.ppermute(value, 'col', [(c, (c + XN) % count) for c in range(count)])  7.99 us
    all_to_all x2, waiting for transfers between devices, over_x(): return lax.all_to_all(value, 'col', 0, 0, axis_index_groups=groups)  7.28 us
  transfers between devices with their start and end apart: 12, of which 6 were waited for; matrix products, arithmetic and copies ran while one was open for 1% of the time, Pallas kernels for 19%

profile of v15, /device:TPU:129, one launch (start us, length us, event | category | flops | bytes accessed | tf_op | source)
XLA Modules:
  0.0 156.7 jit_solution(194520197832437195)
XLA Ops:
  0.6 1.1 pad_maximum_fusion.near
  1.8 3.2 %collective-permute-start.3 = (bf16[2,64,2560]{2,1,0:T(8,128)(2,1)S(1)}, bf16[2,64,2560]{2,1,0:T(8,128)(2,1)S(1)}, u32[]{:S(2)}, u32[]{:S(2)}) collective-permute-start(bf16[2,64,2560]{2,1,0:T(8,128)(2,1)S(1)} %pad_maximum_fusion.near), channel_id=1, source_target_pairs={{0,16},{8,24},{16,32},{24,40},{32,48},{40,56},{48,64},{56,72},{64,... | collective-permute-start | bytes 1966088 | tf_op jit(solution)/shard_map/ppermute | solution.py:375
  5.0 3.0 %pack_queries.1 = bf16[4,64,1408]{2,1,0:T(8,128)(2,1)} custom-call(bf16[64,2560]{1,0:T(8,128)(2,1)} %q_any.1, bf16[64,2560]{1,0:T(8,128)(2,1)} %o_any.1, bf16[64,2560]{1,0:T(8,128)(2,1)} %g_any.1, s32[1,64]{1,0:T(1,128)} %bitcast.25), custom_call_target="tpu_custom_call" | custom-call | flops 327680 | bytes 2293760 | tf_op jit(solution)/shard_map/pack_queries/pallas_call | solution.py:70
  8.0 4.0 %all-to-all-start = ((bf16[4,64,1408]{2,1,0:T(8,128)(2,1)}), bf16[4,64,1408]{2,1,0:T(8,128)(2,1)S(1)}, u32[]{:S(2)}, u32[]{:S(2)}) async-start(bf16[4,64,1408]{2,1,0:T(8,128)(2,1)} %pack_queries.1), calls=%async_computation | async-start | bytes 1441792 | tf_op jit(solution)/shard_map/all_to_all | solution.py:364
  12.0 9.4 %collective-permute-done.3.far = bf16[2,64,2560]{2,1,0:T(8,128)(2,1)S(1)} collective-permute-done((bf16[2,64,2560]{2,1,0:T(8,128)(2,1)S(1)}, bf16[2,64,2560]{2,1,0:T(8,128)(2,1)S(1)}, u32[]{:S(2)}, u32[]{:S(2)}) %collective-permute-start.3) | collective-permute-done | bytes 655392 | tf_op jit(solution)/shard_map/ppermute | solution.py:375
  21.4 1.3 pack_keys.1
  22.7 0.0 all-to-all-done
  22.7 4.0 %all-to-all-start.1 = ((bf16[4,64,2560]{2,1,0:T(8,128)(2,1)}), bf16[4,64,2560]{2,1,0:T(8,128)(2,1)S(1)}, u32[]{:S(2)}, u32[]{:S(2)}) async-start(bf16[4,64,2560]{2,1,0:T(8,128)(2,1)} %pack_keys.1), calls=%async_computation.1 | async-start | bytes 2621440 | tf_op jit(solution)/shard_map/all_to_all | solution.py:364
  26.7 8.8 %collective-permute-start.6 = (bf16[256,1408]{1,0:T(8,128)(2,1)S(1)}, bf16[256,1408]{1,0:T(8,128)(2,1)S(1)}, u32[]{:S(2)}, u32[]{:S(2)}) collective-permute-start(bf16[256,1408]{1,0:T(8,128)(2,1)S(1)} %bitcast.17), channel_id=1, source_target_pairs={{0,4},{1,5},{2,6},{3,7},{4,0},{5,1},{6,2},{7,3},{8,12},{9,13},{10,... | collective-permute-start | bytes 2162696 | tf_op jit(solution)/shard_map/ppermute | solution.py:369
  35.5 7.3 %all-to-all-done.1 = bf16[4,64,2560]{2,1,0:T(8,128)(2,1)S(1)} async-done(((bf16[4,64,2560]{2,1,0:T(8,128)(2,1)}), bf16[4,64,2560]{2,1,0:T(8,128)(2,1)S(1)}, u32[]{:S(2)}, u32[]{:S(2)}) %all-to-all-start.1) | async-done | bytes 1310752 | tf_op jit(solution)/shard_map/all_to_all | solution.py:364
  42.8 0.9 slice_select_fusion
  43.7 5.0 %collective-permute-start.5 = (bf16[256,1280]{1,0:T(8,128)(2,1)}, bf16[256,1280]{1,0:T(8,128)(2,1)}, u32[]{:S(2)}, u32[]{:S(2)}) collective-permute-start(bf16[256,1280]{1,0:T(8,128)(2,1)} %get-tuple-element.70), channel_id=1, source_target_pairs={{0,8},{8,16},{16,24},{24,32},{32,40},{40,48},{48,56},{56,64},{64,7... | collective-permute-start | bytes 1966088 | tf_op jit(solution)/shard_map/ppermute | solution.py:375
  48.8 1.9 %collective-permute-start.4 = (bf16[256,1280]{1,0:T(8,128)(2,1)S(1)}, bf16[256,1280]{1,0:T(8,128)(2,1)}, u32[]{:S(2)}, u32[]{:S(2)}) collective-permute-start(bf16[256,1280]{1,0:T(8,128)(2,1)S(1)} %get-tuple-element.71), channel_id=1, source_target_pairs={{0,8},{8,0},{16,24},{24,16},{32,40},{40,32},{48,56},{56,48},{64,72... | collective-permute-start | bytes 1966088 | tf_op jit(solution)/shard_map/ppermute | solution.py:380
  50.7 0.1 pad_add_fusion.place
  50.8 0.1 add_select_fusion.bias_ref
  50.9 5.7 %collective-permute-done.5.w3.rest_2_ = bf16[256,1280]{1,0:T(8,128)(2,1)} collective-permute-done((bf16[256,1280]{1,0:T(8,128)(2,1)}, bf16[256,1280]{1,0:T(8,128)(2,1)}, u32[]{:S(2)}, u32[]{:S(2)}) %collective-permute-start.5) | collective-permute-done | bytes 655392 | tf_op jit(solution)/shard_map/ppermute | solution.py:375
  56.6 0.0 collective-permute-done.4.w2.rest_1_
  56.6 3.0 %stats_own.1 = f32[16,256]{1,0:T(8,128)S(1)} custom-call(f32[4]{0:T(128)S(1)} %add_select_fusion.bias_ref, bf16[256,1408]{1,0:T(8,128)(2,1)S(1)} %bitcast.18, bf16[256,1408]{1,0:T(8,128)(2,1)S(1)} %bitcast.19, bf16[256,2560]{1,0:T(8,128)(2,1)S(1)} %bitcast.13, bf16[256,1280]{1,0:T(8,128)(2,1)} %collective-permute-done.4.w2.rest_1_, ...), custom_call_target="tpu_custom_call" | custom-call | flops 671088640 | bytes 1638400 | tf_op jit(solution)/shard_map/stats_own/pallas_call | solution.py:153
  59.6 8.8 %collective-permute-start.7 = (f32[16,256]{1,0:T(8,128)S(1)}, f32[16,256]{1,0:T(8,128)S(1)}, u32[]{:S(2)}, u32[]{:S(2)}) collective-permute-start(f32[16,256]{1,0:T(8,128)S(1)} %stats_own.1), channel_id=1, source_target_pairs={{0,4},{1,5},{2,6},{3,7},{4,0},{5,1},{6,2},{7,3},{8,12},{9,13},{10,... | collective-permute-start | bytes 49160 | tf_op jit(solution)/shard_map/ppermute | solution.py:369
  68.4 8.0 %collective-permute-done.6.tokens = bf16[256,1408]{1,0:T(8,128)(2,1)S(1)} collective-permute-done((bf16[256,1408]{1,0:T(8,128)(2,1)S(1)}, bf16[256,1408]{1,0:T(8,128)(2,1)S(1)}, u32[]{:S(2)}, u32[]{:S(2)}) %collective-permute-start.6) | collective-permute-done | bytes 720928 | tf_op jit(solution)/shard_map/ppermute | solution.py:369
  76.4 3.0 %stats_far.1.one = f32[16,256]{1,0:T(8,128)S(1)} custom-call(f32[4]{0:T(128)S(1)} %add_select_fusion.bias_ref, bf16[256,1408]{1,0:T(8,128)(2,1)S(1)} %collective-permute-done.6.tokens, bf16[256,1408]{1,0:T(8,128)(2,1)S(1)} %bitcast.20, bf16[256,2560]{1,0:T(8,128)(2,1)S(1)} %bitcast.14, bf16[256,1280]{1,0:T(8,128)(2,1)} %collective-permute-done.4.w2.rest_1_, ...), custom_call_target="tpu_custom_call" | custom-call | flops 671088640 | bytes 1638400 | tf_op jit(solution)/shard_map/stats_far/pallas_call | solution.py:153
  79.4 5.9 %collective-permute-start.8 = (f32[16,256]{1,0:T(8,128)S(1)}, f32[16,256]{1,0:T(8,128)S(1)}, u32[]{:S(2)}, u32[]{:S(2)}) collective-permute-start(f32[16,256]{1,0:T(8,128)S(1)} %stats_far.1.one), channel_id=1, source_target_pairs={{0,4},{1,5},{2,6},{3,7},{4,0},{5,1},{6,2},{7,3},{8,12},{9,13},{10,... | collective-permute-start | bytes 49160 | tf_op jit(solution)/shard_map/ppermute | solution.py:369
  85.3 0.0 collective-permute-done.7.other
  85.3 7.6 %grads_far.1 = (bf16[256,640]{1,0:T(8,128)(2,1)S(1)}, bf16[256,1280]{1,0:T(8,128)(2,1)}, bf16[256,1280]{1,0:T(8,128)(2,1)}, bf16[256,1280]{1,0:T(8,128)(2,1)}, bf16[256,1280]{1,0:T(8,128)(2,1)}) custom-call(f32[4]{0:T(128)S(1)} %add_select_fusion.bias_ref, s32[2]{0:T(128)S(1)} %pad_add_fusion.place, f32[16,256]{1,0:T(8,128)S(1)} %stats_far.1.one, ...), custom_call_target="tpu_custom_call" | custom-call | flops 1677721600 | bytes 3932160 | tf_op jit(solution)/shard_map/grads_far/pallas_call | solution.py:262
  92.9 0.0 collective-permute-done.8
  92.9 3.3 %collective-permute-start.9 = (bf16[256,640]{1,0:T(8,128)(2,1)S(1)}, bf16[256,640]{1,0:T(8,128)(2,1)S(1)}, u32[]{:S(2)}, u32[]{:S(2)}) collective-permute-start(bf16[256,640]{1,0:T(8,128)(2,1)S(1)} %get-tuple-element.66), channel_id=1, source_target_pairs={{0,4},{1,5},{2,6},{3,7},{4,0},{5,1},{6,2},{7,3},{8,12},{9,13},{10,... | collective-permute-start | bytes 983048 | tf_op jit(solution)/shard_map/ppermute | solution.py:369
  96.2 39.0 %conditional.1 = (f32[256,640]{1,0:T(8,128)S(1)}, bf16[256,1280]{1,0:T(8,128)(2,1)S(1)}, bf16[256,1280]{1,0:T(8,128)(2,1)}, bf16[256,1280]{1,0:T(8,128)(2,1)}) conditional(s32[]{:T(128)} %convert_element_type.4, () %tuple.16, (f32[4]{0:T(128)S(1)}, s32[2]{0:T(128)S(1)}, f32[16,256]{1,0:T(8,128)S(1)}, f32[16,256]{1,0:T(8,128)S(1)}, ...), branch_computations={%region_0.1_spmd, %region_1.2_spmd} | conditional | flops 1678704640 | bytes 23593168 | solution.py:438
  96.2 0.0 copy-start
  96.2 0.0 copy-start.1
  96.2 5.6 %grads_own23.1 = (f32[256,640]{1,0:T(8,128)S(1)}, bf16[256,1280]{1,0:T(8,128)(2,1)S(1)}, bf16[256,1280]{1,0:T(8,128)(2,1)S(1)}) custom-call(f32[4]{0:T(128)S(1)} %get-tuple-element.26.bias_ref, s32[2]{0:T(128)S(1)} %get-tuple-element.27.place, f32[16,256]{1,0:T(8,128)S(1)} %get-tuple-element.28.one, f32[16,256]{1,0:T(8,128)S(1)} %get-tuple-element.29.other, ...), custom_call_target="tpu_custom_call" | custom-call | flops 838860800 | bytes 3932160 | tf_op jit(solution)/shard_map/cond/branch_1_fun/grads_own23/pallas_call | solution.py:262
  101.8 3.1 %collective-permute-start = (bf16[256,1280]{1,0:T(8,128)(2,1)S(1)}, bf16[256,1280]{1,0:T(8,128)(2,1)S(1)}, u32[]{:S(2)}, u32[]{:S(2)}) collective-permute-start(bf16[256,1280]{1,0:T(8,128)(2,1)S(1)} %get-tuple-element.43), channel_id=1, source_target_pairs={{0,8},{8,0},{16,24},{24,16},{32,40},{40,32},{48,56},{56,48},{64,72... | collective-permute-start | bytes 1966088 | tf_op jit(solution)/shard_map/cond/branch_1_fun/ppermute | solution.py:380
  104.9 2.1 %collective-permute-start.1 = (bf16[256,1280]{1,0:T(8,128)(2,1)S(1)}, bf16[256,1280]{1,0:T(8,128)(2,1)}, u32[]{:S(2)}, u32[]{:S(2)}) collective-permute-start(bf16[256,1280]{1,0:T(8,128)(2,1)S(1)} %get-tuple-element.44), channel_id=1, source_target_pairs={{8,0},{16,8},{24,16},{32,24},{40,32},{48,40},{56,48},{64,56},{72,6... | collective-permute-start | bytes 1966088 | tf_op jit(solution)/shard_map/cond/branch_1_fun/ppermute | solution.py:375
  107.0 0.0 copy-done
  107.0 0.0 copy-done.1
  107.0 4.6 %grads_own01.1 = (f32[256,640]{1,0:T(8,128)S(1)}, bf16[256,1280]{1,0:T(8,128)(2,1)S(1)}, bf16[256,1280]{1,0:T(8,128)(2,1)S(1)}) custom-call(f32[4]{0:T(128)S(1)} %get-tuple-element.26.bias_ref, s32[2]{0:T(128)S(1)} %get-tuple-element.27.place, f32[16,256]{1,0:T(8,128)S(1)} %get-tuple-element.28.one, f32[16,256]{1,0:T(8,128)S(1)} %get-tuple-element.29.other, ...), custom_call_target="tpu_custom_call" | custom-call | flops 838860800 | bytes 3932160 | tf_op jit(solution)/shard_map/cond/branch_1_fun/grads_own01/pallas_call | solution.py:262
  111.6 0.0 collective-permute-done.swapped
  111.6 5.2 %collective-permute-done.1.side = bf16[256,1280]{1,0:T(8,128)(2,1)} collective-permute-done((bf16[256,1280]{1,0:T(8,128)(2,1)S(1)}, bf16[256,1280]{1,0:T(8,128)(2,1)}, u32[]{:S(2)}, u32[]{:S(2)}) %collective-permute-start.1) | collective-permute-done | bytes 655392 | tf_op jit(solution)/shard_map/cond/branch_1_fun/ppermute | solution.py:375
  116.9 1.3 fold.1
  118.2 3.6 %collective-permute-start.2 = (bf16[256,1280]{1,0:T(8,128)(2,1)S(1)}, bf16[256,1280]{1,0:T(8,128)(2,1)}, u32[]{:S(2)}, u32[]{:S(2)}) collective-permute-start(bf16[256,1280]{1,0:T(8,128)(2,1)S(1)} %fold.1), channel_id=1, source_target_pairs={{16,0},{24,8},{32,16},{40,24},{48,32},{56,40},{64,48},{72,56},{80,... | collective-permute-start | bytes 1966088 | tf_op jit(solution)/shard_map/cond/branch_1_fun/ppermute | solution.py:375
  121.8 13.4 %collective-permute-done.2 = bf16[256,1280]{1,0:T(8,128)(2,1)} collective-permute-done((bf16[256,1280]{1,0:T(8,128)(2,1)S(1)}, bf16[256,1280]{1,0:T(8,128)(2,1)}, u32[]{:S(2)}, u32[]{:S(2)}) %collective-permute-start.2) | collective-permute-done | bytes 655392 | tf_op jit(solution)/shard_map/cond/branch_1_fun/ppermute | solution.py:375
  135.2 0.0 collective-permute-done.9.dq_back
  135.2 2.2 %close.1 = bf16[4,64,1920]{2,1,0:T(8,128)(2,1)S(1)} custom-call(s32[1]{0:T(128)} %bitcast.even_ref, f32[256,640]{1,0:T(8,128)S(1)} %get-tuple-element.65.dq_own, bf16[256,640]{1,0:T(8,128)(2,1)S(1)} %collective-permute-done.9.dq_back, bf16[256,1280]{1,0:T(8,128)(2,1)S(1)} %get-tuple-element.67.d0, bf16[256,1280]{1,0:T(8,128)(2,1)} %get-tuple-element.68.back, ...), custom_call_target="tpu_custom_call" | custom-call | flops 983040 | bytes 3932160 | tf_op jit(solution)/shard_map/close/pallas_call | solution.py:321
  137.4 18.3 %all_to_all.15.parts = bf16[4,64,1920]{2,1,0:T(8,128)(2,1)S(1)} all-to-all(bf16[4,64,1920]{2,1,0:T(8,128)(2,1)S(1)} %close.1), channel_id=1, replica_groups={{0,1,2,3},{4,5,6,7},{8,9,10,11},{12,13,14,15},{16,17,18,19},{20,21,22,2..., dimensions={0} | all-to-all | bytes 1966080 | tf_op jit(solution)/shard_map/all_to_all | solution.py:364
  155.7 1.1 unpack.1
Async XLA Ops:
  1.8 19.6 %collective-permute-start.3 = (bf16[2,64,2560]{2,1,0:T(8,128)(2,1)S(1)}, bf16[2,64,2560]{2,1,0:T(8,128)(2,1)S(1)}, u32[]{:S(2)}, u32[]{:S(2)}) collective-permute-start(bf16[2,64,2560]{2,1,0:T(8,128)(2,1)S(1)} %pad_maximum_fusion.near), channel_id=1, source_target_pairs={{0,16},{8,24},{16,32},{24,40},{32,48},{40,56},{48,64},{56,72},{64,... | collective-permute-start | bytes 1966088 | tf_op jit(solution)/shard_map/ppermute | solution.py:375
  8.0 14.7 %all-to-all-start = ((bf16[4,64,1408]{2,1,0:T(8,128)(2,1)}), bf16[4,64,1408]{2,1,0:T(8,128)(2,1)S(1)}, u32[]{:S(2)}, u32[]{:S(2)}) async-start(bf16[4,64,1408]{2,1,0:T(8,128)(2,1)} %pack_queries.1), calls=%async_computation | async-start | bytes 1441792 | tf_op jit(solution)/shard_map/all_to_all | solution.py:364
  22.7 20.1 %all-to-all-start.1 = ((bf16[4,64,2560]{2,1,0:T(8,128)(2,1)}), bf16[4,64,2560]{2,1,0:T(8,128)(2,1)S(1)}, u32[]{:S(2)}, u32[]{:S(2)}) async-start(bf16[4,64,2560]{2,1,0:T(8,128)(2,1)} %pack_keys.1), calls=%async_computation.1 | async-start | bytes 2621440 | tf_op jit(solution)/shard_map/all_to_all | solution.py:364
  26.7 49.7 %collective-permute-start.6 = (bf16[256,1408]{1,0:T(8,128)(2,1)S(1)}, bf16[256,1408]{1,0:T(8,128)(2,1)S(1)}, u32[]{:S(2)}, u32[]{:S(2)}) collective-permute-start(bf16[256,1408]{1,0:T(8,128)(2,1)S(1)} %bitcast.17), channel_id=1, source_target_pairs={{0,4},{1,5},{2,6},{3,7},{4,0},{5,1},{6,2},{7,3},{8,12},{9,13},{10,... | collective-permute-start | bytes 2162696 | tf_op jit(solution)/shard_map/ppermute | solution.py:369
  43.7 12.9 %collective-permute-start.5 = (bf16[256,1280]{1,0:T(8,128)(2,1)}, bf16[256,1280]{1,0:T(8,128)(2,1)}, u32[]{:S(2)}, u32[]{:S(2)}) collective-permute-start(bf16[256,1280]{1,0:T(8,128)(2,1)} %get-tuple-element.70), channel_id=1, source_target_pairs={{0,8},{8,16},{16,24},{24,32},{32,40},{40,48},{48,56},{56,64},{64,7... | collective-permute-start | bytes 1966088 | tf_op jit(solution)/shard_map/ppermute | solution.py:375
  48.8 7.8 %collective-permute-start.4 = (bf16[256,1280]{1,0:T(8,128)(2,1)S(1)}, bf16[256,1280]{1,0:T(8,128)(2,1)}, u32[]{:S(2)}, u32[]{:S(2)}) collective-permute-start(bf16[256,1280]{1,0:T(8,128)(2,1)S(1)} %get-tuple-element.71), channel_id=1, source_target_pairs={{0,8},{8,0},{16,24},{24,16},{32,40},{40,32},{48,56},{56,48},{64,72... | collective-permute-start | bytes 1966088 | tf_op jit(solution)/shard_map/ppermute | solution.py:380
  59.6 25.7 %collective-permute-start.7 = (f32[16,256]{1,0:T(8,128)S(1)}, f32[16,256]{1,0:T(8,128)S(1)}, u32[]{:S(2)}, u32[]{:S(2)}) collective-permute-start(f32[16,256]{1,0:T(8,128)S(1)} %stats_own.1), channel_id=1, source_target_pairs={{0,4},{1,5},{2,6},{3,7},{4,0},{5,1},{6,2},{7,3},{8,12},{9,13},{10,... | collective-permute-start | bytes 49160 | tf_op jit(solution)/shard_map/ppermute | solution.py:369
  79.4 13.5 %collective-permute-start.8 = (f32[16,256]{1,0:T(8,128)S(1)}, f32[16,256]{1,0:T(8,128)S(1)}, u32[]{:S(2)}, u32[]{:S(2)}) collective-permute-start(f32[16,256]{1,0:T(8,128)S(1)} %stats_far.1.one), channel_id=1, source_target_pairs={{0,4},{1,5},{2,6},{3,7},{4,0},{5,1},{6,2},{7,3},{8,12},{9,13},{10,... | collective-permute-start | bytes 49160 | tf_op jit(solution)/shard_map/ppermute | solution.py:369
  92.9 42.3 %collective-permute-start.9 = (bf16[256,640]{1,0:T(8,128)(2,1)S(1)}, bf16[256,640]{1,0:T(8,128)(2,1)S(1)}, u32[]{:S(2)}, u32[]{:S(2)}) collective-permute-start(bf16[256,640]{1,0:T(8,128)(2,1)S(1)} %get-tuple-element.66), channel_id=1, source_target_pairs={{0,4},{1,5},{2,6},{3,7},{4,0},{5,1},{6,2},{7,3},{8,12},{9,13},{10,... | collective-permute-start | bytes 983048 | tf_op jit(solution)/shard_map/ppermute | solution.py:369
  96.2 10.8 %copy-start = (bf16[256,1280]{1,0:T(8,128)(2,1)S(1)}, bf16[256,1280]{1,0:T(8,128)(2,1)}, u32[]{:S(2)}) copy-start(bf16[256,1280]{1,0:T(8,128)(2,1)} %get-tuple-element.32.rest_1_) | copy-start | bytes 1966084 | tf_op jit(solution)/shard_map/cond
  96.2 10.8 %copy-start.1 = (bf16[256,1280]{1,0:T(8,128)(2,1)S(1)}, bf16[256,1280]{1,0:T(8,128)(2,1)}, u32[]{:S(2)}) copy-start(bf16[256,1280]{1,0:T(8,128)(2,1)} %get-tuple-element.33.rest_2_) | copy-start | bytes 1966084 | tf_op jit(solution)/shard_map/cond
  101.8 9.8 %collective-permute-start = (bf16[256,1280]{1,0:T(8,128)(2,1)S(1)}, bf16[256,1280]{1,0:T(8,128)(2,1)S(1)}, u32[]{:S(2)}, u32[]{:S(2)}) collective-permute-start(bf16[256,1280]{1,0:T(8,128)(2,1)S(1)} %get-tuple-element.43), channel_id=1, source_target_pairs={{0,8},{8,0},{16,24},{24,16},{32,40},{40,32},{48,56},{56,48},{64,72... | collective-permute-start | bytes 1966088 | tf_op jit(solution)/shard_map/cond/branch_1_fun/ppermute | solution.py:380
  104.9 12.0 %collective-permute-start.1 = (bf16[256,1280]{1,0:T(8,128)(2,1)S(1)}, bf16[256,1280]{1,0:T(8,128)(2,1)}, u32[]{:S(2)}, u32[]{:S(2)}) collective-permute-start(bf16[256,1280]{1,0:T(8,128)(2,1)S(1)} %get-tuple-element.44), channel_id=1, source_target_pairs={{8,0},{16,8},{24,16},{32,24},{40,32},{48,40},{56,48},{64,56},{72,6... | collective-permute-start | bytes 1966088 | tf_op jit(solution)/shard_map/cond/branch_1_fun/ppermute | solution.py:375
  118.2 17.0 %collective-permute-start.2 = (bf16[256,1280]{1,0:T(8,128)(2,1)S(1)}, bf16[256,1280]{1,0:T(8,128)(2,1)}, u32[]{:S(2)}, u32[]{:S(2)}) collective-permute-start(bf16[256,1280]{1,0:T(8,128)(2,1)S(1)} %fold.1), channel_id=1, source_target_pairs={{16,0},{24,8},{32,16},{40,24},{48,32},{56,40},{64,48},{72,56},{80,... | collective-permute-start | bytes 1966088 | tf_op jit(solution)/shard_map/cond/branch_1_fun/ppermute | solution.py:375

commit v16 on v15

--- a/solution.py
+++ b/solution.py
@@ -79,23 +79,22 @@
     )(query, saved_out, grad_out, frames)
 
 
-def pack_keys_kernel(near, far, out):
-    for head in range(HEADS):
-        group, h = divmod(head, GROUP)
-        cols = slice(head * HDIM, (head + 1) * HDIM)
-        for block, ref in enumerate((near, far)):
-            for at in range(2):
-                first = (2 * (block * GROUP + h) + at) * HDIM
-                out[group, :, first : first + HDIM] = ref[at, :, cols]
+def pack_keys_kernel(near, far, *outs):
+    wide = GROUP * HDIM
+    for group in range(XN):
+        here = slice(group * wide, (group + 1) * wide)
+        for at, out in enumerate(outs):
+            out[group, :, :wide] = near[at, :, here]
+            out[group, :, wide:] = far[at, :, here]
 
 
 def pack_keys(near, far):
     _, tok, width = near.shape
     return pl.pallas_call(
         pack_keys_kernel,
-        out_shape=jax.ShapeDtypeStruct((XN, tok, 4 * GROUP * HDIM), BF16),
+        out_shape=[jax.ShapeDtypeStruct((XN, tok, 2 * GROUP * HDIM), BF16)] * 2,
         in_specs=[vmem()] * 2,
-        out_specs=vmem(),
+        out_specs=[vmem()] * 2,
         compiler_params=params(),
         cost_estimate=cost(0, 16 * tok * width),
         name="pack_keys",
@@ -120,8 +119,8 @@
     out_ref[...] = jnp.zeros_like(out_ref)
     for head in range(GROUP):
         queries = tokens[:, head_slice(head)].T
-        at = head_slice(2 * head)
-        keys = [near[:, at], near[:, head_slice(2 * (GROUP + head))], w2[:, at], w3[:, at]]
+        at = head_slice(head)
+        keys = [near[:, at], near[:, head_slice(GROUP + head)], w2[:, at], w3[:, at]]
         scores = jnp.dot(
             jnp.concatenate(keys, axis=0), queries, preferred_element_type=F32
         ) * SCALE2
@@ -171,7 +170,8 @@
 
 def grads_kernel(roles, parts_in, dq_in, bias_ref, place, one, other, tokens, own, *rest):
     count = len(roles)
-    sources, rest = rest[: 1 + (2 in roles) * 2], rest[1 + (2 in roles) * 2 :]
+    given = 6 if 2 in roles else 2
+    sources, rest = rest[:given], rest[given:]
     if parts_in:
         parts, rest = rest[:count], rest[count:]
     if dq_in:
@@ -179,11 +179,14 @@
     dq_out, *outs = rest[: 1 + count]
     rows, dq_acc, sums, window, held, k_meta, load_sems, sems, *rest = rest[1 + count :]
     half = rows.shape[1]
-    near, *others = sources
-    blocks = [near.at[:, : 2 * GROUP * HDIM], near.at[:, 2 * GROUP * HDIM :], *others]
+    wide = GROUP * HDIM
+    blocks = [[near.at[:, :wide] for near in sources[:2]], [near.at[:, wide:] for near in sources[:2]]]
+    blocks += [sources[2:4], sources[4:6]]
 
     moves = [(own.at[:, META], k_meta), (tokens, held)]
-    moves += [(blocks[role], window.at[at]) for at, role in enumerate(roles)]
+    for at, role in enumerate(roles):
+        moves.append((blocks[role][0], window.at[at, :, :wide]))
+        moves.append((blocks[role][1], window.at[at, :, wide:]))
     if parts_in:
         moves += [(part, rest[0].at[at]) for at, part in enumerate(parts)]
     if dq_in:
@@ -203,8 +206,8 @@
         queries, grads = held[:, q_cols], held[:, head_slice(GROUP + head)]
         first = place[0] * GROUP + head
         dot = rows[pl.ds(first, 1), :] + rows[pl.ds(LOW_LANE + first, 1), :]
-        keys = window[:, :, head_slice(2 * head)].reshape(count * half, HDIM)
-        values = window[:, :, head_slice(2 * head + 1)].reshape(count * half, HDIM)
+        keys = window[:, :, head_slice(head)].reshape(count * half, HDIM)
+        values = window[:, :, head_slice(GROUP + head)].reshape(count * half, HDIM)
         scores = jnp.dot(keys, queries.T, preferred_element_type=F32) * SCALE2
         pieces = []
         for at, role in enumerate(roles):
@@ -252,7 +255,7 @@
         blocks,
         pltpu.VMEM(tokens.shape, BF16),
         pltpu.VMEM((half, HDIM), BF16),
-        pltpu.SemaphoreType.DMA((2 * WBLK + 3,)),
+        pltpu.SemaphoreType.DMA((3 * WBLK + 3,)),
         pltpu.SemaphoreType.DMA((WBLK + 1,)),
     ]
     if parts:
@@ -380,9 +383,16 @@
     return lax.ppermute(value, "row", [(r, r ^ 1) for r in range(count)])
 
 
+def halo(near, is_even):
+    wide = GROUP * HDIM
+    own, second = near[:, :wide], near[:, wide:]
+    third = along_row(jnp.where(is_even, own, second), 1)
+    return in_chip(second), third
+
+
 def own_grads(operands):
     common, own, window, parts, even = operands
-    near = window[:1]
+    near = window[:2]
     dq_part, d2, d3 = grads("grads_own23", common, own, own, (2, 3), window, F32, parts[2:])
     side, swapped = along_row(d3, -1), in_chip(d2)
     dq_own, d0, d1 = grads(
@@ -392,8 +402,8 @@
 
 
 def no_grads(operands):
-    own, window = operands[1:3]
-    empty = jnp.zeros_like(window[1])
+    own = operands[1]
+    empty = jnp.zeros((own.shape[0], 2 * GROUP * HDIM), BF16)
     return jnp.zeros((own.shape[0], GROUP * HDIM), F32), empty, empty, empty
 
 
@@ -404,16 +414,18 @@
     even = is_even.astype(jnp.int32).reshape(1)
     tok = query.shape[0]
     half = XN * tok
-    wide = 2 * GROUP * HDIM
 
     kv = jnp.stack([key, value])
     kv_far = along_row(kv, 2)
     own = over_x(pack_queries(query, saved_out, grad_out, frame_ids[None, :])).reshape(half, -1)
     far = across_z(own)
-    near = over_x(pack_keys(kv, kv_far)).reshape(half, -1)
-    w0, w1 = near[:, :wide], near[:, wide:]
-    w3 = along_row(jnp.where(is_even, w0, w1), 1)
-    w2 = in_chip(w1)
+    keys, values = pack_keys(kv, kv_far)
+    keys = over_x(keys)
+    values, keys = lax.optimization_barrier((values, keys))
+    keys = keys.reshape(half, -1)
+    values = over_x(values).reshape(half, -1)
+    k2, k3 = halo(keys, is_even)
+    v2, v3 = halo(values, is_even)
     held = jnp.stack(
         [
             row >= 0,
@@ -424,12 +436,12 @@
     )
     bias = jnp.where(held, 0.0, NEG).astype(F32)
 
-    window = (near, w2, w3)
-    own_near = stats("stats_own", bias, own, own, window)
+    own_near = stats("stats_own", bias, own, own, (keys, k2, k3))
     far_other = across_z(own_near)
-    far_near = stats("stats_far", bias, far, own, window)
+    far_near = stats("stats_far", bias, far, own, (keys, k2, k3))
     own_other = across_z(far_near)
 
+    window = (keys, values, k2, v2, k3, v3)
     common = (bias, place, far_near, far_other)
     dq_far, *parts = grads("grads_far", common, far, own, (0, 1, 2, 3), window, BF16)
     dq_far, own_other = lax.optimization_barrier((dq_far, own_other))

time: 157 us -> 178 us (1.13)
  the two profiles are of different devices: /device:TPU:129 before, /device:TPU:1 now
where the time goes in v16:
time: 178 us; the launch traced here: 177 us
  starting transfers between devices  76.6 us (43%)
  waiting for transfers between devices  45.1 us (25%)
  Pallas kernels  30.7 us (17%)
  blocking collectives  21.6 us (12%)
  other arithmetic  2.23 us (1%)
    ppermute x5, waiting for transfers between devices, along_row(): lax.ppermute(value, 'row', [(r, r + steps) for r in range(first, last)])  31 us
    ppermute x4, starting transfers between devices, across_z(): lax.ppermute(value, 'col', [(c, (c + XN) % count) for c in range(count)])  28.8 us
    all_to_all x1, blocking collectives, over_x(): return lax.all_to_all(value, 'col', 0, 0, axis_index_groups=groups)  21.6 us
    ppermute x5, starting transfers between devices, along_row(): lax.ppermute(value, 'row', [(r, r + steps) for r in range(first, last)])  19.6 us
    pallas_call x3, Pallas kernels, grads(): pl.pallas_call(functools.partial(grads_kernel, roles, bool(parts), dq_par...  17.6 us
    all_to_all x3, starting transfers between devices, over_x(): return lax.all_to_all(value, 'col', 0, 0, axis_index_groups=groups)  14.2 us
    all_to_all x3, waiting for transfers between devices, over_x(): return lax.all_to_all(value, 'col', 0, 0, axis_index_groups=groups)  14.1 us
    ppermute x3, starting transfers between devices, in_chip(): return lax.ppermute(value, 'row', [(r, r ^ 1) for r in range(count)])  14 us
  transfers between devices with their start and end apart: 15, of which 5 were waited for; matrix products, arithmetic and copies ran while one was open for 1% of the time, Pallas kernels for 15%

profile of v16, /device:TPU:1, one launch (start us, length us, event | category | flops | bytes accessed | tf_op | source)
XLA Modules:
  0.0 177.2 jit_solution(2567708193383751184)
XLA Ops:
  0.6 1.1 pad_maximum_fusion.near
  1.8 4.1 %collective-permute-start.3 = (bf16[2,64,2560]{2,1,0:T(8,128)(2,1)S(1)}, bf16[2,64,2560]{2,1,0:T(8,128)(2,1)S(1)}, u32[]{:S(2)}, u32[]{:S(2)}) collective-permute-start(bf16[2,64,2560]{2,1,0:T(8,128)(2,1)S(1)} %pad_maximum_fusion.near), channel_id=1, source_target_pairs={{0,16},{8,24},{16,32},{24,40},{32,48},{40,56},{48,64},{56,72},{64,... | collective-permute-start | bytes 1966088 | tf_op jit(solution)/shard_map/ppermute | solution.py:378
  5.8 10.1 %collective-permute-done.3.far = bf16[2,64,2560]{2,1,0:T(8,128)(2,1)S(1)} collective-permute-done((bf16[2,64,2560]{2,1,0:T(8,128)(2,1)S(1)}, bf16[2,64,2560]{2,1,0:T(8,128)(2,1)S(1)}, u32[]{:S(2)}, u32[]{:S(2)}) %collective-permute-start.3) | collective-permute-done | bytes 655392 | tf_op jit(solution)/shard_map/ppermute | solution.py:378
  16.0 1.2 pack_keys.1
  17.1 7.2 %all-to-all-start.1 = ((bf16[4,64,1280]{2,1,0:T(8,128)(2,1)}), bf16[4,64,1280]{2,1,0:T(8,128)(2,1)S(1)}, u32[]{:S(2)}, u32[]{:S(2)}) async-start(bf16[4,64,1280]{2,1,0:T(8,128)(2,1)} %get-tuple-element.73), calls=%async_computation.1 | async-start | bytes 1310720 | tf_op jit(solution)/shard_map/all_to_all | solution.py:367
  24.4 3.0 %pack_queries.1 = bf16[4,64,1408]{2,1,0:T(8,128)(2,1)} custom-call(bf16[64,2560]{1,0:T(8,128)(2,1)} %q_any.1, bf16[64,2560]{1,0:T(8,128)(2,1)} %o_any.1, bf16[64,2560]{1,0:T(8,128)(2,1)} %g_any.1, s32[1,64]{1,0:T(1,128)} %bitcast.29), custom_call_target="tpu_custom_call" | custom-call | flops 327680 | bytes 2293760 | tf_op jit(solution)/shard_map/pack_queries/pallas_call | solution.py:70
  27.4 5.8 %all-to-all-done.1 = bf16[4,64,1280]{2,1,0:T(8,128)(2,1)S(1)} async-done(((bf16[4,64,1280]{2,1,0:T(8,128)(2,1)}), bf16[4,64,1280]{2,1,0:T(8,128)(2,1)S(1)}, u32[]{:S(2)}, u32[]{:S(2)}) %all-to-all-start.1) | async-done | bytes 655392 | tf_op jit(solution)/shard_map/all_to_all | solution.py:367
  33.2 3.5 %all-to-all-start = ((bf16[4,64,1408]{2,1,0:T(8,128)(2,1)}), bf16[4,64,1408]{2,1,0:T(8,128)(2,1)S(1)}, u32[]{:S(2)}, u32[]{:S(2)}) async-start(bf16[4,64,1408]{2,1,0:T(8,128)(2,1)} %pack_queries.1), calls=%async_computation | async-start | bytes 1441792 | tf_op jit(solution)/shard_map/all_to_all | solution.py:367
  36.7 8.2 %all-to-all-done = bf16[4,64,1408]{2,1,0:T(8,128)(2,1)S(1)} async-done(((bf16[4,64,1408]{2,1,0:T(8,128)(2,1)}), bf16[4,64,1408]{2,1,0:T(8,128)(2,1)S(1)}, u32[]{:S(2)}, u32[]{:S(2)}) %all-to-all-start) | async-done | bytes 720928 | tf_op jit(solution)/shard_map/all_to_all | solution.py:367
  44.9 3.5 %all-to-all-start.2 = ((bf16[4,64,1280]{2,1,0:T(8,128)(2,1)}), bf16[4,64,1280]{2,1,0:T(8,128)(2,1)S(1)}, u32[]{:S(2)}, u32[]{:S(2)}) async-start(bf16[4,64,1280]{2,1,0:T(8,128)(2,1)} %get-tuple-element.75), calls=%async_computation.2 | async-start | bytes 1310720 | tf_op jit(solution)/shard_map/all_to_all | solution.py:367
  48.5 10.6 %collective-permute-start.6 = (bf16[256,1408]{1,0:T(8,128)(2,1)S(1)}, bf16[256,1408]{1,0:T(8,128)(2,1)S(1)}, u32[]{:S(2)}, u32[]{:S(2)}) collective-permute-start(bf16[256,1408]{1,0:T(8,128)(2,1)S(1)} %bitcast.13), channel_id=1, source_target_pairs={{0,4},{1,5},{2,6},{3,7},{4,0},{5,1},{6,2},{7,3},{8,12},{9,13},{10,... | collective-permute-start | bytes 2162696 | tf_op jit(solution)/shard_map/ppermute | solution.py:372
  59.1 0.9 slice_select_fusion.1
  60.0 8.5 %collective-permute-start.5 = (bf16[256,640]{1,0:T(8,128)(2,1)}, bf16[256,640]{1,0:T(8,128)(2,1)S(1)}, u32[]{:S(2)}, u32[]{:S(2)}) collective-permute-start(bf16[256,640]{1,0:T(8,128)(2,1)} %get-tuple-element.89), channel_id=1, source_target_pairs={{0,8},{8,16},{16,24},{24,32},{32,40},{40,48},{48,56},{56,64},{64,7... | collective-permute-start | bytes 983048 | tf_op jit(solution)/shard_map/ppermute | solution.py:378
  68.5 1.9 %collective-permute-start.4 = (bf16[256,640]{1,0:T(8,128)(2,1)}, bf16[256,640]{1,0:T(8,128)(2,1)S(1)}, u32[]{:S(2)}, u32[]{:S(2)}) collective-permute-start(bf16[256,640]{1,0:T(8,128)(2,1)} %get-tuple-element.90), channel_id=1, source_target_pairs={{0,8},{8,0},{16,24},{24,16},{32,40},{40,32},{48,56},{56,48},{64,72... | collective-permute-start | bytes 983048 | tf_op jit(solution)/shard_map/ppermute | solution.py:383
  70.4 0.0 all-to-all-done.2
  70.5 0.1 slice_select_fusion
  70.5 3.6 %collective-permute-start.9 = (bf16[256,640]{1,0:T(8,128)(2,1)S(1)}, bf16[256,640]{1,0:T(8,128)(2,1)S(1)}, u32[]{:S(2)}, u32[]{:S(2)}) collective-permute-start(bf16[256,640]{1,0:T(8,128)(2,1)S(1)} %get-tuple-element.87), channel_id=1, source_target_pairs={{0,8},{8,16},{16,24},{24,32},{32,40},{40,48},{48,56},{56,64},{64,7... | collective-permute-start | bytes 983048 | tf_op jit(solution)/shard_map/ppermute | solution.py:378
  74.1 1.9 %collective-permute-start.8 = (bf16[256,640]{1,0:T(8,128)(2,1)S(1)}, bf16[256,640]{1,0:T(8,128)(2,1)S(1)}, u32[]{:S(2)}, u32[]{:S(2)}) collective-permute-start(bf16[256,640]{1,0:T(8,128)(2,1)S(1)} %get-tuple-element.88), channel_id=1, source_target_pairs={{0,8},{8,0},{16,24},{24,16},{32,40},{40,32},{48,56},{56,48},{64,72... | collective-permute-start | bytes 983048 | tf_op jit(solution)/shard_map/ppermute | solution.py:383
  76.0 0.1 pad_add_fusion.place
  76.1 0.1 add_select_fusion.bias_ref
  76.2 0.0 collective-permute-done.5.w3.rest_4_
  76.2 0.0 collective-permute-done.4.w2.rest_2_
  76.2 0.0 copy-start
  76.2 2.2 %stats_own.1 = f32[16,256]{1,0:T(8,128)S(1)} custom-call(f32[4]{0:T(128)S(1)} %add_select_fusion.bias_ref, bf16[256,1408]{1,0:T(8,128)(2,1)S(1)} %bitcast.14, bf16[256,1408]{1,0:T(8,128)(2,1)S(1)} %bitcast.15, bf16[256,1280]{1,0:T(8,128)(2,1)S(1)} %bitcast.20, bf16[256,640]{1,0:T(8,128)(2,1)S(1)} %collective-permute-done.4.w2.rest_2_, ...), custom_call_target="tpu_custom_call" | custom-call | flops 671088640 | bytes 1638400 | tf_op jit(solution)/shard_map/stats_own/pallas_call | solution.py:152
  78.4 2.0 %collective-permute-start.7 = (f32[16,256]{1,0:T(8,128)S(1)}, f32[16,256]{1,0:T(8,128)S(1)}, u32[]{:S(2)}, u32[]{:S(2)}) collective-permute-start(f32[16,256]{1,0:T(8,128)S(1)} %stats_own.1), channel_id=1, source_target_pairs={{0,4},{1,5},{2,6},{3,7},{4,0},{5,1},{6,2},{7,3},{8,12},{9,13},{10,... | collective-permute-start | bytes 49160 | tf_op jit(solution)/shard_map/ppermute | solution.py:372
  80.4 0.0 collective-permute-done.6.tokens
  80.5 0.0 copy-done
  80.5 2.2 %stats_far.1.one = f32[16,256]{1,0:T(8,128)S(1)} custom-call(f32[4]{0:T(128)S(1)} %add_select_fusion.bias_ref, bf16[256,1408]{1,0:T(8,128)(2,1)S(1)} %collective-permute-done.6.tokens, bf16[256,1408]{1,0:T(8,128)(2,1)S(1)} %bitcast.16, bf16[256,1280]{1,0:T(8,128)(2,1)S(1)} %bitcast.21, bf16[256,640]{1,0:T(8,128)(2,1)S(1)} %collective-permute-done.4.w2.rest_2_, ...), custom_call_target="tpu_custom_call" | custom-call | flops 671088640 | bytes 1638400 | tf_op jit(solution)/shard_map/stats_far/pallas_call | solution.py:152
  82.7 7.2 %collective-permute-start.10 = (f32[16,256]{1,0:T(8,128)S(1)}, f32[16,256]{1,0:T(8,128)S(1)}, u32[]{:S(2)}, u32[]{:S(2)}) collective-permute-start(f32[16,256]{1,0:T(8,128)S(1)} %stats_far.1.one), channel_id=1, source_target_pairs={{0,4},{1,5},{2,6},{3,7},{4,0},{5,1},{6,2},{7,3},{8,12},{9,13},{10,... | collective-permute-start | bytes 49160 | tf_op jit(solution)/shard_map/ppermute | solution.py:372
  89.9 0.0 collective-permute-done.7.other
  89.9 0.0 collective-permute-done.9.rest_5_
  89.9 0.0 copy-start.3
  89.9 0.0 collective-permute-done.8.rest_3_
  89.9 0.0 copy-start.4
  89.9 7.4 %grads_far.1 = (bf16[256,640]{1,0:T(8,128)(2,1)S(1)}, bf16[256,1280]{1,0:T(8,128)(2,1)}, bf16[256,1280]{1,0:T(8,128)(2,1)}, bf16[256,1280]{1,0:T(8,128)(2,1)}, bf16[256,1280]{1,0:T(8,128)(2,1)}) custom-call(f32[4]{0:T(128)S(1)} %add_select_fusion.bias_ref, s32[2]{0:T(128)S(1)} %pad_add_fusion.place, f32[16,256]{1,0:T(8,128)S(1)} %stats_far.1.one, ...), custom_call_target="tpu_custom_call" | custom-call | flops 1677721600 | bytes 3932160 | tf_op jit(solution)/shard_map/grads_far/pallas_call | solution.py:265
  97.3 0.0 copy-done.3
  97.3 0.0 copy-done.4
  97.3 0.0 collective-permute-done.10
  97.4 9.0 %collective-permute-start.11 = (bf16[256,640]{1,0:T(8,128)(2,1)S(1)}, bf16[256,640]{1,0:T(8,128)(2,1)S(1)}, u32[]{:S(2)}, u32[]{:S(2)}) collective-permute-start(bf16[256,640]{1,0:T(8,128)(2,1)S(1)} %get-tuple-element.83), channel_id=1, source_target_pairs={{0,4},{1,5},{2,6},{3,7},{4,0},{5,1},{6,2},{7,3},{8,12},{9,13},{10,... | collective-permute-start | bytes 983048 | tf_op jit(solution)/shard_map/ppermute | solution.py:372
  106.3 46.0 %conditional.1 = (f32[256,640]{1,0:T(8,128)S(1)}, bf16[256,1280]{1,0:T(8,128)(2,1)S(1)}, bf16[256,1280]{1,0:T(8,128)(2,1)}, bf16[256,1280]{1,0:T(8,128)(2,1)}) conditional(s32[]{:T(128)} %convert_element_type.4, () %tuple.17, (f32[4]{0:T(128)S(1)}, s32[2]{0:T(128)S(1)}, f32[16,256]{1,0:T(8,128)S(1)}, f32[16,256]{1,0:T(8,128)S(1)}, ...), branch_computations={%region_0.1_spmd, %region_1.2_spmd} | conditional | flops 1678704640 | bytes 23593168 | solution.py:450
  106.3 0.0 copy-start.1
  106.4 0.0 copy-start.2
  106.4 5.5 %grads_own23.1 = (f32[256,640]{1,0:T(8,128)S(1)}, bf16[256,1280]{1,0:T(8,128)(2,1)S(1)}, bf16[256,1280]{1,0:T(8,128)(2,1)S(1)}) custom-call(f32[4]{0:T(128)S(1)} %get-tuple-element.32.bias_ref, s32[2]{0:T(128)S(1)} %get-tuple-element.33.place, f32[16,256]{1,0:T(8,128)S(1)} %get-tuple-element.34.one, f32[16,256]{1,0:T(8,128)S(1)} %get-tuple-element.35.other, ...), custom_call_target="tpu_custom_call" | custom-call | flops 838860800 | bytes 3932160 | tf_op jit(solution)/shard_map/cond/branch_1_fun/grads_own23/pallas_call | solution.py:265
  111.9 10.1 %collective-permute-start = (bf16[256,1280]{1,0:T(8,128)(2,1)S(1)}, bf16[256,1280]{1,0:T(8,128)(2,1)S(1)}, u32[]{:S(2)}, u32[]{:S(2)}) collective-permute-start(bf16[256,1280]{1,0:T(8,128)(2,1)S(1)} %get-tuple-element.52), channel_id=1, source_target_pairs={{0,8},{8,0},{16,24},{24,16},{32,40},{40,32},{48,56},{56,48},{64,72... | collective-permute-start | bytes 1966088 | tf_op jit(solution)/shard_map/cond/branch_1_fun/ppermute | solution.py:383
  122.0 2.1 %collective-permute-start.1 = (bf16[256,1280]{1,0:T(8,128)(2,1)S(1)}, bf16[256,1280]{1,0:T(8,128)(2,1)}, u32[]{:S(2)}, u32[]{:S(2)}) collective-permute-start(bf16[256,1280]{1,0:T(8,128)(2,1)S(1)} %get-tuple-element.53), channel_id=1, source_target_pairs={{8,0},{16,8},{24,16},{32,24},{40,32},{48,40},{56,48},{64,56},{72,6... | collective-permute-start | bytes 1966088 | tf_op jit(solution)/shard_map/cond/branch_1_fun/ppermute | solution.py:378
  124.1 0.0 copy-done.1
  124.1 0.0 copy-done.2
  124.1 4.7 %grads_own01.1 = (f32[256,640]{1,0:T(8,128)S(1)}, bf16[256,1280]{1,0:T(8,128)(2,1)S(1)}, bf16[256,1280]{1,0:T(8,128)(2,1)S(1)}) custom-call(f32[4]{0:T(128)S(1)} %get-tuple-element.32.bias_ref, s32[2]{0:T(128)S(1)} %get-tuple-element.33.place, f32[16,256]{1,0:T(8,128)S(1)} %get-tuple-element.34.one, f32[16,256]{1,0:T(8,128)S(1)} %get-tuple-element.35.other, ...), custom_call_target="tpu_custom_call" | custom-call | flops 838860800 | bytes 3932160 | tf_op jit(solution)/shard_map/cond/branch_1_fun/grads_own01/pallas_call | solution.py:265
  128.8 0.0 collective-permute-done.swapped
  128.8 5.2 %collective-permute-done.1.side = bf16[256,1280]{1,0:T(8,128)(2,1)} collective-permute-done((bf16[256,1280]{1,0:T(8,128)(2,1)S(1)}, bf16[256,1280]{1,0:T(8,128)(2,1)}, u32[]{:S(2)}, u32[]{:S(2)}) %collective-permute-start.1) | collective-permute-done | bytes 655392 | tf_op jit(solution)/shard_map/cond/branch_1_fun/ppermute | solution.py:378
  134.0 1.3 fold.1
  135.3 1.3 collective-permute-start.2
  136.6 15.7 %collective-permute-done.2 = bf16[256,1280]{1,0:T(8,128)(2,1)} collective-permute-done((bf16[256,1280]{1,0:T(8,128)(2,1)S(1)}, bf16[256,1280]{1,0:T(8,128)(2,1)}, u32[]{:S(2)}, u32[]{:S(2)}) %collective-permute-start.2) | collective-permute-done | bytes 655392 | tf_op jit(solution)/shard_map/cond/branch_1_fun/ppermute | solution.py:378
  152.4 0.0 collective-permute-done.11.dq_back
  152.4 2.2 %close.1 = bf16[4,64,1920]{2,1,0:T(8,128)(2,1)S(1)} custom-call(s32[1]{0:T(128)} %bitcast.even_ref, f32[256,640]{1,0:T(8,128)S(1)} %get-tuple-element.82.dq_own, bf16[256,640]{1,0:T(8,128)(2,1)S(1)} %collective-permute-done.11.dq_back, bf16[256,1280]{1,0:T(8,128)(2,1)S(1)} %get-tuple-element.84.d0, bf16[256,1280]{1,0:T(8,128)(2,1)} %get-tuple-element.85.back, ...), custom_call_target="tpu_custom_call" | custom-call | flops 983040 | bytes 3932160 | tf_op jit(solution)/shard_map/close/pallas_call | solution.py:324
  154.5 21.6 %all_to_all.20.parts = bf16[4,64,1920]{2,1,0:T(8,128)(2,1)S(1)} all-to-all(bf16[4,64,1920]{2,1,0:T(8,128)(2,1)S(1)} %close.1), channel_id=1, replica_groups={{0,1,2,3},{4,5,6,7},{8,9,10,11},{12,13,14,15},{16,17,18,19},{20,21,22,2..., dimensions={0} | all-to-all | bytes 1966080 | tf_op jit(solution)/shard_map/all_to_all | solution.py:367
  176.1 1.1 unpack.1
Async XLA Ops:
  1.8 14.2 %collective-permute-start.3 = (bf16[2,64,2560]{2,1,0:T(8,128)(2,1)S(1)}, bf16[2,64,2560]{2,1,0:T(8,128)(2,1)S(1)}, u32[]{:S(2)}, u32[]{:S(2)}) collective-permute-start(bf16[2,64,2560]{2,1,0:T(8,128)(2,1)S(1)} %pad_maximum_fusion.near), channel_id=1, source_target_pairs={{0,16},{8,24},{16,32},{24,40},{32,48},{40,56},{48,64},{56,72},{64,... | collective-permute-start | bytes 1966088 | tf_op jit(solution)/shard_map/ppermute | solution.py:378
  17.1 16.0 %all-to-all-start.1 = ((bf16[4,64,1280]{2,1,0:T(8,128)(2,1)}), bf16[4,64,1280]{2,1,0:T(8,128)(2,1)S(1)}, u32[]{:S(2)}, u32[]{:S(2)}) async-start(bf16[4,64,1280]{2,1,0:T(8,128)(2,1)} %get-tuple-element.73), calls=%async_computation.1 | async-start | bytes 1310720 | tf_op jit(solution)/shard_map/all_to_all | solution.py:367
  33.2 11.7 %all-to-all-start = ((bf16[4,64,1408]{2,1,0:T(8,128)(2,1)}), bf16[4,64,1408]{2,1,0:T(8,128)(2,1)S(1)}, u32[]{:S(2)}, u32[]{:S(2)}) async-start(bf16[4,64,1408]{2,1,0:T(8,128)(2,1)} %pack_queries.1), calls=%async_computation | async-start | bytes 1441792 | tf_op jit(solution)/shard_map/all_to_all | solution.py:367
  44.9 25.5 %all-to-all-start.2 = ((bf16[4,64,1280]{2,1,0:T(8,128)(2,1)}), bf16[4,64,1280]{2,1,0:T(8,128)(2,1)S(1)}, u32[]{:S(2)}, u32[]{:S(2)}) async-start(bf16[4,64,1280]{2,1,0:T(8,128)(2,1)} %get-tuple-element.75), calls=%async_computation.2 | async-start | bytes 1310720 | tf_op jit(solution)/shard_map/all_to_all | solution.py:367
  48.5 32.0 %collective-permute-start.6 = (bf16[256,1408]{1,0:T(8,128)(2,1)S(1)}, bf16[256,1408]{1,0:T(8,128)(2,1)S(1)}, u32[]{:S(2)}, u32[]{:S(2)}) collective-permute-start(bf16[256,1408]{1,0:T(8,128)(2,1)S(1)} %bitcast.13), channel_id=1, source_target_pairs={{0,4},{1,5},{2,6},{3,7},{4,0},{5,1},{6,2},{7,3},{8,12},{9,13},{10,... | collective-permute-start | bytes 2162696 | tf_op jit(solution)/shard_map/ppermute | solution.py:372
  60.0 16.2 %collective-permute-start.5 = (bf16[256,640]{1,0:T(8,128)(2,1)}, bf16[256,640]{1,0:T(8,128)(2,1)S(1)}, u32[]{:S(2)}, u32[]{:S(2)}) collective-permute-start(bf16[256,640]{1,0:T(8,128)(2,1)} %get-tuple-element.89), channel_id=1, source_target_pairs={{0,8},{8,16},{16,24},{24,32},{32,40},{40,48},{48,56},{56,64},{64,7... | collective-permute-start | bytes 983048 | tf_op jit(solution)/shard_map/ppermute | solution.py:378
  68.5 7.7 %collective-permute-start.4 = (bf16[256,640]{1,0:T(8,128)(2,1)}, bf16[256,640]{1,0:T(8,128)(2,1)S(1)}, u32[]{:S(2)}, u32[]{:S(2)}) collective-permute-start(bf16[256,640]{1,0:T(8,128)(2,1)} %get-tuple-element.90), channel_id=1, source_target_pairs={{0,8},{8,0},{16,24},{24,16},{32,40},{40,32},{48,56},{56,48},{64,72... | collective-permute-start | bytes 983048 | tf_op jit(solution)/shard_map/ppermute | solution.py:383
  70.5 19.4 %collective-permute-start.9 = (bf16[256,640]{1,0:T(8,128)(2,1)S(1)}, bf16[256,640]{1,0:T(8,128)(2,1)S(1)}, u32[]{:S(2)}, u32[]{:S(2)}) collective-permute-start(bf16[256,640]{1,0:T(8,128)(2,1)S(1)} %get-tuple-element.87), channel_id=1, source_target_pairs={{0,8},{8,16},{16,24},{24,32},{32,40},{40,48},{48,56},{56,64},{64,7... | collective-permute-start | bytes 983048 | tf_op jit(solution)/shard_map/ppermute | solution.py:378
  74.1 15.8 %collective-permute-start.8 = (bf16[256,640]{1,0:T(8,128)(2,1)S(1)}, bf16[256,640]{1,0:T(8,128)(2,1)S(1)}, u32[]{:S(2)}, u32[]{:S(2)}) collective-permute-start(bf16[256,640]{1,0:T(8,128)(2,1)S(1)} %get-tuple-element.88), channel_id=1, source_target_pairs={{0,8},{8,0},{16,24},{24,16},{32,40},{40,32},{48,56},{56,48},{64,72... | collective-permute-start | bytes 983048 | tf_op jit(solution)/shard_map/ppermute | solution.py:383
  76.2 4.3 %copy-start = (bf16[256,640]{1,0:T(8,128)(2,1)}, bf16[256,640]{1,0:T(8,128)(2,1)S(1)}, u32[]{:S(2)}) copy-start(bf16[256,640]{1,0:T(8,128)(2,1)S(1)} %collective-permute-done.4.w2.rest_2_) | copy-start | bytes 983044
  78.4 11.4 %collective-permute-start.7 = (f32[16,256]{1,0:T(8,128)S(1)}, f32[16,256]{1,0:T(8,128)S(1)}, u32[]{:S(2)}, u32[]{:S(2)}) collective-permute-start(f32[16,256]{1,0:T(8,128)S(1)} %stats_own.1), channel_id=1, source_target_pairs={{0,4},{1,5},{2,6},{3,7},{4,0},{5,1},{6,2},{7,3},{8,12},{9,13},{10,... | collective-permute-start | bytes 49160 | tf_op jit(solution)/shard_map/ppermute | solution.py:372
  82.7 14.7 %collective-permute-start.10 = (f32[16,256]{1,0:T(8,128)S(1)}, f32[16,256]{1,0:T(8,128)S(1)}, u32[]{:S(2)}, u32[]{:S(2)}) collective-permute-start(f32[16,256]{1,0:T(8,128)S(1)} %stats_far.1.one), channel_id=1, source_target_pairs={{0,4},{1,5},{2,6},{3,7},{4,0},{5,1},{6,2},{7,3},{8,12},{9,13},{10,... | collective-permute-start | bytes 49160 | tf_op jit(solution)/shard_map/ppermute | solution.py:372
  89.9 7.4 %copy-start.3 = (bf16[256,640]{1,0:T(8,128)(2,1)}, bf16[256,640]{1,0:T(8,128)(2,1)S(1)}, u32[]{:S(2)}) copy-start(bf16[256,640]{1,0:T(8,128)(2,1)S(1)} %collective-permute-done.9.rest_5_) | copy-start | bytes 983044
  89.9 7.4 %copy-start.4 = (bf16[256,640]{1,0:T(8,128)(2,1)}, bf16[256,640]{1,0:T(8,128)(2,1)S(1)}, u32[]{:S(2)}) copy-start(bf16[256,640]{1,0:T(8,128)(2,1)S(1)} %collective-permute-done.8.rest_3_) | copy-start | bytes 983044
  97.4 55.0 %collective-permute-start.11 = (bf16[256,640]{1,0:T(8,128)(2,1)S(1)}, bf16[256,640]{1,0:T(8,128)(2,1)S(1)}, u32[]{:S(2)}, u32[]{:S(2)}) collective-permute-start(bf16[256,640]{1,0:T(8,128)(2,1)S(1)} %get-tuple-element.83), channel_id=1, source_target_pairs={{0,4},{1,5},{2,6},{3,7},{4,0},{5,1},{6,2},{7,3},{8,12},{9,13},{10,... | collective-permute-start | bytes 983048 | tf_op jit(solution)/shard_map/ppermute | solution.py:372
  106.3 17.8 %copy-start.1 = (bf16[256,1280]{1,0:T(8,128)(2,1)S(1)}, bf16[256,1280]{1,0:T(8,128)(2,1)}, u32[]{:S(2)}) copy-start(bf16[256,1280]{1,0:T(8,128)(2,1)} %get-tuple-element.39.rest_2_) | copy-start | bytes 1966084 | tf_op jit(solution)/shard_map/cond
  106.4 17.8 %copy-start.2 = (bf16[256,1280]{1,0:T(8,128)(2,1)S(1)}, bf16[256,1280]{1,0:T(8,128)(2,1)}, u32[]{:S(2)}) copy-start(bf16[256,1280]{1,0:T(8,128)(2,1)} %get-tuple-element.40.rest_3_) | copy-start | bytes 1966084 | tf_op jit(solution)/shard_map/cond
  111.9 17.0 %collective-permute-start = (bf16[256,1280]{1,0:T(8,128)(2,1)S(1)}, bf16[256,1280]{1,0:T(8,128)(2,1)S(1)}, u32[]{:S(2)}, u32[]{:S(2)}) collective-permute-start(bf16[256,1280]{1,0:T(8,128)(2,1)S(1)} %get-tuple-element.52), channel_id=1, source_target_pairs={{0,8},{8,0},{16,24},{24,16},{32,40},{40,32},{48,56},{56,48},{64,72... | collective-permute-start | bytes 1966088 | tf_op jit(solution)/shard_map/cond/branch_1_fun/ppermute | solution.py:383
  122.0 12.0 %collective-permute-start.1 = (bf16[256,1280]{1,0:T(8,128)(2,1)S(1)}, bf16[256,1280]{1,0:T(8,128)(2,1)}, u32[]{:S(2)}, u32[]{:S(2)}) collective-permute-start(bf16[256,1280]{1,0:T(8,128)(2,1)S(1)} %get-tuple-element.53), channel_id=1, source_target_pairs={{8,0},{16,8},{24,16},{32,24},{40,32},{48,40},{56,48},{64,56},{72,6... | collective-permute-start | bytes 1966088 | tf_op jit(solution)/shard_map/cond/branch_1_fun/ppermute | solution.py:378
  135.3 17.0 %collective-permute-start.2 = (bf16[256,1280]{1,0:T(8,128)(2,1)S(1)}, bf16[256,1280]{1,0:T(8,128)(2,1)}, u32[]{:S(2)}, u32[]{:S(2)}) collective-permute-start(bf16[256,1280]{1,0:T(8,128)(2,1)S(1)} %fold.1), channel_id=1, source_target_pairs={{16,0},{24,8},{32,16},{40,24},{48,32},{56,40},{64,48},{72,56},{80,... | collective-permute-start | bytes 1966088 | tf_op jit(solution)/shard_map/cond/branch_1_fun/ppermute | solution.py:378

commit v17 on v15

--- a/solution.py
+++ b/solution.py
@@ -193,11 +193,27 @@
     ]
     for load in loads:
         load.start()
-    for load in loads:
+    for load in loads[:2]:
         load.wait()
 
     rows[...] = held[:, META].astype(F32).T
     totals = log_total(one, other)
+    for load in loads[2:]:
+        load.wait()
+
+    split = 3
+
+    def leave(part, cols):
+        copies = [
+            pltpu.make_async_copy(
+                sums.at[at, :, cols], outs[at].at[:, cols], sems.at[part, at]
+            )
+            for at in range(count)
+        ]
+        for copy in copies:
+            copy.start()
+        return copies
+
     for head in range(GROUP):
         q_cols = head_slice(head)
         queries, grads = held[:, q_cols], held[:, head_slice(GROUP + head)]
@@ -228,11 +244,11 @@
         if dq_in:
             turned += rest[1][:, q_cols]
         dq_acc[:, q_cols] = turned.astype(dq_acc.dtype)
-    stores = [pltpu.make_async_copy(dq_acc, dq_out, sems.at[count])]
-    for at in range(count):
-        stores.append(pltpu.make_async_copy(sums.at[at], outs[at], sems.at[at]))
-    for store in stores:
-        store.start()
+        if head == split - 1:
+            stores = leave(0, slice(0, 2 * split * HDIM))
+    stores += leave(1, slice(2 * split * HDIM, 2 * GROUP * HDIM))
+    stores.append(pltpu.make_async_copy(dq_acc, dq_out, sems.at[0, count]))
+    stores[-1].start()
     for store in stores:
         store.wait()
 
@@ -253,7 +269,7 @@
         pltpu.VMEM(tokens.shape, BF16),
         pltpu.VMEM((half, HDIM), BF16),
         pltpu.SemaphoreType.DMA((2 * WBLK + 3,)),
-        pltpu.SemaphoreType.DMA((WBLK + 1,)),
+        pltpu.SemaphoreType.DMA((2, WBLK + 1)),
     ]
     if parts:
         scratch.append(blocks)

time: 157 us -> 157 us (level)
  transfers between devices with their start and end apart: 12 -> 12, of which waited for: 6 -> 6; matrix products, arithmetic and copies ran while one was open for 1% -> 1% of each run, Pallas kernels for 19% -> 18%
where the time goes in v17:
time: 157 us; the launch traced here: 156 us
  starting transfers between devices  53.9 us (34%)
  waiting for transfers between devices  48.9 us (31%)
  Pallas kernels  32 us (20%)
  blocking collectives  18.5 us (12%)
  other arithmetic  2.22 us (1%)
    ppermute x4, waiting for transfers between devices, along_row(): lax.ppermute(value, 'row', [(r, r + steps) for r in range(first, last)])  33.6 us
    ppermute x4, starting transfers between devices, across_z(): lax.ppermute(value, 'col', [(c, (c + XN) % count) for c in range(count)])  26.9 us
    all_to_all x1, blocking collectives, over_x(): return lax.all_to_all(value, 'col', 0, 0, axis_index_groups=groups)  18.5 us
    pallas_call x3, Pallas kernels, grads(): pl.pallas_call(functools.partial(grads_kernel, roles, bool(parts), dq_par...  17.2 us
    ppermute x4, starting transfers between devices, along_row(): lax.ppermute(value, 'row', [(r, r + steps) for r in range(first, last)])  14 us
    all_to_all x2, starting transfers between devices, over_x(): return lax.all_to_all(value, 'col', 0, 0, axis_index_groups=groups)  8.04 us
    ppermute x4, waiting for transfers between devices, across_z(): lax.ppermute(value, 'col', [(c, (c + XN) % count) for c in range(count)])  7.99 us
    all_to_all x2, waiting for transfers between devices, over_x(): return lax.all_to_all(value, 'col', 0, 0, axis_index_groups=groups)  7.28 us
  transfers between devices with their start and end apart: 12, of which 6 were waited for; matrix products, arithmetic and copies ran while one was open for 1% of the time, Pallas kernels for 18%

profile of v17, /device:TPU:129, one launch (start us, length us, event | category | flops | bytes accessed | tf_op | source)
XLA Modules:
  0.0 156.4 jit_solution(4340627104164336307)
XLA Ops:
  0.6 1.1 pad_maximum_fusion.near
  1.8 3.2 %collective-permute-start.3 = (bf16[2,64,2560]{2,1,0:T(8,128)(2,1)S(1)}, bf16[2,64,2560]{2,1,0:T(8,128)(2,1)S(1)}, u32[]{:S(2)}, u32[]{:S(2)}) collective-permute-start(bf16[2,64,2560]{2,1,0:T(8,128)(2,1)S(1)} %pad_maximum_fusion.near), channel_id=1, source_target_pairs={{0,16},{8,24},{16,32},{24,40},{32,48},{40,56},{48,64},{56,72},{64,... | collective-permute-start | bytes 1966088 | tf_op jit(solution)/shard_map/ppermute | solution.py:391
  5.0 3.0 %pack_queries.1 = bf16[4,64,1408]{2,1,0:T(8,128)(2,1)} custom-call(bf16[64,2560]{1,0:T(8,128)(2,1)} %q_any.1, bf16[64,2560]{1,0:T(8,128)(2,1)} %o_any.1, bf16[64,2560]{1,0:T(8,128)(2,1)} %g_any.1, s32[1,64]{1,0:T(1,128)} %bitcast.25), custom_call_target="tpu_custom_call" | custom-call | flops 327680 | bytes 2293760 | tf_op jit(solution)/shard_map/pack_queries/pallas_call | solution.py:70
  8.0 4.0 %all-to-all-start = ((bf16[4,64,1408]{2,1,0:T(8,128)(2,1)}), bf16[4,64,1408]{2,1,0:T(8,128)(2,1)S(1)}, u32[]{:S(2)}, u32[]{:S(2)}) async-start(bf16[4,64,1408]{2,1,0:T(8,128)(2,1)} %pack_queries.1), calls=%async_computation | async-start | bytes 1441792 | tf_op jit(solution)/shard_map/all_to_all | solution.py:380
  12.0 9.4 %collective-permute-done.3.far = bf16[2,64,2560]{2,1,0:T(8,128)(2,1)S(1)} collective-permute-done((bf16[2,64,2560]{2,1,0:T(8,128)(2,1)S(1)}, bf16[2,64,2560]{2,1,0:T(8,128)(2,1)S(1)}, u32[]{:S(2)}, u32[]{:S(2)}) %collective-permute-start.3) | collective-permute-done | bytes 655392 | tf_op jit(solution)/shard_map/ppermute | solution.py:391
  21.4 1.3 pack_keys.1
  22.7 0.0 all-to-all-done
  22.7 4.0 %all-to-all-start.1 = ((bf16[4,64,2560]{2,1,0:T(8,128)(2,1)}), bf16[4,64,2560]{2,1,0:T(8,128)(2,1)S(1)}, u32[]{:S(2)}, u32[]{:S(2)}) async-start(bf16[4,64,2560]{2,1,0:T(8,128)(2,1)} %pack_keys.1), calls=%async_computation.1 | async-start | bytes 2621440 | tf_op jit(solution)/shard_map/all_to_all | solution.py:380
  26.7 8.8 %collective-permute-start.6 = (bf16[256,1408]{1,0:T(8,128)(2,1)S(1)}, bf16[256,1408]{1,0:T(8,128)(2,1)S(1)}, u32[]{:S(2)}, u32[]{:S(2)}) collective-permute-start(bf16[256,1408]{1,0:T(8,128)(2,1)S(1)} %bitcast.17), channel_id=1, source_target_pairs={{0,4},{1,5},{2,6},{3,7},{4,0},{5,1},{6,2},{7,3},{8,12},{9,13},{10,... | collective-permute-start | bytes 2162696 | tf_op jit(solution)/shard_map/ppermute | solution.py:385
  35.5 7.3 %all-to-all-done.1 = bf16[4,64,2560]{2,1,0:T(8,128)(2,1)S(1)} async-done(((bf16[4,64,2560]{2,1,0:T(8,128)(2,1)}), bf16[4,64,2560]{2,1,0:T(8,128)(2,1)S(1)}, u32[]{:S(2)}, u32[]{:S(2)}) %all-to-all-start.1) | async-done | bytes 1310752 | tf_op jit(solution)/shard_map/all_to_all | solution.py:380
  42.8 0.9 slice_select_fusion
  43.7 5.0 %collective-permute-start.5 = (bf16[256,1280]{1,0:T(8,128)(2,1)}, bf16[256,1280]{1,0:T(8,128)(2,1)}, u32[]{:S(2)}, u32[]{:S(2)}) collective-permute-start(bf16[256,1280]{1,0:T(8,128)(2,1)} %get-tuple-element.70), channel_id=1, source_target_pairs={{0,8},{8,16},{16,24},{24,32},{32,40},{40,48},{48,56},{56,64},{64,7... | collective-permute-start | bytes 1966088 | tf_op jit(solution)/shard_map/ppermute | solution.py:391
  48.8 1.9 %collective-permute-start.4 = (bf16[256,1280]{1,0:T(8,128)(2,1)S(1)}, bf16[256,1280]{1,0:T(8,128)(2,1)}, u32[]{:S(2)}, u32[]{:S(2)}) collective-permute-start(bf16[256,1280]{1,0:T(8,128)(2,1)S(1)} %get-tuple-element.71), channel_id=1, source_target_pairs={{0,8},{8,0},{16,24},{24,16},{32,40},{40,32},{48,56},{56,48},{64,72... | collective-permute-start | bytes 1966088 | tf_op jit(solution)/shard_map/ppermute | solution.py:396
  50.7 0.1 pad_add_fusion.place
  50.8 0.1 add_select_fusion.bias_ref
  50.9 5.7 %collective-permute-done.5.w3.rest_2_ = bf16[256,1280]{1,0:T(8,128)(2,1)} collective-permute-done((bf16[256,1280]{1,0:T(8,128)(2,1)}, bf16[256,1280]{1,0:T(8,128)(2,1)}, u32[]{:S(2)}, u32[]{:S(2)}) %collective-permute-start.5) | collective-permute-done | bytes 655392 | tf_op jit(solution)/shard_map/ppermute | solution.py:391
  56.6 0.0 collective-permute-done.4.w2.rest_1_
  56.6 3.0 %stats_own.1 = f32[16,256]{1,0:T(8,128)S(1)} custom-call(f32[4]{0:T(128)S(1)} %add_select_fusion.bias_ref, bf16[256,1408]{1,0:T(8,128)(2,1)S(1)} %bitcast.18, bf16[256,1408]{1,0:T(8,128)(2,1)S(1)} %bitcast.19, bf16[256,2560]{1,0:T(8,128)(2,1)S(1)} %bitcast.13, bf16[256,1280]{1,0:T(8,128)(2,1)} %collective-permute-done.4.w2.rest_1_, ...), custom_call_target="tpu_custom_call" | custom-call | flops 671088640 | bytes 1638400 | tf_op jit(solution)/shard_map/stats_own/pallas_call | solution.py:153
  59.6 8.8 %collective-permute-start.7 = (f32[16,256]{1,0:T(8,128)S(1)}, f32[16,256]{1,0:T(8,128)S(1)}, u32[]{:S(2)}, u32[]{:S(2)}) collective-permute-start(f32[16,256]{1,0:T(8,128)S(1)} %stats_own.1), channel_id=1, source_target_pairs={{0,4},{1,5},{2,6},{3,7},{4,0},{5,1},{6,2},{7,3},{8,12},{9,13},{10,... | collective-permute-start | bytes 49160 | tf_op jit(solution)/shard_map/ppermute | solution.py:385
  68.4 8.0 %collective-permute-done.6.tokens = bf16[256,1408]{1,0:T(8,128)(2,1)S(1)} collective-permute-done((bf16[256,1408]{1,0:T(8,128)(2,1)S(1)}, bf16[256,1408]{1,0:T(8,128)(2,1)S(1)}, u32[]{:S(2)}, u32[]{:S(2)}) %collective-permute-start.6) | collective-permute-done | bytes 720928 | tf_op jit(solution)/shard_map/ppermute | solution.py:385
  76.4 3.0 %stats_far.1.one = f32[16,256]{1,0:T(8,128)S(1)} custom-call(f32[4]{0:T(128)S(1)} %add_select_fusion.bias_ref, bf16[256,1408]{1,0:T(8,128)(2,1)S(1)} %collective-permute-done.6.tokens, bf16[256,1408]{1,0:T(8,128)(2,1)S(1)} %bitcast.20, bf16[256,2560]{1,0:T(8,128)(2,1)S(1)} %bitcast.14, bf16[256,1280]{1,0:T(8,128)(2,1)} %collective-permute-done.4.w2.rest_1_, ...), custom_call_target="tpu_custom_call" | custom-call | flops 671088640 | bytes 1638400 | tf_op jit(solution)/shard_map/stats_far/pallas_call | solution.py:153
  79.4 5.9 %collective-permute-start.8 = (f32[16,256]{1,0:T(8,128)S(1)}, f32[16,256]{1,0:T(8,128)S(1)}, u32[]{:S(2)}, u32[]{:S(2)}) collective-permute-start(f32[16,256]{1,0:T(8,128)S(1)} %stats_far.1.one), channel_id=1, source_target_pairs={{0,4},{1,5},{2,6},{3,7},{4,0},{5,1},{6,2},{7,3},{8,12},{9,13},{10,... | collective-permute-start | bytes 49160 | tf_op jit(solution)/shard_map/ppermute | solution.py:385
  85.3 0.0 collective-permute-done.7.other
  85.3 7.0 %grads_far.1 = (bf16[256,640]{1,0:T(8,128)(2,1)S(1)}, bf16[256,1280]{1,0:T(8,128)(2,1)}, bf16[256,1280]{1,0:T(8,128)(2,1)}, bf16[256,1280]{1,0:T(8,128)(2,1)}, bf16[256,1280]{1,0:T(8,128)(2,1)}) custom-call(f32[4]{0:T(128)S(1)} %add_select_fusion.bias_ref, s32[2]{0:T(128)S(1)} %pad_add_fusion.place, f32[16,256]{1,0:T(8,128)S(1)} %stats_far.1.one, ...), custom_call_target="tpu_custom_call" | custom-call | flops 1677721600 | bytes 3932160 | tf_op jit(solution)/shard_map/grads_far/pallas_call | solution.py:278
  92.3 0.0 collective-permute-done.8
  92.3 3.3 %collective-permute-start.9 = (bf16[256,640]{1,0:T(8,128)(2,1)S(1)}, bf16[256,640]{1,0:T(8,128)(2,1)S(1)}, u32[]{:S(2)}, u32[]{:S(2)}) collective-permute-start(bf16[256,640]{1,0:T(8,128)(2,1)S(1)} %get-tuple-element.66), channel_id=1, source_target_pairs={{0,4},{1,5},{2,6},{3,7},{4,0},{5,1},{6,2},{7,3},{8,12},{9,13},{10,... | collective-permute-start | bytes 983048 | tf_op jit(solution)/shard_map/ppermute | solution.py:385
  95.6 39.0 %conditional.1 = (f32[256,640]{1,0:T(8,128)S(1)}, bf16[256,1280]{1,0:T(8,128)(2,1)S(1)}, bf16[256,1280]{1,0:T(8,128)(2,1)}, bf16[256,1280]{1,0:T(8,128)(2,1)}) conditional(s32[]{:T(128)} %convert_element_type.4, () %tuple.16, (f32[4]{0:T(128)S(1)}, s32[2]{0:T(128)S(1)}, f32[16,256]{1,0:T(8,128)S(1)}, f32[16,256]{1,0:T(8,128)S(1)}, ...), branch_computations={%region_0.1_spmd, %region_1.2_spmd} | conditional | flops 1678704640 | bytes 23593168 | solution.py:454
  95.6 0.0 copy-start
  95.7 0.0 copy-start.1
  95.7 5.5 %grads_own23.1 = (f32[256,640]{1,0:T(8,128)S(1)}, bf16[256,1280]{1,0:T(8,128)(2,1)S(1)}, bf16[256,1280]{1,0:T(8,128)(2,1)S(1)}) custom-call(f32[4]{0:T(128)S(1)} %get-tuple-element.26.bias_ref, s32[2]{0:T(128)S(1)} %get-tuple-element.27.place, f32[16,256]{1,0:T(8,128)S(1)} %get-tuple-element.28.one, f32[16,256]{1,0:T(8,128)S(1)} %get-tuple-element.29.other, ...), custom_call_target="tpu_custom_call" | custom-call | flops 838860800 | bytes 3932160 | tf_op jit(solution)/shard_map/cond/branch_1_fun/grads_own23/pallas_call | solution.py:278
  101.2 3.1 %collective-permute-start = (bf16[256,1280]{1,0:T(8,128)(2,1)S(1)}, bf16[256,1280]{1,0:T(8,128)(2,1)S(1)}, u32[]{:S(2)}, u32[]{:S(2)}) collective-permute-start(bf16[256,1280]{1,0:T(8,128)(2,1)S(1)} %get-tuple-element.43), channel_id=1, source_target_pairs={{0,8},{8,0},{16,24},{24,16},{32,40},{40,32},{48,56},{56,48},{64,72... | collective-permute-start | bytes 1966088 | tf_op jit(solution)/shard_map/cond/branch_1_fun/ppermute | solution.py:396
  104.3 2.1 %collective-permute-start.1 = (bf16[256,1280]{1,0:T(8,128)(2,1)S(1)}, bf16[256,1280]{1,0:T(8,128)(2,1)}, u32[]{:S(2)}, u32[]{:S(2)}) collective-permute-start(bf16[256,1280]{1,0:T(8,128)(2,1)S(1)} %get-tuple-element.44), channel_id=1, source_target_pairs={{8,0},{16,8},{24,16},{32,24},{40,32},{48,40},{56,48},{64,56},{72,6... | collective-permute-start | bytes 1966088 | tf_op jit(solution)/shard_map/cond/branch_1_fun/ppermute | solution.py:391
  106.4 0.0 copy-done
  106.4 0.0 copy-done.1
  106.4 4.7 %grads_own01.1 = (f32[256,640]{1,0:T(8,128)S(1)}, bf16[256,1280]{1,0:T(8,128)(2,1)S(1)}, bf16[256,1280]{1,0:T(8,128)(2,1)S(1)}) custom-call(f32[4]{0:T(128)S(1)} %get-tuple-element.26.bias_ref, s32[2]{0:T(128)S(1)} %get-tuple-element.27.place, f32[16,256]{1,0:T(8,128)S(1)} %get-tuple-element.28.one, f32[16,256]{1,0:T(8,128)S(1)} %get-tuple-element.29.other, ...), custom_call_target="tpu_custom_call" | custom-call | flops 838860800 | bytes 3932160 | tf_op jit(solution)/shard_map/cond/branch_1_fun/grads_own01/pallas_call | solution.py:278
  111.1 0.0 collective-permute-done.swapped
  111.1 5.2 %collective-permute-done.1.side = bf16[256,1280]{1,0:T(8,128)(2,1)} collective-permute-done((bf16[256,1280]{1,0:T(8,128)(2,1)S(1)}, bf16[256,1280]{1,0:T(8,128)(2,1)}, u32[]{:S(2)}, u32[]{:S(2)}) %collective-permute-start.1) | collective-permute-done | bytes 655392 | tf_op jit(solution)/shard_map/cond/branch_1_fun/ppermute | solution.py:391
  116.3 1.3 fold.1
  117.6 3.6 %collective-permute-start.2 = (bf16[256,1280]{1,0:T(8,128)(2,1)S(1)}, bf16[256,1280]{1,0:T(8,128)(2,1)}, u32[]{:S(2)}, u32[]{:S(2)}) collective-permute-start(bf16[256,1280]{1,0:T(8,128)(2,1)S(1)} %fold.1), channel_id=1, source_target_pairs={{16,0},{24,8},{32,16},{40,24},{48,32},{56,40},{64,48},{72,56},{80,... | collective-permute-start | bytes 1966088 | tf_op jit(solution)/shard_map/cond/branch_1_fun/ppermute | solution.py:391
  121.2 13.4 %collective-permute-done.2 = bf16[256,1280]{1,0:T(8,128)(2,1)} collective-permute-done((bf16[256,1280]{1,0:T(8,128)(2,1)S(1)}, bf16[256,1280]{1,0:T(8,128)(2,1)}, u32[]{:S(2)}, u32[]{:S(2)}) %collective-permute-start.2) | collective-permute-done | bytes 655392 | tf_op jit(solution)/shard_map/cond/branch_1_fun/ppermute | solution.py:391
  134.6 0.0 collective-permute-done.9.dq_back
  134.6 2.2 %close.1 = bf16[4,64,1920]{2,1,0:T(8,128)(2,1)S(1)} custom-call(s32[1]{0:T(128)} %bitcast.even_ref, f32[256,640]{1,0:T(8,128)S(1)} %get-tuple-element.65.dq_own, bf16[256,640]{1,0:T(8,128)(2,1)S(1)} %collective-permute-done.9.dq_back, bf16[256,1280]{1,0:T(8,128)(2,1)S(1)} %get-tuple-element.67.d0, bf16[256,1280]{1,0:T(8,128)(2,1)} %get-tuple-element.68.back, ...), custom_call_target="tpu_custom_call" | custom-call | flops 983040 | bytes 3932160 | tf_op jit(solution)/shard_map/close/pallas_call | solution.py:337
  136.8 18.5 %all_to_all.15.parts = bf16[4,64,1920]{2,1,0:T(8,128)(2,1)S(1)} all-to-all(bf16[4,64,1920]{2,1,0:T(8,128)(2,1)S(1)} %close.1), channel_id=1, replica_groups={{0,1,2,3},{4,5,6,7},{8,9,10,11},{12,13,14,15},{16,17,18,19},{20,21,22,2..., dimensions={0} | all-to-all | bytes 1966080 | tf_op jit(solution)/shard_map/all_to_all | solution.py:380
  155.3 1.1 unpack.1
Async XLA Ops:
  1.8 19.6 %collective-permute-start.3 = (bf16[2,64,2560]{2,1,0:T(8,128)(2,1)S(1)}, bf16[2,64,2560]{2,1,0:T(8,128)(2,1)S(1)}, u32[]{:S(2)}, u32[]{:S(2)}) collective-permute-start(bf16[2,64,2560]{2,1,0:T(8,128)(2,1)S(1)} %pad_maximum_fusion.near), channel_id=1, source_target_pairs={{0,16},{8,24},{16,32},{24,40},{32,48},{40,56},{48,64},{56,72},{64,... | collective-permute-start | bytes 1966088 | tf_op jit(solution)/shard_map/ppermute | solution.py:391
  8.0 14.7 %all-to-all-start = ((bf16[4,64,1408]{2,1,0:T(8,128)(2,1)}), bf16[4,64,1408]{2,1,0:T(8,128)(2,1)S(1)}, u32[]{:S(2)}, u32[]{:S(2)}) async-start(bf16[4,64,1408]{2,1,0:T(8,128)(2,1)} %pack_queries.1), calls=%async_computation | async-start | bytes 1441792 | tf_op jit(solution)/shard_map/all_to_all | solution.py:380
  22.7 20.1 %all-to-all-start.1 = ((bf16[4,64,2560]{2,1,0:T(8,128)(2,1)}), bf16[4,64,2560]{2,1,0:T(8,128)(2,1)S(1)}, u32[]{:S(2)}, u32[]{:S(2)}) async-start(bf16[4,64,2560]{2,1,0:T(8,128)(2,1)} %pack_keys.1), calls=%async_computation.1 | async-start | bytes 2621440 | tf_op jit(solution)/shard_map/all_to_all | solution.py:380
  26.7 49.7 %collective-permute-start.6 = (bf16[256,1408]{1,0:T(8,128)(2,1)S(1)}, bf16[256,1408]{1,0:T(8,128)(2,1)S(1)}, u32[]{:S(2)}, u32[]{:S(2)}) collective-permute-start(bf16[256,1408]{1,0:T(8,128)(2,1)S(1)} %bitcast.17), channel_id=1, source_target_pairs={{0,4},{1,5},{2,6},{3,7},{4,0},{5,1},{6,2},{7,3},{8,12},{9,13},{10,... | collective-permute-start | bytes 2162696 | tf_op jit(solution)/shard_map/ppermute | solution.py:385
  43.7 12.9 %collective-permute-start.5 = (bf16[256,1280]{1,0:T(8,128)(2,1)}, bf16[256,1280]{1,0:T(8,128)(2,1)}, u32[]{:S(2)}, u32[]{:S(2)}) collective-permute-start(bf16[256,1280]{1,0:T(8,128)(2,1)} %get-tuple-element.70), channel_id=1, source_target_pairs={{0,8},{8,16},{16,24},{24,32},{32,40},{40,48},{48,56},{56,64},{64,7... | collective-permute-start | bytes 1966088 | tf_op jit(solution)/shard_map/ppermute | solution.py:391
  48.8 7.8 %collective-permute-start.4 = (bf16[256,1280]{1,0:T(8,128)(2,1)S(1)}, bf16[256,1280]{1,0:T(8,128)(2,1)}, u32[]{:S(2)}, u32[]{:S(2)}) collective-permute-start(bf16[256,1280]{1,0:T(8,128)(2,1)S(1)} %get-tuple-element.71), channel_id=1, source_target_pairs={{0,8},{8,0},{16,24},{24,16},{32,40},{40,32},{48,56},{56,48},{64,72... | collective-permute-start | bytes 1966088 | tf_op jit(solution)/shard_map/ppermute | solution.py:396
  59.6 25.7 %collective-permute-start.7 = (f32[16,256]{1,0:T(8,128)S(1)}, f32[16,256]{1,0:T(8,128)S(1)}, u32[]{:S(2)}, u32[]{:S(2)}) collective-permute-start(f32[16,256]{1,0:T(8,128)S(1)} %stats_own.1), channel_id=1, source_target_pairs={{0,4},{1,5},{2,6},{3,7},{4,0},{5,1},{6,2},{7,3},{8,12},{9,13},{10,... | collective-permute-start | bytes 49160 | tf_op jit(solution)/shard_map/ppermute | solution.py:385
  79.4 12.9 %collective-permute-start.8 = (f32[16,256]{1,0:T(8,128)S(1)}, f32[16,256]{1,0:T(8,128)S(1)}, u32[]{:S(2)}, u32[]{:S(2)}) collective-permute-start(f32[16,256]{1,0:T(8,128)S(1)} %stats_far.1.one), channel_id=1, source_target_pairs={{0,4},{1,5},{2,6},{3,7},{4,0},{5,1},{6,2},{7,3},{8,12},{9,13},{10,... | collective-permute-start | bytes 49160 | tf_op jit(solution)/shard_map/ppermute | solution.py:385
  92.3 42.3 %collective-permute-start.9 = (bf16[256,640]{1,0:T(8,128)(2,1)S(1)}, bf16[256,640]{1,0:T(8,128)(2,1)S(1)}, u32[]{:S(2)}, u32[]{:S(2)}) collective-permute-start(bf16[256,640]{1,0:T(8,128)(2,1)S(1)} %get-tuple-element.66), channel_id=1, source_target_pairs={{0,4},{1,5},{2,6},{3,7},{4,0},{5,1},{6,2},{7,3},{8,12},{9,13},{10,... | collective-permute-start | bytes 983048 | tf_op jit(solution)/shard_map/ppermute | solution.py:385
  95.6 10.7 %copy-start = (bf16[256,1280]{1,0:T(8,128)(2,1)S(1)}, bf16[256,1280]{1,0:T(8,128)(2,1)}, u32[]{:S(2)}) copy-start(bf16[256,1280]{1,0:T(8,128)(2,1)} %get-tuple-element.32.rest_1_) | copy-start | bytes 1966084 | tf_op jit(solution)/shard_map/cond
  95.7 10.7 %copy-start.1 = (bf16[256,1280]{1,0:T(8,128)(2,1)S(1)}, bf16[256,1280]{1,0:T(8,128)(2,1)}, u32[]{:S(2)}) copy-start(bf16[256,1280]{1,0:T(8,128)(2,1)} %get-tuple-element.33.rest_2_) | copy-start | bytes 1966084 | tf_op jit(solution)/shard_map/cond
  101.2 9.9 %collective-permute-start = (bf16[256,1280]{1,0:T(8,128)(2,1)S(1)}, bf16[256,1280]{1,0:T(8,128)(2,1)S(1)}, u32[]{:S(2)}, u32[]{:S(2)}) collective-permute-start(bf16[256,1280]{1,0:T(8,128)(2,1)S(1)} %get-tuple-element.43), channel_id=1, source_target_pairs={{0,8},{8,0},{16,24},{24,16},{32,40},{40,32},{48,56},{56,48},{64,72... | collective-permute-start | bytes 1966088 | tf_op jit(solution)/shard_map/cond/branch_1_fun/ppermute | solution.py:396
  104.3 12.0 %collective-permute-start.1 = (bf16[256,1280]{1,0:T(8,128)(2,1)S(1)}, bf16[256,1280]{1,0:T(8,128)(2,1)}, u32[]{:S(2)}, u32[]{:S(2)}) collective-permute-start(bf16[256,1280]{1,0:T(8,128)(2,1)S(1)} %get-tuple-element.44), channel_id=1, source_target_pairs={{8,0},{16,8},{24,16},{32,24},{40,32},{48,40},{56,48},{64,56},{72,6... | collective-permute-start | bytes 1966088 | tf_op jit(solution)/shard_map/cond/branch_1_fun/ppermute | solution.py:391
  117.6 17.0 %collective-permute-start.2 = (bf16[256,1280]{1,0:T(8,128)(2,1)S(1)}, bf16[256,1280]{1,0:T(8,128)(2,1)}, u32[]{:S(2)}, u32[]{:S(2)}) collective-permute-start(bf16[256,1280]{1,0:T(8,128)(2,1)S(1)} %fold.1), channel_id=1, source_target_pairs={{16,0},{24,8},{32,16},{40,24},{48,32},{56,40},{64,48},{72,56},{80,... | collective-permute-start | bytes 1966088 | tf_op jit(solution)/shard_map/cond/branch_1_fun/ppermute | solution.py:391
